TPU v7x, 128 devices: a whole 4x4x4 slice. The times are simulated.
128 devices in a mesh: row: 32 (over z, x, core), col: 4 (over y).
Axes of the slice: x: 4, y: 4, z: 4, core: 2. Of those that a mesh axis runs over, the one named last changes fastest.
Arguments:
- front: float32 [8192, 8192], P('row', 'col'), as said below
- ancestor_front: float32 [8192, 8192], P('row', 'col'), may hold values from -6 to 6
- tile_map: int32 [32], replicated, may hold values from 0 to 31, as said below
Outputs:
- panel_factor: float32 [8192, 512], P('row')
- updated: float32 [8192, 8192], P('row', 'col')
Inputs may be any that keep to these rules, and one draw needn't show every extreme that they name: front is symmetric and positive definite. Each tile column is named once; of the 8 tile columns j of one index of col, the numbers whose tile_map[j] lies in the block of each index of col differ from one another by at most one, so none exceeds 2.
All inputs are finite; a program needn't handle non-finite values.
Results may differ from a plain program's by a relative error of at most 0.0001.
Values sent between devices are 32-bit elements; how exact they have to be, the bound alone decides.
No kernel may reach another device: no remote copies, remote signals or barrier semaphores. Data moves between devices by JAX's collectives and lax.ppermute only.
A program may use at most 64 MiB of HBM per device.

v0:
```python
import jax
import jax.numpy as jnp
from jax import lax
from jax.sharding import PartitionSpec as P

PW = 256
PANELS = 2


def broadcast(block, axis, holder):
    block = jnp.where(lax.axis_index(axis) == holder, block, jnp.zeros_like(block))
    return lax.psum(block, axis)


def shards(front, ancestor_front, tile_map):
    rows_local, col_width = front.shape
    width = PW
    row_index = lax.axis_index("row")
    col_index = lax.axis_index("col")
    global_rows = row_index * rows_local + jnp.arange(rows_local, dtype=jnp.int32)
    global_cols = col_index * col_width + jnp.arange(col_width, dtype=jnp.int32)
    current = front
    panels = []
    for panel in range(PANELS):
        lower = panel * width
        upper = lower + width
        column_block = broadcast(current[:, lower:upper], "col", 0)
        holder_row = lower // rows_local
        offset = lower % rows_local
        diag_block = broadcast(column_block, "row", holder_row)
        factor = jnp.linalg.cholesky(diag_block)
        inverse = jax.scipy.linalg.solve_triangular(
            factor, jnp.eye(width, dtype=jnp.float32), lower=True
        )
        solved = lax.dot_general(
            column_block, inverse, (((1,), (1,)), ((), ())), precision=lax.Precision.HIGHEST
        )
        solved = jnp.where((global_rows >= lower)[:, None], solved, jnp.float32(0.0))
        panels.append(solved)
        trailing = jnp.where((global_rows >= upper)[:, None], solved, jnp.float32(0.0))
        everything = lax.all_gather(trailing, "row", axis=0, tiled=True)
        across = lax.dynamic_slice_in_dim(everything, col_index * col_width, col_width, 0)
        current = current - lax.dot_general(
            trailing, across, (((1,), (1,)), ((), ())), precision=lax.Precision.HIGHEST
        )
    limit = PANELS * width
    keep = (global_rows >= limit)[:, None] & (global_cols >= limit)[None, :]
    schur = jnp.where(keep, current, jnp.float32(0.0))
    mine = col_width // width
    local_ids = jnp.arange(mine, dtype=jnp.int32)
    wanted = col_index * mine + local_ids
    whole = lax.all_gather(schur, "col", axis=1, tiled=True)
    total_tiles = whole.shape[1] // width
    match = tile_map[None, :] == wanted[:, None]
    source = jnp.sum(jnp.where(match, jnp.arange(total_tiles, dtype=jnp.int32)[None, :], 0), axis=1)
    tiles = whole.reshape(rows_local, total_tiles, width)
    picked = jnp.take(tiles, source, axis=1).reshape(rows_local, col_width)
    return (jnp.concatenate(panels, axis=1), ancestor_front + picked)


def solution(mesh):
    return jax.shard_map(
        shards,
        mesh=mesh,
        in_specs=(P("row", "col"), P("row", "col"), P()),
        out_specs=(P("row", None), P("row", "col")),
        check_vma=False,
    )
```

profile of v0, /device:TPU:1, one launch (start us, length us, event | category | flops | bytes accessed | tf_op | source)
XLA Modules:
  0.0 671.3 jit_solution(15059203651956142202)
XLA Ops:
  7.2 1.9 copy.13
  9.2 0.8 slice_select_fusion.1
  10.0 0.0 all-reduce.8.cloned.1.call-start
  10.0 43.6 %all-reduce.6.cloned.1.call-done = f32[256,256]{0,1:T(8,128)} async-done(((f32[256,256]{0,1:T(8,128)}), f32[256,256]{0,1:T(8,128)}) %all-reduce.6.cloned.1.call-update) | async-done | bytes 262160 | tf_op jit(solution)/shard_map/psum | solution.py:12
  53.7 0.7 broadcast_select_fusion.3
  54.4 0.0 all-gather.4.cloned.1.call-start
  54.5 107.5 %all-reduce.8.cloned.1.call-done = f32[256,256]{0,1:T(8,128)} async-done(((f32[256,256]{0,1:T(8,128)}), f32[256,256]{0,1:T(8,128)}) %all-reduce.8.cloned.1.call-update) | async-done | bytes 262160 | tf_op jit(solution)/shard_map/psum | solution.py:12
  162.0 1.1 copy.14
  163.0 1.0 fusion.10
  164.1 11.7 %cholesky.130 = f32[128,128]{1,0:T(8,128)S(1)} custom-call(f32[128,128]{1,0:T(8,128)S(1)} %cholesky.194), custom_call_target="Cholesky" | custom-call | tf_op jit(solution)/shard_map/jit(cholesky)/cholesky | solution.py:31
  175.8 9.8 %custom-call.13 = f32[1,128,128]{1,2,0:T(8,128)S(1)} custom-call(f32[1,128,128]{2,1,0:T(8,128)S(1)} %get-tuple-element.51), custom_call_target="InvertDiagBlocksLowerTriangular" | custom-call | tf_op jit(solution)/shard_map/jit(cholesky)/cholesky | solution.py:31
  185.7 0.2 constant_dynamic-update-slice_fusion.3
  185.9 0.3 convolution_subtract_fusion.5
  186.1 11.7 %cholesky.147 = f32[128,128]{1,0:T(8,128)S(1)} custom-call(f32[128,128]{1,0:T(8,128)S(1)} %convolution_subtract_fusion.5), custom_call_target="Cholesky" | custom-call | tf_op jit(solution)/shard_map/jit(cholesky)/cholesky | solution.py:31
  197.9 0.6 compare_reduce_fusion.2
  199.8 0.1 triangular_solve.75
  199.8 4.3 while.4
  200.3 0.6 fusion.49
  200.9 1.3 bitcast_dynamic-update-slice_fusion.4
  202.2 0.6 fusion.49
  202.8 1.3 bitcast_dynamic-update-slice_fusion.4
  204.1 19.7 %custom-call.14 = f32[2,128,128]{1,2,0:T(8,128)S(1)} custom-call(f32[2,128,128]{2,1,0:T(8,128)S(1)} %get-tuple-element.18), custom_call_target="InvertDiagBlocksLowerTriangular" | custom-call | tf_op jit(solution)/shard_map/jit(_solve_triangular)/triangular_solve | solution.py:32
  223.8 0.3 fusion.14
  224.1 0.3 convolution_subtract_fusion.3
  224.4 0.3 fusion.21
  224.7 1.1 broadcast_select_fusion.2
  225.9 59.7 %all-gather.4.cloned.1.call-done = f32[8192,256]{0,1:T(8,128)} async-done(((f32[256,256]{0,1:T(8,128)}), f32[8192,256]{0,1:T(8,128)}) %all-gather.4.cloned.1.call-update) | async-done | bytes 8388624 | tf_op jit(solution)/shard_map/all_gather | solution.py:41
  285.6 5.7 convolution_subtract_fusion.1
  291.3 0.7 slice_select_fusion
  292.1 0.0 all-reduce.12.cloned.1.call-start
  292.1 38.8 %all-reduce.10.cloned.1.call-done = f32[256,256]{0,1:T(8,128)} async-done(((f32[256,256]{0,1:T(8,128)}), f32[256,256]{0,1:T(8,128)}) %all-reduce.10.cloned.1.call-update) | async-done | bytes 262160 | tf_op jit(solution)/shard_map/psum | solution.py:12
  331.0 1.7 broadcast_select_fusion.1
  332.7 0.2 all-gather.6.cloned.1.call-start
  332.9 106.2 %all-reduce.12.cloned.1.call-done = f32[256,256]{0,1:T(8,128)} async-done(((f32[256,256]{0,1:T(8,128)}), f32[256,256]{0,1:T(8,128)}) %all-reduce.12.cloned.1.call-update) | async-done | bytes 262160 | tf_op jit(solution)/shard_map/psum | solution.py:12
  439.1 1.1 copy.17
  440.2 1.0 fusion.9
  441.2 11.7 %cholesky.164 = f32[128,128]{1,0:T(8,128)S(1)} custom-call(f32[128,128]{1,0:T(8,128)S(1)} %cholesky.197), custom_call_target="Cholesky" | custom-call | tf_op jit(solution)/shard_map/jit(cholesky)/cholesky | solution.py:31
  453.0 9.8 %custom-call.15 = f32[1,128,128]{1,2,0:T(8,128)S(1)} custom-call(f32[1,128,128]{2,1,0:T(8,128)S(1)} %get-tuple-element.47), custom_call_target="InvertDiagBlocksLowerTriangular" | custom-call | tf_op jit(solution)/shard_map/jit(cholesky)/cholesky | solution.py:31
  462.8 1.0 constant_dynamic-update-slice_fusion.1
  463.9 1.1 convolution_subtract_fusion.4
  465.0 11.7 %cholesky.181 = f32[128,128]{1,0:T(8,128)S(1)} custom-call(f32[128,128]{1,0:T(8,128)S(1)} %convolution_subtract_fusion.4), custom_call_target="Cholesky" | custom-call | tf_op jit(solution)/shard_map/jit(cholesky)/cholesky | solution.py:31
  476.7 0.6 compare_reduce_fusion
  477.4 0.6 compare_reduce_fusion.1
  479.4 4.2 while.5
  479.6 0.6 fusion.50
  480.2 1.4 bitcast_dynamic-update-slice_fusion.5
  481.6 0.6 fusion.50
  482.2 1.4 bitcast_dynamic-update-slice_fusion.5
  483.6 19.7 %custom-call.16 = f32[2,128,128]{1,2,0:T(8,128)S(1)} custom-call(f32[2,128,128]{2,1,0:T(8,128)S(1)} %get-tuple-element.19), custom_call_target="InvertDiagBlocksLowerTriangular" | custom-call | tf_op jit(solution)/shard_map/jit(_solve_triangular)/triangular_solve | solution.py:32
  503.3 0.3 fusion.12
  503.6 0.3 convolution_subtract_fusion.2
  503.9 0.3 fusion.17
  504.2 1.1 broadcast_select_fusion
  505.3 0.0 all-gather.8.cloned.1.call-start
  505.4 59.7 %all-gather.6.cloned.1.call-done = f32[8192,256]{0,1:T(8,128)} async-done(((f32[256,256]{0,1:T(8,128)}), f32[8192,256]{0,1:T(8,128)}) %all-gather.6.cloned.1.call-update) | async-done | bytes 8388624 | tf_op jit(solution)/shard_map/all_gather | solution.py:41
  565.0 6.8 %fusion = f32[256,2048]{0,1:T(8,128)} fusion(f32[256,2048]{0,1:T(8,128)S(1)} %convolution_subtract_fusion.1, f32[8192,256]{0,1:T(8,128)} %all-gather.6.cloned.1.call-done, s32[]{:T(128)S(6)} %select_n.79, pred[256]{0:T(512)(128)(4,1)S(1)} %fusion.28, pred[2048]{0:T(1024)(128)(4,1)S(1)} %add_compare_fusion, f32[256,256]{0,1:T(8,128)S(1)} %get-tuple-element.59), kind=kOutput, calls=%fused_computation.6 | convolution fusion | flops 1612251136 | bytes 6556676 | tf_op jit(solution)/shard_map/dot_general | solution.py:43
  571.9 0.6 copy-done.4
  572.5 0.2 select_reduce_fusion.4
  572.7 0.1 broadcast_in_dim.70
  572.9 1.0 copy.20
  573.9 80.6 %all-gather.8.cloned.1.call-done = f32[256,8192]{0,1:T(8,128)} async-done(((f32[256,2048]{0,1:T(8,128)}), f32[256,8192]{0,1:T(8,128)}) %all-gather.8.cloned.1.call-update) | async-done | bytes 8388624 | tf_op jit(solution)/shard_map/all_gather | solution.py:52
  654.4 4.1 gather_fusion
  658.5 1.8 copy.23
  660.3 4.0 select_add_fusion
  (45 shorter events, 0.6 us)
Async XLA Ops:
  7.2 46.5 %all-reduce.6.cloned.1.call-start = ((), (), s32[]{:S(2)}) async-start(), calls=%async_computation | async-start | bytes 524288 | tf_op jit(solution)/shard_map/psum | solution.py:12
  9.1 177.0 %copy-start = (f32[256,2048]{0,1:T(8,128)}, f32[256,2048]{0,1:T(8,128)S(1)}, u32[]{:S(2)}) copy-start(f32[256,2048]{0,1:T(8,128)S(1)} %copy.13) | copy-start | bytes 6291460
  10.0 152.0 %all-reduce.8.cloned.1.call-start = ((), (), s32[]{:S(2)}) async-start(), calls=%async_computation.1 | async-start | bytes 524288 | tf_op jit(solution)/shard_map/psum | solution.py:12
  54.4 231.2 %all-gather.4.cloned.1.call-start = ((), (), s32[]{:S(2)}) async-start(), calls=%async_computation.2 | async-start | bytes 8650752 | tf_op jit(solution)/shard_map/all_gather | solution.py:41
  164.0 60.7 %copy-start.1 = (f32[256,256]{0,1:T(8,128)S(1)}, f32[256,256]{0,1:T(8,128)}, u32[]{:S(2)}) copy-start(f32[256,256]{0,1:T(8,128)} %all-reduce.6.cloned.1.call-done) | copy-start | bytes 786436
  225.8 105.1 %all-reduce.10.cloned.1.call-start = ((), (), s32[]{:S(2)}) async-start(), calls=%async_computation.3 | async-start | bytes 524288 | tf_op jit(solution)/shard_map/psum | solution.py:12
  292.1 147.0 %all-reduce.12.cloned.1.call-start = ((), (), s32[]{:S(2)}) async-start(), calls=%async_computation.4 | async-start | bytes 524288 | tf_op jit(solution)/shard_map/psum | solution.py:12
  332.7 232.4 %all-gather.6.cloned.1.call-start = ((), (), s32[]{:S(2)}) async-start(), calls=%async_computation.5 | async-start | bytes 8650752 | tf_op jit(solution)/shard_map/all_gather | solution.py:41
  441.2 11.7 %copy-start.3 = (f32[256,256]{1,0:T(8,128)}, f32[256,256]{1,0:T(8,128)S(1)}, u32[]{:S(2)}) copy-start(f32[256,256]{1,0:T(8,128)S(1)} %fusion.9) | copy-start | bytes 786436
  441.2 63.0 %copy-start.2 = (f32[256,256]{0,1:T(8,128)S(1)}, f32[256,256]{0,1:T(8,128)}, u32[]{:S(2)}) copy-start(f32[256,256]{0,1:T(8,128)} %all-reduce.10.cloned.1.call-done) | copy-start | bytes 786436
  505.3 149.1 %all-gather.8.cloned.1.call-start = ((), (), s32[]{:S(2)}) async-start(), calls=%async_computation.6 | async-start | bytes 10485760 | tf_op jit(solution)/shard_map/all_gather | solution.py:52
  571.9 0.7 copy-start.4
Sparse Core Ops, SparseCore 0:
  10.9 42.7 all-reduce.5
  57.8 104.1 all-reduce.7
  226.0 59.5 all-gather.3
  292.2 38.7 all-reduce.9
  335.0 104.1 all-reduce.11
  505.4 59.5 all-gather.5
  572.0 82.3 all-gather.7
where the time goes:
time: 680 us; the launch traced here: 671 us
  waiting for transfers between devices  496 us (73%)
  other arithmetic  118 us (17%)
  local copies, waits for them, and re-layouts  19.5 us (3%)
  matrix products  19.1 us (3%)
  between operations  17.2 us (3%)
    psum x4, waiting for transfers between devices, broadcast(): return lax.psum(block, axis)  296 us
    all_gather x2, waiting for transfers between devices, shards(): everything = lax.all_gather(trailing, 'row', axis=0, tiled=True)  119 us
    all_gather x1, waiting for transfers between devices, shards(): whole = lax.all_gather(schur, 'col', axis=1, tiled=True)  80.6 us
    another operation x13, other arithmetic, shards(): factor = jnp.linalg.cholesky(diag_block)  68.5 us
    another operation x5, other arithmetic, shards(): jax.scipy.linalg.solve_triangular(factor, jnp.eye(width, dtype=jnp.float3...  39.4 us
  transfers between devices with their start and end apart: 7, of which 7 were waited for; matrix products, arithmetic and copies ran while one was open for 0% of the time, Pallas kernels for 0%

commit v1 on v0

v1 whole, which is shorter than its diff:
```python
import jax
import jax.numpy as jnp
from jax import lax
from jax.experimental import pallas as pl
from jax.experimental.pallas import tpu as pltpu
from jax.sharding import PartitionSpec as P

PW = 256
LEAD = 512
HALF = 128
STEP = 8
HIGHEST = lax.Precision.HIGHEST


def dot(a, b, ca, cb):
    return lax.dot_general(
        a, b, (((ca,), (cb,)), ((), ())), precision=HIGHEST, preferred_element_type=jnp.float32
    )


def inverse_factor_128(block):
    n = HALF
    lane = lax.broadcasted_iota(jnp.int32, (STEP, n), 1)
    sub = lax.broadcasted_iota(jnp.int32, (STEP, n), 0)
    lane_all = lax.broadcasted_iota(jnp.int32, (n, n), 1)
    work = block
    for start in range(0, n, STEP):
        end = start + STEP
        top = work[start:end, :]
        columns = [jnp.broadcast_to(top[:, start + i : start + i + 1], (STEP, n)) for i in range(STEP)]
        entry = [
            [jnp.broadcast_to(columns[i][j : j + 1, :], (STEP, n)) if i <= j else None for i in range(STEP)]
            for j in range(STEP)
        ]
        inside = (lane >= start) & (lane < end)
        top = jnp.where(inside, jnp.where(lane - start == sub, 1.0, 0.0), top)
        rows = [jnp.broadcast_to(top[j : j + 1, :], (STEP, n)) for j in range(STEP)]
        done = [None] * STEP
        for i in range(STEP):
            scale = lax.rsqrt(entry[i][i])
            done[i] = rows[i] * scale
            below = [None] * STEP
            for j in range(i + 1, STEP):
                below[j] = entry[j][i] * scale
                for k in range(i + 1, j + 1):
                    entry[j][k] = entry[j][k] - below[j] * below[k]
            for j in range(i + 1, STEP):
                rows[j] = rows[j] - below[j] * done[i]
        solved = done[0]
        for i in range(1, STEP):
            solved = jnp.where(sub == i, done[i], solved)
        work = jnp.where((lane_all >= start) & (lane_all < end), 0.0, work)
        pieces = [work[:start]] if start else []
        pieces.append(solved)
        if end < n:
            ahead = jnp.where(lane >= end, solved, 0.0)
            pieces.append(work[end:] - dot(ahead, solved, 0, 0)[end:])
        work = jnp.concatenate(pieces, 0)
    return work


def inverse_factor_256(block):
    first = inverse_factor_128(block[:HALF, :HALF])
    across = dot(block[HALF:, :HALF], first, 1, 1)
    second = inverse_factor_128(block[HALF:, HALF:] - dot(across, across, 1, 1))
    lower = -dot(second, dot(across, first, 1, 0), 1, 0)
    return jnp.concatenate(
        [
            jnp.concatenate([first, jnp.zeros_like(first)], 1),
            jnp.concatenate([lower, second], 1),
        ],
        0,
    )


def factor_kernel(where_ref, own_ref, other_ref, rows_ref, panel_ref, weight_ref):
    row_index, core = where_ref[0], where_ref[1]
    even = core == 0
    own, other = own_ref[...], other_ref[...]
    zero = jnp.where(even, own, other)
    one = jnp.where(even, other, own)
    corner = zero[:, :PW]
    below = one[:, :PW]
    last = jnp.concatenate([zero[:, PW:], one[:, PW:]], 1)
    inv_a = inverse_factor_256(corner)
    across = dot(below, inv_a, 1, 1)
    inv_b = inverse_factor_256(last - dot(across, across, 1, 1))
    rows = rows_ref[...]
    panel_a = dot(rows[:, :PW], inv_a, 1, 1)
    panel_b = dot(rows[:, PW:] - dot(panel_a, across, 1, 1), inv_b, 1, 1)
    weight_b = dot(panel_b, inv_b, 1, 0)
    weight_a = dot(panel_a - dot(weight_b, across, 1, 0), inv_a, 1, 0)
    panel_ref[:, :PW] = panel_a
    panel_ref[:, PW:] = jnp.where(row_index == 0, 0.0, panel_b)
    weight_ref[:, :PW] = weight_a
    weight_ref[:, PW:] = weight_b


def factor(where, own, other, rows):
    whole = pl.BlockSpec(memory_space=pltpu.VMEM)
    return pl.pallas_call(
        factor_kernel,
        out_shape=[jax.ShapeDtypeStruct((PW, LEAD), jnp.float32)] * 2,
        in_specs=[pl.BlockSpec(memory_space=pltpu.SMEM), whole, whole, whole],
        out_specs=[whole, whole],
        compiler_params=pltpu.CompilerParams(vmem_limit_bytes=40 << 20),
        name="factor",
    )(where, own, other, rows)


def pick_kernel(index_ref, front_ref, *refs):
    outs, sem = refs[:-1], refs[-1]
    copies = []
    for place in range(2 * len(outs)):
        start = pl.multiple_of(index_ref[place] * PW, PW)
        half = (place % 2) * PW
        copies.append(
            pltpu.make_async_copy(
                front_ref.at[:, pl.ds(start, PW)],
                outs[place // 2].at[:, pl.ds(half, PW)],
                sem.at[place],
            )
        )
    for copy in copies:
        copy.start()
    for copy in copies:
        copy.wait()


def pick(index, front):
    anywhere = pl.BlockSpec(memory_space=pl.ANY)
    return pl.pallas_call(
        pick_kernel,
        out_shape=[jax.ShapeDtypeStruct((front.shape[0], 2 * PW), jnp.float32)] * 4,
        in_specs=[pl.BlockSpec(memory_space=pltpu.SMEM), anywhere],
        out_specs=[anywhere] * 4,
        scratch_shapes=[pltpu.SemaphoreType.DMA((8,))],
        name="pick",
    )(index, front)


def update_kernel(shift, group, place, live, weight_ref, p0, p1, p2, p3, ahead_ref, base_ref, out_ref):
    slot = pl.program_id(0)
    ahead = ahead_ref[...].reshape(PW, LEAD)
    product = dot(weight_ref[...], ahead, 1, 1)
    column = pl.multiple_of(place[slot] * PW, PW)
    base = base_ref[...]
    out_ref[...] = base
    for index, ref in enumerate((p0, p1, p2, p3)):

        @pl.when((shift[slot] == index) & (live[slot] == 1))
        def _():
            out_ref[...] = base + (ref[:, pl.ds(column, PW)] - product)


def update(shift, group, place, live, weight, pieces, ahead, base):
    rows, cols = base.shape
    full = pl.BlockSpec((rows, 2 * PW), lambda u, *s: (0, 0))
    tile = pl.BlockSpec((rows, PW), lambda u, *s: (0, u))
    return pl.pallas_call(
        update_kernel,
        out_shape=jax.ShapeDtypeStruct(base.shape, jnp.float32),
        grid_spec=pltpu.PrefetchScalarGridSpec(
            num_scalar_prefetch=4,
            grid=(cols // PW,),
            in_specs=[
                full,
                full,
                full,
                full,
                full,
                pl.BlockSpec((8, 1, 32, LEAD), lambda u, shift, group, place, live: (group[u], place[u], 0, 0)),
                tile,
            ],
            out_specs=tile,
        ),
        compiler_params=pltpu.CompilerParams(vmem_limit_bytes=40 << 20),
        name="update",
    )(shift, group, place, live, weight, *pieces, ahead, base)


def device(z, x, core, y):
    return ((z * 4 + x) * 2 + core) * 4 + y


def spread_steps():
    orders = ("yxz", "xzy")
    have = [{(0, 0, 0)}, {(0, 0, 0)}]
    steps = []
    for step in range(6):
        pairs = []
        for core in range(2):
            axis = "zxy".index(orders[core][step // 2])
            new = set()
            for at in sorted(have[core]):
                to = list(at)
                if step % 2 == 0:
                    to[axis] = 1
                else:
                    to[axis] = 3 if at[axis] == 0 else 2
                new.add(tuple(to))
                pairs.append((device(at[0], at[1], core, at[2]), device(to[0], to[1], core, to[2])))
            have[core] |= new
        steps.append(pairs)
    return steps


def shards(front, ancestor, tile_map):
    row = lax.axis_index("row")
    col = lax.axis_index("col")
    core = row % 2
    line = (row // 2) % 4
    plane = row // 8
    swap = [(i, i ^ 1) for i in range(32)]

    owner = (tile_map // 8).reshape(4, 8)
    ids = jnp.arange(8, dtype=jnp.int32)
    same = owner[:, :, None] == owner[:, None, :]
    rank = jnp.sum(jnp.where(same & (ids[None, None, :] < ids[None, :, None]), 1, 0), axis=2)
    cols4 = jnp.arange(4, dtype=jnp.int32)
    hit = (owner[:, None, None, :] == cols4[None, :, None, None]) & (
        rank[:, None, None, :] == jnp.arange(2, dtype=jnp.int32)[None, None, :, None]
    )
    chosen = jnp.sum(jnp.where(hit, ids, 0), axis=3)
    slots = col * 8 + ids
    found = tile_map[None, :] == slots[:, None]
    all_ids = jnp.arange(32, dtype=jnp.int32)
    source = jnp.sum(jnp.where(found, all_ids, 0), axis=1)
    place = jnp.sum(jnp.where(found, rank.reshape(32), 0), axis=1)
    group = source // 8
    shift = (col - group) % 4
    live = jnp.where((source >= 2) & (row >= 2), 1, 0).astype(jnp.int32)

    lead = front[:, :LEAD]
    mate = lax.ppermute(lead, "row", swap)

    tail = jnp.where(core == 0, mate[:, PW : PW + HALF], lead[:, PW + HALF :])
    block = jnp.concatenate([lead[:, :PW], tail], axis=1)
    block = jnp.where((row < 2) & (col == 0), block, 0.0)
    for pairs in spread_steps():
        block = block + lax.ppermute(block, ("row", "col"), pairs)
    other = lax.ppermute(block, "row", swap)

    even = jnp.where(core == 0, lead, mate)
    odd = jnp.where(core == 0, mate, lead)
    both = jnp.stack([even, odd])
    parts = []
    for hop in range(4):
        at = 32 * (2 * ((line + hop) % 4) + core)
        part = lax.dynamic_slice(both, (0, at, 0), (2, 32, LEAD))
        if hop:
            pairs = [(z * 8 + x * 2 + k, z * 8 + (x + hop) % 4 * 2 + k) for z in range(4) for x in range(4) for k in range(2)]
            part = lax.ppermute(part, "row", pairs)
        parts.append(part)
    parts = jnp.concatenate(parts, 0)
    mine = lax.dynamic_index_in_dim(chosen, plane, 0, keepdims=False)
    index = ((line - mine // 2) % 4) * 2 + mine % 2
    sent = jnp.take(parts, index, axis=0)
    kept = jnp.where(col == 0, sent[0], 0.0)
    for to in range(1, 4):
        kept = kept + lax.ppermute(sent[to], "col", [(0, to)])
    ahead = lax.all_gather(kept, "row", axis=0, tiled=False)

    rows = jnp.where(col == 0, lead, 0.0)
    rows = rows + lax.ppermute(rows, "col", [(0, 1)])
    rows = rows + lax.ppermute(rows, "col", [(0, 3), (1, 2)])

    own = lax.dynamic_index_in_dim(chosen, col, 0, keepdims=False)
    order = jnp.take(own, (col + cols4) % 4, axis=0).reshape(8)
    pieces = list(pick(order, front))
    for hop in range(1, 4):
        pieces[hop] = lax.ppermute(pieces[hop], "col", [(i, (i + hop) % 4) for i in range(4)])

    panel, weight = factor(jnp.stack([row, core]), block, other, rows)
    updated = update(shift, group, place, live, weight, pieces, ahead, ancestor)
    return panel, updated


def solution(mesh):
    return jax.shard_map(
        shards,
        mesh=mesh,
        in_specs=(P("row", "col"), P("row", "col"), P()),
        out_specs=(P("row", None), P("row", "col")),
        check_vma=False,
    )
```

time: 680 us -> 237 us (0.35)
  the two profiles are of different devices: /device:TPU:1 before, /device:TPU:60 now
where the time goes in v1:
time: 237 us; the launch traced here: 236 us
  Pallas kernels  111 us (47%)
  waiting for transfers between devices  73.4 us (31%)
  starting transfers between devices  17.5 us (7%)
  between operations  14.6 us (6%)
  other arithmetic  10.7 us (5%)
  local copies, waits for them, and re-layouts  8.88 us (4%)
    pallas_call x1, Pallas kernels, pick(): pl.pallas_call(pick_kernel, out_shape=[jax.ShapeDtypeStruct((front.shape[...  65.5 us
    ppermute x6, waiting for transfers between devices, shards(): block = block + lax.ppermute(block, ('row', 'col'), pairs)  38.5 us
    pallas_call x1, Pallas kernels, factor(): pl.pallas_call(factor_kernel, out_shape=[jax.ShapeDtypeStruct((PW, LEAD),...  36.7 us
    ppermute x1, waiting for transfers between devices, shards(): rows = rows + lax.ppermute(rows, 'col', [(0, 3), (1, 2)])  21.5 us
    pallas_call x1, Pallas kernels, update(): pl.pallas_call(update_kernel, out_shape=jax.ShapeDtypeStruct(base.shape,...  9.19 us
    ppermute x3, waiting for transfers between devices, shards(): part = lax.ppermute(part, 'row', pairs)  6.72 us
    ppermute x6, starting transfers between devices, shards(): block = block + lax.ppermute(block, ('row', 'col'), pairs)  6.1 us
    ppermute x3, waiting for transfers between devices, shards(): kept = kept + lax.ppermute(sent[to], 'col', [(0, to)])  6.09 us
  transfers between devices with their start and end apart: 20, of which 7 were waited for; matrix products, arithmetic and copies ran while one was open for 4% of the time, Pallas kernels for 43%

profile of v1, /device:TPU:60, one launch (start us, length us, event | category | flops | bytes accessed | tf_op | source)
XLA Modules:
  0.0 236.5 jit_solution(18014203721631856410)
XLA Ops:
  7.2 0.0 all-gather.3.cloned.1.call-start
  7.2 1.1 slice.27
  8.3 0.1 collective-permute-start
  8.5 0.7 and_select_fusion.9
  9.2 0.1 eq.93
  9.3 0.2 select_reduce_fusion.1
  9.5 0.2 select_reduce_fusion
  9.8 0.5 collective-permute-done
  10.3 1.4 select_bitcast_fusion
  11.8 1.3 collective-permute-start.13
  13.1 0.8 collective-permute-start.14
  13.9 1.1 collective-permute-start.15
  15.0 0.1 copy.15
  15.1 0.1 copy.16
  15.2 0.1 reshape.270
  15.3 2.4 %collective-permute-done.13 = f32[2,32,512]{2,1,0:T(8,128)S(1)} collective-permute-done((f32[2,32,512]{2,1,0:T(8,128)S(1)}, f32[2,32,512]{2,1,0:T(8,128)S(1)}, u32[]{:S(2)}, u32[]{:S(2)}) %collective-permute-start.13) | collective-permute-done | bytes 131104 | tf_op jit(solution)/shard_map/ppermute | solution.py:253
  17.7 2.5 %collective-permute-done.14 = f32[2,32,512]{2,1,0:T(8,128)S(1)} collective-permute-done((f32[2,32,512]{2,1,0:T(8,128)S(1)}, f32[2,32,512]{2,1,0:T(8,128)S(1)}, u32[]{:S(2)}, u32[]{:S(2)}) %collective-permute-start.14) | collective-permute-done | bytes 131104 | tf_op jit(solution)/shard_map/ppermute | solution.py:253
  20.2 1.8 collective-permute-done.15
  22.1 0.0 copy-start.6
  22.1 0.0 slice-start
  22.1 1.4 gather_fusion.1
  23.5 1.1 broadcast_select_fusion
  24.7 0.7 collective-permute-start.16
  25.3 1.3 collective-permute-start.18
  26.6 0.7 collective-permute-start.17
  27.3 6.1 %collective-permute-done.18 = f32[2,32,512]{2,1,0:T(8,128)S(1)} collective-permute-done((f32[2,32,512]{2,1,0:T(8,128)S(1)}, f32[2,32,512]{2,1,0:T(8,128)S(1)}, u32[]{:S(2)}, u32[]{:S(2)}) %collective-permute-start.18) | collective-permute-done | bytes 131104 | tf_op jit(solution)/shard_map/ppermute | solution.py:261
  33.4 0.7 fusion.7
  34.1 0.0 all-gather.3.cloned.1.call-update
  34.2 0.9 slice_select_fusion.1
  35.1 0.7 collective-permute-start.1
  35.9 0.7 collective-permute-start.2
  36.7 0.7 collective-permute-start.3
  37.4 0.1 add.237
  37.4 0.7 collective-permute-start.4
  38.2 1.3 collective-permute-start.5
  39.5 0.1 copy.14
  39.6 0.7 collective-permute-start.8
  40.3 0.6 gather_fusion
  40.9 38.5 %collective-permute-done.5 = f32[256,384]{1,0:T(8,128)S(1)} collective-permute-done((f32[256,384]{1,0:T(8,128)S(1)}, f32[256,384]{1,0:T(8,128)S(1)}, u32[]{:S(2)}, u32[]{:S(2)}) %collective-permute-start.5) | collective-permute-done | bytes 393248 | tf_op jit(solution)/shard_map/ppermute | solution.py:241
  79.4 0.8 add.239
  80.2 2.1 collective-permute-start.6
  82.3 0.1 broadcast_select_fusion.2
  82.3 0.6 select_n.264.index_ref
  82.9 65.5 %pick.1 = (f32[256,512]{1,0:T(8,128)}, f32[256,512]{1,0:T(8,128)}, f32[256,512]{1,0:T(8,128)}, f32[256,512]{1,0:T(8,128)}) custom-call(s32[8]{0:T(128)} %select_n.264.index_ref, f32[256,2048]{1,0:T(8,128)} %front_ref.1), custom_call_target="tpu_custom_call" | custom-call | tf_op jit(solution)/shard_map/pick/pallas_call | solution.py:132
  148.5 0.5 collective-permute-start.10
  148.9 2.5 %collective-permute-start.11 = (f32[256,512]{1,0:T(8,128)}, f32[256,512]{1,0:T(8,128)}, u32[]{:S(2)}, u32[]{:S(2)}) collective-permute-start(f32[256,512]{1,0:T(8,128)} %get-tuple-element.12), channel_id=1, source_target_pairs={{0,2},{1,3},{2,0},{3,1},{4,6},{5,7},{6,4},{7,5},{8,10},{9,11},{10,... | collective-permute-start | bytes 1572872 | tf_op jit(solution)/shard_map/ppermute | solution.py:272
  151.4 0.9 add.241
  152.3 1.5 collective-permute-start.9
  153.9 1.2 add.240.own_ref
  155.0 0.3 collective-permute-start.7
  155.3 0.6 pad_add_fusion.where_ref
  155.9 0.1 reshape.259
  156.0 0.2 fusion.9
  156.2 21.5 %collective-permute-done.9 = f32[256,512]{1,0:T(8,128)} collective-permute-done((f32[256,512]{1,0:T(8,128)}, f32[256,512]{1,0:T(8,128)}, u32[]{:S(2)}, u32[]{:S(2)}) %collective-permute-start.9) | collective-permute-done | bytes 524320 | tf_op jit(solution)/shard_map/ppermute | solution.py:266
  177.7 1.3 add.242.rows_ref
  179.0 0.0 copy-start.5
  179.0 0.6 copy-done.5
  179.7 36.7 %factor.1 = (f32[256,512]{1,0:T(8,128)}, f32[256,512]{1,0:T(8,128)S(1)}) custom-call(s32[2]{0:T(128)S(1)} %copy-done.5, f32[256,384]{1,0:T(8,128)S(1)} %add.240.own_ref, f32[256,384]{1,0:T(8,128)} %collective-permute-done.7.other_ref, f32[256,512]{1,0:T(8,128)S(1)} %add.242.rows_ref), custom_call_target="tpu_custom_call" | custom-call | tf_op jit(solution)/shard_map/factor/pallas_call | solution.py:101
  216.4 0.0 copy-start.3
  216.4 0.8 copy-done.3
  217.2 0.0 all-gather.3.cloned.1.call-done
  217.2 2.2 copy-done
  219.4 1.0 copy-done.4
  220.4 9.2 %update.1 = f32[256,2048]{1,0:T(8,128)} custom-call(s32[8]{0:T(128)S(1)} %get-tuple-element.16.shift, s32[8]{0:T(128)S(1)} %get-tuple-element.17.group, s32[8]{0:T(128)S(1)} %get-tuple-element.14.place, s32[8]{0:T(128)S(1)} %get-tuple-element.28.live, f32[256,512]{1,0:T(8,128)S(1)} %copy-done.4, f32[256,512]{1,0:T(8,128)S(1)} %copy-done.2, ...), custom_call_target="tpu_custom_call" | custom-call | tf_op jit(solution)/shard_map/update/pallas_call | solution.py:160
  (44 shorter events, 0.5 us)
Async XLA Ops:
  7.2 210.0 %all-gather.3.cloned.1.call-start = ((), (), s32[]{:S(2)}) async-start(), calls=%async_computation | async-start | bytes 4325376 | tf_op jit(solution)/shard_map/all_gather | solution.py:262
  8.3 2.0 collective-permute-start
  10.3 1.5 copy-start.7
  11.8 5.9 %collective-permute-start.13 = (f32[2,32,512]{2,1,0:T(8,128)S(1)}, f32[2,32,512]{2,1,0:T(8,128)S(1)}, u32[]{:S(2)}, u32[]{:S(2)}) collective-permute-start(f32[2,32,512]{2,1,0:T(8,128)S(1)} %get-tuple-element.22), channel_id=1, source_target_pairs={{0,8},{4,12},{8,16},{12,20},{16,24},{20,28},{24,0},{28,4},{32,40},... | collective-permute-start | bytes 393224 | tf_op jit(solution)/shard_map/ppermute | solution.py:253
  13.1 7.1 %collective-permute-start.14 = (f32[2,32,512]{2,1,0:T(8,128)S(1)}, f32[2,32,512]{2,1,0:T(8,128)S(1)}, u32[]{:S(2)}, u32[]{:S(2)}) collective-permute-start(f32[2,32,512]{2,1,0:T(8,128)S(1)} %get-tuple-element.23), channel_id=1, source_target_pairs={{0,16},{4,20},{8,24},{12,28},{16,0},{20,4},{24,8},{28,12},{32,48},... | collective-permute-start | bytes 393224 | tf_op jit(solution)/shard_map/ppermute | solution.py:253
  13.9 8.2 %collective-permute-start.15 = (f32[2,32,512]{2,1,0:T(8,128)S(1)}, f32[2,32,512]{2,1,0:T(8,128)S(1)}, u32[]{:S(2)}, u32[]{:S(2)}) collective-permute-start(f32[2,32,512]{2,1,0:T(8,128)S(1)} %get-tuple-element.24), channel_id=1, source_target_pairs={{0,24},{4,28},{8,0},{12,4},{16,8},{20,12},{24,16},{28,20},{32,56},... | collective-permute-start | bytes 393224 | tf_op jit(solution)/shard_map/ppermute | solution.py:253
  22.1 12.1 %copy-start.6 = (f32[256,2048]{1,0:T(8,128)S(1)}, f32[256,2048]{1,0:T(8,128)}, u32[]{:S(2)}) copy-start(f32[256,2048]{1,0:T(8,128)} %front_ref.1) | copy-start | bytes 6291460
  22.1 13.0 %slice-start = ((f32[256,2048]{1,0:T(8,128)}), f32[256,256]{1,0:T(8,128)S(1)}, s32[]{:S(2)}) async-start(f32[256,2048]{1,0:T(8,128)} %front_ref.1), calls=%async_computation.1 | async-start | bytes 524288 | tf_op jit(solution)/shard_map/slice | solution.py:238
  24.7 2.7 %collective-permute-start.16 = (f32[2,32,512]{2,1,0:T(8,128)S(1)}, f32[2,32,512]{2,1,0:T(8,128)S(1)}, u32[]{:S(2)}, u32[]{:S(2)}) collective-permute-start(f32[2,32,512]{2,1,0:T(8,128)S(1)} %get-tuple-element.25), channel_id=1, source_target_pairs={{0,1},{4,5},{8,9},{12,13},{16,17},{20,21},{24,25},{28,29},{32,33},... | collective-permute-start | bytes 393224 | tf_op jit(solution)/shard_map/ppermute | solution.py:261
  25.3 8.1 %collective-permute-start.18 = (f32[2,32,512]{2,1,0:T(8,128)S(1)}, f32[2,32,512]{2,1,0:T(8,128)S(1)}, u32[]{:S(2)}, u32[]{:S(2)}) collective-permute-start(f32[2,32,512]{2,1,0:T(8,128)S(1)} %get-tuple-element.26), channel_id=1, source_target_pairs={{0,3},{4,7},{8,11},{12,15},{16,19},{20,23},{24,27},{28,31},{32,35}... | collective-permute-start | bytes 393224 | tf_op jit(solution)/shard_map/ppermute | solution.py:261
  26.6 6.8 %collective-permute-start.17 = (f32[2,32,512]{2,1,0:T(8,128)S(1)}, f32[2,32,512]{2,1,0:T(8,128)S(1)}, u32[]{:S(2)}, u32[]{:S(2)}) collective-permute-start(f32[2,32,512]{2,1,0:T(8,128)S(1)} %get-tuple-element.27), channel_id=1, source_target_pairs={{0,2},{4,6},{8,10},{12,14},{16,18},{20,22},{24,26},{28,30},{32,34}... | collective-permute-start | bytes 393224 | tf_op jit(solution)/shard_map/ppermute | solution.py:261
  35.1 0.7 collective-permute-start.1
  35.9 0.7 collective-permute-start.2
  36.7 0.7 collective-permute-start.3
  37.4 0.7 collective-permute-start.4
  38.2 41.2 %collective-permute-start.5 = (f32[256,384]{1,0:T(8,128)S(1)}, f32[256,384]{1,0:T(8,128)S(1)}, u32[]{:S(2)}, u32[]{:S(2)}) collective-permute-start(f32[256,384]{1,0:T(8,128)S(1)} %add.238), channel_id=1, source_target_pairs={{0,32},{1,33},{2,34},{3,35},{8,40},{9,41},{10,42},{11,43},{16,48},... | collective-permute-start | bytes 1179656 | tf_op jit(solution)/shard_map/ppermute | solution.py:241
  39.6 111.8 %collective-permute-start.8 = (f32[256,512]{1,0:T(8,128)S(1)}, f32[256,512]{1,0:T(8,128)S(1)}, u32[]{:S(2)}, u32[]{:S(2)}) collective-permute-start(f32[256,512]{1,0:T(8,128)S(1)} %get-tuple-element.20), channel_id=1, source_target_pairs={{0,1},{4,5},{8,9},{12,13},{16,17},{20,21},{24,25},{28,29},{32,33},... | collective-permute-start | bytes 1572872 | tf_op jit(solution)/shard_map/ppermute | solution.py:265
  80.2 73.7 %collective-permute-start.6 = (f32[256,384]{1,0:T(8,128)}, f32[256,384]{1,0:T(8,128)}, u32[]{:S(2)}, u32[]{:S(2)}) collective-permute-start(f32[256,384]{1,0:T(8,128)} %add.239), channel_id=1, source_target_pairs={{0,96},{1,97},{2,98},{3,99},{8,104},{9,105},{10,106},{11,107},{16,... | collective-permute-start | bytes 1179656 | tf_op jit(solution)/shard_map/ppermute | solution.py:241
  82.9 73.0 %copy-start.8 = (s32[32]{0:T(128)S(1)}, s32[32]{0:T(128)}, u32[]{:S(2)}) copy-start(s32[32]{0:T(128)} %param.5) | copy-start | bytes 388
  148.5 68.7 %collective-permute-start.10 = (f32[256,512]{1,0:T(8,128)}, f32[256,512]{1,0:T(8,128)S(1)}, u32[]{:S(2)}, u32[]{:S(2)}) collective-permute-start(f32[256,512]{1,0:T(8,128)} %get-tuple-element.11), channel_id=1, source_target_pairs={{0,1},{1,2},{2,3},{3,0},{4,5},{5,6},{6,7},{7,4},{8,9},{9,10},{10,1... | collective-permute-start | bytes 1572872 | tf_op jit(solution)/shard_map/ppermute | solution.py:272
  148.9 68.2 %collective-permute-start.11 = (f32[256,512]{1,0:T(8,128)}, f32[256,512]{1,0:T(8,128)}, u32[]{:S(2)}, u32[]{:S(2)}) collective-permute-start(f32[256,512]{1,0:T(8,128)} %get-tuple-element.12), channel_id=1, source_target_pairs={{0,2},{1,3},{2,0},{3,1},{4,6},{5,7},{6,4},{7,5},{8,10},{9,11},{10,... | collective-permute-start | bytes 1572872 | tf_op jit(solution)/shard_map/ppermute | solution.py:272
  151.4 65.7 %collective-permute-start.12 = (f32[256,512]{1,0:T(8,128)}, f32[256,512]{1,0:T(8,128)}, u32[]{:S(2)}, u32[]{:S(2)}) collective-permute-start(f32[256,512]{1,0:T(8,128)} %get-tuple-element.13), channel_id=1, source_target_pairs={{0,3},{1,0},{2,1},{3,2},{4,7},{5,4},{6,5},{7,6},{8,11},{9,8},{10,9... | collective-permute-start | bytes 1572872 | tf_op jit(solution)/shard_map/ppermute | solution.py:272
  152.3 64.9 %copy-start.1 = (f32[256,2048]{1,0:T(8,128)S(1)}, f32[256,2048]{1,0:T(8,128)}, u32[]{:S(2)}) copy-start(f32[256,2048]{1,0:T(8,128)} %base_ref.1) | copy-start | bytes 6291460
  152.3 64.9 %copy-start.2 = (f32[256,512]{1,0:T(8,128)S(1)}, f32[256,512]{1,0:T(8,128)}, u32[]{:S(2)}) copy-start(f32[256,512]{1,0:T(8,128)} %get-tuple-element.10.p0) | copy-start | bytes 1572868
  152.3 25.4 %collective-permute-start.9 = (f32[256,512]{1,0:T(8,128)}, f32[256,512]{1,0:T(8,128)}, u32[]{:S(2)}, u32[]{:S(2)}) collective-permute-start(f32[256,512]{1,0:T(8,128)} %add.241), channel_id=1, source_target_pairs={{0,3},{1,2},{4,7},{5,6},{8,11},{9,10},{12,15},{13,14},{16,19},{17,... | collective-permute-start | bytes 1572872 | tf_op jit(solution)/shard_map/ppermute | solution.py:266
  155.0 24.0 %collective-permute-start.7 = (f32[256,384]{1,0:T(8,128)S(1)}, f32[256,384]{1,0:T(8,128)}, u32[]{:S(2)}, u32[]{:S(2)}) collective-permute-start(f32[256,384]{1,0:T(8,128)S(1)} %add.240.own_ref), channel_id=1, source_target_pairs={{0,4},{4,0},{8,12},{12,8},{16,20},{20,16},{24,28},{28,24},{32,36},... | collective-permute-start | bytes 1179656 | tf_op jit(solution)/shard_map/ppermute | solution.py:242
  179.0 0.7 copy-start.5
  216.4 0.8 copy-start.3
  217.2 2.2 copy-start
  219.4 1.0 copy-start.4
Sparse Core Ops, SparseCore 0:
  34.3 48.8 all-gather.2

commit v2 on v1

v2 whole, which is shorter than its diff:
```python
import jax
import jax.numpy as jnp
from jax import lax
from jax.experimental import pallas as pl
from jax.experimental.pallas import tpu as pltpu
from jax.sharding import PartitionSpec as P

PW = 256
LEAD = 512
HALF = 128
STEP = 8
HIGHEST = lax.Precision.HIGHEST


def dot(a, b, ca, cb):
    return lax.dot_general(
        a, b, (((ca,), (cb,)), ((), ())), precision=HIGHEST, preferred_element_type=jnp.float32
    )


def inverse_factor_128(block):
    n = HALF
    lane = lax.broadcasted_iota(jnp.int32, (STEP, n), 1)
    sub = lax.broadcasted_iota(jnp.int32, (STEP, n), 0)
    lane_all = lax.broadcasted_iota(jnp.int32, (n, n), 1)
    work = block
    for start in range(0, n, STEP):
        end = start + STEP
        top = work[start:end, :]
        columns = [jnp.broadcast_to(top[:, start + i : start + i + 1], (STEP, n)) for i in range(STEP)]
        entry = [
            [jnp.broadcast_to(columns[i][j : j + 1, :], (STEP, n)) if i <= j else None for i in range(STEP)]
            for j in range(STEP)
        ]
        inside = (lane >= start) & (lane < end)
        top = jnp.where(inside, jnp.where(lane - start == sub, 1.0, 0.0), top)
        rows = [jnp.broadcast_to(top[j : j + 1, :], (STEP, n)) for j in range(STEP)]
        done = [None] * STEP
        for i in range(STEP):
            scale = lax.rsqrt(entry[i][i])
            done[i] = rows[i] * scale
            below = [None] * STEP
            for j in range(i + 1, STEP):
                below[j] = entry[j][i] * scale
                for k in range(i + 1, j + 1):
                    entry[j][k] = entry[j][k] - below[j] * below[k]
            for j in range(i + 1, STEP):
                rows[j] = rows[j] - below[j] * done[i]
        solved = done[0]
        for i in range(1, STEP):
            solved = jnp.where(sub == i, done[i], solved)
        work = jnp.where((lane_all >= start) & (lane_all < end), 0.0, work)
        pieces = [work[:start]] if start else []
        pieces.append(solved)
        if end < n:
            ahead = jnp.where(lane >= end, solved, 0.0)
            pieces.append(work[end:] - dot(ahead, solved, 0, 0)[end:])
        work = jnp.concatenate(pieces, 0)
    return work


def inverse_factor_256(top, left, bottom):
    first = inverse_factor_128(top)
    across = dot(left, first, 1, 1)
    second = inverse_factor_128(bottom - dot(across, across, 1, 1))
    lower = -dot(second, dot(across, first, 1, 0), 1, 0)
    return jnp.concatenate(
        [
            jnp.concatenate([first, jnp.zeros_like(first)], 1),
            jnp.concatenate([lower, second], 1),
        ],
        0,
    )


def factor_kernel(core_ref, own_ref, other_ref, inv_a_ref, across_ref, inv_b_ref):
    even = core_ref[0] == 0
    own, other = own_ref[...], other_ref[...]
    zero = jnp.where(even, own, other)
    one = jnp.where(even, other, own)

    def piece(blocks, index):
        return blocks[index * HALF : (index + 1) * HALF]

    inv_a = inverse_factor_256(piece(zero, 0), piece(zero, 1), piece(zero, 2))
    across = jnp.concatenate(
        [
            dot(jnp.concatenate([piece(zero, 3), piece(zero, 4)], 0), inv_a, 0, 1),
            dot(jnp.concatenate([piece(one, 3), piece(one, 4)], 1), inv_a, 1, 1),
        ],
        0,
    )
    square = dot(across, across, 1, 1)
    inv_b = inverse_factor_256(
        piece(one, 0) - square[:HALF, :HALF],
        piece(one, 1) - square[HALF:, :HALF],
        piece(one, 2) - square[HALF:, HALF:],
    )
    inv_a_ref[...] = inv_a
    across_ref[...] = across
    inv_b_ref[...] = inv_b


def factor(core, own, other):
    whole = pl.BlockSpec(memory_space=pltpu.VMEM)
    return pl.pallas_call(
        factor_kernel,
        out_shape=[jax.ShapeDtypeStruct((PW, PW), jnp.float32)] * 3,
        in_specs=[pl.BlockSpec(memory_space=pltpu.SMEM), whole, whole],
        out_specs=[whole] * 3,
        compiler_params=pltpu.CompilerParams(vmem_limit_bytes=24 << 20),
        name="factor",
    )(core, own, other)


def pick_kernel(index_ref, front_ref, *outs):
    for place in range(2 * len(outs)):
        start = pl.multiple_of(index_ref[place] * PW, PW)
        half = (place % 2) * PW
        outs[place // 2][:, half : half + PW] = front_ref[:, pl.ds(start, PW)]


def pick(index, front):
    whole = pl.BlockSpec(memory_space=pltpu.VMEM)
    return pl.pallas_call(
        pick_kernel,
        out_shape=[jax.ShapeDtypeStruct((front.shape[0], 2 * PW), jnp.float32)] * 4,
        in_specs=[pl.BlockSpec(memory_space=pltpu.SMEM), whole],
        out_specs=[whole] * 4,
        compiler_params=pltpu.CompilerParams(vmem_limit_bytes=16 << 20),
        name="pick",
    )(index, front)


def update_kernel(
    shift, group, place, live, at, r0, r1, r2, r3, inv_a_ref, across_ref, inv_b_ref, p0, p1, p2, p3, ahead_ref, base_ref,
    panel_ref, out_ref, weight_ref,
):
    slot = pl.program_id(0)

    @pl.when(slot == 0)
    def _():
        inv_a, across, inv_b = inv_a_ref[...], across_ref[...], inv_b_ref[...]
        rows_ref = jnp.where(at[1] == 0, r0[...], r1[...] + r2[...] + r3[...])
        panel_a = dot(rows_ref[:, :PW], inv_a, 1, 1)
        panel_b = dot(rows_ref[:, PW:] - dot(panel_a, across, 1, 1), inv_b, 1, 1)
        weight_b = dot(panel_b, inv_b, 1, 0)
        panel_ref[:, :PW] = panel_a
        panel_ref[:, PW:] = jnp.where(at[0] == 0, 0.0, panel_b)
        weight_ref[:, :PW] = dot(panel_a - dot(weight_b, across, 1, 0), inv_a, 1, 0)
        weight_ref[:, PW:] = weight_b

    product = dot(weight_ref[...], ahead_ref[...].reshape(PW, LEAD), 1, 1)
    column = pl.multiple_of(place[slot] * PW, PW)
    base = base_ref[...]
    out_ref[...] = base
    for index, ref in enumerate((p0, p1, p2, p3)):

        @pl.when((shift[slot] == index) & (live[slot] == 1))
        def _():
            out_ref[...] = base + (ref[:, pl.ds(column, PW)] - product)


def update(scalars, rows, inverse, pieces, ahead, base):
    height, width = base.shape
    full = pl.BlockSpec((height, LEAD), lambda u, *s: (0, 0))
    square = pl.BlockSpec((PW, PW), lambda u, *s: (0, 0))
    tile = pl.BlockSpec((height, PW), lambda u, *s: (0, u))
    return pl.pallas_call(
        update_kernel,
        out_shape=[
            jax.ShapeDtypeStruct((height, LEAD), jnp.float32),
            jax.ShapeDtypeStruct(base.shape, jnp.float32),
        ],
        grid_spec=pltpu.PrefetchScalarGridSpec(
            num_scalar_prefetch=5,
            grid=(width // PW,),
            in_specs=[
                *[full] * 4,
                *[square] * 3,
                *[full] * 4,
                pl.BlockSpec((8, 1, 32, LEAD), lambda u, shift, group, place, live, at: (group[u], place[u], 0, 0)),
                tile,
            ],
            out_specs=[full, tile],
            scratch_shapes=[pltpu.VMEM((height, LEAD), jnp.float32)],
        ),
        compiler_params=pltpu.CompilerParams(vmem_limit_bytes=56 << 20),
        name="update",
    )(*scalars, *rows, *inverse, *pieces, ahead, base)


def spread_steps():
    have = [{(0, 0)}, {(0, 0)}]
    steps = []
    for step in range(4):
        pairs = []
        for core in range(2):
            axis = (step // 2 + 1 - core) % 2
            new = set()
            for at in sorted(have[core]):
                to = list(at)
                if step % 2 == 0:
                    to[axis] = 1
                else:
                    to[axis] = 3 if at[axis] == 0 else 2
                new.add(tuple(to))
                pairs.append(((at[0] * 4 + at[1]) * 2 + core, (to[0] * 4 + to[1]) * 2 + core))
            have[core] |= new
        steps.append(pairs)
    return steps


def corner_blocks(rows, core):
    first = [rows[:HALF, :HALF], rows[HALF:, :HALF], rows[HALF:, HALF:PW], rows[:HALF, PW : PW + HALF], rows[HALF:, PW : PW + HALF]]
    second = [rows[:HALF, PW : PW + HALF], rows[HALF:, PW : PW + HALF], rows[HALF:, PW + HALF :], rows[HALF:, :HALF], rows[HALF:, HALF:PW]]
    return jnp.where(core == 0, jnp.concatenate(first, 0), jnp.concatenate(second, 0))


def shards(front, ancestor, tile_map):
    row = lax.axis_index("row")
    col = lax.axis_index("col")
    core = row % 2
    line = (row // 2) % 4
    plane = row // 8
    swap = [(i, i ^ 1) for i in range(32)]

    owner = (tile_map // 8).reshape(4, 8)
    ids = jnp.arange(8, dtype=jnp.int32)
    same = owner[:, :, None] == owner[:, None, :]
    rank = jnp.sum(jnp.where(same & (ids[None, None, :] < ids[None, :, None]), 1, 0), axis=2)
    cols4 = jnp.arange(4, dtype=jnp.int32)
    hit = (owner[:, None, None, :] == cols4[None, :, None, None]) & (
        rank[:, None, None, :] == jnp.arange(2, dtype=jnp.int32)[None, None, :, None]
    )
    chosen = jnp.sum(jnp.where(hit, ids, 0), axis=3)
    slots = col * 8 + ids
    found = tile_map[None, :] == slots[:, None]
    all_ids = jnp.arange(32, dtype=jnp.int32)
    source = jnp.sum(jnp.where(found, all_ids, 0), axis=1)
    place = jnp.sum(jnp.where(found, rank.reshape(32), 0), axis=1)
    group = source // 8
    shift = (col - group) % 4
    live = jnp.where((source >= 2) & (row >= 2), 1, 0).astype(jnp.int32)

    lead = front[:, :LEAD]
    copies = [lax.ppermute(lead, "col", [(0, to)]) for to in (1, 3, 2)]
    mate = lax.ppermute(lead, "row", swap)

    even = jnp.where(core == 0, lead, mate)
    odd = jnp.where(core == 0, mate, lead)
    both = jnp.stack([even, odd])
    parts = []
    for hop in range(4):
        at = 32 * (2 * ((line + hop) % 4) + core)
        parts.append(lax.dynamic_slice(both, (0, at, 0), (2, 32, LEAD)))
    parts = list(lax.optimization_barrier(tuple(parts)))
    for hop in range(1, 4):
        pairs = [(z * 8 + x * 2 + k, z * 8 + (x + hop) % 4 * 2 + k) for z in range(4) for x in range(4) for k in range(2)]
        parts[hop] = lax.ppermute(parts[hop], "row", pairs)

    own = lax.dynamic_index_in_dim(chosen, col, 0, keepdims=False)
    order = jnp.take(own, (col + cols4) % 4, axis=0).reshape(8)
    order, mate = lax.optimization_barrier((order, mate))
    pieces = list(pick(order, front))

    parts = jnp.concatenate(parts, 0)
    mine = lax.dynamic_index_in_dim(chosen, plane, 0, keepdims=False)
    index = ((line - mine // 2) % 4) * 2 + mine % 2
    sent = jnp.take(parts, index, axis=0)
    kept = jnp.where(col == 0, sent[0], 0.0)
    for to in range(1, 4):
        kept = kept + lax.ppermute(sent[to], "col", [(0, to)])
    copies[0], kept, *pieces = lax.optimization_barrier((copies[0], kept, *pieces))
    ahead = lax.all_gather(kept, "row", axis=0, tiled=False)

    rows = jnp.where(col == 0, lead, copies[0] + copies[1] + copies[2])
    block = jnp.where(row < 2, corner_blocks(rows, core), 0.0)
    for hop, pairs in enumerate(spread_steps()):
        if hop:
            pieces[hop] = lax.ppermute(pieces[hop], "col", [(i, (i + hop) % 4) for i in range(4)])
        block = block + lax.ppermute(block, "row", pairs)
        if hop < 3:
            block, pieces[hop + 1] = lax.optimization_barrier((block, pieces[hop + 1]))
    other = lax.ppermute(block, "row", swap)

    inverse = factor(core[None], block, other)
    panel, updated = update(
        (shift, group, place, live, jnp.stack([row, col])), [lead, *copies], inverse, pieces, ahead, ancestor
    )
    return panel, updated


def solution(mesh):
    return jax.shard_map(
        shards,
        mesh=mesh,
        in_specs=(P("row", "col"), P("row", "col"), P()),
        out_specs=(P("row", None), P("row", "col")),
        check_vma=False,
    )
```

time: 237 us -> 154 us (0.65)
  the two profiles are of different devices: /device:TPU:60 before, /device:TPU:1 now
where the time goes in v2:
time: 154 us; the launch traced here: 153 us
  Pallas kernels  48.8 us (32%)
  starting transfers between devices  41.8 us (27%)
  waiting for transfers between devices  30.5 us (20%)
  between operations  14.4 us (9%)
  local copies, waits for them, and re-layouts  9.31 us (6%)
  other arithmetic  7.93 us (5%)
    pallas_call x1, Pallas kernels, factor(): pl.pallas_call(factor_kernel, out_shape=[jax.ShapeDtypeStruct((PW, PW), j...  33.5 us
    ppermute x4, waiting for transfers between devices, shards(): block = block + lax.ppermute(block, 'row', pairs)  17.3 us
    pallas_call x1, Pallas kernels, update(): pl.pallas_call(update_kernel, out_shape=[jax.ShapeDtypeStruct((height, LE...  14.6 us
    ppermute x3, starting transfers between devices, shards(): copies = [lax.ppermute(lead, 'col', [(0, to)]) for to in (1, 3, 2)]  11 us
    ppermute x3, waiting for transfers between devices, shards(): copies = [lax.ppermute(lead, 'col', [(0, to)]) for to in (1, 3, 2)]  9.03 us
    ppermute x4, starting transfers between devices, shards(): block = block + lax.ppermute(block, 'row', pairs)  7.62 us
    ppermute x1, starting transfers between devices, shards(): other = lax.ppermute(block, 'row', swap)  6.35 us
    ppermute x3, starting transfers between devices, shards(): lax.ppermute(pieces[hop], 'col', [(i, (i + hop) % 4) for i in range(4)])  5.53 us
  transfers between devices with their start and end apart: 19, of which 9 were waited for; matrix products, arithmetic and copies ran while one was open for 7% of the time, Pallas kernels for 22%

profile of v2, /device:TPU:1, one launch (start us, length us, event | category | flops | bytes accessed | tf_op | source)
XLA Modules:
  0.0 152.7 jit_solution(14617465763739506476)
XLA Ops:
  7.2 0.0 all-gather.3.cloned.1.call-start
  7.2 1.9 %slice.38.r0 = f32[256,512]{1,0:T(8,128)} slice(f32[256,2048]{1,0:T(8,128)} %front_ref.1), slice={[0:256], [0:512]} | slice | bytes 1048576 | tf_op jit(solution)/shard_map/slice | solution.py:246
  9.1 1.4 collective-permute-start.1
  10.5 4.1 %collective-permute-start = (f32[256,512]{1,0:T(8,128)}, f32[256,512]{1,0:T(8,128)}, u32[]{:S(2)}, u32[]{:S(2)}) collective-permute-start(f32[256,512]{1,0:T(8,128)} %slice.38.r0), channel_id=1, source_target_pairs={{0,1},{4,5},{8,9},{12,13},{16,17},{20,21},{24,25},{28,29},{32,33},... | collective-permute-start | bytes 1572872 | tf_op jit(solution)/shard_map/ppermute | solution.py:247
  14.6 0.7 and_select_fusion.9
  15.3 0.1 eq.90
  15.4 0.2 select_reduce_fusion.1
  15.7 0.2 select_reduce_fusion
  16.0 1.1 select_bitcast_fusion
  17.1 0.1 fusion.1
  17.2 1.3 collective-permute-start.2
  18.5 2.5 %collective-permute-start.3 = (f32[2,32,512]{2,1,0:T(8,128)S(1)}, f32[2,32,512]{2,1,0:T(8,128)S(1)}, u32[]{:S(2)}, u32[]{:S(2)}) collective-permute-start(f32[2,32,512]{2,1,0:T(8,128)S(1)} %get-tuple-element.28), channel_id=1, source_target_pairs={{0,16},{4,20},{8,24},{12,28},{16,0},{20,4},{24,8},{28,12},{32,48},... | collective-permute-start | bytes 393224 | tf_op jit(solution)/shard_map/ppermute | solution.py:260
  20.9 1.2 collective-permute-start.4
  22.1 0.1 copy.14
  22.2 0.1 copy.15
  22.3 0.1 reshape.262
  22.4 0.1 copy.16
  22.5 0.6 gather_fusion.1
  23.0 0.2 collective-permute-done.2
  23.3 3.8 %collective-permute-done.3 = f32[2,32,512]{2,1,0:T(8,128)S(1)} collective-permute-done((f32[2,32,512]{2,1,0:T(8,128)S(1)}, f32[2,32,512]{2,1,0:T(8,128)S(1)}, u32[]{:S(2)}, u32[]{:S(2)}) %collective-permute-start.3) | collective-permute-done | bytes 131104 | tf_op jit(solution)/shard_map/ppermute | solution.py:260
  27.1 0.6 gather_fusion
  27.7 0.1 broadcast_select_fusion
  27.8 0.8 slice_bitcast_fusion.2
  28.6 1.3 collective-permute-start.5
  29.9 1.8 %collective-permute-start.7 = (f32[2,32,512]{2,1,0:T(8,128)}, f32[2,32,512]{2,1,0:T(8,128)S(1)}, u32[]{:S(2)}, u32[]{:S(2)}) collective-permute-start(f32[2,32,512]{2,1,0:T(8,128)} %get-tuple-element.66), channel_id=1, source_target_pairs={{0,3},{4,7},{8,11},{12,15},{16,19},{20,23},{24,27},{28,31},{32,35}... | collective-permute-start | bytes 393224 | tf_op jit(solution)/shard_map/ppermute | solution.py:273
  31.7 1.9 %collective-permute-start.6 = (f32[2,32,512]{2,1,0:T(8,128)S(1)}, f32[2,32,512]{2,1,0:T(8,128)}, u32[]{:S(2)}, u32[]{:S(2)}) collective-permute-start(f32[2,32,512]{2,1,0:T(8,128)S(1)} %get-tuple-element.67), channel_id=1, source_target_pairs={{0,2},{4,6},{8,10},{12,14},{16,18},{20,22},{24,26},{28,30},{32,34}... | collective-permute-start | bytes 393224 | tf_op jit(solution)/shard_map/ppermute | solution.py:273
  33.7 0.1 broadcast_select_fusion.1
  33.7 0.1 select_n.283.index_ref
  33.8 0.7 pick.1
  34.6 0.8 copy-done.1
  35.4 0.8 copy-done.5
  36.2 1.7 %fusion.8 = f32[2,32,512]{2,1,0:T(8,128)} fusion(f32[2,32,512]{2,1,0:T(8,128)S(1)} %collective-permute-done.7, f32[2,32,512]{2,1,0:T(8,128)} %collective-permute-done.6, f32[2,32,512]{2,1,0:T(8,128)S(1)} %collective-permute-done.5, f32[4,2,32,512]{3,2,1,0:T(8,128)} %copy-done.7, pred[]{:T(512)S(6)} %eq.94), kind=kLoop, calls=%fused_computation.28 | loop fusion | flops 131072 | bytes 655361 | tf_op jit(solution)/shard_map/add | solution.py:273
  37.8 0.0 all-gather.3.cloned.1.call-update
  37.9 3.9 %collective-permute-start.8 = (f32[256,512]{1,0:T(8,128)}, f32[256,512]{1,0:T(8,128)}, u32[]{:S(2)}, u32[]{:S(2)}) collective-permute-start(f32[256,512]{1,0:T(8,128)} %slice.38.r0), channel_id=1, source_target_pairs={{0,3},{4,7},{8,11},{12,15},{16,19},{20,23},{24,27},{28,31},{32,35}... | collective-permute-start | bytes 1572872 | tf_op jit(solution)/shard_map/ppermute | solution.py:247
  41.8 3.0 %collective-permute-start.9 = (f32[256,512]{1,0:T(8,128)}, f32[256,512]{1,0:T(8,128)}, u32[]{:S(2)}, u32[]{:S(2)}) collective-permute-start(f32[256,512]{1,0:T(8,128)} %slice.38.r0), channel_id=1, source_target_pairs={{0,2},{4,6},{8,10},{12,14},{16,18},{20,22},{24,26},{28,30},{32,34}... | collective-permute-start | bytes 1572872 | tf_op jit(solution)/shard_map/ppermute | solution.py:247
  44.7 6.1 %collective-permute-done.8.r2 = f32[256,512]{1,0:T(8,128)} collective-permute-done((f32[256,512]{1,0:T(8,128)}, f32[256,512]{1,0:T(8,128)}, u32[]{:S(2)}, u32[]{:S(2)}) %collective-permute-start.8) | collective-permute-done | bytes 524320 | tf_op jit(solution)/shard_map/ppermute | solution.py:247
  50.8 3.0 %collective-permute-done.9.r3 = f32[256,512]{1,0:T(8,128)} collective-permute-done((f32[256,512]{1,0:T(8,128)}, f32[256,512]{1,0:T(8,128)}, u32[]{:S(2)}, u32[]{:S(2)}) %collective-permute-start.9) | collective-permute-done | bytes 524320 | tf_op jit(solution)/shard_map/ppermute | solution.py:247
  53.8 1.6 %add_select_fusion = f32[256,512]{1,0:T(8,128)S(1)} fusion(f32[256,512]{1,0:T(8,128)} %collective-permute-done.9.r3, f32[256,512]{1,0:T(8,128)} %collective-permute-done.r1, f32[256,512]{1,0:T(8,128)} %collective-permute-done.8.r2, pred[]{:T(512)S(6)} %eq.94, f32[256,2048]{1,0:T(8,128)S(1)} %copy-done), kind=kLoop, calls=%fused_computation.11 | loop fusion | flops 393216 | bytes 2621441 | tf_op jit(solution)/shard_map/jit(_where)/select_n | solution.py:277
  55.4 0.0 copy-start.6
  55.5 3.7 %collective-permute-start.10 = (f32[640,128]{1,0:T(8,128)S(1)}, f32[640,128]{1,0:T(8,128)S(1)}, u32[]{:S(2)}, u32[]{:S(2)}) collective-permute-start(f32[640,128]{1,0:T(8,128)S(1)} %fusion), channel_id=1, source_target_pairs={{0,8},{4,36},{1,9},{5,37},{2,10},{6,38},{3,11},{7,39}} | collective-permute-start | bytes 983048 | tf_op jit(solution)/shard_map/ppermute | solution.py:282
  59.2 4.5 %collective-permute-done.10 = f32[640,128]{1,0:T(8,128)S(1)} collective-permute-done((f32[640,128]{1,0:T(8,128)S(1)}, f32[640,128]{1,0:T(8,128)S(1)}, u32[]{:S(2)}, u32[]{:S(2)}) %collective-permute-start.10) | collective-permute-done | bytes 327712 | tf_op jit(solution)/shard_map/ppermute | solution.py:282
  63.7 1.3 collective-permute-start.11
  65.0 4.0 %collective-permute-done.11 = f32[640,128]{1,0:T(8,128)S(1)} collective-permute-done((f32[640,128]{1,0:T(8,128)S(1)}, f32[640,128]{1,0:T(8,128)S(1)}, u32[]{:S(2)}, u32[]{:S(2)}) %collective-permute-start.11) | collective-permute-done | bytes 327712 | tf_op jit(solution)/shard_map/ppermute | solution.py:282
  69.0 1.3 collective-permute-start.12
  70.4 8.8 %collective-permute-done.12 = f32[640,128]{1,0:T(8,128)S(1)} collective-permute-done((f32[640,128]{1,0:T(8,128)S(1)}, f32[640,128]{1,0:T(8,128)S(1)}, u32[]{:S(2)}, u32[]{:S(2)}) %collective-permute-start.12) | collective-permute-done | bytes 327712 | tf_op jit(solution)/shard_map/ppermute | solution.py:282
  79.2 1.3 collective-permute-start.13
  80.5 0.1 reshape.259
  80.6 0.0 collective-permute-start.15
  80.6 3.5 %collective-permute-start.16 = (f32[256,512]{1,0:T(8,128)S(1)}, f32[256,512]{1,0:T(8,128)S(1)}, u32[]{:S(2)}, u32[]{:S(2)}) collective-permute-start(f32[256,512]{1,0:T(8,128)S(1)} %get-tuple-element.47), channel_id=1, source_target_pairs={{0,2},{1,3},{2,0},{3,1},{4,6},{5,7},{6,4},{7,5},{8,10},{9,11},{10,... | collective-permute-start | bytes 1572872 | tf_op jit(solution)/shard_map/ppermute | solution.py:281
  84.1 2.0 %collective-permute-start.17 = (f32[256,512]{1,0:T(8,128)S(1)}, f32[256,512]{1,0:T(8,128)}, u32[]{:S(2)}, u32[]{:S(2)}) collective-permute-start(f32[256,512]{1,0:T(8,128)S(1)} %get-tuple-element.48), channel_id=1, source_target_pairs={{0,3},{1,0},{2,1},{3,2},{4,7},{5,4},{6,5},{7,6},{8,11},{9,8},{10,9... | collective-permute-start | bytes 1572872 | tf_op jit(solution)/shard_map/ppermute | solution.py:281
  86.1 0.7 fusion.10
  86.8 0.1 collective-permute-done.13
  87.0 6.4 %collective-permute-start.14 = (f32[640,128]{1,0:T(8,128)S(1)}, f32[640,128]{1,0:T(8,128)S(1)}, u32[]{:S(2)}, u32[]{:S(2)}) collective-permute-start(f32[640,128]{1,0:T(8,128)S(1)} %add.274.own_ref), channel_id=1, source_target_pairs={{0,4},{4,0},{8,12},{12,8},{16,20},{20,16},{24,28},{28,24},{32,36},... | collective-permute-start | bytes 983048 | tf_op jit(solution)/shard_map/ppermute | solution.py:285
  93.3 0.6 pad_add_fusion.at
  93.9 0.6 and_select_fusion.10
  94.5 0.1 collective-permute-done.14.other_ref
  94.6 33.5 %factor.1 = (f32[256,256]{1,0:T(8,128)S(1)}, f32[256,256]{1,0:T(8,128)S(1)}, f32[256,256]{1,0:T(8,128)S(1)}) custom-call(s32[1]{0:T(128)} %bitcast.13.core_ref, f32[640,128]{1,0:T(8,128)S(1)} %add.274.own_ref, f32[640,128]{1,0:T(8,128)S(1)} %collective-permute-done.14.other_ref), custom_call_target="tpu_custom_call" | custom-call | tf_op jit(solution)/shard_map/factor/pallas_call | solution.py:106
  128.0 0.7 copy-done.2
  128.8 0.7 copy-done.3
  129.5 0.7 copy-done.4
  130.2 0.0 all-gather.3.cloned.1.call-done
  130.3 0.7 copy-done.8
  131.0 0.3 copy-done.9
  131.3 14.6 %update.1 = (f32[256,512]{1,0:T(8,128)}, f32[256,2048]{1,0:T(8,128)}) custom-call(s32[8]{0:T(128)} %get-tuple-element.52.shift, s32[8]{0:T(128)} %get-tuple-element.53.group, s32[8]{0:T(128)} %get-tuple-element.50.place, s32[8]{0:T(128)} %get-tuple-element.68.live, s32[2]{0:T(128)} %pad_add_fusion.at, f32[256,512]{1,0:T(8,128)} %slice.38.r0, ...), custom_call_target="tpu_custom_call" | custom-call | tf_op jit(solution)/shard_map/update/pallas_call | solution.py:169
  (42 shorter events, 0.4 us)
Async XLA Ops:
  7.2 123.1 %all-gather.3.cloned.1.call-start = ((), (), s32[]{:S(2)}) async-start(), calls=%async_computation | async-start | bytes 4325376 | tf_op jit(solution)/shard_map/all_gather | solution.py:275
  9.1 6.9 %collective-permute-start.1 = (f32[256,512]{1,0:T(8,128)}, f32[256,512]{1,0:T(8,128)S(1)}, u32[]{:S(2)}, u32[]{:S(2)}) collective-permute-start(f32[256,512]{1,0:T(8,128)} %slice.38.r0), channel_id=1, source_target_pairs={{0,4},{4,0},{8,12},{12,8},{16,20},{20,16},{24,28},{28,24},{32,36},... | collective-permute-start | bytes 1572872 | tf_op jit(solution)/shard_map/ppermute | solution.py:248
  10.5 27.3 %collective-permute-start = (f32[256,512]{1,0:T(8,128)}, f32[256,512]{1,0:T(8,128)}, u32[]{:S(2)}, u32[]{:S(2)}) collective-permute-start(f32[256,512]{1,0:T(8,128)} %slice.38.r0), channel_id=1, source_target_pairs={{0,1},{4,5},{8,9},{12,13},{16,17},{20,21},{24,25},{28,29},{32,33},... | collective-permute-start | bytes 1572872 | tf_op jit(solution)/shard_map/ppermute | solution.py:247
  17.2 16.7 %copy-start = (f32[256,2048]{1,0:T(8,128)S(1)}, f32[256,2048]{1,0:T(8,128)}, u32[]{:S(2)}) copy-start(f32[256,2048]{1,0:T(8,128)} %front_ref.1) | copy-start | bytes 6291460
  17.2 6.1 %collective-permute-start.2 = (f32[2,32,512]{2,1,0:T(8,128)S(1)}, f32[2,32,512]{2,1,0:T(8,128)S(1)}, u32[]{:S(2)}, u32[]{:S(2)}) collective-permute-start(f32[2,32,512]{2,1,0:T(8,128)S(1)} %get-tuple-element.27), channel_id=1, source_target_pairs={{0,8},{4,12},{8,16},{12,20},{16,24},{20,28},{24,0},{28,4},{32,40},... | collective-permute-start | bytes 393224 | tf_op jit(solution)/shard_map/ppermute | solution.py:260
  18.5 8.6 %collective-permute-start.3 = (f32[2,32,512]{2,1,0:T(8,128)S(1)}, f32[2,32,512]{2,1,0:T(8,128)S(1)}, u32[]{:S(2)}, u32[]{:S(2)}) collective-permute-start(f32[2,32,512]{2,1,0:T(8,128)S(1)} %get-tuple-element.28), channel_id=1, source_target_pairs={{0,16},{4,20},{8,24},{12,28},{16,0},{20,4},{24,8},{28,12},{32,48},... | collective-permute-start | bytes 393224 | tf_op jit(solution)/shard_map/ppermute | solution.py:260
  20.9 6.2 %collective-permute-start.4 = (f32[2,32,512]{2,1,0:T(8,128)S(1)}, f32[2,32,512]{2,1,0:T(8,128)S(1)}, u32[]{:S(2)}, u32[]{:S(2)}) collective-permute-start(f32[2,32,512]{2,1,0:T(8,128)S(1)} %get-tuple-element.29), channel_id=1, source_target_pairs={{0,24},{4,28},{8,0},{12,4},{16,8},{20,12},{24,16},{28,20},{32,56},... | collective-permute-start | bytes 393224 | tf_op jit(solution)/shard_map/ppermute | solution.py:260
  27.8 5.9 %copy-start.7 = (f32[4,2,32,512]{3,2,1,0:T(8,128)}, f32[4,2,32,512]{3,2,1,0:T(8,128)S(1)}, u32[]{:S(2)}) copy-start(f32[4,2,32,512]{3,2,1,0:T(8,128)S(1)} %broadcast_select_fusion) | copy-start | bytes 1572868
  28.6 7.5 %collective-permute-start.5 = (f32[2,32,512]{2,1,0:T(8,128)}, f32[2,32,512]{2,1,0:T(8,128)S(1)}, u32[]{:S(2)}, u32[]{:S(2)}) collective-permute-start(f32[2,32,512]{2,1,0:T(8,128)} %get-tuple-element.65), channel_id=1, source_target_pairs={{0,1},{4,5},{8,9},{12,13},{16,17},{20,21},{24,25},{28,29},{32,33},... | collective-permute-start | bytes 393224 | tf_op jit(solution)/shard_map/ppermute | solution.py:273
  29.9 6.2 %collective-permute-start.7 = (f32[2,32,512]{2,1,0:T(8,128)}, f32[2,32,512]{2,1,0:T(8,128)S(1)}, u32[]{:S(2)}, u32[]{:S(2)}) collective-permute-start(f32[2,32,512]{2,1,0:T(8,128)} %get-tuple-element.66), channel_id=1, source_target_pairs={{0,3},{4,7},{8,11},{12,15},{16,19},{20,23},{24,27},{28,31},{32,35}... | collective-permute-start | bytes 393224 | tf_op jit(solution)/shard_map/ppermute | solution.py:273
  31.7 4.4 %collective-permute-start.6 = (f32[2,32,512]{2,1,0:T(8,128)S(1)}, f32[2,32,512]{2,1,0:T(8,128)}, u32[]{:S(2)}, u32[]{:S(2)}) collective-permute-start(f32[2,32,512]{2,1,0:T(8,128)S(1)} %get-tuple-element.67), channel_id=1, source_target_pairs={{0,2},{4,6},{8,10},{12,14},{16,18},{20,22},{24,26},{28,30},{32,34}... | collective-permute-start | bytes 393224 | tf_op jit(solution)/shard_map/ppermute | solution.py:273
  34.6 0.8 copy-start.1
  35.4 0.8 copy-start.5
  37.9 12.9 %collective-permute-start.8 = (f32[256,512]{1,0:T(8,128)}, f32[256,512]{1,0:T(8,128)}, u32[]{:S(2)}, u32[]{:S(2)}) collective-permute-start(f32[256,512]{1,0:T(8,128)} %slice.38.r0), channel_id=1, source_target_pairs={{0,3},{4,7},{8,11},{12,15},{16,19},{20,23},{24,27},{28,31},{32,35}... | collective-permute-start | bytes 1572872 | tf_op jit(solution)/shard_map/ppermute | solution.py:247
  41.8 12.0 %collective-permute-start.9 = (f32[256,512]{1,0:T(8,128)}, f32[256,512]{1,0:T(8,128)}, u32[]{:S(2)}, u32[]{:S(2)}) collective-permute-start(f32[256,512]{1,0:T(8,128)} %slice.38.r0), channel_id=1, source_target_pairs={{0,2},{4,6},{8,10},{12,14},{16,18},{20,22},{24,26},{28,30},{32,34}... | collective-permute-start | bytes 1572872 | tf_op jit(solution)/shard_map/ppermute | solution.py:247
  55.4 25.2 %copy-start.6 = (f32[256,512]{1,0:T(8,128)S(1)}, f32[256,512]{1,0:T(8,128)}, u32[]{:S(2)}) copy-start(f32[256,512]{1,0:T(8,128)} %copy-done.5) | copy-start | bytes 1572868
  55.4 30.7 %copy-start.10 = (s32[32]{0:T(128)S(1)}, s32[32]{0:T(128)}, u32[]{:S(2)}) copy-start(s32[32]{0:T(128)} %param.5) | copy-start | bytes 388
  55.5 8.2 %collective-permute-start.10 = (f32[640,128]{1,0:T(8,128)S(1)}, f32[640,128]{1,0:T(8,128)S(1)}, u32[]{:S(2)}, u32[]{:S(2)}) collective-permute-start(f32[640,128]{1,0:T(8,128)S(1)} %fusion), channel_id=1, source_target_pairs={{0,8},{4,36},{1,9},{5,37},{2,10},{6,38},{3,11},{7,39}} | collective-permute-start | bytes 983048 | tf_op jit(solution)/shard_map/ppermute | solution.py:282
  63.7 5.3 %collective-permute-start.11 = (f32[640,128]{1,0:T(8,128)S(1)}, f32[640,128]{1,0:T(8,128)S(1)}, u32[]{:S(2)}, u32[]{:S(2)}) collective-permute-start(f32[640,128]{1,0:T(8,128)S(1)} %add.271), channel_id=1, source_target_pairs={{0,24},{8,16},{4,100},{36,68},{1,25},{9,17},{5,101},{37,69},{2,26}... | collective-permute-start | bytes 983048 | tf_op jit(solution)/shard_map/ppermute | solution.py:282
  69.0 10.1 %collective-permute-start.12 = (f32[640,128]{1,0:T(8,128)S(1)}, f32[640,128]{1,0:T(8,128)S(1)}, u32[]{:S(2)}, u32[]{:S(2)}) collective-permute-start(f32[640,128]{1,0:T(8,128)S(1)} %add.272), channel_id=1, source_target_pairs={{0,32},{8,40},{16,48},{24,56},{4,12},{36,44},{68,76},{100,108},{1,... | collective-permute-start | bytes 983048 | tf_op jit(solution)/shard_map/ppermute | solution.py:282
  79.2 7.8 %collective-permute-start.13 = (f32[640,128]{1,0:T(8,128)S(1)}, f32[640,128]{1,0:T(8,128)S(1)}, u32[]{:S(2)}, u32[]{:S(2)}) collective-permute-start(f32[640,128]{1,0:T(8,128)S(1)} %add.273), channel_id=1, source_target_pairs={{0,96},{8,104},{16,112},{24,120},{32,64},{40,72},{48,80},{56,88},{... | collective-permute-start | bytes 983048 | tf_op jit(solution)/shard_map/ppermute | solution.py:282
  80.6 49.6 %collective-permute-start.15 = (f32[256,512]{1,0:T(8,128)S(1)}, f32[256,512]{1,0:T(8,128)S(1)}, u32[]{:S(2)}, u32[]{:S(2)}) collective-permute-start(f32[256,512]{1,0:T(8,128)S(1)} %copy-done.6), channel_id=1, source_target_pairs={{0,1},{1,2},{2,3},{3,0},{4,5},{5,6},{6,7},{7,4},{8,9},{9,10},{10,1... | collective-permute-start | bytes 1572872 | tf_op jit(solution)/shard_map/ppermute | solution.py:281
  80.6 49.6 %collective-permute-start.16 = (f32[256,512]{1,0:T(8,128)S(1)}, f32[256,512]{1,0:T(8,128)S(1)}, u32[]{:S(2)}, u32[]{:S(2)}) collective-permute-start(f32[256,512]{1,0:T(8,128)S(1)} %get-tuple-element.47), channel_id=1, source_target_pairs={{0,2},{1,3},{2,0},{3,1},{4,6},{5,7},{6,4},{7,5},{8,10},{9,11},{10,... | collective-permute-start | bytes 1572872 | tf_op jit(solution)/shard_map/ppermute | solution.py:281
  84.1 46.1 %collective-permute-start.17 = (f32[256,512]{1,0:T(8,128)S(1)}, f32[256,512]{1,0:T(8,128)}, u32[]{:S(2)}, u32[]{:S(2)}) collective-permute-start(f32[256,512]{1,0:T(8,128)S(1)} %get-tuple-element.48), channel_id=1, source_target_pairs={{0,3},{1,0},{2,1},{3,2},{4,7},{5,4},{6,5},{7,6},{8,11},{9,8},{10,9... | collective-permute-start | bytes 1572872 | tf_op jit(solution)/shard_map/ppermute | solution.py:281
  87.0 7.6 %collective-permute-start.14 = (f32[640,128]{1,0:T(8,128)S(1)}, f32[640,128]{1,0:T(8,128)S(1)}, u32[]{:S(2)}, u32[]{:S(2)}) collective-permute-start(f32[640,128]{1,0:T(8,128)S(1)} %add.274.own_ref), channel_id=1, source_target_pairs={{0,4},{4,0},{8,12},{12,8},{16,20},{20,16},{24,28},{28,24},{32,36},... | collective-permute-start | bytes 983048 | tf_op jit(solution)/shard_map/ppermute | solution.py:285
  128.0 0.7 copy-start.2
  128.8 0.7 copy-start.3
  129.5 0.7 copy-start.4
  130.2 0.8 copy-start.8
  130.2 1.1 copy-start.9
Sparse Core Ops, SparseCore 0:
  38.0 49.4 all-gather.2

commit v3 on v2

--- a/solution.py
+++ b/solution.py
@@ -268,20 +268,25 @@
     mine = lax.dynamic_index_in_dim(chosen, plane, 0, keepdims=False)
     index = ((line - mine // 2) % 4) * 2 + mine % 2
     sent = jnp.take(parts, index, axis=0)
+    sent, *copies = lax.optimization_barrier((sent, *copies))
+
+    spread = spread_steps()
+    rows = jnp.where(col == 0, lead, copies[0] + copies[1] + copies[2])
+    block = jnp.where(row < 2, corner_blocks(rows, core), 0.0)
+    block = block + lax.ppermute(block, "row", spread[0])
     kept = jnp.where(col == 0, sent[0], 0.0)
     for to in range(1, 4):
         kept = kept + lax.ppermute(sent[to], "col", [(0, to)])
-    copies[0], kept, *pieces = lax.optimization_barrier((copies[0], kept, *pieces))
+    block, kept, *pieces = lax.optimization_barrier((block, kept, *pieces))
     ahead = lax.all_gather(kept, "row", axis=0, tiled=False)
 
-    rows = jnp.where(col == 0, lead, copies[0] + copies[1] + copies[2])
-    block = jnp.where(row < 2, corner_blocks(rows, core), 0.0)
-    for hop, pairs in enumerate(spread_steps()):
-        if hop:
-            pieces[hop] = lax.ppermute(pieces[hop], "col", [(i, (i + hop) % 4) for i in range(4)])
-        block = block + lax.ppermute(block, "row", pairs)
-        if hop < 3:
-            block, pieces[hop + 1] = lax.optimization_barrier((block, pieces[hop + 1]))
+    for hop in (1, 3, 2):
+        pieces[hop] = lax.ppermute(pieces[hop], "col", [(i, (i + hop) % 4) for i in range(4)])
+    block = block + lax.ppermute(block, "row", spread[1])
+    block = block + lax.ppermute(block, "row", spread[2])
+    block, pieces[1] = lax.optimization_barrier((block, pieces[1]))
+    block = block + lax.ppermute(block, "row", spread[3])
+    block, pieces[3] = lax.optimization_barrier((block, pieces[3]))
     other = lax.ppermute(block, "row", swap)
 
     inverse = factor(core[None], block, other)

time: 154 us -> 145 us (0.942)
  waiting for transfers between devices: 30.5 us -> 18.8 us
  starting transfers between devices: 41.8 us -> 33.3 us
  other arithmetic: 7.93 us -> 14.3 us
  local copies, waits for them, and re-layouts: 9.31 us -> 13 us
    ppermute x3, waiting for transfers between devices: 9.03 us -> 0.01 us  [shards(): copies = [lax.ppermute(lead, 'col', [(0, to)]) for to in (1, 3, 2)]]
    ppermute x4, waiting for transfers between devices: 17.3 us -> 11.8 us  [the longest x1 4.6 us: shards(): block = block + lax.ppermute(block, 'row', spread[2])]
    ppermute x3, starting transfers between devices: 5.53 us -> 0.17 us  [shards(): lax.ppermute(pieces[hop], 'col', [(i, (i + hop) % 4) for i in range(4)])]
    ppermute x3, waiting for transfers between devices: 0.01 us -> 4.72 us  [shards(): lax.ppermute(pieces[hop], 'col', [(i, (i + hop) % 4) for i in range(4)])]
    ppermute x1, starting transfers between devices: 6.35 us -> 1.87 us  [shards(): other = lax.ppermute(block, 'row', swap)]
    ppermute x4, starting transfers between devices: 7.62 us -> 9.69 us  [the longest x1 4.28 us: shards(): block = block + lax.ppermute(block, 'row', spread[0])]
    ppermute x3, waiting for transfers between devices: 4.02 us -> 2.16 us  [shards(): parts[hop] = lax.ppermute(parts[hop], 'row', pairs)]
    gather x1, local copies, waits for them, and re-layouts: 0.58 us -> 2.41 us  [shards(): sent = jnp.take(parts, index, axis=0)]
  transfers between devices with their start and end apart: 19 -> 19, of which waited for: 9 -> 6; matrix products, arithmetic and copies ran while one was open for 7% -> 13% of each run, Pallas kernels for 22% -> 24%
where the time goes in v3:
time: 145 us; the launch traced here: 143 us
  Pallas kernels  48.8 us (34%)
  starting transfers between devices  33.3 us (23%)
  waiting for transfers between devices  18.8 us (13%)
  between operations  14.4 us (10%)
  other arithmetic  14.3 us (10%)
  local copies, waits for them, and re-layouts  13 us (9%)
    pallas_call x1, Pallas kernels, factor(): pl.pallas_call(factor_kernel, out_shape=[jax.ShapeDtypeStruct((PW, PW), j...  33.5 us
    pallas_call x1, Pallas kernels, update(): pl.pallas_call(update_kernel, out_shape=[jax.ShapeDtypeStruct((height, LE...  14.6 us
    ppermute x3, starting transfers between devices, shards(): copies = [lax.ppermute(lead, 'col', [(0, to)]) for to in (1, 3, 2)]  9.71 us
    ppermute x3, starting transfers between devices, shards(): kept = kept + lax.ppermute(sent[to], 'col', [(0, to)])  5.82 us
    ppermute x3, starting transfers between devices, shards(): parts[hop] = lax.ppermute(parts[hop], 'row', pairs)  5.08 us
    ppermute x3, waiting for transfers between devices, shards(): lax.ppermute(pieces[hop], 'col', [(i, (i + hop) % 4) for i in range(4)])  4.72 us
    ppermute x1, waiting for transfers between devices, shards(): block = block + lax.ppermute(block, 'row', spread[2])  4.6 us
    unnamed x32, local copies, waits for them, and re-layouts  4.6 us
  transfers between devices with their start and end apart: 19, of which 6 were waited for; matrix products, arithmetic and copies ran while one was open for 13% of the time, Pallas kernels for 24%

profile of v3, /device:TPU:1, one launch (start us, length us, event | category | flops | bytes accessed | tf_op | source)
XLA Modules:
  0.0 142.6 jit_solution(8335747063059818829)
XLA Ops:
  7.2 0.0 all-gather.3.cloned.1.call-start
  7.2 1.1 slice.38.r0
  8.3 5.5 %collective-permute-start.5 = (f32[256,512]{1,0:T(8,128)S(1)}, f32[256,512]{1,0:T(8,128)S(1)}, u32[]{:S(2)}, u32[]{:S(2)}) collective-permute-start(f32[256,512]{1,0:T(8,128)S(1)} %slice.38.r0), channel_id=1, source_target_pairs={{0,3},{4,7},{8,11},{12,15},{16,19},{20,23},{24,27},{28,31},{32,35}... | collective-permute-start | bytes 1572872 | tf_op jit(solution)/shard_map/ppermute | solution.py:247
  13.8 2.1 %collective-permute-start.4 = (f32[256,512]{1,0:T(8,128)S(1)}, f32[256,512]{1,0:T(8,128)}, u32[]{:S(2)}, u32[]{:S(2)}) collective-permute-start(f32[256,512]{1,0:T(8,128)S(1)} %slice.38.r0), channel_id=1, source_target_pairs={{0,1},{4,5},{8,9},{12,13},{16,17},{20,21},{24,25},{28,29},{32,33},... | collective-permute-start | bytes 1572872 | tf_op jit(solution)/shard_map/ppermute | solution.py:247
  15.9 2.1 %collective-permute-start.6 = (f32[256,512]{1,0:T(8,128)S(1)}, f32[256,512]{1,0:T(8,128)}, u32[]{:S(2)}, u32[]{:S(2)}) collective-permute-start(f32[256,512]{1,0:T(8,128)S(1)} %slice.38.r0), channel_id=1, source_target_pairs={{0,2},{4,6},{8,10},{12,14},{16,18},{20,22},{24,26},{28,30},{32,34}... | collective-permute-start | bytes 1572872 | tf_op jit(solution)/shard_map/ppermute | solution.py:247
  18.0 1.0 collective-permute-start
  19.0 0.5 fusion.19
  19.5 0.7 and_select_fusion.9
  20.2 0.1 eq.90
  20.3 0.2 select_reduce_fusion.1
  20.5 0.2 select_reduce_fusion
  20.8 0.6 fusion.15
  21.4 1.1 select_bitcast_fusion
  22.5 0.1 fusion.1
  22.6 1.3 collective-permute-start.1
  23.8 0.5 compare_and_fusion
  24.4 2.5 %collective-permute-start.2 = (f32[2,32,512]{2,1,0:T(8,128)S(1)}, f32[2,32,512]{2,1,0:T(8,128)}, u32[]{:S(2)}, u32[]{:S(2)}) collective-permute-start(f32[2,32,512]{2,1,0:T(8,128)S(1)} %get-tuple-element.30), channel_id=1, source_target_pairs={{0,16},{4,20},{8,24},{12,28},{16,0},{20,4},{24,8},{28,12},{32,48},... | collective-permute-start | bytes 393224 | tf_op jit(solution)/shard_map/ppermute | solution.py:260
  26.9 2.2 %collective-permute-done.1 = f32[2,32,512]{2,1,0:T(8,128)} collective-permute-done((f32[2,32,512]{2,1,0:T(8,128)S(1)}, f32[2,32,512]{2,1,0:T(8,128)}, u32[]{:S(2)}, u32[]{:S(2)}) %collective-permute-start.1) | collective-permute-done | bytes 131104 | tf_op jit(solution)/shard_map/ppermute | solution.py:260
  29.1 1.3 collective-permute-start.3
  30.3 0.5 compare_and_fusion.1
  30.9 1.3 copy.14
  32.2 0.1 copy.15
  32.3 0.6 reshape.262
  32.9 0.8 copy.16
  33.6 0.6 gather_fusion.1
  34.2 0.7 pad_clamp_fusion.1
  34.9 1.9 %pad_maximum_fusion = f32[8,32,512]{2,1,0:T(8,128)} fusion(f32[2,32,512]{2,1,0:T(8,128)} %collective-permute-done.3, f32[2,32,512]{2,1,0:T(8,128)} %collective-permute-done.2, f32[2,32,512]{2,1,0:T(8,128)} %collective-permute-done.1, f32[2,32,512]{2,1,0:T(8,128)S(1)} %get-tuple-element.28), kind=kLoop, calls=%fused_computation.10 | loop fusion | flops 393216 | bytes 1048576 | tf_op jit(solution)/shard_map/concatenate | solution.py:267
  36.7 2.4 %gather_fusion = f32[8,32,512]{2,1,0:T(8,128)} fusion(f32[8,32,512]{2,1,0:T(8,128)} %pad_maximum_fusion, s32[1024]{0:T(1024)S(1)} %pad_clamp_fusion.1), kind=kCustom, calls=%fused_computation | custom fusion | bytes 1048608 | tf_op jit(solution)/shard_map/jit(_take)/gather | solution.py:270
  39.1 1.1 broadcast_select_fusion
  40.4 1.7 %add_select_fusion = f32[256,512]{1,0:T(8,128)S(1)} fusion(f32[256,512]{1,0:T(8,128)} %collective-permute-done.6.r3, f32[256,512]{1,0:T(8,128)} %collective-permute-done.4.r1, f32[256,512]{1,0:T(8,128)S(1)} %collective-permute-done.5.r2, pred[]{:T(512)S(6)} %eq.101, f32[256,2048]{1,0:T(8,128)S(1)} %copy-done), kind=kLoop, calls=%fused_computation.11 | loop fusion | flops 393216 | bytes 2621441 | tf_op jit(solution)/shard_map/jit(_where)/select_n | solution.py:274
  42.2 0.8 slice_bitcast_fusion.2
  42.9 1.9 %collective-permute-start.8 = (f32[2,32,512]{2,1,0:T(8,128)}, f32[2,32,512]{2,1,0:T(8,128)}, u32[]{:S(2)}, u32[]{:S(2)}) collective-permute-start(f32[2,32,512]{2,1,0:T(8,128)} %get-tuple-element.64), channel_id=1, source_target_pairs={{0,1},{4,5},{8,9},{12,13},{16,17},{20,21},{24,25},{28,29},{32,33},... | collective-permute-start | bytes 393224 | tf_op jit(solution)/shard_map/ppermute | solution.py:279
  44.9 1.9 %collective-permute-start.10 = (f32[2,32,512]{2,1,0:T(8,128)}, f32[2,32,512]{2,1,0:T(8,128)}, u32[]{:S(2)}, u32[]{:S(2)}) collective-permute-start(f32[2,32,512]{2,1,0:T(8,128)} %get-tuple-element.65), channel_id=1, source_target_pairs={{0,3},{4,7},{8,11},{12,15},{16,19},{20,23},{24,27},{28,31},{32,35}... | collective-permute-start | bytes 393224 | tf_op jit(solution)/shard_map/ppermute | solution.py:279
  46.8 1.9 %collective-permute-start.9 = (f32[2,32,512]{2,1,0:T(8,128)}, f32[2,32,512]{2,1,0:T(8,128)}, u32[]{:S(2)}, u32[]{:S(2)}) collective-permute-start(f32[2,32,512]{2,1,0:T(8,128)} %get-tuple-element.66), channel_id=1, source_target_pairs={{0,2},{4,6},{8,10},{12,14},{16,18},{20,22},{24,26},{28,30},{32,34}... | collective-permute-start | bytes 393224 | tf_op jit(solution)/shard_map/ppermute | solution.py:279
  48.8 4.3 %collective-permute-start.7 = (f32[640,128]{1,0:T(8,128)S(1)}, f32[640,128]{1,0:T(8,128)}, u32[]{:S(2)}, u32[]{:S(2)}) collective-permute-start(f32[640,128]{1,0:T(8,128)S(1)} %fusion), channel_id=1, source_target_pairs={{0,8},{4,36},{1,9},{5,37},{2,10},{6,38},{3,11},{7,39}} | collective-permute-start | bytes 983048 | tf_op jit(solution)/shard_map/ppermute | solution.py:276
  53.1 0.1 broadcast_select_fusion.1
  53.1 0.1 select_n.289.index_ref
  53.2 0.7 pick.1
  54.0 0.8 copy-done.1
  54.8 0.8 copy-done.5
  55.6 1.8 %fusion.6 = f32[2,32,512]{2,1,0:T(8,128)} fusion(f32[2,32,512]{2,1,0:T(8,128)} %collective-permute-done.10, f32[2,32,512]{2,1,0:T(8,128)} %collective-permute-done.9, f32[2,32,512]{2,1,0:T(8,128)} %collective-permute-done.8, f32[4,2,32,512]{3,2,1,0:T(8,128)} %copy-done.8, pred[]{:T(512)S(6)} %eq.101), kind=kLoop, calls=%fused_computation.23 | loop fusion | flops 131072 | bytes 655361 | tf_op jit(solution)/shard_map/add | solution.py:279
  57.4 1.0 add.259
  58.4 2.8 %collective-permute-start.11 = (f32[640,128]{1,0:T(8,128)S(1)}, f32[640,128]{1,0:T(8,128)S(1)}, u32[]{:S(2)}, u32[]{:S(2)}) collective-permute-start(f32[640,128]{1,0:T(8,128)S(1)} %add.259), channel_id=1, source_target_pairs={{0,24},{8,16},{4,100},{36,68},{1,25},{9,17},{5,101},{37,69},{2,26}... | collective-permute-start | bytes 983048 | tf_op jit(solution)/shard_map/ppermute | solution.py:285
  61.2 0.1 collective-permute-start.13
  61.3 3.9 %collective-permute-done.11 = f32[640,128]{1,0:T(8,128)S(1)} collective-permute-done((f32[640,128]{1,0:T(8,128)S(1)}, f32[640,128]{1,0:T(8,128)S(1)}, u32[]{:S(2)}, u32[]{:S(2)}) %collective-permute-start.11) | collective-permute-done | bytes 327712 | tf_op jit(solution)/shard_map/ppermute | solution.py:285
  65.2 1.3 collective-permute-start.12
  66.5 0.1 collective-permute-start.15
  66.6 4.6 %collective-permute-done.12 = f32[640,128]{1,0:T(8,128)S(1)} collective-permute-done((f32[640,128]{1,0:T(8,128)S(1)}, f32[640,128]{1,0:T(8,128)S(1)}, u32[]{:S(2)}, u32[]{:S(2)}) %collective-permute-start.12) | collective-permute-done | bytes 327712 | tf_op jit(solution)/shard_map/ppermute | solution.py:286
  71.3 4.7 %collective-permute-done.13.p1 = f32[256,512]{1,0:T(8,128)S(1)} collective-permute-done((f32[256,512]{1,0:T(8,128)}, f32[256,512]{1,0:T(8,128)S(1)}, u32[]{:S(2)}, u32[]{:S(2)}) %collective-permute-start.13) | collective-permute-done | bytes 524320 | tf_op jit(solution)/shard_map/ppermute | solution.py:284
  76.0 1.3 collective-permute-start.14
  77.3 0.1 reshape.259
  77.4 0.0 collective-permute-start.17
  77.4 0.8 fusion.8
  78.2 3.3 %collective-permute-done.14 = f32[640,128]{1,0:T(8,128)S(1)} collective-permute-done((f32[640,128]{1,0:T(8,128)S(1)}, f32[640,128]{1,0:T(8,128)S(1)}, u32[]{:S(2)}, u32[]{:S(2)}) %collective-permute-start.14) | collective-permute-done | bytes 327712 | tf_op jit(solution)/shard_map/ppermute | solution.py:288
  81.6 1.9 %collective-permute-start.16 = (f32[640,128]{1,0:T(8,128)S(1)}, f32[640,128]{1,0:T(8,128)S(1)}, u32[]{:S(2)}, u32[]{:S(2)}) collective-permute-start(f32[640,128]{1,0:T(8,128)S(1)} %add.274.own_ref), channel_id=1, source_target_pairs={{0,4},{4,0},{8,12},{12,8},{16,20},{20,16},{24,28},{28,24},{32,36},... | collective-permute-start | bytes 983048 | tf_op jit(solution)/shard_map/ppermute | solution.py:290
  83.5 0.6 pad_add_fusion.at
  84.1 0.6 and_select_fusion.10
  84.7 0.1 collective-permute-done.16.other_ref
  84.7 33.5 %factor.1 = (f32[256,256]{1,0:T(8,128)S(1)}, f32[256,256]{1,0:T(8,128)S(1)}, f32[256,256]{1,0:T(8,128)S(1)}) custom-call(s32[1]{0:T(128)} %bitcast.7.core_ref, f32[640,128]{1,0:T(8,128)S(1)} %add.274.own_ref, f32[640,128]{1,0:T(8,128)S(1)} %collective-permute-done.16.other_ref), custom_call_target="tpu_custom_call" | custom-call | tf_op jit(solution)/shard_map/factor/pallas_call | solution.py:106
  118.2 0.7 copy-done.2
  118.9 0.7 copy-done.3
  119.6 0.7 copy-done.4
  120.4 0.8 copy-done.11
  121.2 14.6 %update.1 = (f32[256,512]{1,0:T(8,128)}, f32[256,2048]{1,0:T(8,128)}) custom-call(s32[8]{0:T(128)} %get-tuple-element.56.shift, s32[8]{0:T(128)} %get-tuple-element.57.group, s32[8]{0:T(128)} %get-tuple-element.54.place, s32[8]{0:T(128)} %get-tuple-element.72.live, s32[2]{0:T(128)} %pad_add_fusion.at, f32[256,512]{1,0:T(8,128)} %copy-done.6, ...), custom_call_target="tpu_custom_call" | custom-call | tf_op jit(solution)/shard_map/update/pallas_call | solution.py:169
  (52 shorter events, 0.3 us)
Async XLA Ops:
  7.2 113.2 %all-gather.3.cloned.1.call-start = ((), (), s32[]{:S(2)}) async-start(), calls=%async_computation | async-start | bytes 4325376 | tf_op jit(solution)/shard_map/all_gather | solution.py:281
  8.3 28.4 %copy-start.6 = (f32[256,512]{1,0:T(8,128)}, f32[256,512]{1,0:T(8,128)S(1)}, u32[]{:S(2)}) copy-start(f32[256,512]{1,0:T(8,128)S(1)} %slice.38.r0) | copy-start | bytes 1572868
  8.3 32.0 %collective-permute-start.5 = (f32[256,512]{1,0:T(8,128)S(1)}, f32[256,512]{1,0:T(8,128)S(1)}, u32[]{:S(2)}, u32[]{:S(2)}) collective-permute-start(f32[256,512]{1,0:T(8,128)S(1)} %slice.38.r0), channel_id=1, source_target_pairs={{0,3},{4,7},{8,11},{12,15},{16,19},{20,23},{24,27},{28,31},{32,35}... | collective-permute-start | bytes 1572872 | tf_op jit(solution)/shard_map/ppermute | solution.py:247
  13.8 26.5 %collective-permute-start.4 = (f32[256,512]{1,0:T(8,128)S(1)}, f32[256,512]{1,0:T(8,128)}, u32[]{:S(2)}, u32[]{:S(2)}) collective-permute-start(f32[256,512]{1,0:T(8,128)S(1)} %slice.38.r0), channel_id=1, source_target_pairs={{0,1},{4,5},{8,9},{12,13},{16,17},{20,21},{24,25},{28,29},{32,33},... | collective-permute-start | bytes 1572872 | tf_op jit(solution)/shard_map/ppermute | solution.py:247
  15.9 24.4 %collective-permute-start.6 = (f32[256,512]{1,0:T(8,128)S(1)}, f32[256,512]{1,0:T(8,128)}, u32[]{:S(2)}, u32[]{:S(2)}) collective-permute-start(f32[256,512]{1,0:T(8,128)S(1)} %slice.38.r0), channel_id=1, source_target_pairs={{0,2},{4,6},{8,10},{12,14},{16,18},{20,22},{24,26},{28,30},{32,34}... | collective-permute-start | bytes 1572872 | tf_op jit(solution)/shard_map/ppermute | solution.py:247
  18.0 3.3 %collective-permute-start = (f32[256,512]{1,0:T(8,128)S(1)}, f32[256,512]{1,0:T(8,128)S(1)}, u32[]{:S(2)}, u32[]{:S(2)}) collective-permute-start(f32[256,512]{1,0:T(8,128)S(1)} %slice.38.r0), channel_id=1, source_target_pairs={{0,4},{4,0},{8,12},{12,8},{16,20},{20,16},{24,28},{28,24},{32,36},... | collective-permute-start | bytes 1572872 | tf_op jit(solution)/shard_map/ppermute | solution.py:248
  20.5 3.9 %copy-start.15 = (s32[4]{0:T(128)S(1)}, s32[4]{0:T(128)}, u32[]{:S(2)}) copy-start(s32[4]{0:T(128)} %fusion.19) | copy-start | bytes 52
  22.5 17.9 %copy-start = (f32[256,2048]{1,0:T(8,128)S(1)}, f32[256,2048]{1,0:T(8,128)}, u32[]{:S(2)}) copy-start(f32[256,2048]{1,0:T(8,128)} %front_ref.1) | copy-start | bytes 6291460
  22.6 6.5 %collective-permute-start.1 = (f32[2,32,512]{2,1,0:T(8,128)S(1)}, f32[2,32,512]{2,1,0:T(8,128)}, u32[]{:S(2)}, u32[]{:S(2)}) collective-permute-start(f32[2,32,512]{2,1,0:T(8,128)S(1)} %get-tuple-element.29), channel_id=1, source_target_pairs={{0,8},{4,12},{8,16},{12,20},{16,24},{20,28},{24,0},{28,4},{32,40},... | collective-permute-start | bytes 393224 | tf_op jit(solution)/shard_map/ppermute | solution.py:260
  24.4 10.5 %collective-permute-start.2 = (f32[2,32,512]{2,1,0:T(8,128)S(1)}, f32[2,32,512]{2,1,0:T(8,128)}, u32[]{:S(2)}, u32[]{:S(2)}) collective-permute-start(f32[2,32,512]{2,1,0:T(8,128)S(1)} %get-tuple-element.30), channel_id=1, source_target_pairs={{0,16},{4,20},{8,24},{12,28},{16,0},{20,4},{24,8},{28,12},{32,48},... | collective-permute-start | bytes 393224 | tf_op jit(solution)/shard_map/ppermute | solution.py:260
  29.1 5.8 %collective-permute-start.3 = (f32[2,32,512]{2,1,0:T(8,128)S(1)}, f32[2,32,512]{2,1,0:T(8,128)}, u32[]{:S(2)}, u32[]{:S(2)}) collective-permute-start(f32[2,32,512]{2,1,0:T(8,128)S(1)} %get-tuple-element.31), channel_id=1, source_target_pairs={{0,24},{4,28},{8,0},{12,4},{16,8},{20,12},{24,16},{28,20},{32,56},... | collective-permute-start | bytes 393224 | tf_op jit(solution)/shard_map/ppermute | solution.py:260
  34.2 5.0 %copy-start.12 = (pred[4,2]{1,0:T(4,128)(4,1)S(1)}, pred[4,2]{1,0:T(4,128)(4,1)}, u32[]{:S(2)}) copy-start(pred[4,2]{1,0:T(4,128)(4,1)} %copy.14) | copy-start | bytes 28
  40.3 2.6 %copy-start.8 = (f32[4,2,32,512]{3,2,1,0:T(8,128)}, f32[4,2,32,512]{3,2,1,0:T(8,128)S(1)}, u32[]{:S(2)}) copy-start(f32[4,2,32,512]{3,2,1,0:T(8,128)S(1)} %broadcast_select_fusion) | copy-start | bytes 1572868
  40.3 12.8 %copy-start.14 = (pred[4]{0:T(512)(128)(4,1)S(1)}, pred[4]{0:T(512)(128)(4,1)}, u32[]{:S(2)}) copy-start(pred[4]{0:T(512)(128)(4,1)} %compare_and_fusion) | copy-start | bytes 16
  40.3 2.6 %copy-start.7 = (f32[256,512]{1,0:T(8,128)}, f32[256,512]{1,0:T(8,128)S(1)}, u32[]{:S(2)}) copy-start(f32[256,512]{1,0:T(8,128)S(1)} %collective-permute-done.5.r2) | copy-start | bytes 1572868
  42.9 12.6 %collective-permute-start.8 = (f32[2,32,512]{2,1,0:T(8,128)}, f32[2,32,512]{2,1,0:T(8,128)}, u32[]{:S(2)}, u32[]{:S(2)}) collective-permute-start(f32[2,32,512]{2,1,0:T(8,128)} %get-tuple-element.64), channel_id=1, source_target_pairs={{0,1},{4,5},{8,9},{12,13},{16,17},{20,21},{24,25},{28,29},{32,33},... | collective-permute-start | bytes 393224 | tf_op jit(solution)/shard_map/ppermute | solution.py:279
  44.9 10.7 %collective-permute-start.10 = (f32[2,32,512]{2,1,0:T(8,128)}, f32[2,32,512]{2,1,0:T(8,128)}, u32[]{:S(2)}, u32[]{:S(2)}) collective-permute-start(f32[2,32,512]{2,1,0:T(8,128)} %get-tuple-element.65), channel_id=1, source_target_pairs={{0,3},{4,7},{8,11},{12,15},{16,19},{20,23},{24,27},{28,31},{32,35}... | collective-permute-start | bytes 393224 | tf_op jit(solution)/shard_map/ppermute | solution.py:279
  46.8 8.8 %collective-permute-start.9 = (f32[2,32,512]{2,1,0:T(8,128)}, f32[2,32,512]{2,1,0:T(8,128)}, u32[]{:S(2)}, u32[]{:S(2)}) collective-permute-start(f32[2,32,512]{2,1,0:T(8,128)} %get-tuple-element.66), channel_id=1, source_target_pairs={{0,2},{4,6},{8,10},{12,14},{16,18},{20,22},{24,26},{28,30},{32,34}... | collective-permute-start | bytes 393224 | tf_op jit(solution)/shard_map/ppermute | solution.py:279
  48.8 8.6 %collective-permute-start.7 = (f32[640,128]{1,0:T(8,128)S(1)}, f32[640,128]{1,0:T(8,128)}, u32[]{:S(2)}, u32[]{:S(2)}) collective-permute-start(f32[640,128]{1,0:T(8,128)S(1)} %fusion), channel_id=1, source_target_pairs={{0,8},{4,36},{1,9},{5,37},{2,10},{6,38},{3,11},{7,39}} | collective-permute-start | bytes 983048 | tf_op jit(solution)/shard_map/ppermute | solution.py:276
  53.9 0.8 copy-start.1
  54.8 0.8 copy-start.5
  55.5 21.9 %copy-start.13 = (s32[32]{0:T(128)S(1)}, s32[32]{0:T(128)}, u32[]{:S(2)}) copy-start(s32[32]{0:T(128)} %param.5) | copy-start | bytes 388
  58.4 6.8 %collective-permute-start.11 = (f32[640,128]{1,0:T(8,128)S(1)}, f32[640,128]{1,0:T(8,128)S(1)}, u32[]{:S(2)}, u32[]{:S(2)}) collective-permute-start(f32[640,128]{1,0:T(8,128)S(1)} %add.259), channel_id=1, source_target_pairs={{0,24},{8,16},{4,100},{36,68},{1,25},{9,17},{5,101},{37,69},{2,26}... | collective-permute-start | bytes 983048 | tf_op jit(solution)/shard_map/ppermute | solution.py:285
  61.2 14.8 %collective-permute-start.13 = (f32[256,512]{1,0:T(8,128)}, f32[256,512]{1,0:T(8,128)S(1)}, u32[]{:S(2)}, u32[]{:S(2)}) collective-permute-start(f32[256,512]{1,0:T(8,128)} %copy-done.5), channel_id=1, source_target_pairs={{0,1},{1,2},{2,3},{3,0},{4,5},{5,6},{6,7},{7,4},{8,9},{9,10},{10,1... | collective-permute-start | bytes 1572872 | tf_op jit(solution)/shard_map/ppermute | solution.py:284
  65.2 6.0 %collective-permute-start.12 = (f32[640,128]{1,0:T(8,128)S(1)}, f32[640,128]{1,0:T(8,128)S(1)}, u32[]{:S(2)}, u32[]{:S(2)}) collective-permute-start(f32[640,128]{1,0:T(8,128)S(1)} %add.272), channel_id=1, source_target_pairs={{0,32},{8,40},{16,48},{24,56},{4,12},{36,44},{68,76},{100,108},{1,... | collective-permute-start | bytes 983048 | tf_op jit(solution)/shard_map/ppermute | solution.py:286
  66.5 15.0 %collective-permute-start.15 = (f32[256,512]{1,0:T(8,128)S(1)}, f32[256,512]{1,0:T(8,128)S(1)}, u32[]{:S(2)}, u32[]{:S(2)}) collective-permute-start(f32[256,512]{1,0:T(8,128)S(1)} %get-tuple-element.44), channel_id=1, source_target_pairs={{0,3},{1,0},{2,1},{3,2},{4,7},{5,4},{6,5},{7,6},{8,11},{9,8},{10,9... | collective-permute-start | bytes 1572872 | tf_op jit(solution)/shard_map/ppermute | solution.py:284
  76.0 44.4 %copy-start.9 = (f32[256,512]{1,0:T(8,128)}, f32[256,512]{1,0:T(8,128)S(1)}, u32[]{:S(2)}) copy-start(f32[256,512]{1,0:T(8,128)S(1)} %collective-permute-done.13.p1) | copy-start | bytes 1572868
  76.0 5.6 %collective-permute-start.14 = (f32[640,128]{1,0:T(8,128)S(1)}, f32[640,128]{1,0:T(8,128)S(1)}, u32[]{:S(2)}, u32[]{:S(2)}) collective-permute-start(f32[640,128]{1,0:T(8,128)S(1)} %add.273), channel_id=1, source_target_pairs={{0,96},{8,104},{16,112},{24,120},{32,64},{40,72},{48,80},{56,88},{... | collective-permute-start | bytes 983048 | tf_op jit(solution)/shard_map/ppermute | solution.py:288
  77.4 43.0 %collective-permute-start.17 = (f32[256,512]{1,0:T(8,128)S(1)}, f32[256,512]{1,0:T(8,128)S(1)}, u32[]{:S(2)}, u32[]{:S(2)}) collective-permute-start(f32[256,512]{1,0:T(8,128)S(1)} %get-tuple-element.51), channel_id=1, source_target_pairs={{0,2},{1,3},{2,0},{3,1},{4,6},{5,7},{6,4},{7,5},{8,10},{9,11},{10,... | collective-permute-start | bytes 1572872 | tf_op jit(solution)/shard_map/ppermute | solution.py:284
  81.6 38.8 %copy-start.10 = (f32[256,512]{1,0:T(8,128)}, f32[256,512]{1,0:T(8,128)S(1)}, u32[]{:S(2)}) copy-start(f32[256,512]{1,0:T(8,128)S(1)} %collective-permute-done.15.p3) | copy-start | bytes 1572868
  81.6 3.1 %collective-permute-start.16 = (f32[640,128]{1,0:T(8,128)S(1)}, f32[640,128]{1,0:T(8,128)S(1)}, u32[]{:S(2)}, u32[]{:S(2)}) collective-permute-start(f32[640,128]{1,0:T(8,128)S(1)} %add.274.own_ref), channel_id=1, source_target_pairs={{0,4},{4,0},{8,12},{12,8},{16,20},{20,16},{24,28},{28,24},{32,36},... | collective-permute-start | bytes 983048 | tf_op jit(solution)/shard_map/ppermute | solution.py:290
  118.2 0.7 copy-start.2
  118.9 0.7 copy-start.3
  119.6 0.7 copy-start.4
  120.3 0.8 copy-start.11
Sparse Core Ops, SparseCore 0:
  58.5 46.1 all-gather.2

commit v4 on v3

v4 whole, which is shorter than its diff:
```python
import jax
import jax.numpy as jnp
from jax import lax
from jax.experimental import pallas as pl
from jax.experimental.pallas import tpu as pltpu
from jax.sharding import PartitionSpec as P

PW = 256
LEAD = 512
HALF = 128
STEP = 8
TURN = 2
HIGHEST = lax.Precision.HIGHEST


def dot(a, b, ca, cb):
    return lax.dot_general(
        a, b, (((ca,), (cb,)), ((), ())), precision=HIGHEST, preferred_element_type=jnp.float32
    )


def spread_lane(rows, index):
    return jnp.broadcast_to(rows[:, index : index + 1], rows.shape)


def spread_row(rows, index):
    return jnp.broadcast_to(rows[index : index + 1, :], rows.shape)


def inverse_factor_128(square):
    n = HALF
    lane = lax.broadcasted_iota(jnp.int32, (STEP, n), 1)
    sub = lax.broadcasted_iota(jnp.int32, (STEP, n), 0)
    lane_turn = lax.broadcasted_iota(jnp.int32, (TURN * STEP, n), 1)
    count = n // STEP
    groups = [square[STEP * t : STEP * (t + 1), :] for t in range(count)]
    for turn in range(0, count, TURN):
        for step in range(turn, turn + TURN):
            start = STEP * step
            inside = (lane >= start) & (lane < start + STEP)
            top = groups[step]
            columns = [spread_lane(top, start + i) for i in range(STEP)]
            entry = [[spread_row(columns[i], j) if i <= j else None for i in range(STEP)] for j in range(STEP)]
            top = jnp.where(inside, jnp.where(lane - start == sub, 1.0, 0.0), top)
            rows = [spread_row(top, j) for j in range(STEP)]
            near = range(step + 1, min(turn + 2 * TURN, count))
            beside = {t: [spread_lane(groups[t], start + i) for i in range(STEP)] for t in near}
            for t in near:
                groups[t] = jnp.where(inside, 0.0, groups[t])
            done = [None] * STEP
            for i in range(STEP):
                scale = lax.rsqrt(entry[i][i])
                below = [None] * STEP
                for j in range(i + 1, STEP):
                    below[j] = entry[j][i] * scale
                    for k in range(i + 1, j + 1):
                        entry[j][k] = entry[j][k] - below[j] * below[k]
                done[i] = rows[i] * scale
                for j in range(i + 1, STEP):
                    rows[j] = rows[j] - below[j] * done[i]
                for t in near:
                    column = beside[t][i] * scale
                    for k in range(i + 1, STEP):
                        beside[t][k] = beside[t][k] - column * below[k]
                    groups[t] = groups[t] - column * done[i]
            solved = done[0]
            for i in range(1, STEP):
                solved = jnp.where(sub == i, done[i], solved)
            for t in range(step):
                groups[t] = jnp.where(inside, 0.0, groups[t])
            groups[step] = solved
        far = range(turn + 2 * TURN, count)
        if far:
            start, end = STEP * turn, STEP * (turn + TURN)
            solved = jnp.concatenate(groups[turn : turn + TURN], 0)
            ahead = jnp.where(lane_turn >= end + STEP * TURN, solved, 0.0)
            product = dot(ahead, solved, 0, 0)
            inside = (lane >= start) & (lane < end)
            for t in far:
                groups[t] = jnp.where(inside, 0.0, groups[t]) - product[STEP * t : STEP * (t + 1), :]
    return jnp.concatenate(groups, 0)


def inverse_factor_256(top, left, bottom):
    first = inverse_factor_128(top)
    across = dot(left, first, 1, 1)
    second = inverse_factor_128(bottom - dot(across, across, 1, 1))
    lower = -dot(second, dot(across, first, 1, 0), 1, 0)
    return jnp.concatenate(
        [
            jnp.concatenate([first, jnp.zeros_like(first)], 1),
            jnp.concatenate([lower, second], 1),
        ],
        0,
    )


def local_call(kernel, name, shapes, scalars=0, plan=()):
    whole = pl.BlockSpec(memory_space=pltpu.VMEM)
    small = pl.BlockSpec(memory_space=pltpu.SMEM)

    def call(*args):
        return pl.pallas_call(
            kernel,
            out_shape=[jax.ShapeDtypeStruct(shape, jnp.float32) for shape in shapes]
            + [jax.ShapeDtypeStruct(shape, jnp.int32) for shape in plan],
            in_specs=[small] * scalars + [whole] * (len(args) - scalars),
            out_specs=[whole] * len(shapes) + [small] * len(plan),
            compiler_params=pltpu.CompilerParams(vmem_limit_bytes=16 << 20),
            name=name,
        )(*args)

    return call


def position():
    row = lax.axis_index("row")
    return row // 8, (row // 2) % 4, row % 2, lax.axis_index("col")


def factor_kernel(own_ref, other_ref, inv_a_ref, across_ref, inv_b_ref):
    even = lax.axis_index("row") % 2 == 0
    own, other = own_ref[...], other_ref[...]
    zero = jnp.where(even, own, other)
    one = jnp.where(even, other, own)

    def piece(blocks, index):
        return blocks[index * HALF : (index + 1) * HALF]

    inv_a = inverse_factor_256(piece(zero, 0), piece(zero, 1), piece(zero, 2))
    across = jnp.concatenate(
        [
            dot(jnp.concatenate([piece(zero, 3), piece(zero, 4)], 0), inv_a, 0, 1),
            dot(jnp.concatenate([piece(one, 3), piece(one, 4)], 1), inv_a, 1, 1),
        ],
        0,
    )
    square = dot(across, across, 1, 1)
    inv_b = inverse_factor_256(
        piece(one, 0) - square[:HALF, :HALF],
        piece(one, 1) - square[HALF:, :HALF],
        piece(one, 2) - square[HALF:, HALF:],
    )
    inv_a_ref[...] = inv_a
    across_ref[...] = across
    inv_b_ref[...] = inv_b


def factor(own, other):
    return local_call(factor_kernel, "factor", [(PW, PW)] * 3)(own, other)


def share_kernel(lead_ref, mate_ref, *outs):
    _, line, core, _ = position()
    for hop in range(4):
        rows = pl.ds(pl.multiple_of(32 * (2 * ((line + hop) % 4) + core), 32), 32)
        for parity in range(2):

            @pl.when(core == parity)
            def _():
                outs[hop][parity] = lead_ref[rows, :]
                outs[hop][1 - parity] = mate_ref[rows, :]


def owners_and_ranks(map_ref, group):
    owners = [map_ref[8 * group + t] // 8 for t in range(8)]
    ranks = [sum((owners[p] == owners[t]).astype(jnp.int32) for p in range(t)) + jnp.int32(0) for t in range(8)]
    return owners, ranks


def sort_kernel(map_ref, *refs):
    ins, outs = refs[:4], refs[4:]
    plane, line, _, _ = position()
    owners, ranks = owners_and_ranks(map_ref, plane)
    for tile in range(8):
        for hop in range(4):

            @pl.when((line - tile // 2) % 4 == hop)
            def _():
                piece = ins[hop][tile % 2]
                for owner in range(4):

                    @pl.when(owners[tile] == owner)
                    def _():
                        outs[owner][pl.ds(ranks[tile], 1)] = piece[None]


def merge_kernel(*refs):
    for index, ref in enumerate(refs[:4]):

        @pl.when(lax.axis_index("col") == index)
        def _():
            refs[4][...] = ref[...]


def corner_kernel(*refs):
    plane, line, core, col = position()
    out = refs[4]
    out[...] = jnp.zeros_like(out)
    for index, ref in enumerate(refs[:4]):

        @pl.when((col == index) & (plane == 0) & (line == 0))
        def _():
            @pl.when(core == 0)
            def _():
                out[0 : 2 * HALF] = ref[:, :HALF]
                out[2 * HALF : 3 * HALF] = ref[HALF:, HALF:PW]
                out[3 * HALF :] = ref[:, PW : PW + HALF]

            @pl.when(core == 1)
            def _():
                out[0 : 2 * HALF] = ref[:, PW : PW + HALF]
                out[2 * HALF : 3 * HALF] = ref[HALF:, PW + HALF :]
                out[3 * HALF : 4 * HALF] = ref[HALF:, :HALF]
                out[4 * HALF :] = ref[HALF:, HALF:PW]


def pick_kernel(map_ref, front_ref, *refs):
    outs, plan_ref = refs[:4], refs[4]
    col = lax.axis_index("col")
    row = lax.axis_index("row")
    for group in range(4):
        owners, ranks = owners_and_ranks(map_ref, group)

        @pl.when(col == group)
        def _():
            for tile in range(8):
                for hop in range(4):

                    @pl.when((owners[tile] - col) % 4 == hop)
                    def _():
                        column = pl.multiple_of(ranks[tile] * PW, PW)
                        outs[hop][:, pl.ds(column, PW)] = front_ref[:, tile * PW : (tile + 1) * PW]

        for tile in range(8):
            slot = map_ref[8 * group + tile] % 8

            @pl.when(owners[tile] == col)
            def _():
                plan_ref[0, slot] = (col - group) % 4
                plan_ref[1, slot] = jnp.int32(group)
                plan_ref[2, slot] = ranks[tile]
                plan_ref[3, slot] = ((row >= 2) & (8 * group + tile >= 2)).astype(jnp.int32)


def update_kernel(plan, *refs):
    rows, inverse, pieces = refs[:4], refs[4:7], refs[7:11]
    ahead_ref, base_ref, panel_ref, out_ref, rows_ref, weight_ref = refs[11:]
    slot = pl.program_id(0)

    @pl.when(slot == 0)
    def _():
        for index, ref in enumerate(rows):

            @pl.when(lax.axis_index("col") == index)
            def _():
                rows_ref[...] = ref[...]

        inv_a, across, inv_b = [ref[...] for ref in inverse]
        panel_a = dot(rows_ref[:, :PW], inv_a, 1, 1)
        panel_b = dot(rows_ref[:, PW:] - dot(panel_a, across, 1, 1), inv_b, 1, 1)
        weight_b = dot(panel_b, inv_b, 1, 0)
        panel_ref[:, :PW] = panel_a
        panel_ref[:, PW:] = jnp.where(lax.axis_index("row") == 0, 0.0, panel_b)
        weight_ref[:, :PW] = dot(panel_a - dot(weight_b, across, 1, 0), inv_a, 1, 0)
        weight_ref[:, PW:] = weight_b

    product = dot(weight_ref[...], ahead_ref[...].reshape(PW, LEAD), 1, 1)
    column = pl.multiple_of(plan[2, slot] * PW, PW)
    base = base_ref[...]
    out_ref[...] = base
    for index, ref in enumerate(pieces):

        @pl.when((plan[0, slot] == index) & (plan[3, slot] == 1))
        def _():
            out_ref[...] = base + (ref[:, pl.ds(column, PW)] - product)


def update(plan, rows, inverse, pieces, ahead, base):
    height, width = base.shape
    whole = pl.BlockSpec(memory_space=pltpu.VMEM)
    tile = pl.BlockSpec((height, PW), lambda u, plan: (0, u))
    return pl.pallas_call(
        update_kernel,
        out_shape=[
            jax.ShapeDtypeStruct((height, LEAD), jnp.float32),
            jax.ShapeDtypeStruct(base.shape, jnp.float32),
        ],
        grid_spec=pltpu.PrefetchScalarGridSpec(
            num_scalar_prefetch=1,
            grid=(width // PW,),
            in_specs=[whole] * 11
            + [pl.BlockSpec((8, 1, 32, LEAD), lambda u, plan: (plan[1, u], plan[2, u], 0, 0)), tile],
            out_specs=[pl.BlockSpec((height, LEAD), lambda u, plan: (0, 0)), tile],
            scratch_shapes=[pltpu.VMEM((height, LEAD), jnp.float32)] * 2,
        ),
        compiler_params=pltpu.CompilerParams(vmem_limit_bytes=16 << 20),
        name="update",
    )(plan, *rows, *inverse, *pieces, ahead, base)


def spread_steps():
    have = [{(0, 0)}, {(0, 0)}]
    steps = []
    for step in range(4):
        pairs = []
        for core in range(2):
            axis = (step // 2 + 1 - core) % 2
            new = set()
            for at in sorted(have[core]):
                to = list(at)
                if step % 2 == 0:
                    to[axis] = 1
                else:
                    to[axis] = 3 if at[axis] == 0 else 2
                new.add(tuple(to))
                pairs.append(((at[0] * 4 + at[1]) * 2 + core, (to[0] * 4 + to[1]) * 2 + core))
            have[core] |= new
        steps.append(pairs)
    return steps


def shards(front, ancestor, tile_map):
    height = front.shape[0]
    swap = [(i, i ^ 1) for i in range(32)]
    part = (2, 32, LEAD)
    lead = front[:, :LEAD]

    copies = [lax.ppermute(lead, "col", [(0, to)]) for to in (1, 2, 3)]

    mate = lax.ppermute(lead, "row", swap)
    parts = list(local_call(share_kernel, "share", [part] * 4)(lead, mate))
    for hop in range(1, 4):
        pairs = [(z * 8 + x * 2 + k, z * 8 + (x + hop) % 4 * 2 + k) for z in range(4) for x in range(4) for k in range(2)]
        parts[hop] = lax.ppermute(parts[hop], "row", pairs)
    parts = list(local_call(sort_kernel, "sort", [part] * 4, 1)(tile_map, *parts))
    for to in range(1, 4):
        parts[to] = lax.ppermute(parts[to], "col", [(0, to)])
    copies, parts = lax.optimization_barrier((copies, parts))
    ahead = lax.all_gather(local_call(merge_kernel, "merge", [part])(*parts)[0], "row", axis=0, tiled=False)

    *pieces, plan = local_call(pick_kernel, "pick", [(height, 2 * PW)] * 4, 1, [(4, 8)])(tile_map, front)

    block = local_call(corner_kernel, "corner", [(5 * HALF, HALF)])(lead, *copies)[0]
    spread = spread_steps()
    block = block + lax.ppermute(block, "row", spread[0])
    block, *pieces = lax.optimization_barrier((block, *pieces))
    for hop in (1, 3, 2):
        pieces[hop] = lax.ppermute(pieces[hop], "col", [(i, (i + hop) % 4) for i in range(4)])
    block = block + lax.ppermute(block, "row", spread[1])
    block = block + lax.ppermute(block, "row", spread[2])
    block = block + lax.ppermute(block, "row", spread[3])
    block, pieces[1], pieces[3] = lax.optimization_barrier((block, pieces[1], pieces[3]))
    other = lax.ppermute(block, "row", swap)

    inverse = factor(block, other)
    panel, updated = update(plan, [lead, *copies], inverse, pieces, ahead, ancestor)
    return panel, updated


def solution(mesh):
    return jax.shard_map(
        shards,
        mesh=mesh,
        in_specs=(P("row", "col"), P("row", "col"), P()),
        out_specs=(P("row", None), P("row", "col")),
        check_vma=False,
    )
```

time: 145 us -> 138 us (0.952)
  the two profiles are of different devices: /device:TPU:1 before, /device:TPU:9 now
where the time goes in v4:
time: 138 us
  starting transfers between devices  38.9 us (28%)
  waiting for transfers between devices  35.1 us (25%)
  Pallas kernels  32.7 us (24%)
  local copies, waits for them, and re-layouts  16.6 us (12%)
  between operations  14.3 us (10%)
    pallas_call x6, Pallas kernels, call(): pl.pallas_call(kernel, out_shape=[jax.ShapeDtypeStruct(shape, jnp.float32...  22 us
    unnamed x40, local copies, waits for them, and re-layouts  15.5 us
    ppermute x1, starting transfers between devices, shards(): other = lax.ppermute(block, 'row', swap)  14.2 us
    ppermute x3, waiting for transfers between devices, shards(): copies = [lax.ppermute(lead, 'col', [(0, to)]) for to in (1, 2, 3)]  11.6 us
    pallas_call x1, Pallas kernels, update(): pl.pallas_call(update_kernel, out_shape=[jax.ShapeDtypeStruct((height, LE...  10.7 us
    ppermute x3, starting transfers between devices, shards(): lax.ppermute(pieces[hop], 'col', [(i, (i + hop) % 4) for i in range(4)])  6.1 us
    ppermute x3, waiting for transfers between devices, shards(): parts[hop] = lax.ppermute(parts[hop], 'row', pairs)  5.55 us
    ppermute x3, waiting for transfers between devices, shards(): lax.ppermute(pieces[hop], 'col', [(i, (i + hop) % 4) for i in range(4)])  5.32 us
  transfers between devices with their start and end apart: 19, of which 11 were waited for; matrix products, arithmetic and copies ran while one was open for 0% of the time, Pallas kernels for 16%

profile of v4, /device:TPU:9, one launch (start us, length us, event | category | flops | bytes accessed | tf_op | source)
XLA Modules:
  0.0 137.7 jit_solution(10913040775362824847)
XLA Ops:
  7.2 0.0 all-gather.3.cloned.1.call-start
  7.2 1.1 slice.3.lead_ref.refs_0_
  8.3 0.8 collective-permute-start.3
  9.1 0.7 collective-permute-start.2
  9.7 0.7 collective-permute-start.1
  10.4 1.3 collective-permute-start
  11.7 0.0 collective-permute-done.3.mate_ref
  11.8 0.1 share.1
  11.9 0.0 copy-start.1
  11.9 1.3 collective-permute-start.4
  13.1 2.5 %collective-permute-start.5 = (f32[2,32,512]{2,1,0:T(8,128)S(1)}, f32[2,32,512]{2,1,0:T(8,128)S(1)}, u32[]{:S(2)}, u32[]{:S(2)}) collective-permute-start(f32[2,32,512]{2,1,0:T(8,128)S(1)} %get-tuple-element.36), channel_id=1, source_target_pairs={{0,16},{4,20},{8,24},{12,28},{16,0},{20,4},{24,8},{28,12},{32,48},... | collective-permute-start | bytes 393224 | tf_op jit(solution)/shard_map/ppermute | solution.py:335
  15.6 2.6 %collective-permute-done.4.refs_1_ = f32[2,32,512]{2,1,0:T(8,128)S(1)} collective-permute-done((f32[2,32,512]{2,1,0:T(8,128)S(1)}, f32[2,32,512]{2,1,0:T(8,128)S(1)}, u32[]{:S(2)}, u32[]{:S(2)}) %collective-permute-start.4) | collective-permute-done | bytes 131104 | tf_op jit(solution)/shard_map/ppermute | solution.py:335
  18.2 1.3 collective-permute-start.6
  19.5 2.5 %collective-permute-done.5.refs_2_ = f32[2,32,512]{2,1,0:T(8,128)S(1)} collective-permute-done((f32[2,32,512]{2,1,0:T(8,128)S(1)}, f32[2,32,512]{2,1,0:T(8,128)S(1)}, u32[]{:S(2)}, u32[]{:S(2)}) %collective-permute-start.5) | collective-permute-done | bytes 131104 | tf_op jit(solution)/shard_map/ppermute | solution.py:335
  22.0 0.4 collective-permute-done.6.refs_3_
  22.4 1.0 sort.1
  23.4 1.3 collective-permute-start.7
  24.7 0.7 collective-permute-start.8
  25.4 0.0 collective-permute-done.2.refs_3_
  25.4 0.7 collective-permute-start.9
  26.1 0.0 copy-start.2
  26.1 0.8 copy-done.2
  26.9 11.6 %collective-permute-done.refs_1_ = f32[256,512]{1,0:T(8,128)S(1)} collective-permute-done((f32[256,512]{1,0:T(8,128)S(1)}, f32[256,512]{1,0:T(8,128)S(1)}, u32[]{:S(2)}, u32[]{:S(2)}) %collective-permute-start) | collective-permute-done | bytes 524320 | tf_op jit(solution)/shard_map/ppermute | solution.py:329
  38.5 0.8 copy-done.5
  39.3 2.0 %collective-permute-done.7.refs_1_ = f32[2,32,512]{2,1,0:T(8,128)S(1)} collective-permute-done((f32[2,32,512]{2,1,0:T(8,128)S(1)}, f32[2,32,512]{2,1,0:T(8,128)S(1)}, u32[]{:S(2)}, u32[]{:S(2)}) %collective-permute-start.7) | collective-permute-done | bytes 131104 | tf_op jit(solution)/shard_map/ppermute | solution.py:338
  41.3 0.0 collective-permute-done.8.refs_2_
  41.3 0.0 collective-permute-done.9.refs_3_
  41.3 0.7 merge.1
  42.0 0.0 all-gather.3.cloned.1.call-update
  42.0 0.0 copy-start.3
  42.0 1.0 copy-done.3
  43.0 1.0 copy-done.6
  44.1 0.1 corner.1
  44.1 3.5 %collective-permute-start.10 = (f32[640,128]{1,0:T(8,128)S(1)}, f32[640,128]{1,0:T(8,128)S(1)}, u32[]{:S(2)}, u32[]{:S(2)}) collective-permute-start(f32[640,128]{1,0:T(8,128)S(1)} %corner.1), channel_id=1, source_target_pairs={{0,8},{4,36},{1,9},{5,37},{2,10},{6,38},{3,11},{7,39}} | collective-permute-start | bytes 983048 | tf_op jit(solution)/shard_map/ppermute | solution.py:346
  47.7 2.0 %pick.1 = (f32[256,512]{1,0:T(8,128)S(1)}, f32[256,512]{1,0:T(8,128)S(1)}, f32[256,512]{1,0:T(8,128)S(1)}, f32[256,512]{1,0:T(8,128)S(1)}, s32[4,8]{1,0:T(4,128)S(1)}) custom-call(s32[32]{0:T(128)S(1)} %copy-done.19, f32[256,2048]{1,0:T(8,128)S(1)} %copy-done.1), custom_call_target="tpu_custom_call" | custom-call | tf_op jit(solution)/shard_map/pick/pallas_call | solution.py:103
  49.7 0.0 copy-start.4
  49.7 0.0 copy-start.7
  49.7 1.9 %collective-permute-done.10 = f32[640,128]{1,0:T(8,128)S(1)} collective-permute-done((f32[640,128]{1,0:T(8,128)S(1)}, f32[640,128]{1,0:T(8,128)S(1)}, u32[]{:S(2)}, u32[]{:S(2)}) %collective-permute-start.10) | collective-permute-done | bytes 327712 | tf_op jit(solution)/shard_map/ppermute | solution.py:346
  51.7 1.3 collective-permute-start.11
  53.0 4.0 %collective-permute-done.11 = f32[640,128]{1,0:T(8,128)S(1)} collective-permute-done((f32[640,128]{1,0:T(8,128)S(1)}, f32[640,128]{1,0:T(8,128)S(1)}, u32[]{:S(2)}, u32[]{:S(2)}) %collective-permute-start.11) | collective-permute-done | bytes 327712 | tf_op jit(solution)/shard_map/ppermute | solution.py:350
  57.0 1.3 collective-permute-start.12
  58.4 4.8 %collective-permute-start.14 = (f32[256,512]{1,0:T(8,128)S(1)}, f32[256,512]{1,0:T(8,128)S(1)}, u32[]{:S(2)}, u32[]{:S(2)}) collective-permute-start(f32[256,512]{1,0:T(8,128)S(1)} %get-tuple-element.50), channel_id=1, source_target_pairs={{0,1},{1,2},{2,3},{3,0},{4,5},{5,6},{6,7},{7,4},{8,9},{9,10},{10,1... | collective-permute-start | bytes 1572872 | tf_op jit(solution)/shard_map/ppermute | solution.py:349
  63.1 0.0 collective-permute-done.12
  63.2 1.3 collective-permute-start.13
  64.5 1.3 collective-permute-start.17
  65.8 3.3 %collective-permute-done.13 = f32[640,128]{1,0:T(8,128)S(1)} collective-permute-done((f32[640,128]{1,0:T(8,128)S(1)}, f32[640,128]{1,0:T(8,128)S(1)}, u32[]{:S(2)}, u32[]{:S(2)}) %collective-permute-start.13) | collective-permute-done | bytes 327712 | tf_op jit(solution)/shard_map/ppermute | solution.py:352
  69.1 3.7 %collective-permute-done.14.refs_8_ = f32[256,512]{1,0:T(8,128)S(1)} collective-permute-done((f32[256,512]{1,0:T(8,128)S(1)}, f32[256,512]{1,0:T(8,128)S(1)}, u32[]{:S(2)}, u32[]{:S(2)}) %collective-permute-start.14) | collective-permute-done | bytes 524320 | tf_op jit(solution)/shard_map/ppermute | solution.py:349
  72.8 1.6 %collective-permute-done.15.refs_10_ = f32[256,512]{1,0:T(8,128)S(1)} collective-permute-done((f32[256,512]{1,0:T(8,128)S(1)}, f32[256,512]{1,0:T(8,128)S(1)}, u32[]{:S(2)}, u32[]{:S(2)}) %collective-permute-start.15) | collective-permute-done | bytes 524320 | tf_op jit(solution)/shard_map/ppermute | solution.py:349
  74.4 0.8 copy-done.11
  75.3 14.2 %collective-permute-start.16 = (f32[640,128]{1,0:T(8,128)S(1)}, f32[640,128]{1,0:T(8,128)S(1)}, u32[]{:S(2)}, u32[]{:S(2)}) collective-permute-start(f32[640,128]{1,0:T(8,128)S(1)} %add.15.own_ref), channel_id=1, source_target_pairs={{0,4},{4,0},{8,12},{12,8},{16,20},{20,16},{24,28},{28,24},{32,36},... | collective-permute-start | bytes 983048 | tf_op jit(solution)/shard_map/ppermute | solution.py:354
  89.5 1.4 %collective-permute-done.16.other_ref = f32[640,128]{1,0:T(8,128)S(1)} collective-permute-done((f32[640,128]{1,0:T(8,128)S(1)}, f32[640,128]{1,0:T(8,128)S(1)}, u32[]{:S(2)}, u32[]{:S(2)}) %collective-permute-start.16) | collective-permute-done | bytes 327712 | tf_op jit(solution)/shard_map/ppermute | solution.py:354
  90.9 18.2 %factor.1 = (f32[256,256]{1,0:T(8,128)S(1)}, f32[256,256]{1,0:T(8,128)S(1)}, f32[256,256]{1,0:T(8,128)S(1)}) custom-call(f32[640,128]{1,0:T(8,128)S(1)} %add.15.own_ref, f32[640,128]{1,0:T(8,128)S(1)} %collective-permute-done.16.other_ref), custom_call_target="tpu_custom_call" | custom-call | tf_op jit(solution)/shard_map/factor/pallas_call | solution.py:103
  109.2 0.7 copy-done.15
  109.9 0.7 copy-done.17
  110.6 0.0 collective-permute-done.17.refs_9_
  110.6 0.8 copy-done.13
  111.4 2.2 %copy-done = f32[64,32,512]{2,1,0:T(8,128)S(1)} copy-done((f32[64,32,512]{2,1,0:T(8,128)S(1)}, f32[64,32,512]{2,1,0:T(8,128)}, u32[]{:S(2)}) %copy-start) | copy-done | bytes 4194328
  113.6 1.6 %copy-done.8 = f32[256,2048]{1,0:T(8,128)S(1)} copy-done((f32[256,2048]{1,0:T(8,128)S(1)}, f32[256,2048]{1,0:T(8,128)}, u32[]{:S(2)}) %copy-start.8) | copy-done | bytes 2097176
  115.2 1.0 copy-done.10
  116.2 1.0 copy-done.12
  117.3 1.0 copy-done.14
  118.3 0.9 copy-done.16
  119.2 0.9 copy-done.18
  120.2 10.7 %update.1 = (f32[256,512]{1,0:T(8,128)}, f32[256,2048]{1,0:T(8,128)}) custom-call(s32[4,8]{1,0:T(4,128)S(1)} %get-tuple-element.33.plan, f32[256,512]{1,0:T(8,128)S(1)} %slice.3.lead_ref.refs_0_, f32[256,512]{1,0:T(8,128)S(1)} %copy-done.7, f32[256,512]{1,0:T(8,128)S(1)} %copy-done.4, f32[256,512]{1,0:T(8,128)S(1)} %collective-permute-done.2.refs_3_, ...), custom_call_target="tpu_custom_call" | custom-call | tf_op jit(solution)/shard_map/update/pallas_call | solution.py:283
  (27 shorter events, 0.2 us)
Async XLA Ops:
  7.2 15.3 %copy-start.19 = (s32[32]{0:T(128)S(1)}, s32[32]{0:T(128)}, u32[]{:S(2)}) copy-start(s32[32]{0:T(128)} %map_ref.3) | copy-start | bytes 388
  7.2 104.2 %all-gather.3.cloned.1.call-start = ((), (), s32[]{:S(2)}) async-start(), calls=%async_computation | async-start | bytes 4325376 | tf_op jit(solution)/shard_map/all_gather | solution.py:340
  8.3 3.5 %collective-permute-start.3 = (f32[256,512]{1,0:T(8,128)S(1)}, f32[256,512]{1,0:T(8,128)S(1)}, u32[]{:S(2)}, u32[]{:S(2)}) collective-permute-start(f32[256,512]{1,0:T(8,128)S(1)} %slice.3.lead_ref.refs_0_), channel_id=1, source_target_pairs={{0,4},{4,0},{8,12},{12,8},{16,20},{20,16},{24,28},{28,24},{32,36},... | collective-permute-start | bytes 1572872 | tf_op jit(solution)/shard_map/ppermute | solution.py:331
  9.1 16.4 %collective-permute-start.2 = (f32[256,512]{1,0:T(8,128)S(1)}, f32[256,512]{1,0:T(8,128)S(1)}, u32[]{:S(2)}, u32[]{:S(2)}) collective-permute-start(f32[256,512]{1,0:T(8,128)S(1)} %slice.3.lead_ref.refs_0_), channel_id=1, source_target_pairs={{0,3},{4,7},{8,11},{12,15},{16,19},{20,23},{24,27},{28,31},{32,35}... | collective-permute-start | bytes 1572872 | tf_op jit(solution)/shard_map/ppermute | solution.py:329
  9.7 16.4 %collective-permute-start.1 = (f32[256,512]{1,0:T(8,128)S(1)}, f32[256,512]{1,0:T(8,128)S(1)}, u32[]{:S(2)}, u32[]{:S(2)}) collective-permute-start(f32[256,512]{1,0:T(8,128)S(1)} %slice.3.lead_ref.refs_0_), channel_id=1, source_target_pairs={{0,2},{4,6},{8,10},{12,14},{16,18},{20,22},{24,26},{28,30},{32,34}... | collective-permute-start | bytes 1572872 | tf_op jit(solution)/shard_map/ppermute | solution.py:329
  10.4 28.0 %collective-permute-start = (f32[256,512]{1,0:T(8,128)S(1)}, f32[256,512]{1,0:T(8,128)S(1)}, u32[]{:S(2)}, u32[]{:S(2)}) collective-permute-start(f32[256,512]{1,0:T(8,128)S(1)} %slice.3.lead_ref.refs_0_), channel_id=1, source_target_pairs={{0,1},{4,5},{8,9},{12,13},{16,17},{20,21},{24,25},{28,29},{32,33},... | collective-permute-start | bytes 1572872 | tf_op jit(solution)/shard_map/ppermute | solution.py:329
  11.9 35.8 %copy-start.1 = (f32[256,2048]{1,0:T(8,128)S(1)}, f32[256,2048]{1,0:T(8,128)}, u32[]{:S(2)}) copy-start(f32[256,2048]{1,0:T(8,128)} %front_ref.1) | copy-start | bytes 6291460
  11.9 6.4 %collective-permute-start.4 = (f32[2,32,512]{2,1,0:T(8,128)S(1)}, f32[2,32,512]{2,1,0:T(8,128)S(1)}, u32[]{:S(2)}, u32[]{:S(2)}) collective-permute-start(f32[2,32,512]{2,1,0:T(8,128)S(1)} %get-tuple-element.35), channel_id=1, source_target_pairs={{0,8},{4,12},{8,16},{12,20},{16,24},{20,28},{24,0},{28,4},{32,40},... | collective-permute-start | bytes 393224 | tf_op jit(solution)/shard_map/ppermute | solution.py:335
  13.1 8.9 %collective-permute-start.5 = (f32[2,32,512]{2,1,0:T(8,128)S(1)}, f32[2,32,512]{2,1,0:T(8,128)S(1)}, u32[]{:S(2)}, u32[]{:S(2)}) collective-permute-start(f32[2,32,512]{2,1,0:T(8,128)S(1)} %get-tuple-element.36), channel_id=1, source_target_pairs={{0,16},{4,20},{8,24},{12,28},{16,0},{20,4},{24,8},{28,12},{32,48},... | collective-permute-start | bytes 393224 | tf_op jit(solution)/shard_map/ppermute | solution.py:335
  18.2 4.2 %collective-permute-start.6 = (f32[2,32,512]{2,1,0:T(8,128)S(1)}, f32[2,32,512]{2,1,0:T(8,128)S(1)}, u32[]{:S(2)}, u32[]{:S(2)}) collective-permute-start(f32[2,32,512]{2,1,0:T(8,128)S(1)} %get-tuple-element.37), channel_id=1, source_target_pairs={{0,24},{4,28},{8,0},{12,4},{16,8},{20,12},{24,16},{28,20},{32,56},... | collective-permute-start | bytes 393224 | tf_op jit(solution)/shard_map/ppermute | solution.py:335
  23.4 17.9 %collective-permute-start.7 = (f32[2,32,512]{2,1,0:T(8,128)S(1)}, f32[2,32,512]{2,1,0:T(8,128)S(1)}, u32[]{:S(2)}, u32[]{:S(2)}) collective-permute-start(f32[2,32,512]{2,1,0:T(8,128)S(1)} %get-tuple-element.39), channel_id=1, source_target_pairs={{0,1},{4,5},{8,9},{12,13},{16,17},{20,21},{24,25},{28,29},{32,33},... | collective-permute-start | bytes 393224 | tf_op jit(solution)/shard_map/ppermute | solution.py:338
  24.7 16.6 %collective-permute-start.8 = (f32[2,32,512]{2,1,0:T(8,128)S(1)}, f32[2,32,512]{2,1,0:T(8,128)S(1)}, u32[]{:S(2)}, u32[]{:S(2)}) collective-permute-start(f32[2,32,512]{2,1,0:T(8,128)S(1)} %get-tuple-element.40), channel_id=1, source_target_pairs={{0,2},{4,6},{8,10},{12,14},{16,18},{20,22},{24,26},{28,30},{32,34}... | collective-permute-start | bytes 393224 | tf_op jit(solution)/shard_map/ppermute | solution.py:338
  25.4 15.9 %collective-permute-start.9 = (f32[2,32,512]{2,1,0:T(8,128)S(1)}, f32[2,32,512]{2,1,0:T(8,128)S(1)}, u32[]{:S(2)}, u32[]{:S(2)}) collective-permute-start(f32[2,32,512]{2,1,0:T(8,128)S(1)} %get-tuple-element.41), channel_id=1, source_target_pairs={{0,3},{4,7},{8,11},{12,15},{16,19},{20,23},{24,27},{28,31},{32,35}... | collective-permute-start | bytes 393224 | tf_op jit(solution)/shard_map/ppermute | solution.py:338
  26.1 0.8 copy-start.2
  38.5 0.8 copy-start.5
  42.0 1.0 copy-start.3
  43.0 1.0 copy-start.6
  44.1 7.5 %collective-permute-start.10 = (f32[640,128]{1,0:T(8,128)S(1)}, f32[640,128]{1,0:T(8,128)S(1)}, u32[]{:S(2)}, u32[]{:S(2)}) collective-permute-start(f32[640,128]{1,0:T(8,128)S(1)} %corner.1), channel_id=1, source_target_pairs={{0,8},{4,36},{1,9},{5,37},{2,10},{6,38},{3,11},{7,39}} | collective-permute-start | bytes 983048 | tf_op jit(solution)/shard_map/ppermute | solution.py:346
  49.7 23.1 %copy-start.9 = (f32[256,512]{1,0:T(8,128)}, f32[256,512]{1,0:T(8,128)S(1)}, u32[]{:S(2)}) copy-start(f32[256,512]{1,0:T(8,128)S(1)} %get-tuple-element.56.refs_7_) | copy-start | bytes 1572868
  49.7 61.7 %copy-start.4 = (f32[256,512]{1,0:T(8,128)S(1)}, f32[256,512]{1,0:T(8,128)}, u32[]{:S(2)}) copy-start(f32[256,512]{1,0:T(8,128)} %copy-done.2) | copy-start | bytes 1572868
  49.7 61.7 %copy-start.7 = (f32[256,512]{1,0:T(8,128)S(1)}, f32[256,512]{1,0:T(8,128)}, u32[]{:S(2)}) copy-start(f32[256,512]{1,0:T(8,128)} %copy-done.5) | copy-start | bytes 1572868
  51.7 5.3 %collective-permute-start.11 = (f32[640,128]{1,0:T(8,128)S(1)}, f32[640,128]{1,0:T(8,128)S(1)}, u32[]{:S(2)}, u32[]{:S(2)}) collective-permute-start(f32[640,128]{1,0:T(8,128)S(1)} %add.12), channel_id=1, source_target_pairs={{0,24},{8,16},{4,100},{36,68},{1,25},{9,17},{5,101},{37,69},{2,26}... | collective-permute-start | bytes 983048 | tf_op jit(solution)/shard_map/ppermute | solution.py:350
  57.0 6.1 %collective-permute-start.12 = (f32[640,128]{1,0:T(8,128)S(1)}, f32[640,128]{1,0:T(8,128)S(1)}, u32[]{:S(2)}, u32[]{:S(2)}) collective-permute-start(f32[640,128]{1,0:T(8,128)S(1)} %add.13), channel_id=1, source_target_pairs={{0,32},{8,40},{16,48},{24,56},{4,12},{36,44},{68,76},{100,108},{1,... | collective-permute-start | bytes 983048 | tf_op jit(solution)/shard_map/ppermute | solution.py:351
  58.4 14.5 %collective-permute-start.14 = (f32[256,512]{1,0:T(8,128)S(1)}, f32[256,512]{1,0:T(8,128)S(1)}, u32[]{:S(2)}, u32[]{:S(2)}) collective-permute-start(f32[256,512]{1,0:T(8,128)S(1)} %get-tuple-element.50), channel_id=1, source_target_pairs={{0,1},{1,2},{2,3},{3,0},{4,5},{5,6},{6,7},{7,4},{8,9},{9,10},{10,1... | collective-permute-start | bytes 1572872 | tf_op jit(solution)/shard_map/ppermute | solution.py:349
  63.1 11.3 %collective-permute-start.15 = (f32[256,512]{1,0:T(8,128)S(1)}, f32[256,512]{1,0:T(8,128)S(1)}, u32[]{:S(2)}, u32[]{:S(2)}) collective-permute-start(f32[256,512]{1,0:T(8,128)S(1)} %get-tuple-element.51), channel_id=1, source_target_pairs={{0,3},{1,0},{2,1},{3,2},{4,7},{5,4},{6,5},{7,6},{8,11},{9,8},{10,9... | collective-permute-start | bytes 1572872 | tf_op jit(solution)/shard_map/ppermute | solution.py:349
  63.2 5.9 %collective-permute-start.13 = (f32[640,128]{1,0:T(8,128)S(1)}, f32[640,128]{1,0:T(8,128)S(1)}, u32[]{:S(2)}, u32[]{:S(2)}) collective-permute-start(f32[640,128]{1,0:T(8,128)S(1)} %add.14), channel_id=1, source_target_pairs={{0,96},{8,104},{16,112},{24,120},{32,64},{40,72},{48,80},{56,88},{... | collective-permute-start | bytes 983048 | tf_op jit(solution)/shard_map/ppermute | solution.py:352
  64.5 46.1 %collective-permute-start.17 = (f32[256,512]{1,0:T(8,128)S(1)}, f32[256,512]{1,0:T(8,128)S(1)}, u32[]{:S(2)}, u32[]{:S(2)}) collective-permute-start(f32[256,512]{1,0:T(8,128)S(1)} %get-tuple-element.58), channel_id=1, source_target_pairs={{0,2},{1,3},{2,0},{3,1},{4,6},{5,7},{6,4},{7,5},{8,10},{9,11},{10,... | collective-permute-start | bytes 1572872 | tf_op jit(solution)/shard_map/ppermute | solution.py:349
  74.4 0.8 copy-start.11
  75.3 15.7 %collective-permute-start.16 = (f32[640,128]{1,0:T(8,128)S(1)}, f32[640,128]{1,0:T(8,128)S(1)}, u32[]{:S(2)}, u32[]{:S(2)}) collective-permute-start(f32[640,128]{1,0:T(8,128)S(1)} %add.15.own_ref), channel_id=1, source_target_pairs={{0,4},{4,0},{8,12},{12,8},{16,20},{20,16},{24,28},{28,24},{32,36},... | collective-permute-start | bytes 983048 | tf_op jit(solution)/shard_map/ppermute | solution.py:354
  109.2 0.7 copy-start.15
  109.9 0.7 copy-start.17
  110.6 0.8 copy-start.13
  111.4 2.2 %copy-start = (f32[64,32,512]{2,1,0:T(8,128)S(1)}, f32[64,32,512]{2,1,0:T(8,128)}, u32[]{:S(2)}) copy-start(f32[64,32,512]{2,1,0:T(8,128)} %all-gather.3.cloned.1.call-done) | copy-start | bytes 12582916
  113.6 1.6 %copy-start.8 = (f32[256,2048]{1,0:T(8,128)S(1)}, f32[256,2048]{1,0:T(8,128)}, u32[]{:S(2)}) copy-start(f32[256,2048]{1,0:T(8,128)} %refs_12_.1) | copy-start | bytes 6291460
  115.2 1.0 copy-start.10
  116.2 1.0 copy-start.12
  117.2 1.0 copy-start.14
  118.3 0.9 copy-start.16
  119.2 0.9 copy-start.18
Sparse Core Ops, SparseCore 0:
  42.1 51.9 all-gather.2

commit v5 on v4

--- a/solution.py
+++ b/solution.py
@@ -243,30 +243,62 @@
                 plan_ref[3, slot] = ((row >= 2) & (8 * group + tile >= 2)).astype(jnp.int32)
 
 
+def weight_kernel(*refs):
+    rows, inverse = refs[:4], refs[4:7]
+    panel_ref, weight_ref, rows_ref = refs[7:]
+    for index, ref in enumerate(rows):
+
+        @pl.when(lax.axis_index("col") == index)
+        def _():
+            rows_ref[...] = ref[...]
+
+    inv_a, across, inv_b = [ref[...] for ref in inverse]
+    panel_a = dot(rows_ref[:, :PW], inv_a, 1, 1)
+    panel_b = dot(rows_ref[:, PW:] - dot(panel_a, across, 1, 1), inv_b, 1, 1)
+    weight_b = dot(panel_b, inv_b, 1, 0)
+    panel_ref[:, :PW] = panel_a
+    panel_ref[:, PW:] = jnp.where(lax.axis_index("row") == 0, 0.0, panel_b)
+    weight_ref[:, :PW] = dot(panel_a - dot(weight_b, across, 1, 0), inv_a, 1, 0)
+    weight_ref[:, PW:] = weight_b
+
+
+def weigh(rows, inverse):
+    whole = pl.BlockSpec(memory_space=pltpu.VMEM)
+    shape = (rows[0].shape[0], LEAD)
+    return pl.pallas_call(
+        weight_kernel,
+        out_shape=[jax.ShapeDtypeStruct(shape, jnp.float32)] * 2,
+        in_specs=[whole] * 7,
+        out_specs=[whole] * 2,
+        scratch_shapes=[pltpu.VMEM(shape, jnp.float32)],
+        compiler_params=pltpu.CompilerParams(vmem_limit_bytes=16 << 20),
+        name="weigh",
+    )(*rows, *inverse)
+
+
 def update_kernel(plan, *refs):
-    rows, inverse, pieces = refs[:4], refs[4:7], refs[7:11]
-    ahead_ref, base_ref, panel_ref, out_ref, rows_ref, weight_ref = refs[11:]
+    weight_ref, pieces, gathered = refs[0], refs[1:5], refs[5:9]
+    base_ref, out_ref, ahead_ref = refs[9:]
     slot = pl.program_id(0)
-
-    @pl.when(slot == 0)
-    def _():
-        for index, ref in enumerate(rows):
-
-            @pl.when(lax.axis_index("col") == index)
-            def _():
-                rows_ref[...] = ref[...]
-
-        inv_a, across, inv_b = [ref[...] for ref in inverse]
-        panel_a = dot(rows_ref[:, :PW], inv_a, 1, 1)
-        panel_b = dot(rows_ref[:, PW:] - dot(panel_a, across, 1, 1), inv_b, 1, 1)
-        weight_b = dot(panel_b, inv_b, 1, 0)
-        panel_ref[:, :PW] = panel_a
-        panel_ref[:, PW:] = jnp.where(lax.axis_index("row") == 0, 0.0, panel_b)
-        weight_ref[:, :PW] = dot(panel_a - dot(weight_b, across, 1, 0), inv_a, 1, 0)
-        weight_ref[:, PW:] = weight_b
-
-    product = dot(weight_ref[...], ahead_ref[...].reshape(PW, LEAD), 1, 1)
-    column = pl.multiple_of(plan[2, slot] * PW, PW)
+    plane, line, core, _ = position()
+    group, place = plan[1, slot], plan[2, slot]
+    for parity in range(2):
+        holder = core if parity == 0 else 1 - core
+        for x in range(4):
+            off_z, off_x = plane ^ group, line ^ x
+            first = jnp.where(holder == 0, off_x, off_z)
+            second = jnp.where(holder == 0, off_z, off_x)
+            index = ((first & 1) ^ (first >> 1)) + 2 * (first >> 1) + 4 * ((second & 1) ^ (second >> 1))
+            rows = pl.ds(pl.multiple_of(index * 64 + place * 32, 32), 32)
+            into = pl.ds(pl.multiple_of((2 * x + holder) * 32, 32), 32)
+            for late in range(2):
+
+                @pl.when((second >> 1) == late)
+                def _():
+                    ahead_ref[into, :] = gathered[2 * parity + late][rows, :]
+
+    product = dot(weight_ref[...], ahead_ref[...], 1, 1)
+    column = pl.multiple_of(place * PW, PW)
     base = base_ref[...]
     out_ref[...] = base
     for index, ref in enumerate(pieces):
@@ -276,48 +308,41 @@
             out_ref[...] = base + (ref[:, pl.ds(column, PW)] - product)
 
 
-def update(plan, rows, inverse, pieces, ahead, base):
+def update(plan, weight, pieces, gathered, base):
     height, width = base.shape
     whole = pl.BlockSpec(memory_space=pltpu.VMEM)
     tile = pl.BlockSpec((height, PW), lambda u, plan: (0, u))
     return pl.pallas_call(
         update_kernel,
-        out_shape=[
-            jax.ShapeDtypeStruct((height, LEAD), jnp.float32),
-            jax.ShapeDtypeStruct(base.shape, jnp.float32),
-        ],
+        out_shape=jax.ShapeDtypeStruct(base.shape, jnp.float32),
         grid_spec=pltpu.PrefetchScalarGridSpec(
             num_scalar_prefetch=1,
             grid=(width // PW,),
-            in_specs=[whole] * 11
-            + [pl.BlockSpec((8, 1, 32, LEAD), lambda u, plan: (plan[1, u], plan[2, u], 0, 0)), tile],
-            out_specs=[pl.BlockSpec((height, LEAD), lambda u, plan: (0, 0)), tile],
-            scratch_shapes=[pltpu.VMEM((height, LEAD), jnp.float32)] * 2,
+            in_specs=[whole] * 9 + [tile],
+            out_specs=tile,
+            scratch_shapes=[pltpu.VMEM((PW, LEAD), jnp.float32)],
         ),
         compiler_params=pltpu.CompilerParams(vmem_limit_bytes=16 << 20),
         name="update",
-    )(plan, *rows, *inverse, *pieces, ahead, base)
-
-
-def spread_steps():
+    )(plan, weight, *pieces, *gathered, base)
+
+
+def doubling_steps():
+    every, spread = [], []
     have = [{(0, 0)}, {(0, 0)}]
-    steps = []
     for step in range(4):
+        flip = 1 if step % 2 == 0 else 3
         pairs = []
+        for z in range(4):
+            for x in range(4):
+                for core in range(2):
+                    to = (z, x ^ flip) if step // 2 == core else (z ^ flip, x)
+                    pairs.append(((z * 4 + x) * 2 + core, (to[0] * 4 + to[1]) * 2 + core, (z, x), to, core))
+        every.append([pair[:2] for pair in pairs])
+        spread.append([pair[:2] for pair in pairs if pair[2] in have[pair[4]]])
         for core in range(2):
-            axis = (step // 2 + 1 - core) % 2
-            new = set()
-            for at in sorted(have[core]):
-                to = list(at)
-                if step % 2 == 0:
-                    to[axis] = 1
-                else:
-                    to[axis] = 3 if at[axis] == 0 else 2
-                new.add(tuple(to))
-                pairs.append(((at[0] * 4 + at[1]) * 2 + core, (to[0] * 4 + to[1]) * 2 + core))
-            have[core] |= new
-        steps.append(pairs)
-    return steps
+            have[core] |= {pair[3] for pair in pairs if pair[4] == core and pair[2] in have[core]}
+    return every, spread
 
 
 def shards(front, ancestor, tile_map):
@@ -337,24 +362,33 @@
     for to in range(1, 4):
         parts[to] = lax.ppermute(parts[to], "col", [(0, to)])
     copies, parts = lax.optimization_barrier((copies, parts))
-    ahead = lax.all_gather(local_call(merge_kernel, "merge", [part])(*parts)[0], "row", axis=0, tiled=False)
+    gathered = local_call(merge_kernel, "merge", [part])(*parts)[0].reshape(64, LEAD)
 
     *pieces, plan = local_call(pick_kernel, "pick", [(height, 2 * PW)] * 4, 1, [(4, 8)])(tile_map, front)
 
     block = local_call(corner_kernel, "corner", [(5 * HALF, HALF)])(lead, *copies)[0]
-    spread = spread_steps()
-    block = block + lax.ppermute(block, "row", spread[0])
-    block, *pieces = lax.optimization_barrier((block, *pieces))
-    for hop in (1, 3, 2):
-        pieces[hop] = lax.ppermute(pieces[hop], "col", [(i, (i + hop) % 4) for i in range(4)])
-    block = block + lax.ppermute(block, "row", spread[1])
-    block = block + lax.ppermute(block, "row", spread[2])
+    every, spread = doubling_steps()
+    ring = [[(i, (i + hop) % 4) for i in range(4)] for hop in range(4)]
+    for step in range(3):
+        block = block + lax.ppermute(block, "row", spread[step])
+        gathered = jnp.concatenate([gathered, lax.ppermute(gathered, "row", every[step])], 0)
+        if step == 1:
+            pieces[1], pieces[3] = [lax.ppermute(pieces[hop], "col", ring[hop]) for hop in (1, 3)]
+        if step != 1:
+            block, gathered, *pieces = lax.optimization_barrier((block, gathered, *pieces))
+        else:
+            block, gathered = lax.optimization_barrier((block, gathered))
+    pieces[2] = lax.ppermute(pieces[2], "col", ring[2])
+    late = lax.ppermute(gathered, "row", every[3])
     block = block + lax.ppermute(block, "row", spread[3])
-    block, pieces[1], pieces[3] = lax.optimization_barrier((block, pieces[1], pieces[3]))
     other = lax.ppermute(block, "row", swap)
+    other_gathered = lax.ppermute(gathered, "row", swap)
 
     inverse = factor(block, other)
-    panel, updated = update(plan, [lead, *copies], inverse, pieces, ahead, ancestor)
+    late, inverse = lax.optimization_barrier((late, inverse))
+    other_late = lax.ppermute(late, "row", swap)
+    panel, weight = weigh([lead, *copies], inverse)
+    updated = update(plan, weight, pieces, [gathered, late, other_gathered, other_late], ancestor)
     return panel, updated
 
 

time: 138 us -> 133 us (0.964)
  the two profiles are of different devices: /device:TPU:9 before, /device:TPU:1 now
where the time goes in v5:
time: 133 us; the launch traced here: 131 us
  waiting for transfers between devices  52.2 us (39%)
  starting transfers between devices  43.5 us (33%)
  Pallas kernels  32.9 us (25%)
    pallas_call x6, Pallas kernels, call(): pl.pallas_call(kernel, out_shape=[jax.ShapeDtypeStruct(shape, jnp.float32...  21.4 us
    ppermute x3, starting transfers between devices, shards(): block = block + lax.ppermute(block, 'row', spread[step])  11.4 us
    ppermute x1, waiting for transfers between devices, shards(): block = block + lax.ppermute(block, 'row', spread[3])  10.7 us
    ppermute x1, waiting for transfers between devices, shards(): pieces[2] = lax.ppermute(pieces[2], 'col', ring[2])  10.1 us
    pallas_call x1, Pallas kernels, update(): pl.pallas_call(update_kernel, out_shape=jax.ShapeDtypeStruct(base.shape,...  8.6 us
    ppermute x3, starting transfers between devices, shards(): copies = [lax.ppermute(lead, 'col', [(0, to)]) for to in (1, 2, 3)]  7.39 us
    ppermute x3, waiting for transfers between devices, shards(): copies = [lax.ppermute(lead, 'col', [(0, to)]) for to in (1, 2, 3)]  5.97 us
    ppermute x3, waiting for transfers between devices, shards(): block = block + lax.ppermute(block, 'row', spread[step])  5.8 us
  transfers between devices with their start and end apart: 24, of which 15 were waited for; matrix products, arithmetic and copies ran while one was open for 0% of the time, Pallas kernels for 19%

profile of v5, /device:TPU:1, one launch (start us, length us, event | category | flops | bytes accessed | tf_op | source)
XLA Modules:
  0.0 130.9 jit_solution(10535250271912546261)
XLA Ops:
  0.6 0.0 copy-start.2
  0.6 1.1 slice.3.lead_ref.refs_0_
  1.7 0.0 copy-start
  1.7 1.5 %collective-permute-start.3 = (f32[256,512]{1,0:T(8,128)S(1)}, f32[256,512]{1,0:T(8,128)S(1)}, u32[]{:S(2)}, u32[]{:S(2)}) collective-permute-start(f32[256,512]{1,0:T(8,128)S(1)} %slice.3.lead_ref.refs_0_), channel_id=1, source_target_pairs={{0,4},{4,0},{8,12},{12,8},{16,20},{20,16},{24,28},{28,24},{32,36},... | collective-permute-start | bytes 1572872 | tf_op jit(solution)/shard_map/ppermute | solution.py:356
  3.2 4.7 %collective-permute-start.2 = (f32[256,512]{1,0:T(8,128)S(1)}, f32[256,512]{1,0:T(8,128)S(1)}, u32[]{:S(2)}, u32[]{:S(2)}) collective-permute-start(f32[256,512]{1,0:T(8,128)S(1)} %slice.3.lead_ref.refs_0_), channel_id=1, source_target_pairs={{0,3},{4,7},{8,11},{12,15},{16,19},{20,23},{24,27},{28,31},{32,35}... | collective-permute-start | bytes 1572872 | tf_op jit(solution)/shard_map/ppermute | solution.py:354
  8.0 1.3 %collective-permute-start.1 = (f32[256,512]{1,0:T(8,128)S(1)}, f32[256,512]{1,0:T(8,128)S(1)}, u32[]{:S(2)}, u32[]{:S(2)}) collective-permute-start(f32[256,512]{1,0:T(8,128)S(1)} %slice.3.lead_ref.refs_0_), channel_id=1, source_target_pairs={{0,2},{4,6},{8,10},{12,14},{16,18},{20,22},{24,26},{28,30},{32,34}... | collective-permute-start | bytes 1572872 | tf_op jit(solution)/shard_map/ppermute | solution.py:354
  9.3 1.3 %collective-permute-start = (f32[256,512]{1,0:T(8,128)S(1)}, f32[256,512]{1,0:T(8,128)S(1)}, u32[]{:S(2)}, u32[]{:S(2)}) collective-permute-start(f32[256,512]{1,0:T(8,128)S(1)} %slice.3.lead_ref.refs_0_), channel_id=1, source_target_pairs={{0,1},{4,5},{8,9},{12,13},{16,17},{20,21},{24,25},{28,29},{32,33},... | collective-permute-start | bytes 1572872 | tf_op jit(solution)/shard_map/ppermute | solution.py:354
  10.6 0.0 collective-permute-done.3.mate_ref
  10.7 0.1 share.1
  10.8 1.3 collective-permute-start.4
  12.0 2.5 %collective-permute-start.5 = (f32[2,32,512]{2,1,0:T(8,128)S(1)}, f32[2,32,512]{2,1,0:T(8,128)S(1)}, u32[]{:S(2)}, u32[]{:S(2)}) collective-permute-start(f32[2,32,512]{2,1,0:T(8,128)S(1)} %get-tuple-element.47), channel_id=1, source_target_pairs={{0,16},{4,20},{8,24},{12,28},{16,0},{20,4},{24,8},{28,12},{32,48},... | collective-permute-start | bytes 393224 | tf_op jit(solution)/shard_map/ppermute | solution.py:360
  14.5 2.2 %collective-permute-done.4.refs_1_ = f32[2,32,512]{2,1,0:T(8,128)S(1)} collective-permute-done((f32[2,32,512]{2,1,0:T(8,128)S(1)}, f32[2,32,512]{2,1,0:T(8,128)S(1)}, u32[]{:S(2)}, u32[]{:S(2)}) %collective-permute-start.4) | collective-permute-done | bytes 131104 | tf_op jit(solution)/shard_map/ppermute | solution.py:360
  16.7 1.3 collective-permute-start.6
  17.9 2.5 %collective-permute-done.5.refs_2_ = f32[2,32,512]{2,1,0:T(8,128)S(1)} collective-permute-done((f32[2,32,512]{2,1,0:T(8,128)S(1)}, f32[2,32,512]{2,1,0:T(8,128)S(1)}, u32[]{:S(2)}, u32[]{:S(2)}) %collective-permute-start.5) | collective-permute-done | bytes 131104 | tf_op jit(solution)/shard_map/ppermute | solution.py:360
  20.4 0.3 collective-permute-done.6.refs_3_
  20.8 0.0 copy-done.2
  20.8 1.0 sort.1
  21.8 1.3 collective-permute-start.7
  23.1 1.3 collective-permute-start.8
  24.4 0.0 collective-permute-done.2.refs_3_
  24.4 1.3 collective-permute-start.9
  25.7 0.0 collective-permute-done.1.refs_2_
  25.7 6.0 %collective-permute-done.refs_1_ = f32[256,512]{1,0:T(8,128)S(1)} collective-permute-done((f32[256,512]{1,0:T(8,128)S(1)}, f32[256,512]{1,0:T(8,128)S(1)}, u32[]{:S(2)}, u32[]{:S(2)}) %collective-permute-start) | collective-permute-done | bytes 524320 | tf_op jit(solution)/shard_map/ppermute | solution.py:354
  31.7 2.8 %collective-permute-done.7.refs_1_ = f32[2,32,512]{2,1,0:T(8,128)S(1)} collective-permute-done((f32[2,32,512]{2,1,0:T(8,128)S(1)}, f32[2,32,512]{2,1,0:T(8,128)S(1)}, u32[]{:S(2)}, u32[]{:S(2)}) %collective-permute-start.7) | collective-permute-done | bytes 131104 | tf_op jit(solution)/shard_map/ppermute | solution.py:363
  34.5 2.8 %collective-permute-done.8.refs_2_ = f32[2,32,512]{2,1,0:T(8,128)S(1)} collective-permute-done((f32[2,32,512]{2,1,0:T(8,128)S(1)}, f32[2,32,512]{2,1,0:T(8,128)S(1)}, u32[]{:S(2)}, u32[]{:S(2)}) %collective-permute-start.8) | collective-permute-done | bytes 131104 | tf_op jit(solution)/shard_map/ppermute | solution.py:363
  37.3 0.0 collective-permute-done.9.refs_3_
  37.3 0.1 corner.1
  37.4 3.5 %collective-permute-start.10 = (f32[640,128]{1,0:T(8,128)S(1)}, f32[640,128]{1,0:T(8,128)S(1)}, u32[]{:S(2)}, u32[]{:S(2)}) collective-permute-start(f32[640,128]{1,0:T(8,128)S(1)} %corner.1), channel_id=1, source_target_pairs={{0,8},{4,36},{1,9},{5,37},{2,10},{6,38},{3,11},{7,39}} | collective-permute-start | bytes 983048 | tf_op jit(solution)/shard_map/ppermute | solution.py:373
  41.0 0.1 collective-permute-start.11
  41.1 0.0 copy-done
  41.1 2.0 %pick.1 = (f32[256,512]{1,0:T(8,128)S(1)}, f32[256,512]{1,0:T(8,128)S(1)}, f32[256,512]{1,0:T(8,128)S(1)}, f32[256,512]{1,0:T(8,128)S(1)}, s32[4,8]{1,0:T(4,128)S(1)}) custom-call(s32[32]{0:T(128)S(1)} %copy-done.2, f32[256,2048]{1,0:T(8,128)S(1)} %copy-done), custom_call_target="tpu_custom_call" | custom-call | tf_op jit(solution)/shard_map/pick/pallas_call | solution.py:103
  43.1 3.2 %collective-permute-done.11 = f32[64,512]{1,0:T(8,128)S(1)} collective-permute-done((f32[64,512]{1,0:T(8,128)S(1)}, f32[64,512]{1,0:T(8,128)S(1)}, u32[]{:S(2)}, u32[]{:S(2)}) %collective-permute-start.11) | collective-permute-done | bytes 131104 | tf_op jit(solution)/shard_map/ppermute | solution.py:374
  46.3 0.0 collective-permute-done.10
  46.4 0.1 collective-permute-start.13
  46.5 4.6 %collective-permute-start.12 = (f32[640,128]{1,0:T(8,128)S(1)}, f32[640,128]{1,0:T(8,128)S(1)}, u32[]{:S(2)}, u32[]{:S(2)}) collective-permute-start(f32[640,128]{1,0:T(8,128)S(1)} %add.12), channel_id=1, source_target_pairs={{0,24},{4,100},{8,16},{36,68},{1,25},{5,101},{9,17},{37,69},{2,26}... | collective-permute-start | bytes 983048 | tf_op jit(solution)/shard_map/ppermute | solution.py:373
  51.1 2.1 %collective-permute-done.13 = f32[128,512]{1,0:T(8,128)S(1)} collective-permute-done((f32[128,512]{1,0:T(8,128)S(1)}, f32[128,512]{1,0:T(8,128)S(1)}, u32[]{:S(2)}, u32[]{:S(2)}) %collective-permute-start.13) | collective-permute-done | bytes 262176 | tf_op jit(solution)/shard_map/ppermute | solution.py:374
  53.2 1.8 %collective-permute-done.12 = f32[640,128]{1,0:T(8,128)S(1)} collective-permute-done((f32[640,128]{1,0:T(8,128)S(1)}, f32[640,128]{1,0:T(8,128)S(1)}, u32[]{:S(2)}, u32[]{:S(2)}) %collective-permute-start.12) | collective-permute-done | bytes 327712 | tf_op jit(solution)/shard_map/ppermute | solution.py:373
  55.1 0.1 collective-permute-start.15
  55.2 0.1 collective-permute-start.16
  55.3 2.7 %collective-permute-start.17 = (f32[256,512]{1,0:T(8,128)S(1)}, f32[256,512]{1,0:T(8,128)S(1)}, u32[]{:S(2)}, u32[]{:S(2)}) collective-permute-start(f32[256,512]{1,0:T(8,128)S(1)} %get-tuple-element.71), channel_id=1, source_target_pairs={{0,3},{1,0},{2,1},{3,2},{4,7},{5,4},{6,5},{7,6},{8,11},{9,8},{10,9... | collective-permute-start | bytes 1572872 | tf_op jit(solution)/shard_map/ppermute | solution.py:376
  57.9 3.3 %collective-permute-start.14 = (f32[640,128]{1,0:T(8,128)S(1)}, f32[640,128]{1,0:T(8,128)S(1)}, u32[]{:S(2)}, u32[]{:S(2)}) collective-permute-start(f32[640,128]{1,0:T(8,128)S(1)} %add.13), channel_id=1, source_target_pairs={{0,32},{4,12},{8,40},{16,48},{24,56},{36,44},{68,76},{100,108},{1,... | collective-permute-start | bytes 983048 | tf_op jit(solution)/shard_map/ppermute | solution.py:373
  61.2 4.0 %collective-permute-done.14 = f32[640,128]{1,0:T(8,128)S(1)} collective-permute-done((f32[640,128]{1,0:T(8,128)S(1)}, f32[640,128]{1,0:T(8,128)S(1)}, u32[]{:S(2)}, u32[]{:S(2)}) %collective-permute-start.14) | collective-permute-done | bytes 327712 | tf_op jit(solution)/shard_map/ppermute | solution.py:373
  65.3 0.0 collective-permute-done.15
  65.3 0.1 pad_maximum_fusion.refs_5_
  65.3 0.0 copy-start.1
  65.4 2.0 %collective-permute-done.16.refs_2_ = f32[256,512]{1,0:T(8,128)S(1)} collective-permute-done((f32[256,512]{1,0:T(8,128)S(1)}, f32[256,512]{1,0:T(8,128)S(1)}, u32[]{:S(2)}, u32[]{:S(2)}) %collective-permute-start.16) | collective-permute-done | bytes 524320 | tf_op jit(solution)/shard_map/ppermute | solution.py:376
  67.4 0.7 collective-permute-done.17.refs_4_
  68.1 0.0 collective-permute-start.18
  68.1 4.6 %collective-permute-start.19 = (f32[640,128]{1,0:T(8,128)S(1)}, f32[640,128]{1,0:T(8,128)S(1)}, u32[]{:S(2)}, u32[]{:S(2)}) collective-permute-start(f32[640,128]{1,0:T(8,128)S(1)} %add.14), channel_id=1, source_target_pairs={{0,96},{4,28},{8,104},{12,20},{16,112},{24,120},{32,64},{36,60},{4... | collective-permute-start | bytes 983048 | tf_op jit(solution)/shard_map/ppermute | solution.py:383
  72.7 10.7 %collective-permute-done.19 = f32[640,128]{1,0:T(8,128)S(1)} collective-permute-done((f32[640,128]{1,0:T(8,128)S(1)}, f32[640,128]{1,0:T(8,128)S(1)}, u32[]{:S(2)}, u32[]{:S(2)}) %collective-permute-start.19) | collective-permute-done | bytes 327712 | tf_op jit(solution)/shard_map/ppermute | solution.py:383
  83.4 4.1 %collective-permute-start.20 = (f32[640,128]{1,0:T(8,128)S(1)}, f32[640,128]{1,0:T(8,128)S(1)}, u32[]{:S(2)}, u32[]{:S(2)}) collective-permute-start(f32[640,128]{1,0:T(8,128)S(1)} %add.15.own_ref), channel_id=1, source_target_pairs={{0,4},{4,0},{8,12},{12,8},{16,20},{20,16},{24,28},{28,24},{32,36},... | collective-permute-start | bytes 983048 | tf_op jit(solution)/shard_map/ppermute | solution.py:384
  87.5 0.3 collective-permute-start.22
  87.7 1.0 collective-permute-done.20.other_ref
  88.7 18.2 %factor.1 = (f32[256,256]{1,0:T(8,128)S(1)}, f32[256,256]{1,0:T(8,128)S(1)}, f32[256,256]{1,0:T(8,128)S(1)}) custom-call(f32[640,128]{1,0:T(8,128)S(1)} %add.15.own_ref, f32[640,128]{1,0:T(8,128)S(1)} %collective-permute-done.20.other_ref), custom_call_target="tpu_custom_call" | custom-call | tf_op jit(solution)/shard_map/factor/pallas_call | solution.py:103
  106.9 0.0 collective-permute-done.18.refs_6_
  107.0 0.5 collective-permute-start.23
  107.4 1.9 %collective-permute-start.21 = (f32[256,512]{1,0:T(8,128)S(1)}, f32[256,512]{1,0:T(8,128)S(1)}, u32[]{:S(2)}, u32[]{:S(2)}) collective-permute-start(f32[256,512]{1,0:T(8,128)S(1)} %get-tuple-element.85), channel_id=1, source_target_pairs={{0,2},{1,3},{2,0},{3,1},{4,6},{5,7},{6,4},{7,5},{8,10},{9,11},{10,... | collective-permute-start | bytes 1572872 | tf_op jit(solution)/shard_map/ppermute | solution.py:381
  109.3 2.9 %weigh.1 = (f32[256,512]{1,0:T(8,128)}, f32[256,512]{1,0:T(8,128)S(1)}) custom-call(f32[256,512]{1,0:T(8,128)S(1)} %slice.3.lead_ref.refs_0_, f32[256,512]{1,0:T(8,128)S(1)} %collective-permute-done.refs_1_, f32[256,512]{1,0:T(8,128)S(1)} %collective-permute-done.1.refs_2_, f32[256,512]{1,0:T(8,128)S(1)} %collective-permute-done.2.refs_3_, ...), custom_call_target="tpu_custom_call" | custom-call | tf_op jit(solution)/shard_map/weigh/pallas_call | solution.py:268
  112.2 10.1 %collective-permute-done.21.refs_3_ = f32[256,512]{1,0:T(8,128)S(1)} collective-permute-done((f32[256,512]{1,0:T(8,128)S(1)}, f32[256,512]{1,0:T(8,128)S(1)}, u32[]{:S(2)}, u32[]{:S(2)}) %collective-permute-start.21) | collective-permute-done | bytes 524320 | tf_op jit(solution)/shard_map/ppermute | solution.py:381
  122.3 0.0 collective-permute-done.22.refs_7_
  122.3 0.0 collective-permute-done.23.refs_8_
  122.3 0.0 copy-done.1
  122.3 8.6 %update.1 = f32[256,2048]{1,0:T(8,128)} custom-call(s32[4,8]{1,0:T(4,128)S(1)} %get-tuple-element.81.plan, f32[256,512]{1,0:T(8,128)S(1)} %get-tuple-element.82.refs_0_, f32[256,512]{1,0:T(8,128)S(1)} %get-tuple-element.83.refs_1_, f32[256,512]{1,0:T(8,128)S(1)} %collective-permute-done.16.refs_2_, f32[256,512]{1,0:T(8,128)S(1)} %collective-permute-done.21.refs_3_, ...), custom_call_target="tpu_custom_call" | custom-call | tf_op jit(solution)/shard_map/update/pallas_call | solution.py:315
  (7 shorter events, 0.2 us)
Async XLA Ops:
  0.6 20.1 %copy-start.2 = (s32[32]{0:T(128)S(1)}, s32[32]{0:T(128)}, u32[]{:S(2)}) copy-start(s32[32]{0:T(128)} %map_ref.3) | copy-start | bytes 388
  1.7 39.3 %copy-start = (f32[256,2048]{1,0:T(8,128)S(1)}, f32[256,2048]{1,0:T(8,128)}, u32[]{:S(2)}) copy-start(f32[256,2048]{1,0:T(8,128)} %front_ref.1) | copy-start | bytes 6291460
  1.7 8.9 %collective-permute-start.3 = (f32[256,512]{1,0:T(8,128)S(1)}, f32[256,512]{1,0:T(8,128)S(1)}, u32[]{:S(2)}, u32[]{:S(2)}) collective-permute-start(f32[256,512]{1,0:T(8,128)S(1)} %slice.3.lead_ref.refs_0_), channel_id=1, source_target_pairs={{0,4},{4,0},{8,12},{12,8},{16,20},{20,16},{24,28},{28,24},{32,36},... | collective-permute-start | bytes 1572872 | tf_op jit(solution)/shard_map/ppermute | solution.py:356
  3.2 21.2 %collective-permute-start.2 = (f32[256,512]{1,0:T(8,128)S(1)}, f32[256,512]{1,0:T(8,128)S(1)}, u32[]{:S(2)}, u32[]{:S(2)}) collective-permute-start(f32[256,512]{1,0:T(8,128)S(1)} %slice.3.lead_ref.refs_0_), channel_id=1, source_target_pairs={{0,3},{4,7},{8,11},{12,15},{16,19},{20,23},{24,27},{28,31},{32,35}... | collective-permute-start | bytes 1572872 | tf_op jit(solution)/shard_map/ppermute | solution.py:354
  8.0 17.7 %collective-permute-start.1 = (f32[256,512]{1,0:T(8,128)S(1)}, f32[256,512]{1,0:T(8,128)S(1)}, u32[]{:S(2)}, u32[]{:S(2)}) collective-permute-start(f32[256,512]{1,0:T(8,128)S(1)} %slice.3.lead_ref.refs_0_), channel_id=1, source_target_pairs={{0,2},{4,6},{8,10},{12,14},{16,18},{20,22},{24,26},{28,30},{32,34}... | collective-permute-start | bytes 1572872 | tf_op jit(solution)/shard_map/ppermute | solution.py:354
  9.3 22.4 %collective-permute-start = (f32[256,512]{1,0:T(8,128)S(1)}, f32[256,512]{1,0:T(8,128)S(1)}, u32[]{:S(2)}, u32[]{:S(2)}) collective-permute-start(f32[256,512]{1,0:T(8,128)S(1)} %slice.3.lead_ref.refs_0_), channel_id=1, source_target_pairs={{0,1},{4,5},{8,9},{12,13},{16,17},{20,21},{24,25},{28,29},{32,33},... | collective-permute-start | bytes 1572872 | tf_op jit(solution)/shard_map/ppermute | solution.py:354
  10.8 5.9 %collective-permute-start.4 = (f32[2,32,512]{2,1,0:T(8,128)S(1)}, f32[2,32,512]{2,1,0:T(8,128)S(1)}, u32[]{:S(2)}, u32[]{:S(2)}) collective-permute-start(f32[2,32,512]{2,1,0:T(8,128)S(1)} %get-tuple-element.46), channel_id=1, source_target_pairs={{0,8},{4,12},{8,16},{12,20},{16,24},{20,28},{24,0},{28,4},{32,40},... | collective-permute-start | bytes 393224 | tf_op jit(solution)/shard_map/ppermute | solution.py:360
  12.0 8.4 %collective-permute-start.5 = (f32[2,32,512]{2,1,0:T(8,128)S(1)}, f32[2,32,512]{2,1,0:T(8,128)S(1)}, u32[]{:S(2)}, u32[]{:S(2)}) collective-permute-start(f32[2,32,512]{2,1,0:T(8,128)S(1)} %get-tuple-element.47), channel_id=1, source_target_pairs={{0,16},{4,20},{8,24},{12,28},{16,0},{20,4},{24,8},{28,12},{32,48},... | collective-permute-start | bytes 393224 | tf_op jit(solution)/shard_map/ppermute | solution.py:360
  16.7 4.1 %collective-permute-start.6 = (f32[2,32,512]{2,1,0:T(8,128)S(1)}, f32[2,32,512]{2,1,0:T(8,128)S(1)}, u32[]{:S(2)}, u32[]{:S(2)}) collective-permute-start(f32[2,32,512]{2,1,0:T(8,128)S(1)} %get-tuple-element.48), channel_id=1, source_target_pairs={{0,24},{4,28},{8,0},{12,4},{16,8},{20,12},{24,16},{28,20},{32,56},... | collective-permute-start | bytes 393224 | tf_op jit(solution)/shard_map/ppermute | solution.py:360
  21.8 12.7 %collective-permute-start.7 = (f32[2,32,512]{2,1,0:T(8,128)S(1)}, f32[2,32,512]{2,1,0:T(8,128)S(1)}, u32[]{:S(2)}, u32[]{:S(2)}) collective-permute-start(f32[2,32,512]{2,1,0:T(8,128)S(1)} %get-tuple-element.50), channel_id=1, source_target_pairs={{0,1},{4,5},{8,9},{12,13},{16,17},{20,21},{24,25},{28,29},{32,33},... | collective-permute-start | bytes 393224 | tf_op jit(solution)/shard_map/ppermute | solution.py:363
  23.1 14.2 %collective-permute-start.8 = (f32[2,32,512]{2,1,0:T(8,128)S(1)}, f32[2,32,512]{2,1,0:T(8,128)S(1)}, u32[]{:S(2)}, u32[]{:S(2)}) collective-permute-start(f32[2,32,512]{2,1,0:T(8,128)S(1)} %get-tuple-element.51), channel_id=1, source_target_pairs={{0,2},{4,6},{8,10},{12,14},{16,18},{20,22},{24,26},{28,30},{32,34}... | collective-permute-start | bytes 393224 | tf_op jit(solution)/shard_map/ppermute | solution.py:363
  24.4 12.9 %collective-permute-start.9 = (f32[2,32,512]{2,1,0:T(8,128)S(1)}, f32[2,32,512]{2,1,0:T(8,128)S(1)}, u32[]{:S(2)}, u32[]{:S(2)}) collective-permute-start(f32[2,32,512]{2,1,0:T(8,128)S(1)} %get-tuple-element.52), channel_id=1, source_target_pairs={{0,3},{4,7},{8,11},{12,15},{16,19},{20,23},{24,27},{28,31},{32,35}... | collective-permute-start | bytes 393224 | tf_op jit(solution)/shard_map/ppermute | solution.py:363
  37.4 9.0 %collective-permute-start.10 = (f32[640,128]{1,0:T(8,128)S(1)}, f32[640,128]{1,0:T(8,128)S(1)}, u32[]{:S(2)}, u32[]{:S(2)}) collective-permute-start(f32[640,128]{1,0:T(8,128)S(1)} %corner.1), channel_id=1, source_target_pairs={{0,8},{4,36},{1,9},{5,37},{2,10},{6,38},{3,11},{7,39}} | collective-permute-start | bytes 983048 | tf_op jit(solution)/shard_map/ppermute | solution.py:373
  41.0 5.3 %collective-permute-start.11 = (f32[64,512]{1,0:T(8,128)S(1)}, f32[64,512]{1,0:T(8,128)S(1)}, u32[]{:S(2)}, u32[]{:S(2)}) collective-permute-start(f32[64,512]{1,0:T(8,128)S(1)} %bitcast.1), channel_id=1, source_target_pairs={{0,8},{4,36},{8,0},{12,44},{16,24},{20,52},{24,16},{28,60},{32,40}... | collective-permute-start | bytes 393224 | tf_op jit(solution)/shard_map/ppermute | solution.py:374
  46.4 6.8 %collective-permute-start.13 = (f32[128,512]{1,0:T(8,128)S(1)}, f32[128,512]{1,0:T(8,128)S(1)}, u32[]{:S(2)}, u32[]{:S(2)}) collective-permute-start(f32[128,512]{1,0:T(8,128)S(1)} %pad_maximum_fusion.2), channel_id=1, source_target_pairs={{0,24},{4,100},{8,16},{12,108},{16,8},{20,116},{24,0},{28,124},{32... | collective-permute-start | bytes 786440 | tf_op jit(solution)/shard_map/ppermute | solution.py:374
  46.5 8.6 %collective-permute-start.12 = (f32[640,128]{1,0:T(8,128)S(1)}, f32[640,128]{1,0:T(8,128)S(1)}, u32[]{:S(2)}, u32[]{:S(2)}) collective-permute-start(f32[640,128]{1,0:T(8,128)S(1)} %add.12), channel_id=1, source_target_pairs={{0,24},{4,100},{8,16},{36,68},{1,25},{5,101},{9,17},{37,69},{2,26}... | collective-permute-start | bytes 983048 | tf_op jit(solution)/shard_map/ppermute | solution.py:373
  55.1 10.2 %collective-permute-start.15 = (f32[256,512]{1,0:T(8,128)S(1)}, f32[256,512]{1,0:T(8,128)S(1)}, u32[]{:S(2)}, u32[]{:S(2)}) collective-permute-start(f32[256,512]{1,0:T(8,128)S(1)} %pad_maximum_fusion.1), channel_id=1, source_target_pairs={{0,32},{4,12},{8,40},{12,4},{16,48},{20,28},{24,56},{28,20},{32,0}... | collective-permute-start | bytes 1572872 | tf_op jit(solution)/shard_map/ppermute | solution.py:374
  55.2 12.2 %collective-permute-start.16 = (f32[256,512]{1,0:T(8,128)S(1)}, f32[256,512]{1,0:T(8,128)S(1)}, u32[]{:S(2)}, u32[]{:S(2)}) collective-permute-start(f32[256,512]{1,0:T(8,128)S(1)} %get-tuple-element.69), channel_id=1, source_target_pairs={{0,1},{1,2},{2,3},{3,0},{4,5},{5,6},{6,7},{7,4},{8,9},{9,10},{10,1... | collective-permute-start | bytes 1572872 | tf_op jit(solution)/shard_map/ppermute | solution.py:376
  55.3 12.8 %collective-permute-start.17 = (f32[256,512]{1,0:T(8,128)S(1)}, f32[256,512]{1,0:T(8,128)S(1)}, u32[]{:S(2)}, u32[]{:S(2)}) collective-permute-start(f32[256,512]{1,0:T(8,128)S(1)} %get-tuple-element.71), channel_id=1, source_target_pairs={{0,3},{1,0},{2,1},{3,2},{4,7},{5,4},{6,5},{7,6},{8,11},{9,8},{10,9... | collective-permute-start | bytes 1572872 | tf_op jit(solution)/shard_map/ppermute | solution.py:376
  57.9 7.3 %collective-permute-start.14 = (f32[640,128]{1,0:T(8,128)S(1)}, f32[640,128]{1,0:T(8,128)S(1)}, u32[]{:S(2)}, u32[]{:S(2)}) collective-permute-start(f32[640,128]{1,0:T(8,128)S(1)} %add.13), channel_id=1, source_target_pairs={{0,32},{4,12},{8,40},{16,48},{24,56},{36,44},{68,76},{100,108},{1,... | collective-permute-start | bytes 983048 | tf_op jit(solution)/shard_map/ppermute | solution.py:373
  65.3 57.0 %copy-start.1 = (f32[256,2048]{1,0:T(8,128)S(1)}, f32[256,2048]{1,0:T(8,128)}, u32[]{:S(2)}) copy-start(f32[256,2048]{1,0:T(8,128)} %refs_9_.1) | copy-start | bytes 6291460
  68.1 38.9 %collective-permute-start.18 = (f32[512,512]{1,0:T(8,128)S(1)}, f32[512,512]{1,0:T(8,128)S(1)}, u32[]{:S(2)}, u32[]{:S(2)}) collective-permute-start(f32[512,512]{1,0:T(8,128)S(1)} %pad_maximum_fusion.refs_5_), channel_id=1, source_target_pairs={{0,96},{4,28},{8,104},{12,20},{16,112},{20,12},{24,120},{28,4},{32... | collective-permute-start | bytes 3145736 | tf_op jit(solution)/shard_map/ppermute | solution.py:382
  68.1 15.3 %collective-permute-start.19 = (f32[640,128]{1,0:T(8,128)S(1)}, f32[640,128]{1,0:T(8,128)S(1)}, u32[]{:S(2)}, u32[]{:S(2)}) collective-permute-start(f32[640,128]{1,0:T(8,128)S(1)} %add.14), channel_id=1, source_target_pairs={{0,96},{4,28},{8,104},{12,20},{16,112},{24,120},{32,64},{36,60},{4... | collective-permute-start | bytes 983048 | tf_op jit(solution)/shard_map/ppermute | solution.py:383
  83.4 5.4 %collective-permute-start.20 = (f32[640,128]{1,0:T(8,128)S(1)}, f32[640,128]{1,0:T(8,128)S(1)}, u32[]{:S(2)}, u32[]{:S(2)}) collective-permute-start(f32[640,128]{1,0:T(8,128)S(1)} %add.15.own_ref), channel_id=1, source_target_pairs={{0,4},{4,0},{8,12},{12,8},{16,20},{20,16},{24,28},{28,24},{32,36},... | collective-permute-start | bytes 983048 | tf_op jit(solution)/shard_map/ppermute | solution.py:384
  87.5 34.8 %collective-permute-start.22 = (f32[512,512]{1,0:T(8,128)S(1)}, f32[512,512]{1,0:T(8,128)S(1)}, u32[]{:S(2)}, u32[]{:S(2)}) collective-permute-start(f32[512,512]{1,0:T(8,128)S(1)} %pad_maximum_fusion.refs_5_), channel_id=1, source_target_pairs={{0,4},{4,0},{8,12},{12,8},{16,20},{20,16},{24,28},{28,24},{32,36},... | collective-permute-start | bytes 3145736 | tf_op jit(solution)/shard_map/ppermute | solution.py:385
  107.0 15.4 %collective-permute-start.23 = (f32[512,512]{1,0:T(8,128)S(1)}, f32[512,512]{1,0:T(8,128)S(1)}, u32[]{:S(2)}, u32[]{:S(2)}) collective-permute-start(f32[512,512]{1,0:T(8,128)S(1)} %collective-permute-done.18.refs_6_), channel_id=1, source_target_pairs={{0,4},{4,0},{8,12},{12,8},{16,20},{20,16},{24,28},{28,24},{32,36},... | collective-permute-start | bytes 3145736 | tf_op jit(solution)/shard_map/ppermute | solution.py:389
  107.4 14.9 %collective-permute-start.21 = (f32[256,512]{1,0:T(8,128)S(1)}, f32[256,512]{1,0:T(8,128)S(1)}, u32[]{:S(2)}, u32[]{:S(2)}) collective-permute-start(f32[256,512]{1,0:T(8,128)S(1)} %get-tuple-element.85), channel_id=1, source_target_pairs={{0,2},{1,3},{2,0},{3,1},{4,6},{5,7},{6,4},{7,5},{8,10},{9,11},{10,... | collective-permute-start | bytes 1572872 | tf_op jit(solution)/shard_map/ppermute | solution.py:381

commit v6 on v5

--- a/solution.py
+++ b/solution.py
@@ -10,6 +10,9 @@
 HALF = 128
 STEP = 8
 TURN = 2
+BLOCK = 160
+LARGE = pl.CostEstimate(flops=20 << 30, bytes_accessed=1 << 20, transcendentals=0)
+SMALL = pl.CostEstimate(flops=1 << 10, bytes_accessed=1 << 10, transcendentals=0)
 HIGHEST = lax.Precision.HIGHEST
 
 
@@ -95,7 +98,7 @@
     )
 
 
-def local_call(kernel, name, shapes, scalars=0, plan=()):
+def local_call(kernel, name, shapes, scalars=0, plan=(), cost=SMALL):
     whole = pl.BlockSpec(memory_space=pltpu.VMEM)
     small = pl.BlockSpec(memory_space=pltpu.SMEM)
 
@@ -107,6 +110,7 @@
             in_specs=[small] * scalars + [whole] * (len(args) - scalars),
             out_specs=[whole] * len(shapes) + [small] * len(plan),
             compiler_params=pltpu.CompilerParams(vmem_limit_bytes=16 << 20),
+            cost_estimate=cost,
             name=name,
         )(*args)
 
@@ -125,7 +129,8 @@
     one = jnp.where(even, other, own)
 
     def piece(blocks, index):
-        return blocks[index * HALF : (index + 1) * HALF]
+        rows = blocks[index * 32 : (index + 1) * 32]
+        return jnp.concatenate([rows[:, part * HALF : (part + 1) * HALF] for part in range(4)], 0)
 
     inv_a = inverse_factor_256(piece(zero, 0), piece(zero, 1), piece(zero, 2))
     across = jnp.concatenate(
@@ -147,7 +152,7 @@
 
 
 def factor(own, other):
-    return local_call(factor_kernel, "factor", [(PW, PW)] * 3)(own, other)
+    return local_call(factor_kernel, "factor", [(PW, PW)] * 3, cost=LARGE)(own, other)
 
 
 def share_kernel(lead_ref, mate_ref, *outs):
@@ -185,34 +190,43 @@
                         outs[owner][pl.ds(ranks[tile], 1)] = piece[None]
 
 
+def corner_kernel(lead_ref, out_ref):
+    plane, line, core, col = position()
+    out_ref[...] = jnp.zeros_like(out_ref)
+    places = [[(0, 0), (1, 0), (1, 1), (0, 2), (1, 2)], [(0, 2), (1, 2), (1, 3), (1, 0), (1, 1)]]
+    for holder in range(2):
+
+        @pl.when((col == 0) & (plane == 0) & (line == 0) & (core == holder))
+        def _():
+            for index, (down, right) in enumerate(places[holder]):
+                for part in range(4):
+                    rows = slice(down * HALF + part * 32, down * HALF + part * 32 + 32)
+                    out_ref[index * 32 : index * 32 + 32, part * HALF : part * HALF + HALF] = lead_ref[
+                        rows, right * HALF : right * HALF + HALF
+                    ]
+
+
 def merge_kernel(*refs):
-    for index, ref in enumerate(refs[:4]):
+    parts, blocks, out_ref = refs[:4], refs[4:8], refs[8]
+    for index, ref in enumerate(parts):
 
         @pl.when(lax.axis_index("col") == index)
         def _():
-            refs[4][...] = ref[...]
-
-
-def corner_kernel(*refs):
-    plane, line, core, col = position()
-    out = refs[4]
-    out[...] = jnp.zeros_like(out)
-    for index, ref in enumerate(refs[:4]):
-
-        @pl.when((col == index) & (plane == 0) & (line == 0))
-        def _():
-            @pl.when(core == 0)
-            def _():
-                out[0 : 2 * HALF] = ref[:, :HALF]
-                out[2 * HALF : 3 * HALF] = ref[HALF:, HALF:PW]
-                out[3 * HALF :] = ref[:, PW : PW + HALF]
-
-            @pl.when(core == 1)
-            def _():
-                out[0 : 2 * HALF] = ref[:, PW : PW + HALF]
-                out[2 * HALF : 3 * HALF] = ref[HALF:, PW + HALF :]
-                out[3 * HALF : 4 * HALF] = ref[HALF:, :HALF]
-                out[4 * HALF :] = ref[HALF:, HALF:PW]
+            out_ref[:32] = ref[0]
+            out_ref[32:64] = ref[1]
+
+    out_ref[64:] = (blocks[0][...] + blocks[1][...]) + (blocks[2][...] + blocks[3][...])
+
+
+def join_kernel(own_ref, got_ref, *outs):
+    rows = own_ref.shape[0] - BLOCK
+    outs[0][:rows] = own_ref[:rows]
+    outs[0][rows : 2 * rows] = got_ref[:rows]
+    block = own_ref[rows:] + got_ref[rows:]
+    if len(outs) == 1:
+        outs[0][2 * rows :] = block
+    else:
+        outs[1][...] = block
 
 
 def pick_kernel(map_ref, front_ref, *refs):
@@ -272,6 +286,7 @@
         out_specs=[whole] * 2,
         scratch_shapes=[pltpu.VMEM(shape, jnp.float32)],
         compiler_params=pltpu.CompilerParams(vmem_limit_bytes=16 << 20),
+        cost_estimate=SMALL,
         name="weigh",
     )(*rows, *inverse)
 
@@ -351,7 +366,11 @@
     part = (2, 32, LEAD)
     lead = front[:, :LEAD]
 
-    copies = [lax.ppermute(lead, "col", [(0, to)]) for to in (1, 2, 3)]
+    ring = [[(i, (i + hop) % 4) for i in range(4)] for hop in range(4)]
+
+    blocks = [local_call(corner_kernel, "corner", [(BLOCK, LEAD)])(lead)[0]]
+    for to in range(1, 4):
+        blocks.append(lax.ppermute(blocks[0], ("row", "col"), [(4 * core, 4 * core + to) for core in range(2)]))
 
     mate = lax.ppermute(lead, "row", swap)
     parts = list(local_call(share_kernel, "share", [part] * 4)(lead, mate))
@@ -361,32 +380,32 @@
     parts = list(local_call(sort_kernel, "sort", [part] * 4, 1)(tile_map, *parts))
     for to in range(1, 4):
         parts[to] = lax.ppermute(parts[to], "col", [(0, to)])
-    copies, parts = lax.optimization_barrier((copies, parts))
-    gathered = local_call(merge_kernel, "merge", [part])(*parts)[0].reshape(64, LEAD)
+    blocks, parts = lax.optimization_barrier((blocks, parts))
+    load = local_call(merge_kernel, "merge", [(64 + BLOCK, LEAD)])(*parts, *blocks)[0]
 
     *pieces, plan = local_call(pick_kernel, "pick", [(height, 2 * PW)] * 4, 1, [(4, 8)])(tile_map, front)
 
-    block = local_call(corner_kernel, "corner", [(5 * HALF, HALF)])(lead, *copies)[0]
     every, spread = doubling_steps()
-    ring = [[(i, (i + hop) % 4) for i in range(4)] for hop in range(4)]
-    for step in range(3):
-        block = block + lax.ppermute(block, "row", spread[step])
-        gathered = jnp.concatenate([gathered, lax.ppermute(gathered, "row", every[step])], 0)
-        if step == 1:
-            pieces[1], pieces[3] = [lax.ppermute(pieces[hop], "col", ring[hop]) for hop in (1, 3)]
-        if step != 1:
-            block, gathered, *pieces = lax.optimization_barrier((block, gathered, *pieces))
-        else:
-            block, gathered = lax.optimization_barrier((block, gathered))
-    pieces[2] = lax.ppermute(pieces[2], "col", ring[2])
+    load, lead = lax.optimization_barrier((load, lead))
+    copies = [lax.ppermute(lead, "col", [(0, to)]) for to in (1, 2, 3)]
+    load = local_call(join_kernel, "join", [(128 + BLOCK, LEAD)])(load, lax.ppermute(load, "row", every[0]))[0]
+    load = local_call(join_kernel, "join", [(256 + BLOCK, LEAD)])(load, lax.ppermute(load, "row", every[1]))[0]
+    load, copies[0], copies[2], *pieces = lax.optimization_barrier((load, copies[0], copies[2], *pieces))
+    gathered, block = local_call(join_kernel, "join", [(512, LEAD), (BLOCK, LEAD)])(load, lax.ppermute(load, "row", every[2]))
+    block, gathered, copies[1] = lax.optimization_barrier((block, gathered, copies[1]))
+    block = block + lax.ppermute(block, "row", spread[3])
+    pieces[3] = lax.ppermute(pieces[3], "col", ring[3])
+    block, gathered, *pieces = lax.optimization_barrier((block, gathered, *pieces))
+    other = lax.ppermute(block, "row", swap)
     late = lax.ppermute(gathered, "row", every[3])
-    block = block + lax.ppermute(block, "row", spread[3])
-    other = lax.ppermute(block, "row", swap)
     other_gathered = lax.ppermute(gathered, "row", swap)
+    for hop in (1, 2):
+        pieces[hop] = lax.ppermute(pieces[hop], "col", ring[hop])
 
     inverse = factor(block, other)
     late, inverse = lax.optimization_barrier((late, inverse))
     other_late = lax.ppermute(late, "row", swap)
+    inverse, pieces = lax.optimization_barrier((inverse, pieces))
     panel, weight = weigh([lead, *copies], inverse)
     updated = update(plan, weight, pieces, [gathered, late, other_gathered, other_late], ancestor)
     return panel, updated

time: 133 us -> 139 us (1.045)
  waiting for transfers between devices: 52.2 us -> 62 us
  starting transfers between devices: 43.5 us -> 40.4 us
    ppermute x9, waiting for transfers between devices: 24 us -> 42.8 us  [the longest x2 23.2 us: shards(): pieces[hop] = lax.ppermute(pieces[hop], 'col', ring[hop])]
    ppermute x1, waiting for transfers between devices: 10.7 us -> 3.98 us  [shards(): block = block + lax.ppermute(block, 'row', spread[3])]
    ppermute x3, starting transfers between devices: 5 us -> 0.16 us  [shards(): parts[hop] = lax.ppermute(parts[hop], 'row', pairs)]
    ppermute x9, starting transfers between devices: 16.3 us -> 20.7 us  [the longest x3 8.84 us: shards(): lax.ppermute(blocks[0], ('row', 'col'), [(4 * core, 4 * core + to) for co...]
    ppermute x1, starting transfers between devices: 4.59 us -> 1.3 us  [shards(): block = block + lax.ppermute(block, 'row', spread[3])]
    ppermute x1, starting transfers between devices: 0.01 us -> 3.24 us  [shards(): late = lax.ppermute(gathered, 'row', every[3])]
    ppermute x3, waiting for transfers between devices: 5.97 us -> 3.46 us  [shards(): copies = [lax.ppermute(lead, 'col', [(0, to)]) for to in (1, 2, 3)]]
    ppermute x1, starting transfers between devices: 4.1 us -> 2.31 us  [shards(): other = lax.ppermute(block, 'row', swap)]
  transfers between devices with their start and end apart: 24 -> 24, of which waited for: 15 -> 15; matrix products, arithmetic and copies ran while one was open for 0% -> 0% of each run, Pallas kernels for 19% -> 18%
where the time goes in v6:
time: 139 us; the launch traced here: 138 us
  waiting for transfers between devices  62 us (45%)
  starting transfers between devices  40.4 us (29%)
  Pallas kernels  33.2 us (24%)
    ppermute x2, waiting for transfers between devices, shards(): pieces[hop] = lax.ppermute(pieces[hop], 'col', ring[hop])  23.2 us
    pallas_call x9, Pallas kernels, call(): pl.pallas_call(kernel, out_shape=[jax.ShapeDtypeStruct(shape, jnp.float32...  21.7 us
    ppermute x3, starting transfers between devices, shards(): lax.ppermute(blocks[0], ('row', 'col'), [(4 * core, 4 * core + to) for co...  8.84 us
    pallas_call x1, Pallas kernels, update(): pl.pallas_call(update_kernel, out_shape=jax.ShapeDtypeStruct(base.shape,...  8.6 us
    ppermute x1, waiting for transfers between devices, shards(): lax.ppermute(load, 'row', every[2])  7.82 us
    ppermute x1, waiting for transfers between devices, shards(): lax.ppermute(load, 'row', every[0])  7.61 us
    ppermute x1, starting transfers between devices, shards(): lax.ppermute(load, 'row', every[2])  7.22 us
    ppermute x3, starting transfers between devices, shards(): copies = [lax.ppermute(lead, 'col', [(0, to)]) for to in (1, 2, 3)]  6.25 us
  transfers between devices with their start and end apart: 24, of which 15 were waited for; matrix products, arithmetic and copies ran while one was open for 0% of the time, Pallas kernels for 18%

profile of v6, /device:TPU:1, one launch (start us, length us, event | category | flops | bytes accessed | tf_op | source)
XLA Modules:
  0.0 137.7 jit_solution(16691118468759193535)
XLA Ops:
  0.6 0.0 copy-start.2
  0.6 1.1 slice.3.lead_ref.refs_0_
  1.7 1.5 %collective-permute-start.3 = (f32[256,512]{1,0:T(8,128)S(1)}, f32[256,512]{1,0:T(8,128)S(1)}, u32[]{:S(2)}, u32[]{:S(2)}) collective-permute-start(f32[256,512]{1,0:T(8,128)S(1)} %slice.3.lead_ref.refs_0_), channel_id=1, source_target_pairs={{0,4},{4,0},{8,12},{12,8},{16,20},{20,16},{24,28},{28,24},{32,36},... | collective-permute-start | bytes 1572872 | tf_op jit(solution)/shard_map/ppermute | solution.py:375
  3.2 0.1 corner.1.refs_4_
  3.3 4.7 %collective-permute-start.2 = (f32[160,512]{1,0:T(8,128)S(1)}, f32[160,512]{1,0:T(8,128)S(1)}, u32[]{:S(2)}, u32[]{:S(2)}) collective-permute-start(f32[160,512]{1,0:T(8,128)S(1)} %corner.1.refs_4_), channel_id=1, source_target_pairs={{0,3},{4,7}} | collective-permute-start | bytes 983048 | tf_op jit(solution)/shard_map/ppermute | solution.py:373
  8.0 0.0 collective-permute-done.3.mate_ref
  8.0 0.1 share.1
  8.1 0.1 collective-permute-start.4
  8.2 2.8 %collective-permute-start.1 = (f32[160,512]{1,0:T(8,128)S(1)}, f32[160,512]{1,0:T(8,128)S(1)}, u32[]{:S(2)}, u32[]{:S(2)}) collective-permute-start(f32[160,512]{1,0:T(8,128)S(1)} %corner.1.refs_4_), channel_id=1, source_target_pairs={{0,2},{4,6}} | collective-permute-start | bytes 983048 | tf_op jit(solution)/shard_map/ppermute | solution.py:373
  11.0 1.3 collective-permute-start
  12.3 0.1 collective-permute-start.5
  12.4 1.7 %collective-permute-done.4.refs_1_ = f32[2,32,512]{2,1,0:T(8,128)S(1)} collective-permute-done((f32[2,32,512]{2,1,0:T(8,128)S(1)}, f32[2,32,512]{2,1,0:T(8,128)S(1)}, u32[]{:S(2)}, u32[]{:S(2)}) %collective-permute-start.4) | collective-permute-done | bytes 131104 | tf_op jit(solution)/shard_map/ppermute | solution.py:379
  14.2 0.0 collective-permute-start.6
  14.2 3.6 %collective-permute-done.5.refs_2_ = f32[2,32,512]{2,1,0:T(8,128)S(1)} collective-permute-done((f32[2,32,512]{2,1,0:T(8,128)S(1)}, f32[2,32,512]{2,1,0:T(8,128)S(1)}, u32[]{:S(2)}, u32[]{:S(2)}) %collective-permute-start.5) | collective-permute-done | bytes 131104 | tf_op jit(solution)/shard_map/ppermute | solution.py:379
  17.7 0.9 collective-permute-done.6.refs_3_
  18.6 0.0 copy-done.2
  18.6 1.0 sort.1
  19.6 1.3 collective-permute-start.7
  21.0 1.3 collective-permute-start.8
  22.3 0.0 collective-permute-done.2.refs_7_
  22.3 1.3 collective-permute-start.9
  23.6 0.0 collective-permute-done.1.refs_6_
  23.6 0.8 collective-permute-done.refs_5_
  24.4 2.8 %collective-permute-done.7.refs_1_ = f32[2,32,512]{2,1,0:T(8,128)S(1)} collective-permute-done((f32[2,32,512]{2,1,0:T(8,128)S(1)}, f32[2,32,512]{2,1,0:T(8,128)S(1)}, u32[]{:S(2)}, u32[]{:S(2)}) %collective-permute-start.7) | collective-permute-done | bytes 131104 | tf_op jit(solution)/shard_map/ppermute | solution.py:382
  27.2 2.8 %collective-permute-done.8.refs_2_ = f32[2,32,512]{2,1,0:T(8,128)S(1)} collective-permute-done((f32[2,32,512]{2,1,0:T(8,128)S(1)}, f32[2,32,512]{2,1,0:T(8,128)S(1)}, u32[]{:S(2)}, u32[]{:S(2)}) %collective-permute-start.8) | collective-permute-done | bytes 131104 | tf_op jit(solution)/shard_map/ppermute | solution.py:382
  30.0 0.0 collective-permute-done.9.refs_3_
  30.0 0.1 merge.1.own_ref
  30.1 0.1 collective-permute-start.10
  30.2 7.6 %collective-permute-done.10.got_ref = f32[224,512]{1,0:T(8,128)S(1)} collective-permute-done((f32[224,512]{1,0:T(8,128)S(1)}, f32[224,512]{1,0:T(8,128)S(1)}, u32[]{:S(2)}, u32[]{:S(2)}) %collective-permute-start.10) | collective-permute-done | bytes 458784 | tf_op jit(solution)/shard_map/ppermute | solution.py:391
  37.8 0.1 join.3.own_ref
  37.9 0.1 collective-permute-start.11
  38.0 3.6 %collective-permute-start.13 = (f32[256,512]{1,0:T(8,128)S(1)}, f32[256,512]{1,0:T(8,128)S(1)}, u32[]{:S(2)}, u32[]{:S(2)}) collective-permute-start(f32[256,512]{1,0:T(8,128)S(1)} %slice.3.lead_ref.refs_0_), channel_id=1, source_target_pairs={{0,3},{4,7},{8,11},{12,15},{16,19},{20,23},{24,27},{28,31},{32,35}... | collective-permute-start | bytes 1572872 | tf_op jit(solution)/shard_map/ppermute | solution.py:390
  41.6 1.3 collective-permute-start.12
  42.9 0.0 copy-done
  42.9 2.0 %pick.1 = (f32[256,512]{1,0:T(8,128)S(1)}, f32[256,512]{1,0:T(8,128)S(1)}, f32[256,512]{1,0:T(8,128)S(1)}, f32[256,512]{1,0:T(8,128)S(1)}, s32[4,8]{1,0:T(4,128)S(1)}) custom-call(s32[32]{0:T(128)S(1)} %copy-done.2, f32[256,2048]{1,0:T(8,128)S(1)} %copy-done), custom_call_target="tpu_custom_call" | custom-call | flops 1024 | bytes 1024 | tf_op jit(solution)/shard_map/pick/pallas_call | solution.py:106
  44.9 3.3 %collective-permute-done.11.got_ref = f32[288,512]{1,0:T(8,128)S(1)} collective-permute-done((f32[288,512]{1,0:T(8,128)S(1)}, f32[288,512]{1,0:T(8,128)S(1)}, u32[]{:S(2)}, u32[]{:S(2)}) %collective-permute-start.11) | collective-permute-done | bytes 589856 | tf_op jit(solution)/shard_map/ppermute | solution.py:392
  48.2 0.1 join.4.own_ref
  48.3 1.0 collective-permute-done.13.refs_3_
  49.3 1.3 collective-permute-done.12.refs_1_
  50.6 7.2 %collective-permute-start.14 = (f32[416,512]{1,0:T(8,128)S(1)}, f32[416,512]{1,0:T(8,128)S(1)}, u32[]{:S(2)}, u32[]{:S(2)}) collective-permute-start(f32[416,512]{1,0:T(8,128)S(1)} %join.4.own_ref), channel_id=1, source_target_pairs={{0,32},{4,12},{8,40},{12,4},{16,48},{20,28},{24,56},{28,20},{32,0}... | collective-permute-start | bytes 2555912 | tf_op jit(solution)/shard_map/ppermute | solution.py:394
  57.8 1.3 collective-permute-start.15
  59.1 1.2 collective-permute-start.17
  60.4 7.8 %collective-permute-done.14.got_ref = f32[416,512]{1,0:T(8,128)S(1)} collective-permute-done((f32[416,512]{1,0:T(8,128)S(1)}, f32[416,512]{1,0:T(8,128)S(1)}, u32[]{:S(2)}, u32[]{:S(2)}) %collective-permute-start.14) | collective-permute-done | bytes 852000 | tf_op jit(solution)/shard_map/ppermute | solution.py:394
  68.2 0.1 join.5
  68.3 1.1 collective-permute-done.15.refs_2_
  69.4 1.3 collective-permute-start.16
  70.7 4.0 %collective-permute-done.16 = f32[160,512]{1,0:T(8,128)S(1)} collective-permute-done((f32[160,512]{1,0:T(8,128)S(1)}, f32[160,512]{1,0:T(8,128)S(1)}, u32[]{:S(2)}, u32[]{:S(2)}) %collective-permute-start.16) | collective-permute-done | bytes 327712 | tf_op jit(solution)/shard_map/ppermute | solution.py:396
  74.8 0.0 collective-permute-done.17.refs_4_
  74.8 2.3 %collective-permute-start.19 = (f32[160,512]{1,0:T(8,128)S(1)}, f32[160,512]{1,0:T(8,128)S(1)}, u32[]{:S(2)}, u32[]{:S(2)}) collective-permute-start(f32[160,512]{1,0:T(8,128)S(1)} %add.3.own_ref), channel_id=1, source_target_pairs={{0,4},{4,0},{8,12},{12,8},{16,20},{20,16},{24,28},{28,24},{32,36},... | collective-permute-start | bytes 983048 | tf_op jit(solution)/shard_map/ppermute | solution.py:399
  77.1 0.1 collective-permute-start.22
  77.2 3.2 %collective-permute-start.18 = (f32[512,512]{1,0:T(8,128)S(1)}, f32[512,512]{1,0:T(8,128)S(1)}, u32[]{:S(2)}, u32[]{:S(2)}) collective-permute-start(f32[512,512]{1,0:T(8,128)S(1)} %get-tuple-element.93.refs_5_), channel_id=1, source_target_pairs={{0,96},{4,28},{8,104},{12,20},{16,112},{20,12},{24,120},{28,4},{32... | collective-permute-start | bytes 3145736 | tf_op jit(solution)/shard_map/ppermute | solution.py:400
  80.4 0.0 collective-permute-done.19.other_ref
  80.4 18.2 %factor.1 = (f32[256,256]{1,0:T(8,128)S(1)}, f32[256,256]{1,0:T(8,128)S(1)}, f32[256,256]{1,0:T(8,128)S(1)}) custom-call(f32[160,512]{1,0:T(8,128)S(1)} %add.3.own_ref, f32[160,512]{1,0:T(8,128)S(1)} %collective-permute-done.19.other_ref), custom_call_target="tpu_custom_call" | custom-call | flops 21474836480 | bytes 1048576 | tf_op jit(solution)/shard_map/factor/pallas_call | solution.py:106
  98.6 0.0 copy-start.1
  98.7 0.0 collective-permute-done.18.refs_6_
  98.7 1.0 collective-permute-start.23
  99.6 2.2 %collective-permute-start.20 = (f32[256,512]{1,0:T(8,128)S(1)}, f32[256,512]{1,0:T(8,128)S(1)}, u32[]{:S(2)}, u32[]{:S(2)}) collective-permute-start(f32[256,512]{1,0:T(8,128)S(1)} %get-tuple-element.102), channel_id=1, source_target_pairs={{0,1},{1,2},{2,3},{3,0},{4,5},{5,6},{6,7},{7,4},{8,9},{9,10},{10,1... | collective-permute-start | bytes 1572872 | tf_op jit(solution)/shard_map/ppermute | solution.py:403
  101.8 1.1 collective-permute-start.21
  102.9 11.4 %collective-permute-done.20.refs_2_ = f32[256,512]{1,0:T(8,128)S(1)} collective-permute-done((f32[256,512]{1,0:T(8,128)S(1)}, f32[256,512]{1,0:T(8,128)S(1)}, u32[]{:S(2)}, u32[]{:S(2)}) %collective-permute-start.20) | collective-permute-done | bytes 524320 | tf_op jit(solution)/shard_map/ppermute | solution.py:403
  114.3 11.8 %collective-permute-done.21.refs_3_ = f32[256,512]{1,0:T(8,128)S(1)} collective-permute-done((f32[256,512]{1,0:T(8,128)S(1)}, f32[256,512]{1,0:T(8,128)S(1)}, u32[]{:S(2)}, u32[]{:S(2)}) %collective-permute-start.21) | collective-permute-done | bytes 524320 | tf_op jit(solution)/shard_map/ppermute | solution.py:403
  126.1 2.9 %weigh.1 = (f32[256,512]{1,0:T(8,128)}, f32[256,512]{1,0:T(8,128)S(1)}) custom-call(f32[256,512]{1,0:T(8,128)S(1)} %slice.3.lead_ref.refs_0_, f32[256,512]{1,0:T(8,128)S(1)} %collective-permute-done.12.refs_1_, f32[256,512]{1,0:T(8,128)S(1)} %collective-permute-done.15.refs_2_, f32[256,512]{1,0:T(8,128)S(1)} %collective-permute-done.13.refs_3_, ...), custom_call_target="tpu_custom_call" | custom-call | flops 1024 | bytes 1024 | tf_op jit(solution)/shard_map/weigh/pallas_call | solution.py:282
  129.1 0.0 collective-permute-done.22.refs_7_
  129.1 0.0 collective-permute-done.23.refs_8_
  129.1 8.6 %update.1 = f32[256,2048]{1,0:T(8,128)} custom-call(s32[4,8]{1,0:T(4,128)S(1)} %get-tuple-element.109.plan, f32[256,512]{1,0:T(8,128)S(1)} %get-tuple-element.110.refs_0_, f32[256,512]{1,0:T(8,128)S(1)} %get-tuple-element.111.refs_1_, f32[256,512]{1,0:T(8,128)S(1)} %collective-permute-done.20.refs_2_, f32[256,512]{1,0:T(8,128)S(1)} %collective-permute-done.21.refs_3_, ...), custom_call_target="tpu_custom_call" | custom-call | tf_op jit(solution)/shard_map/update/pallas_call | solution.py:330
  (3 shorter events, 0.0 us)
Async XLA Ops:
  0.6 18.0 %copy-start.2 = (s32[32]{0:T(128)S(1)}, s32[32]{0:T(128)}, u32[]{:S(2)}) copy-start(s32[32]{0:T(128)} %map_ref.3) | copy-start | bytes 388
  1.7 6.3 %collective-permute-start.3 = (f32[256,512]{1,0:T(8,128)S(1)}, f32[256,512]{1,0:T(8,128)S(1)}, u32[]{:S(2)}, u32[]{:S(2)}) collective-permute-start(f32[256,512]{1,0:T(8,128)S(1)} %slice.3.lead_ref.refs_0_), channel_id=1, source_target_pairs={{0,4},{4,0},{8,12},{12,8},{16,20},{20,16},{24,28},{28,24},{32,36},... | collective-permute-start | bytes 1572872 | tf_op jit(solution)/shard_map/ppermute | solution.py:375
  3.3 19.0 %collective-permute-start.2 = (f32[160,512]{1,0:T(8,128)S(1)}, f32[160,512]{1,0:T(8,128)S(1)}, u32[]{:S(2)}, u32[]{:S(2)}) collective-permute-start(f32[160,512]{1,0:T(8,128)S(1)} %corner.1.refs_4_), channel_id=1, source_target_pairs={{0,3},{4,7}} | collective-permute-start | bytes 983048 | tf_op jit(solution)/shard_map/ppermute | solution.py:373
  8.1 6.1 %collective-permute-start.4 = (f32[2,32,512]{2,1,0:T(8,128)S(1)}, f32[2,32,512]{2,1,0:T(8,128)S(1)}, u32[]{:S(2)}, u32[]{:S(2)}) collective-permute-start(f32[2,32,512]{2,1,0:T(8,128)S(1)} %get-tuple-element.60), channel_id=1, source_target_pairs={{0,8},{4,12},{8,16},{12,20},{16,24},{20,28},{24,0},{28,4},{32,40},... | collective-permute-start | bytes 393224 | tf_op jit(solution)/shard_map/ppermute | solution.py:379
  8.2 15.4 %collective-permute-start.1 = (f32[160,512]{1,0:T(8,128)S(1)}, f32[160,512]{1,0:T(8,128)S(1)}, u32[]{:S(2)}, u32[]{:S(2)}) collective-permute-start(f32[160,512]{1,0:T(8,128)S(1)} %corner.1.refs_4_), channel_id=1, source_target_pairs={{0,2},{4,6}} | collective-permute-start | bytes 983048 | tf_op jit(solution)/shard_map/ppermute | solution.py:373
  11.0 13.4 %collective-permute-start = (f32[160,512]{1,0:T(8,128)S(1)}, f32[160,512]{1,0:T(8,128)S(1)}, u32[]{:S(2)}, u32[]{:S(2)}) collective-permute-start(f32[160,512]{1,0:T(8,128)S(1)} %corner.1.refs_4_), channel_id=1, source_target_pairs={{0,1},{4,5}} | collective-permute-start | bytes 983048 | tf_op jit(solution)/shard_map/ppermute | solution.py:373
  12.3 5.4 %collective-permute-start.5 = (f32[2,32,512]{2,1,0:T(8,128)S(1)}, f32[2,32,512]{2,1,0:T(8,128)S(1)}, u32[]{:S(2)}, u32[]{:S(2)}) collective-permute-start(f32[2,32,512]{2,1,0:T(8,128)S(1)} %get-tuple-element.61), channel_id=1, source_target_pairs={{0,16},{4,20},{8,24},{12,28},{16,0},{20,4},{24,8},{28,12},{32,48},... | collective-permute-start | bytes 393224 | tf_op jit(solution)/shard_map/ppermute | solution.py:379
  14.2 4.5 %collective-permute-start.6 = (f32[2,32,512]{2,1,0:T(8,128)S(1)}, f32[2,32,512]{2,1,0:T(8,128)S(1)}, u32[]{:S(2)}, u32[]{:S(2)}) collective-permute-start(f32[2,32,512]{2,1,0:T(8,128)S(1)} %get-tuple-element.62), channel_id=1, source_target_pairs={{0,24},{4,28},{8,0},{12,4},{16,8},{20,12},{24,16},{28,20},{32,56},... | collective-permute-start | bytes 393224 | tf_op jit(solution)/shard_map/ppermute | solution.py:379
  18.6 24.3 %copy-start = (f32[256,2048]{1,0:T(8,128)S(1)}, f32[256,2048]{1,0:T(8,128)}, u32[]{:S(2)}) copy-start(f32[256,2048]{1,0:T(8,128)} %front_ref.1) | copy-start | bytes 6291460
  19.6 7.6 %collective-permute-start.7 = (f32[2,32,512]{2,1,0:T(8,128)S(1)}, f32[2,32,512]{2,1,0:T(8,128)S(1)}, u32[]{:S(2)}, u32[]{:S(2)}) collective-permute-start(f32[2,32,512]{2,1,0:T(8,128)S(1)} %get-tuple-element.64), channel_id=1, source_target_pairs={{0,1},{4,5},{8,9},{12,13},{16,17},{20,21},{24,25},{28,29},{32,33},... | collective-permute-start | bytes 393224 | tf_op jit(solution)/shard_map/ppermute | solution.py:382
  21.0 9.1 %collective-permute-start.8 = (f32[2,32,512]{2,1,0:T(8,128)S(1)}, f32[2,32,512]{2,1,0:T(8,128)S(1)}, u32[]{:S(2)}, u32[]{:S(2)}) collective-permute-start(f32[2,32,512]{2,1,0:T(8,128)S(1)} %get-tuple-element.65), channel_id=1, source_target_pairs={{0,2},{4,6},{8,10},{12,14},{16,18},{20,22},{24,26},{28,30},{32,34}... | collective-permute-start | bytes 393224 | tf_op jit(solution)/shard_map/ppermute | solution.py:382
  22.3 7.7 %collective-permute-start.9 = (f32[2,32,512]{2,1,0:T(8,128)S(1)}, f32[2,32,512]{2,1,0:T(8,128)S(1)}, u32[]{:S(2)}, u32[]{:S(2)}) collective-permute-start(f32[2,32,512]{2,1,0:T(8,128)S(1)} %get-tuple-element.66), channel_id=1, source_target_pairs={{0,3},{4,7},{8,11},{12,15},{16,19},{20,23},{24,27},{28,31},{32,35}... | collective-permute-start | bytes 393224 | tf_op jit(solution)/shard_map/ppermute | solution.py:382
  30.1 7.7 %collective-permute-start.10 = (f32[224,512]{1,0:T(8,128)S(1)}, f32[224,512]{1,0:T(8,128)S(1)}, u32[]{:S(2)}, u32[]{:S(2)}) collective-permute-start(f32[224,512]{1,0:T(8,128)S(1)} %merge.1.own_ref), channel_id=1, source_target_pairs={{0,8},{4,36},{8,0},{12,44},{16,24},{20,52},{24,16},{28,60},{32,40}... | collective-permute-start | bytes 1376264 | tf_op jit(solution)/shard_map/ppermute | solution.py:391
  37.9 10.3 %collective-permute-start.11 = (f32[288,512]{1,0:T(8,128)S(1)}, f32[288,512]{1,0:T(8,128)S(1)}, u32[]{:S(2)}, u32[]{:S(2)}) collective-permute-start(f32[288,512]{1,0:T(8,128)S(1)} %join.3.own_ref), channel_id=1, source_target_pairs={{0,24},{4,100},{8,16},{12,108},{16,8},{20,116},{24,0},{28,124},{32... | collective-permute-start | bytes 1769480 | tf_op jit(solution)/shard_map/ppermute | solution.py:392
  38.0 11.3 %collective-permute-start.13 = (f32[256,512]{1,0:T(8,128)S(1)}, f32[256,512]{1,0:T(8,128)S(1)}, u32[]{:S(2)}, u32[]{:S(2)}) collective-permute-start(f32[256,512]{1,0:T(8,128)S(1)} %slice.3.lead_ref.refs_0_), channel_id=1, source_target_pairs={{0,3},{4,7},{8,11},{12,15},{16,19},{20,23},{24,27},{28,31},{32,35}... | collective-permute-start | bytes 1572872 | tf_op jit(solution)/shard_map/ppermute | solution.py:390
  41.6 9.0 %collective-permute-start.12 = (f32[256,512]{1,0:T(8,128)S(1)}, f32[256,512]{1,0:T(8,128)S(1)}, u32[]{:S(2)}, u32[]{:S(2)}) collective-permute-start(f32[256,512]{1,0:T(8,128)S(1)} %slice.3.lead_ref.refs_0_), channel_id=1, source_target_pairs={{0,1},{4,5},{8,9},{12,13},{16,17},{20,21},{24,25},{28,29},{32,33},... | collective-permute-start | bytes 1572872 | tf_op jit(solution)/shard_map/ppermute | solution.py:390
  50.6 17.6 %collective-permute-start.14 = (f32[416,512]{1,0:T(8,128)S(1)}, f32[416,512]{1,0:T(8,128)S(1)}, u32[]{:S(2)}, u32[]{:S(2)}) collective-permute-start(f32[416,512]{1,0:T(8,128)S(1)} %join.4.own_ref), channel_id=1, source_target_pairs={{0,32},{4,12},{8,40},{12,4},{16,48},{20,28},{24,56},{28,20},{32,0}... | collective-permute-start | bytes 2555912 | tf_op jit(solution)/shard_map/ppermute | solution.py:394
  57.8 11.6 %collective-permute-start.15 = (f32[256,512]{1,0:T(8,128)S(1)}, f32[256,512]{1,0:T(8,128)S(1)}, u32[]{:S(2)}, u32[]{:S(2)}) collective-permute-start(f32[256,512]{1,0:T(8,128)S(1)} %slice.3.lead_ref.refs_0_), channel_id=1, source_target_pairs={{0,2},{4,6},{8,10},{12,14},{16,18},{20,22},{24,26},{28,30},{32,34}... | collective-permute-start | bytes 1572872 | tf_op jit(solution)/shard_map/ppermute | solution.py:390
  59.1 15.6 %collective-permute-start.17 = (f32[256,512]{1,0:T(8,128)S(1)}, f32[256,512]{1,0:T(8,128)S(1)}, u32[]{:S(2)}, u32[]{:S(2)}) collective-permute-start(f32[256,512]{1,0:T(8,128)S(1)} %get-tuple-element.92), channel_id=1, source_target_pairs={{0,3},{1,0},{2,1},{3,2},{4,7},{5,4},{6,5},{7,6},{8,11},{9,8},{10,9... | collective-permute-start | bytes 1572872 | tf_op jit(solution)/shard_map/ppermute | solution.py:397
  69.4 5.3 %collective-permute-start.16 = (f32[160,512]{1,0:T(8,128)S(1)}, f32[160,512]{1,0:T(8,128)S(1)}, u32[]{:S(2)}, u32[]{:S(2)}) collective-permute-start(f32[160,512]{1,0:T(8,128)S(1)} %get-tuple-element.87), channel_id=1, source_target_pairs={{0,96},{4,28},{8,104},{12,20},{16,112},{24,120},{32,64},{36,60},{4... | collective-permute-start | bytes 983048 | tf_op jit(solution)/shard_map/ppermute | solution.py:396
  74.8 5.6 %collective-permute-start.19 = (f32[160,512]{1,0:T(8,128)S(1)}, f32[160,512]{1,0:T(8,128)S(1)}, u32[]{:S(2)}, u32[]{:S(2)}) collective-permute-start(f32[160,512]{1,0:T(8,128)S(1)} %add.3.own_ref), channel_id=1, source_target_pairs={{0,4},{4,0},{8,12},{12,8},{16,20},{20,16},{24,28},{28,24},{32,36},... | collective-permute-start | bytes 983048 | tf_op jit(solution)/shard_map/ppermute | solution.py:399
  77.1 52.0 %collective-permute-start.22 = (f32[512,512]{1,0:T(8,128)S(1)}, f32[512,512]{1,0:T(8,128)S(1)}, u32[]{:S(2)}, u32[]{:S(2)}) collective-permute-start(f32[512,512]{1,0:T(8,128)S(1)} %get-tuple-element.93.refs_5_), channel_id=1, source_target_pairs={{0,4},{4,0},{8,12},{12,8},{16,20},{20,16},{24,28},{28,24},{32,36},... | collective-permute-start | bytes 3145736 | tf_op jit(solution)/shard_map/ppermute | solution.py:401
  77.2 21.5 %collective-permute-start.18 = (f32[512,512]{1,0:T(8,128)S(1)}, f32[512,512]{1,0:T(8,128)S(1)}, u32[]{:S(2)}, u32[]{:S(2)}) collective-permute-start(f32[512,512]{1,0:T(8,128)S(1)} %get-tuple-element.93.refs_5_), channel_id=1, source_target_pairs={{0,96},{4,28},{8,104},{12,20},{16,112},{20,12},{24,120},{28,4},{32... | collective-permute-start | bytes 3145736 | tf_op jit(solution)/shard_map/ppermute | solution.py:400
  98.6 30.5 %copy-start.1 = (f32[256,2048]{1,0:T(8,128)S(1)}, f32[256,2048]{1,0:T(8,128)}, u32[]{:S(2)}) copy-start(f32[256,2048]{1,0:T(8,128)} %refs_9_.1) | copy-start | bytes 6291460
  98.7 30.4 %collective-permute-start.23 = (f32[512,512]{1,0:T(8,128)S(1)}, f32[512,512]{1,0:T(8,128)S(1)}, u32[]{:S(2)}, u32[]{:S(2)}) collective-permute-start(f32[512,512]{1,0:T(8,128)S(1)} %collective-permute-done.18.refs_6_), channel_id=1, source_target_pairs={{0,4},{4,0},{8,12},{12,8},{16,20},{20,16},{24,28},{28,24},{32,36},... | collective-permute-start | bytes 3145736 | tf_op jit(solution)/shard_map/ppermute | solution.py:407
  99.6 14.7 %collective-permute-start.20 = (f32[256,512]{1,0:T(8,128)S(1)}, f32[256,512]{1,0:T(8,128)S(1)}, u32[]{:S(2)}, u32[]{:S(2)}) collective-permute-start(f32[256,512]{1,0:T(8,128)S(1)} %get-tuple-element.102), channel_id=1, source_target_pairs={{0,1},{1,2},{2,3},{3,0},{4,5},{5,6},{6,7},{7,4},{8,9},{9,10},{10,1... | collective-permute-start | bytes 1572872 | tf_op jit(solution)/shard_map/ppermute | solution.py:403
  101.8 24.3 %collective-permute-start.21 = (f32[256,512]{1,0:T(8,128)S(1)}, f32[256,512]{1,0:T(8,128)S(1)}, u32[]{:S(2)}, u32[]{:S(2)}) collective-permute-start(f32[256,512]{1,0:T(8,128)S(1)} %get-tuple-element.103), channel_id=1, source_target_pairs={{0,2},{1,3},{2,0},{3,1},{4,6},{5,7},{6,4},{7,5},{8,10},{9,11},{10,... | collective-permute-start | bytes 1572872 | tf_op jit(solution)/shard_map/ppermute | solution.py:403

commit v7 on v6

--- a/solution.py
+++ b/solution.py
@@ -398,14 +398,13 @@
     block, gathered, *pieces = lax.optimization_barrier((block, gathered, *pieces))
     other = lax.ppermute(block, "row", swap)
     late = lax.ppermute(gathered, "row", every[3])
-    other_gathered = lax.ppermute(gathered, "row", swap)
     for hop in (1, 2):
         pieces[hop] = lax.ppermute(pieces[hop], "col", ring[hop])
 
     inverse = factor(block, other)
-    late, inverse = lax.optimization_barrier((late, inverse))
+    late, gathered, inverse, pieces = lax.optimization_barrier((late, gathered, inverse, pieces))
     other_late = lax.ppermute(late, "row", swap)
-    inverse, pieces = lax.optimization_barrier((inverse, pieces))
+    other_gathered = lax.ppermute(gathered, "row", swap)
     panel, weight = weigh([lead, *copies], inverse)
     updated = update(plan, weight, pieces, [gathered, late, other_gathered, other_late], ancestor)
     return panel, updated

time: 139 us -> 118 us (0.85)
  waiting for transfers between devices: 62 us -> 42.4 us
    ppermute x2, waiting for transfers between devices: 23.2 us -> 2.82 us  [shards(): pieces[hop] = lax.ppermute(pieces[hop], 'col', ring[hop])]
  transfers between devices with their start and end apart: 24 -> 24, of which waited for: 15 -> 15; matrix products, arithmetic and copies ran while one was open for 0% -> 0% of each run, Pallas kernels for 18% -> 21%
where the time goes in v7:
time: 118 us; the launch traced here: 117 us
  waiting for transfers between devices  42.4 us (36%)
  starting transfers between devices  39.2 us (33%)
  Pallas kernels  33.2 us (28%)
    pallas_call x9, Pallas kernels, call(): pl.pallas_call(kernel, out_shape=[jax.ShapeDtypeStruct(shape, jnp.float32...  21.7 us
    ppermute x3, starting transfers between devices, shards(): lax.ppermute(blocks[0], ('row', 'col'), [(4 * core, 4 * core + to) for co...  8.84 us
    pallas_call x1, Pallas kernels, update(): pl.pallas_call(update_kernel, out_shape=jax.ShapeDtypeStruct(base.shape,...  8.59 us
    ppermute x1, waiting for transfers between devices, shards(): lax.ppermute(load, 'row', every[2])  7.82 us
    ppermute x1, waiting for transfers between devices, shards(): lax.ppermute(load, 'row', every[0])  7.61 us
    ppermute x1, starting transfers between devices, shards(): lax.ppermute(load, 'row', every[2])  7.22 us
    ppermute x3, starting transfers between devices, shards(): copies = [lax.ppermute(lead, 'col', [(0, to)]) for to in (1, 2, 3)]  6.25 us
    ppermute x3, waiting for transfers between devices, shards(): parts[hop] = lax.ppermute(parts[hop], 'row', pairs)  6.2 us
  transfers between devices with their start and end apart: 24, of which 15 were waited for; matrix products, arithmetic and copies ran while one was open for 0% of the time, Pallas kernels for 21%

profile of v7, /device:TPU:1, one launch (start us, length us, event | category | flops | bytes accessed | tf_op | source)
XLA Modules:
  0.0 116.9 jit_solution(11646555433238719151)
XLA Ops:
  0.6 0.0 copy-start.2
  0.6 1.1 slice.3.lead_ref.refs_0_
  1.7 1.5 %collective-permute-start.3 = (f32[256,512]{1,0:T(8,128)S(1)}, f32[256,512]{1,0:T(8,128)S(1)}, u32[]{:S(2)}, u32[]{:S(2)}) collective-permute-start(f32[256,512]{1,0:T(8,128)S(1)} %slice.3.lead_ref.refs_0_), channel_id=1, source_target_pairs={{0,4},{4,0},{8,12},{12,8},{16,20},{20,16},{24,28},{28,24},{32,36},... | collective-permute-start | bytes 1572872 | tf_op jit(solution)/shard_map/ppermute | solution.py:375
  3.2 0.1 corner.1.refs_4_
  3.3 4.7 %collective-permute-start.2 = (f32[160,512]{1,0:T(8,128)S(1)}, f32[160,512]{1,0:T(8,128)S(1)}, u32[]{:S(2)}, u32[]{:S(2)}) collective-permute-start(f32[160,512]{1,0:T(8,128)S(1)} %corner.1.refs_4_), channel_id=1, source_target_pairs={{0,3},{4,7}} | collective-permute-start | bytes 983048 | tf_op jit(solution)/shard_map/ppermute | solution.py:373
  8.0 0.0 collective-permute-done.3.mate_ref
  8.0 0.1 share.1
  8.1 0.1 collective-permute-start.4
  8.2 2.8 %collective-permute-start.1 = (f32[160,512]{1,0:T(8,128)S(1)}, f32[160,512]{1,0:T(8,128)S(1)}, u32[]{:S(2)}, u32[]{:S(2)}) collective-permute-start(f32[160,512]{1,0:T(8,128)S(1)} %corner.1.refs_4_), channel_id=1, source_target_pairs={{0,2},{4,6}} | collective-permute-start | bytes 983048 | tf_op jit(solution)/shard_map/ppermute | solution.py:373
  11.0 1.3 %collective-permute-start = (f32[160,512]{1,0:T(8,128)S(1)}, f32[160,512]{1,0:T(8,128)S(1)}, u32[]{:S(2)}, u32[]{:S(2)}) collective-permute-start(f32[160,512]{1,0:T(8,128)S(1)} %corner.1.refs_4_), channel_id=1, source_target_pairs={{0,1},{4,5}} | collective-permute-start | bytes 983048 | tf_op jit(solution)/shard_map/ppermute | solution.py:373
  12.3 0.1 collective-permute-start.5
  12.4 1.7 %collective-permute-done.4.refs_1_ = f32[2,32,512]{2,1,0:T(8,128)S(1)} collective-permute-done((f32[2,32,512]{2,1,0:T(8,128)S(1)}, f32[2,32,512]{2,1,0:T(8,128)S(1)}, u32[]{:S(2)}, u32[]{:S(2)}) %collective-permute-start.4) | collective-permute-done | bytes 131104 | tf_op jit(solution)/shard_map/ppermute | solution.py:379
  14.2 0.0 collective-permute-start.6
  14.2 3.6 %collective-permute-done.5.refs_2_ = f32[2,32,512]{2,1,0:T(8,128)S(1)} collective-permute-done((f32[2,32,512]{2,1,0:T(8,128)S(1)}, f32[2,32,512]{2,1,0:T(8,128)S(1)}, u32[]{:S(2)}, u32[]{:S(2)}) %collective-permute-start.5) | collective-permute-done | bytes 131104 | tf_op jit(solution)/shard_map/ppermute | solution.py:379
  17.7 0.9 collective-permute-done.6.refs_3_
  18.6 0.0 copy-done.2
  18.6 1.0 sort.1
  19.6 1.3 %collective-permute-start.7 = (f32[2,32,512]{2,1,0:T(8,128)S(1)}, f32[2,32,512]{2,1,0:T(8,128)S(1)}, u32[]{:S(2)}, u32[]{:S(2)}) collective-permute-start(f32[2,32,512]{2,1,0:T(8,128)S(1)} %get-tuple-element.62), channel_id=1, source_target_pairs={{0,1},{4,5},{8,9},{12,13},{16,17},{20,21},{24,25},{28,29},{32,33},... | collective-permute-start | bytes 393224 | tf_op jit(solution)/shard_map/ppermute | solution.py:382
  21.0 1.3 %collective-permute-start.8 = (f32[2,32,512]{2,1,0:T(8,128)S(1)}, f32[2,32,512]{2,1,0:T(8,128)S(1)}, u32[]{:S(2)}, u32[]{:S(2)}) collective-permute-start(f32[2,32,512]{2,1,0:T(8,128)S(1)} %get-tuple-element.63), channel_id=1, source_target_pairs={{0,2},{4,6},{8,10},{12,14},{16,18},{20,22},{24,26},{28,30},{32,34}... | collective-permute-start | bytes 393224 | tf_op jit(solution)/shard_map/ppermute | solution.py:382
  22.3 0.0 collective-permute-done.2.refs_7_
  22.3 1.3 %collective-permute-start.9 = (f32[2,32,512]{2,1,0:T(8,128)S(1)}, f32[2,32,512]{2,1,0:T(8,128)S(1)}, u32[]{:S(2)}, u32[]{:S(2)}) collective-permute-start(f32[2,32,512]{2,1,0:T(8,128)S(1)} %get-tuple-element.64), channel_id=1, source_target_pairs={{0,3},{4,7},{8,11},{12,15},{16,19},{20,23},{24,27},{28,31},{32,35}... | collective-permute-start | bytes 393224 | tf_op jit(solution)/shard_map/ppermute | solution.py:382
  23.6 0.0 collective-permute-done.1.refs_6_
  23.6 0.8 collective-permute-done.refs_5_
  24.4 2.8 %collective-permute-done.7.refs_1_ = f32[2,32,512]{2,1,0:T(8,128)S(1)} collective-permute-done((f32[2,32,512]{2,1,0:T(8,128)S(1)}, f32[2,32,512]{2,1,0:T(8,128)S(1)}, u32[]{:S(2)}, u32[]{:S(2)}) %collective-permute-start.7) | collective-permute-done | bytes 131104 | tf_op jit(solution)/shard_map/ppermute | solution.py:382
  27.2 2.8 %collective-permute-done.8.refs_2_ = f32[2,32,512]{2,1,0:T(8,128)S(1)} collective-permute-done((f32[2,32,512]{2,1,0:T(8,128)S(1)}, f32[2,32,512]{2,1,0:T(8,128)S(1)}, u32[]{:S(2)}, u32[]{:S(2)}) %collective-permute-start.8) | collective-permute-done | bytes 131104 | tf_op jit(solution)/shard_map/ppermute | solution.py:382
  30.0 0.0 collective-permute-done.9.refs_3_
  30.0 0.1 merge.1.own_ref
  30.1 0.1 collective-permute-start.10
  30.2 7.6 %collective-permute-done.10.got_ref = f32[224,512]{1,0:T(8,128)S(1)} collective-permute-done((f32[224,512]{1,0:T(8,128)S(1)}, f32[224,512]{1,0:T(8,128)S(1)}, u32[]{:S(2)}, u32[]{:S(2)}) %collective-permute-start.10) | collective-permute-done | bytes 458784 | tf_op jit(solution)/shard_map/ppermute | solution.py:391
  37.8 0.1 join.3.own_ref
  37.9 0.1 collective-permute-start.11
  38.0 3.6 %collective-permute-start.13 = (f32[256,512]{1,0:T(8,128)S(1)}, f32[256,512]{1,0:T(8,128)S(1)}, u32[]{:S(2)}, u32[]{:S(2)}) collective-permute-start(f32[256,512]{1,0:T(8,128)S(1)} %slice.3.lead_ref.refs_0_), channel_id=1, source_target_pairs={{0,3},{4,7},{8,11},{12,15},{16,19},{20,23},{24,27},{28,31},{32,35}... | collective-permute-start | bytes 1572872 | tf_op jit(solution)/shard_map/ppermute | solution.py:390
  41.6 1.3 %collective-permute-start.12 = (f32[256,512]{1,0:T(8,128)S(1)}, f32[256,512]{1,0:T(8,128)S(1)}, u32[]{:S(2)}, u32[]{:S(2)}) collective-permute-start(f32[256,512]{1,0:T(8,128)S(1)} %slice.3.lead_ref.refs_0_), channel_id=1, source_target_pairs={{0,1},{4,5},{8,9},{12,13},{16,17},{20,21},{24,25},{28,29},{32,33},... | collective-permute-start | bytes 1572872 | tf_op jit(solution)/shard_map/ppermute | solution.py:390
  42.9 0.0 copy-done
  42.9 2.0 %pick.1 = (f32[256,512]{1,0:T(8,128)S(1)}, f32[256,512]{1,0:T(8,128)S(1)}, f32[256,512]{1,0:T(8,128)S(1)}, f32[256,512]{1,0:T(8,128)S(1)}, s32[4,8]{1,0:T(4,128)S(1)}) custom-call(s32[32]{0:T(128)S(1)} %copy-done.2, f32[256,2048]{1,0:T(8,128)S(1)} %copy-done), custom_call_target="tpu_custom_call" | custom-call | flops 1024 | bytes 1024 | tf_op jit(solution)/shard_map/pick/pallas_call | solution.py:106
  44.9 3.3 %collective-permute-done.11.got_ref = f32[288,512]{1,0:T(8,128)S(1)} collective-permute-done((f32[288,512]{1,0:T(8,128)S(1)}, f32[288,512]{1,0:T(8,128)S(1)}, u32[]{:S(2)}, u32[]{:S(2)}) %collective-permute-start.11) | collective-permute-done | bytes 589856 | tf_op jit(solution)/shard_map/ppermute | solution.py:392
  48.2 0.1 join.4.own_ref
  48.3 1.0 collective-permute-done.13.refs_3_
  49.3 1.3 %collective-permute-done.12.refs_1_ = f32[256,512]{1,0:T(8,128)S(1)} collective-permute-done((f32[256,512]{1,0:T(8,128)S(1)}, f32[256,512]{1,0:T(8,128)S(1)}, u32[]{:S(2)}, u32[]{:S(2)}) %collective-permute-start.12) | collective-permute-done | bytes 524320 | tf_op jit(solution)/shard_map/ppermute | solution.py:390
  50.6 7.2 %collective-permute-start.14 = (f32[416,512]{1,0:T(8,128)S(1)}, f32[416,512]{1,0:T(8,128)S(1)}, u32[]{:S(2)}, u32[]{:S(2)}) collective-permute-start(f32[416,512]{1,0:T(8,128)S(1)} %join.4.own_ref), channel_id=1, source_target_pairs={{0,32},{4,12},{8,40},{12,4},{16,48},{20,28},{24,56},{28,20},{32,0}... | collective-permute-start | bytes 2555912 | tf_op jit(solution)/shard_map/ppermute | solution.py:394
  57.8 1.3 %collective-permute-start.15 = (f32[256,512]{1,0:T(8,128)S(1)}, f32[256,512]{1,0:T(8,128)S(1)}, u32[]{:S(2)}, u32[]{:S(2)}) collective-permute-start(f32[256,512]{1,0:T(8,128)S(1)} %slice.3.lead_ref.refs_0_), channel_id=1, source_target_pairs={{0,2},{4,6},{8,10},{12,14},{16,18},{20,22},{24,26},{28,30},{32,34}... | collective-permute-start | bytes 1572872 | tf_op jit(solution)/shard_map/ppermute | solution.py:390
  59.1 1.2 %collective-permute-start.17 = (f32[256,512]{1,0:T(8,128)S(1)}, f32[256,512]{1,0:T(8,128)S(1)}, u32[]{:S(2)}, u32[]{:S(2)}) collective-permute-start(f32[256,512]{1,0:T(8,128)S(1)} %get-tuple-element.90), channel_id=1, source_target_pairs={{0,3},{1,0},{2,1},{3,2},{4,7},{5,4},{6,5},{7,6},{8,11},{9,8},{10,9... | collective-permute-start | bytes 1572872 | tf_op jit(solution)/shard_map/ppermute | solution.py:397
  60.4 7.8 %collective-permute-done.14.got_ref = f32[416,512]{1,0:T(8,128)S(1)} collective-permute-done((f32[416,512]{1,0:T(8,128)S(1)}, f32[416,512]{1,0:T(8,128)S(1)}, u32[]{:S(2)}, u32[]{:S(2)}) %collective-permute-start.14) | collective-permute-done | bytes 852000 | tf_op jit(solution)/shard_map/ppermute | solution.py:394
  68.2 0.1 join.5
  68.3 1.1 collective-permute-done.15.refs_2_
  69.4 1.3 %collective-permute-start.16 = (f32[160,512]{1,0:T(8,128)S(1)}, f32[160,512]{1,0:T(8,128)S(1)}, u32[]{:S(2)}, u32[]{:S(2)}) collective-permute-start(f32[160,512]{1,0:T(8,128)S(1)} %get-tuple-element.85), channel_id=1, source_target_pairs={{0,96},{4,28},{8,104},{12,20},{16,112},{24,120},{32,64},{36,60},{4... | collective-permute-start | bytes 983048 | tf_op jit(solution)/shard_map/ppermute | solution.py:396
  70.7 4.0 %collective-permute-done.16 = f32[160,512]{1,0:T(8,128)S(1)} collective-permute-done((f32[160,512]{1,0:T(8,128)S(1)}, f32[160,512]{1,0:T(8,128)S(1)}, u32[]{:S(2)}, u32[]{:S(2)}) %collective-permute-start.16) | collective-permute-done | bytes 327712 | tf_op jit(solution)/shard_map/ppermute | solution.py:396
  74.8 0.0 collective-permute-done.17.refs_4_
  74.8 2.3 %collective-permute-start.19 = (f32[160,512]{1,0:T(8,128)S(1)}, f32[160,512]{1,0:T(8,128)S(1)}, u32[]{:S(2)}, u32[]{:S(2)}) collective-permute-start(f32[160,512]{1,0:T(8,128)S(1)} %add.3.own_ref), channel_id=1, source_target_pairs={{0,4},{4,0},{8,12},{12,8},{16,20},{20,16},{24,28},{28,24},{32,36},... | collective-permute-start | bytes 983048 | tf_op jit(solution)/shard_map/ppermute | solution.py:399
  77.1 2.2 %collective-permute-start.20 = (f32[256,512]{1,0:T(8,128)S(1)}, f32[256,512]{1,0:T(8,128)S(1)}, u32[]{:S(2)}, u32[]{:S(2)}) collective-permute-start(f32[256,512]{1,0:T(8,128)S(1)} %get-tuple-element.97), channel_id=1, source_target_pairs={{0,1},{1,2},{2,3},{3,0},{4,5},{5,6},{6,7},{7,4},{8,9},{9,10},{10,1... | collective-permute-start | bytes 1572872 | tf_op jit(solution)/shard_map/ppermute | solution.py:402
  79.3 1.1 collective-permute-start.21
  80.4 2.2 %collective-permute-start.18 = (f32[512,512]{1,0:T(8,128)S(1)}, f32[512,512]{1,0:T(8,128)S(1)}, u32[]{:S(2)}, u32[]{:S(2)}) collective-permute-start(f32[512,512]{1,0:T(8,128)S(1)} %get-tuple-element.110.refs_5_), channel_id=1, source_target_pairs={{0,96},{4,28},{8,104},{12,20},{16,112},{20,12},{24,120},{28,4},{32... | collective-permute-start | bytes 3145736 | tf_op jit(solution)/shard_map/ppermute | solution.py:400
  82.5 0.0 collective-permute-done.19.other_ref
  82.5 18.2 %factor.1 = (f32[256,256]{1,0:T(8,128)S(1)}, f32[256,256]{1,0:T(8,128)S(1)}, f32[256,256]{1,0:T(8,128)S(1)}) custom-call(f32[160,512]{1,0:T(8,128)S(1)} %add.3.own_ref, f32[160,512]{1,0:T(8,128)S(1)} %collective-permute-done.19.other_ref), custom_call_target="tpu_custom_call" | custom-call | flops 21474836480 | bytes 1048576 | tf_op jit(solution)/shard_map/factor/pallas_call | solution.py:106
  100.8 0.0 copy-start.1
  100.8 0.0 collective-permute-done.20.refs_2_
  100.8 2.8 %collective-permute-done.21.refs_3_ = f32[256,512]{1,0:T(8,128)S(1)} collective-permute-done((f32[256,512]{1,0:T(8,128)S(1)}, f32[256,512]{1,0:T(8,128)S(1)}, u32[]{:S(2)}, u32[]{:S(2)}) %collective-permute-start.21) | collective-permute-done | bytes 524320 | tf_op jit(solution)/shard_map/ppermute | solution.py:402
  103.6 0.0 collective-permute-done.18.refs_6_
  103.6 0.9 collective-permute-start.22
  104.5 0.0 collective-permute-start.23
  104.5 2.9 %weigh.1 = (f32[256,512]{1,0:T(8,128)}, f32[256,512]{1,0:T(8,128)S(1)}) custom-call(f32[256,512]{1,0:T(8,128)S(1)} %slice.3.lead_ref.refs_0_, f32[256,512]{1,0:T(8,128)S(1)} %collective-permute-done.12.refs_1_, f32[256,512]{1,0:T(8,128)S(1)} %collective-permute-done.15.refs_2_, f32[256,512]{1,0:T(8,128)S(1)} %collective-permute-done.13.refs_3_, ...), custom_call_target="tpu_custom_call" | custom-call | flops 1024 | bytes 1024 | tf_op jit(solution)/shard_map/weigh/pallas_call | solution.py:282
  107.4 0.0 collective-permute-done.22.refs_7_
  107.4 0.8 collective-permute-done.23.refs_8_
  108.3 8.6 %update.1 = f32[256,2048]{1,0:T(8,128)} custom-call(s32[4,8]{1,0:T(4,128)S(1)} %get-tuple-element.104.plan, f32[256,512]{1,0:T(8,128)S(1)} %get-tuple-element.105.refs_0_, f32[256,512]{1,0:T(8,128)S(1)} %get-tuple-element.106.refs_1_, f32[256,512]{1,0:T(8,128)S(1)} %collective-permute-done.20.refs_2_, f32[256,512]{1,0:T(8,128)S(1)} %collective-permute-done.21.refs_3_, ...), custom_call_target="tpu_custom_call" | custom-call | tf_op jit(solution)/shard_map/update/pallas_call | solution.py:330
  (3 shorter events, 0.0 us)
Async XLA Ops:
  0.6 18.0 %copy-start.2 = (s32[32]{0:T(128)S(1)}, s32[32]{0:T(128)}, u32[]{:S(2)}) copy-start(s32[32]{0:T(128)} %map_ref.3) | copy-start | bytes 388
  1.7 6.3 %collective-permute-start.3 = (f32[256,512]{1,0:T(8,128)S(1)}, f32[256,512]{1,0:T(8,128)S(1)}, u32[]{:S(2)}, u32[]{:S(2)}) collective-permute-start(f32[256,512]{1,0:T(8,128)S(1)} %slice.3.lead_ref.refs_0_), channel_id=1, source_target_pairs={{0,4},{4,0},{8,12},{12,8},{16,20},{20,16},{24,28},{28,24},{32,36},... | collective-permute-start | bytes 1572872 | tf_op jit(solution)/shard_map/ppermute | solution.py:375
  3.3 19.0 %collective-permute-start.2 = (f32[160,512]{1,0:T(8,128)S(1)}, f32[160,512]{1,0:T(8,128)S(1)}, u32[]{:S(2)}, u32[]{:S(2)}) collective-permute-start(f32[160,512]{1,0:T(8,128)S(1)} %corner.1.refs_4_), channel_id=1, source_target_pairs={{0,3},{4,7}} | collective-permute-start | bytes 983048 | tf_op jit(solution)/shard_map/ppermute | solution.py:373
  8.1 6.1 %collective-permute-start.4 = (f32[2,32,512]{2,1,0:T(8,128)S(1)}, f32[2,32,512]{2,1,0:T(8,128)S(1)}, u32[]{:S(2)}, u32[]{:S(2)}) collective-permute-start(f32[2,32,512]{2,1,0:T(8,128)S(1)} %get-tuple-element.58), channel_id=1, source_target_pairs={{0,8},{4,12},{8,16},{12,20},{16,24},{20,28},{24,0},{28,4},{32,40},... | collective-permute-start | bytes 393224 | tf_op jit(solution)/shard_map/ppermute | solution.py:379
  8.2 15.4 %collective-permute-start.1 = (f32[160,512]{1,0:T(8,128)S(1)}, f32[160,512]{1,0:T(8,128)S(1)}, u32[]{:S(2)}, u32[]{:S(2)}) collective-permute-start(f32[160,512]{1,0:T(8,128)S(1)} %corner.1.refs_4_), channel_id=1, source_target_pairs={{0,2},{4,6}} | collective-permute-start | bytes 983048 | tf_op jit(solution)/shard_map/ppermute | solution.py:373
  11.0 13.4 %collective-permute-start = (f32[160,512]{1,0:T(8,128)S(1)}, f32[160,512]{1,0:T(8,128)S(1)}, u32[]{:S(2)}, u32[]{:S(2)}) collective-permute-start(f32[160,512]{1,0:T(8,128)S(1)} %corner.1.refs_4_), channel_id=1, source_target_pairs={{0,1},{4,5}} | collective-permute-start | bytes 983048 | tf_op jit(solution)/shard_map/ppermute | solution.py:373
  12.3 5.4 %collective-permute-start.5 = (f32[2,32,512]{2,1,0:T(8,128)S(1)}, f32[2,32,512]{2,1,0:T(8,128)S(1)}, u32[]{:S(2)}, u32[]{:S(2)}) collective-permute-start(f32[2,32,512]{2,1,0:T(8,128)S(1)} %get-tuple-element.59), channel_id=1, source_target_pairs={{0,16},{4,20},{8,24},{12,28},{16,0},{20,4},{24,8},{28,12},{32,48},... | collective-permute-start | bytes 393224 | tf_op jit(solution)/shard_map/ppermute | solution.py:379
  14.2 4.5 %collective-permute-start.6 = (f32[2,32,512]{2,1,0:T(8,128)S(1)}, f32[2,32,512]{2,1,0:T(8,128)S(1)}, u32[]{:S(2)}, u32[]{:S(2)}) collective-permute-start(f32[2,32,512]{2,1,0:T(8,128)S(1)} %get-tuple-element.60), channel_id=1, source_target_pairs={{0,24},{4,28},{8,0},{12,4},{16,8},{20,12},{24,16},{28,20},{32,56},... | collective-permute-start | bytes 393224 | tf_op jit(solution)/shard_map/ppermute | solution.py:379
  18.6 24.3 %copy-start = (f32[256,2048]{1,0:T(8,128)S(1)}, f32[256,2048]{1,0:T(8,128)}, u32[]{:S(2)}) copy-start(f32[256,2048]{1,0:T(8,128)} %front_ref.1) | copy-start | bytes 6291460
  19.6 7.6 %collective-permute-start.7 = (f32[2,32,512]{2,1,0:T(8,128)S(1)}, f32[2,32,512]{2,1,0:T(8,128)S(1)}, u32[]{:S(2)}, u32[]{:S(2)}) collective-permute-start(f32[2,32,512]{2,1,0:T(8,128)S(1)} %get-tuple-element.62), channel_id=1, source_target_pairs={{0,1},{4,5},{8,9},{12,13},{16,17},{20,21},{24,25},{28,29},{32,33},... | collective-permute-start | bytes 393224 | tf_op jit(solution)/shard_map/ppermute | solution.py:382
  21.0 9.1 %collective-permute-start.8 = (f32[2,32,512]{2,1,0:T(8,128)S(1)}, f32[2,32,512]{2,1,0:T(8,128)S(1)}, u32[]{:S(2)}, u32[]{:S(2)}) collective-permute-start(f32[2,32,512]{2,1,0:T(8,128)S(1)} %get-tuple-element.63), channel_id=1, source_target_pairs={{0,2},{4,6},{8,10},{12,14},{16,18},{20,22},{24,26},{28,30},{32,34}... | collective-permute-start | bytes 393224 | tf_op jit(solution)/shard_map/ppermute | solution.py:382
  22.3 7.7 %collective-permute-start.9 = (f32[2,32,512]{2,1,0:T(8,128)S(1)}, f32[2,32,512]{2,1,0:T(8,128)S(1)}, u32[]{:S(2)}, u32[]{:S(2)}) collective-permute-start(f32[2,32,512]{2,1,0:T(8,128)S(1)} %get-tuple-element.64), channel_id=1, source_target_pairs={{0,3},{4,7},{8,11},{12,15},{16,19},{20,23},{24,27},{28,31},{32,35}... | collective-permute-start | bytes 393224 | tf_op jit(solution)/shard_map/ppermute | solution.py:382
  30.1 7.7 %collective-permute-start.10 = (f32[224,512]{1,0:T(8,128)S(1)}, f32[224,512]{1,0:T(8,128)S(1)}, u32[]{:S(2)}, u32[]{:S(2)}) collective-permute-start(f32[224,512]{1,0:T(8,128)S(1)} %merge.1.own_ref), channel_id=1, source_target_pairs={{0,8},{4,36},{8,0},{12,44},{16,24},{20,52},{24,16},{28,60},{32,40}... | collective-permute-start | bytes 1376264 | tf_op jit(solution)/shard_map/ppermute | solution.py:391
  37.9 10.3 %collective-permute-start.11 = (f32[288,512]{1,0:T(8,128)S(1)}, f32[288,512]{1,0:T(8,128)S(1)}, u32[]{:S(2)}, u32[]{:S(2)}) collective-permute-start(f32[288,512]{1,0:T(8,128)S(1)} %join.3.own_ref), channel_id=1, source_target_pairs={{0,24},{4,100},{8,16},{12,108},{16,8},{20,116},{24,0},{28,124},{32... | collective-permute-start | bytes 1769480 | tf_op jit(solution)/shard_map/ppermute | solution.py:392
  38.0 11.3 %collective-permute-start.13 = (f32[256,512]{1,0:T(8,128)S(1)}, f32[256,512]{1,0:T(8,128)S(1)}, u32[]{:S(2)}, u32[]{:S(2)}) collective-permute-start(f32[256,512]{1,0:T(8,128)S(1)} %slice.3.lead_ref.refs_0_), channel_id=1, source_target_pairs={{0,3},{4,7},{8,11},{12,15},{16,19},{20,23},{24,27},{28,31},{32,35}... | collective-permute-start | bytes 1572872 | tf_op jit(solution)/shard_map/ppermute | solution.py:390
  41.6 9.0 %collective-permute-start.12 = (f32[256,512]{1,0:T(8,128)S(1)}, f32[256,512]{1,0:T(8,128)S(1)}, u32[]{:S(2)}, u32[]{:S(2)}) collective-permute-start(f32[256,512]{1,0:T(8,128)S(1)} %slice.3.lead_ref.refs_0_), channel_id=1, source_target_pairs={{0,1},{4,5},{8,9},{12,13},{16,17},{20,21},{24,25},{28,29},{32,33},... | collective-permute-start | bytes 1572872 | tf_op jit(solution)/shard_map/ppermute | solution.py:390
  50.6 17.6 %collective-permute-start.14 = (f32[416,512]{1,0:T(8,128)S(1)}, f32[416,512]{1,0:T(8,128)S(1)}, u32[]{:S(2)}, u32[]{:S(2)}) collective-permute-start(f32[416,512]{1,0:T(8,128)S(1)} %join.4.own_ref), channel_id=1, source_target_pairs={{0,32},{4,12},{8,40},{12,4},{16,48},{20,28},{24,56},{28,20},{32,0}... | collective-permute-start | bytes 2555912 | tf_op jit(solution)/shard_map/ppermute | solution.py:394
  57.8 11.6 %collective-permute-start.15 = (f32[256,512]{1,0:T(8,128)S(1)}, f32[256,512]{1,0:T(8,128)S(1)}, u32[]{:S(2)}, u32[]{:S(2)}) collective-permute-start(f32[256,512]{1,0:T(8,128)S(1)} %slice.3.lead_ref.refs_0_), channel_id=1, source_target_pairs={{0,2},{4,6},{8,10},{12,14},{16,18},{20,22},{24,26},{28,30},{32,34}... | collective-permute-start | bytes 1572872 | tf_op jit(solution)/shard_map/ppermute | solution.py:390
  59.1 15.6 %collective-permute-start.17 = (f32[256,512]{1,0:T(8,128)S(1)}, f32[256,512]{1,0:T(8,128)S(1)}, u32[]{:S(2)}, u32[]{:S(2)}) collective-permute-start(f32[256,512]{1,0:T(8,128)S(1)} %get-tuple-element.90), channel_id=1, source_target_pairs={{0,3},{1,0},{2,1},{3,2},{4,7},{5,4},{6,5},{7,6},{8,11},{9,8},{10,9... | collective-permute-start | bytes 1572872 | tf_op jit(solution)/shard_map/ppermute | solution.py:397
  69.4 5.3 %collective-permute-start.16 = (f32[160,512]{1,0:T(8,128)S(1)}, f32[160,512]{1,0:T(8,128)S(1)}, u32[]{:S(2)}, u32[]{:S(2)}) collective-permute-start(f32[160,512]{1,0:T(8,128)S(1)} %get-tuple-element.85), channel_id=1, source_target_pairs={{0,96},{4,28},{8,104},{12,20},{16,112},{24,120},{32,64},{36,60},{4... | collective-permute-start | bytes 983048 | tf_op jit(solution)/shard_map/ppermute | solution.py:396
  74.8 7.8 %collective-permute-start.19 = (f32[160,512]{1,0:T(8,128)S(1)}, f32[160,512]{1,0:T(8,128)S(1)}, u32[]{:S(2)}, u32[]{:S(2)}) collective-permute-start(f32[160,512]{1,0:T(8,128)S(1)} %add.3.own_ref), channel_id=1, source_target_pairs={{0,4},{4,0},{8,12},{12,8},{16,20},{20,16},{24,28},{28,24},{32,36},... | collective-permute-start | bytes 983048 | tf_op jit(solution)/shard_map/ppermute | solution.py:399
  77.1 23.7 %collective-permute-start.20 = (f32[256,512]{1,0:T(8,128)S(1)}, f32[256,512]{1,0:T(8,128)S(1)}, u32[]{:S(2)}, u32[]{:S(2)}) collective-permute-start(f32[256,512]{1,0:T(8,128)S(1)} %get-tuple-element.97), channel_id=1, source_target_pairs={{0,1},{1,2},{2,3},{3,0},{4,5},{5,6},{6,7},{7,4},{8,9},{9,10},{10,1... | collective-permute-start | bytes 1572872 | tf_op jit(solution)/shard_map/ppermute | solution.py:402
  79.3 24.3 %collective-permute-start.21 = (f32[256,512]{1,0:T(8,128)S(1)}, f32[256,512]{1,0:T(8,128)S(1)}, u32[]{:S(2)}, u32[]{:S(2)}) collective-permute-start(f32[256,512]{1,0:T(8,128)S(1)} %get-tuple-element.98), channel_id=1, source_target_pairs={{0,2},{1,3},{2,0},{3,1},{4,6},{5,7},{6,4},{7,5},{8,10},{9,11},{10,... | collective-permute-start | bytes 1572872 | tf_op jit(solution)/shard_map/ppermute | solution.py:402
  80.4 23.2 %collective-permute-start.18 = (f32[512,512]{1,0:T(8,128)S(1)}, f32[512,512]{1,0:T(8,128)S(1)}, u32[]{:S(2)}, u32[]{:S(2)}) collective-permute-start(f32[512,512]{1,0:T(8,128)S(1)} %get-tuple-element.110.refs_5_), channel_id=1, source_target_pairs={{0,96},{4,28},{8,104},{12,20},{16,112},{20,12},{24,120},{28,4},{32... | collective-permute-start | bytes 3145736 | tf_op jit(solution)/shard_map/ppermute | solution.py:400
  100.8 7.5 %copy-start.1 = (f32[256,2048]{1,0:T(8,128)S(1)}, f32[256,2048]{1,0:T(8,128)}, u32[]{:S(2)}) copy-start(f32[256,2048]{1,0:T(8,128)} %refs_9_.1) | copy-start | bytes 6291460
  103.6 3.8 %collective-permute-start.22 = (f32[512,512]{1,0:T(8,128)S(1)}, f32[512,512]{1,0:T(8,128)S(1)}, u32[]{:S(2)}, u32[]{:S(2)}) collective-permute-start(f32[512,512]{1,0:T(8,128)S(1)} %get-tuple-element.110.refs_5_), channel_id=1, source_target_pairs={{0,4},{4,0},{8,12},{12,8},{16,20},{20,16},{24,28},{28,24},{32,36},... | collective-permute-start | bytes 3145736 | tf_op jit(solution)/shard_map/ppermute | solution.py:407
  104.5 3.8 %collective-permute-start.23 = (f32[512,512]{1,0:T(8,128)S(1)}, f32[512,512]{1,0:T(8,128)S(1)}, u32[]{:S(2)}, u32[]{:S(2)}) collective-permute-start(f32[512,512]{1,0:T(8,128)S(1)} %collective-permute-done.18.refs_6_), channel_id=1, source_target_pairs={{0,4},{4,0},{8,12},{12,8},{16,20},{20,16},{24,28},{28,24},{32,36},... | collective-permute-start | bytes 3145736 | tf_op jit(solution)/shard_map/ppermute | solution.py:406

commit v8 on v7

--- a/solution.py
+++ b/solution.py
@@ -207,7 +207,7 @@
 
 
 def merge_kernel(*refs):
-    parts, blocks, out_ref = refs[:4], refs[4:8], refs[8]
+    parts, block_ref, got_ref, out_ref = refs[:4], refs[4], refs[5], refs[6]
     for index, ref in enumerate(parts):
 
         @pl.when(lax.axis_index("col") == index)
@@ -215,7 +215,7 @@
             out_ref[:32] = ref[0]
             out_ref[32:64] = ref[1]
 
-    out_ref[64:] = (blocks[0][...] + blocks[1][...]) + (blocks[2][...] + blocks[3][...])
+    out_ref[64:] = block_ref[...] + got_ref[...]
 
 
 def join_kernel(own_ref, got_ref, *outs):
@@ -303,12 +303,12 @@
             off_z, off_x = plane ^ group, line ^ x
             first = jnp.where(holder == 0, off_x, off_z)
             second = jnp.where(holder == 0, off_z, off_x)
-            index = ((first & 1) ^ (first >> 1)) + 2 * (first >> 1) + 4 * ((second & 1) ^ (second >> 1))
+            index = (first >> 1) + 2 * ((second & 1) ^ (second >> 1)) + 4 * (second >> 1)
             rows = pl.ds(pl.multiple_of(index * 64 + place * 32, 32), 32)
             into = pl.ds(pl.multiple_of((2 * x + holder) * 32, 32), 32)
             for late in range(2):
 
-                @pl.when((second >> 1) == late)
+                @pl.when(((first & 1) ^ (first >> 1)) == late)
                 def _():
                     ahead_ref[into, :] = gathered[2 * parity + late][rows, :]
 
@@ -343,8 +343,7 @@
 
 
 def doubling_steps():
-    every, spread = [], []
-    have = [{(0, 0)}, {(0, 0)}]
+    every = []
     for step in range(4):
         flip = 1 if step % 2 == 0 else 3
         pairs = []
@@ -352,12 +351,9 @@
             for x in range(4):
                 for core in range(2):
                     to = (z, x ^ flip) if step // 2 == core else (z ^ flip, x)
-                    pairs.append(((z * 4 + x) * 2 + core, (to[0] * 4 + to[1]) * 2 + core, (z, x), to, core))
-        every.append([pair[:2] for pair in pairs])
-        spread.append([pair[:2] for pair in pairs if pair[2] in have[pair[4]]])
-        for core in range(2):
-            have[core] |= {pair[3] for pair in pairs if pair[4] == core and pair[2] in have[core]}
-    return every, spread
+                    pairs.append(((z * 4 + x) * 2 + core, (to[0] * 4 + to[1]) * 2 + core))
+        every.append(pairs)
+    return every, [pair for pair in every[0] if pair[0] < 2]
 
 
 def shards(front, ancestor, tile_map):
@@ -378,28 +374,31 @@
         pairs = [(z * 8 + x * 2 + k, z * 8 + (x + hop) % 4 * 2 + k) for z in range(4) for x in range(4) for k in range(2)]
         parts[hop] = lax.ppermute(parts[hop], "row", pairs)
     parts = list(local_call(sort_kernel, "sort", [part] * 4, 1)(tile_map, *parts))
+    blocks, parts = lax.optimization_barrier((blocks, parts))
+
+    every, spread = doubling_steps()
     for to in range(1, 4):
         parts[to] = lax.ppermute(parts[to], "col", [(0, to)])
-    blocks, parts = lax.optimization_barrier((blocks, parts))
-    load = local_call(merge_kernel, "merge", [(64 + BLOCK, LEAD)])(*parts, *blocks)[0]
+    block = (blocks[0] + blocks[1]) + (blocks[2] + blocks[3])
+    got = lax.ppermute(block, "row", spread)
+    block, got, parts = lax.optimization_barrier((block, got, parts))
+    load = local_call(merge_kernel, "merge", [(64 + BLOCK, LEAD)])(*parts, block, got)[0]
 
     *pieces, plan = local_call(pick_kernel, "pick", [(height, 2 * PW)] * 4, 1, [(4, 8)])(tile_map, front)
 
-    every, spread = doubling_steps()
     load, lead = lax.optimization_barrier((load, lead))
     copies = [lax.ppermute(lead, "col", [(0, to)]) for to in (1, 2, 3)]
-    load = local_call(join_kernel, "join", [(128 + BLOCK, LEAD)])(load, lax.ppermute(load, "row", every[0]))[0]
-    load = local_call(join_kernel, "join", [(256 + BLOCK, LEAD)])(load, lax.ppermute(load, "row", every[1]))[0]
+    load = local_call(join_kernel, "join", [(128 + BLOCK, LEAD)])(load, lax.ppermute(load, "row", every[1]))[0]
     load, copies[0], copies[2], *pieces = lax.optimization_barrier((load, copies[0], copies[2], *pieces))
-    gathered, block = local_call(join_kernel, "join", [(512, LEAD), (BLOCK, LEAD)])(load, lax.ppermute(load, "row", every[2]))
-    block, gathered, copies[1] = lax.optimization_barrier((block, gathered, copies[1]))
-    block = block + lax.ppermute(block, "row", spread[3])
-    pieces[3] = lax.ppermute(pieces[3], "col", ring[3])
+    load = local_call(join_kernel, "join", [(256 + BLOCK, LEAD)])(load, lax.ppermute(load, "row", every[2]))[0]
+    load, copies[1], *pieces = lax.optimization_barrier((load, copies[1], *pieces))
+    gathered, block = local_call(join_kernel, "join", [(512, LEAD), (BLOCK, LEAD)])(load, lax.ppermute(load, "row", every[3]))
+    for hop in (1, 3):
+        pieces[hop] = lax.ppermute(pieces[hop], "col", ring[hop])
     block, gathered, *pieces = lax.optimization_barrier((block, gathered, *pieces))
     other = lax.ppermute(block, "row", swap)
-    late = lax.ppermute(gathered, "row", every[3])
-    for hop in (1, 2):
-        pieces[hop] = lax.ppermute(pieces[hop], "col", ring[hop])
+    late = lax.ppermute(gathered, "row", every[0])
+    pieces[2] = lax.ppermute(pieces[2], "col", ring[2])
 
     inverse = factor(block, other)
     late, gathered, inverse, pieces = lax.optimization_barrier((late, gathered, inverse, pieces))

time: 118 us -> 116 us (0.983)
  starting transfers between devices: 39.2 us -> 37.5 us
    ppermute x1, starting transfers between devices: 7.22 us -> 0.01 us  [shards(): lax.ppermute(load, 'row', every[2])]
    ppermute x3, waiting for transfers between devices: 6.2 us -> 13.1 us  [shards(): parts[hop] = lax.ppermute(parts[hop], 'row', pairs)]
    ppermute x1, waiting for transfers between devices: 3.25 us -> 6.8 us  [shards(): lax.ppermute(load, 'row', every[1])]
    ppermute x3, waiting for transfers between devices: 5.62 us -> 2.19 us  [shards(): parts[to] = lax.ppermute(parts[to], 'col', [(0, to)])]
    ppermute x1, starting transfers between devices: 2.31 us -> 5.52 us  [shards(): other = lax.ppermute(block, 'row', swap)]
    ppermute x2, waiting for transfers between devices: 2.82 us -> 0.01 us  [shards(): pieces[hop] = lax.ppermute(pieces[hop], 'col', ring[hop])]
    ppermute x4, starting transfers between devices: 4.79 us -> 6.81 us  [the longest x1 3.72 us: shards(): pieces[2] = lax.ppermute(pieces[2], 'col', ring[2])]
    ppermute x3, starting transfers between devices: 6.25 us -> 7.76 us  [shards(): copies = [lax.ppermute(lead, 'col', [(0, to)]) for to in (1, 2, 3)]]
  transfers between devices with their start and end apart: 24 -> 24, of which waited for: 15 -> 9; matrix products, arithmetic and copies ran while one was open for 0% -> 0% of each run, Pallas kernels for 21% -> 21%
where the time goes in v8:
time: 116 us
  waiting for transfers between devices  43 us (37%)
  starting transfers between devices  37.5 us (32%)
  Pallas kernels  33.2 us (29%)
    pallas_call x9, Pallas kernels, call(): pl.pallas_call(kernel, out_shape=[jax.ShapeDtypeStruct(shape, jnp.float32...  21.6 us
    ppermute x3, waiting for transfers between devices, shards(): parts[hop] = lax.ppermute(parts[hop], 'row', pairs)  13.1 us
    ppermute x1, waiting for transfers between devices, shards(): lax.ppermute(load, 'row', every[3])  10.4 us
    pallas_call x1, Pallas kernels, update(): pl.pallas_call(update_kernel, out_shape=jax.ShapeDtypeStruct(base.shape,...  8.58 us
    ppermute x3, starting transfers between devices, shards(): copies = [lax.ppermute(lead, 'col', [(0, to)]) for to in (1, 2, 3)]  7.76 us
    ppermute x1, waiting for transfers between devices, shards(): lax.ppermute(load, 'row', every[2])  7.71 us
    ppermute x3, starting transfers between devices, shards(): lax.ppermute(blocks[0], ('row', 'col'), [(4 * core, 4 * core + to) for co...  7.34 us
    ppermute x1, waiting for transfers between devices, shards(): lax.ppermute(load, 'row', every[1])  6.8 us
  transfers between devices with their start and end apart: 24, of which 9 were waited for; matrix products, arithmetic and copies ran while one was open for 0% of the time, Pallas kernels for 21%

profile of v8, /device:TPU:1, one launch (start us, length us, event | category | flops | bytes accessed | tf_op | source)
XLA Modules:
  0.0 115.8 jit_solution(2589661206277587854)
XLA Ops:
  0.6 0.0 copy-start.2
  0.6 1.1 slice.3.lead_ref.refs_0_
  1.7 1.5 %collective-permute-start.3 = (f32[256,512]{1,0:T(8,128)S(1)}, f32[256,512]{1,0:T(8,128)S(1)}, u32[]{:S(2)}, u32[]{:S(2)}) collective-permute-start(f32[256,512]{1,0:T(8,128)S(1)} %slice.3.lead_ref.refs_0_), channel_id=1, source_target_pairs={{0,4},{4,0},{8,12},{12,8},{16,20},{20,16},{24,28},{28,24},{32,36},... | collective-permute-start | bytes 1572872 | tf_op jit(solution)/shard_map/ppermute | solution.py:371
  3.2 0.1 corner.1
  3.3 4.7 %collective-permute-start.2 = (f32[160,512]{1,0:T(8,128)S(1)}, f32[160,512]{1,0:T(8,128)S(1)}, u32[]{:S(2)}, u32[]{:S(2)}) collective-permute-start(f32[160,512]{1,0:T(8,128)S(1)} %corner.1), channel_id=1, source_target_pairs={{0,3},{4,7}} | collective-permute-start | bytes 983048 | tf_op jit(solution)/shard_map/ppermute | solution.py:369
  8.0 1.3 %collective-permute-start.1 = (f32[160,512]{1,0:T(8,128)S(1)}, f32[160,512]{1,0:T(8,128)S(1)}, u32[]{:S(2)}, u32[]{:S(2)}) collective-permute-start(f32[160,512]{1,0:T(8,128)S(1)} %corner.1), channel_id=1, source_target_pairs={{0,2},{4,6}} | collective-permute-start | bytes 983048 | tf_op jit(solution)/shard_map/ppermute | solution.py:369
  9.3 1.3 %collective-permute-start = (f32[160,512]{1,0:T(8,128)S(1)}, f32[160,512]{1,0:T(8,128)S(1)}, u32[]{:S(2)}, u32[]{:S(2)}) collective-permute-start(f32[160,512]{1,0:T(8,128)S(1)} %corner.1), channel_id=1, source_target_pairs={{0,1},{4,5}} | collective-permute-start | bytes 983048 | tf_op jit(solution)/shard_map/ppermute | solution.py:369
  10.6 0.0 collective-permute-done.3.mate_ref
  10.7 0.1 share.1
  10.8 0.0 copy-start
  10.8 0.1 collective-permute-start.4
  10.9 0.1 collective-permute-start.5
  10.9 9.0 %collective-permute-done.4.refs_1_ = f32[2,32,512]{2,1,0:T(8,128)S(1)} collective-permute-done((f32[2,32,512]{2,1,0:T(8,128)S(1)}, f32[2,32,512]{2,1,0:T(8,128)S(1)}, u32[]{:S(2)}, u32[]{:S(2)}) %collective-permute-start.4) | collective-permute-done | bytes 131104 | tf_op jit(solution)/shard_map/ppermute | solution.py:375
  19.9 0.0 collective-permute-start.6
  19.9 0.0 collective-permute-done.5.refs_2_
  19.9 4.2 %collective-permute-done.6.refs_3_ = f32[2,32,512]{2,1,0:T(8,128)S(1)} collective-permute-done((f32[2,32,512]{2,1,0:T(8,128)S(1)}, f32[2,32,512]{2,1,0:T(8,128)S(1)}, u32[]{:S(2)}, u32[]{:S(2)}) %collective-permute-start.6) | collective-permute-done | bytes 131104 | tf_op jit(solution)/shard_map/ppermute | solution.py:375
  24.1 1.0 sort.1
  25.1 0.0 collective-permute-done.2
  25.1 0.0 collective-permute-done.1
  25.1 0.0 collective-permute-done
  25.1 0.1 add_add_fusion.refs_4_
  25.3 1.3 %collective-permute-start.7 = (f32[160,512]{1,0:T(8,128)S(1)}, f32[160,512]{1,0:T(8,128)S(1)}, u32[]{:S(2)}, u32[]{:S(2)}) collective-permute-start(f32[160,512]{1,0:T(8,128)S(1)} %add_add_fusion.refs_4_), channel_id=1, source_target_pairs={{0,8},{4,36},{1,9},{5,37},{2,10},{6,38},{3,11},{7,39}} | collective-permute-start | bytes 983048 | tf_op jit(solution)/shard_map/ppermute | solution.py:383
  26.6 2.4 %collective-permute-start.8 = (f32[2,32,512]{2,1,0:T(8,128)S(1)}, f32[2,32,512]{2,1,0:T(8,128)S(1)}, u32[]{:S(2)}, u32[]{:S(2)}) collective-permute-start(f32[2,32,512]{2,1,0:T(8,128)S(1)} %get-tuple-element.79), channel_id=1, source_target_pairs={{0,1},{4,5},{8,9},{12,13},{16,17},{20,21},{24,25},{28,29},{32,33},... | collective-permute-start | bytes 393224 | tf_op jit(solution)/shard_map/ppermute | solution.py:381
  29.0 1.3 %collective-permute-start.9 = (f32[2,32,512]{2,1,0:T(8,128)S(1)}, f32[2,32,512]{2,1,0:T(8,128)S(1)}, u32[]{:S(2)}, u32[]{:S(2)}) collective-permute-start(f32[2,32,512]{2,1,0:T(8,128)S(1)} %get-tuple-element.80), channel_id=1, source_target_pairs={{0,2},{4,6},{8,10},{12,14},{16,18},{20,22},{24,26},{28,30},{32,34}... | collective-permute-start | bytes 393224 | tf_op jit(solution)/shard_map/ppermute | solution.py:381
  30.3 1.3 %collective-permute-start.10 = (f32[2,32,512]{2,1,0:T(8,128)S(1)}, f32[2,32,512]{2,1,0:T(8,128)S(1)}, u32[]{:S(2)}, u32[]{:S(2)}) collective-permute-start(f32[2,32,512]{2,1,0:T(8,128)S(1)} %get-tuple-element.81), channel_id=1, source_target_pairs={{0,3},{4,7},{8,11},{12,15},{16,19},{20,23},{24,27},{28,31},{32,35}... | collective-permute-start | bytes 393224 | tf_op jit(solution)/shard_map/ppermute | solution.py:381
  31.6 0.0 collective-permute-done.8.refs_1_
  31.6 2.2 %collective-permute-done.9.refs_2_ = f32[2,32,512]{2,1,0:T(8,128)S(1)} collective-permute-done((f32[2,32,512]{2,1,0:T(8,128)S(1)}, f32[2,32,512]{2,1,0:T(8,128)S(1)}, u32[]{:S(2)}, u32[]{:S(2)}) %collective-permute-start.9) | collective-permute-done | bytes 131104 | tf_op jit(solution)/shard_map/ppermute | solution.py:381
  33.8 0.0 collective-permute-done.10.refs_3_
  33.8 0.0 collective-permute-done.7.refs_5_
  33.8 0.1 merge.1.own_ref
  33.9 5.1 %collective-permute-start.13 = (f32[256,512]{1,0:T(8,128)S(1)}, f32[256,512]{1,0:T(8,128)S(1)}, u32[]{:S(2)}, u32[]{:S(2)}) collective-permute-start(f32[256,512]{1,0:T(8,128)S(1)} %slice.3.lead_ref.refs_0_), channel_id=1, source_target_pairs={{0,3},{4,7},{8,11},{12,15},{16,19},{20,23},{24,27},{28,31},{32,35}... | collective-permute-start | bytes 1572872 | tf_op jit(solution)/shard_map/ppermute | solution.py:390
  39.0 1.3 %collective-permute-start.12 = (f32[256,512]{1,0:T(8,128)S(1)}, f32[256,512]{1,0:T(8,128)S(1)}, u32[]{:S(2)}, u32[]{:S(2)}) collective-permute-start(f32[256,512]{1,0:T(8,128)S(1)} %slice.3.lead_ref.refs_0_), channel_id=1, source_target_pairs={{0,1},{4,5},{8,9},{12,13},{16,17},{20,21},{24,25},{28,29},{32,33},... | collective-permute-start | bytes 1572872 | tf_op jit(solution)/shard_map/ppermute | solution.py:390
  40.3 0.1 collective-permute-start.11
  40.4 2.0 %pick.1 = (f32[256,512]{1,0:T(8,128)S(1)}, f32[256,512]{1,0:T(8,128)S(1)}, f32[256,512]{1,0:T(8,128)S(1)}, f32[256,512]{1,0:T(8,128)S(1)}, s32[4,8]{1,0:T(4,128)S(1)}) custom-call(s32[32]{0:T(128)S(1)} %copy-done.2, f32[256,2048]{1,0:T(8,128)S(1)} %copy-done), custom_call_target="tpu_custom_call" | custom-call | flops 1024 | bytes 1024 | tf_op jit(solution)/shard_map/pick/pallas_call | solution.py:106
  42.5 6.8 %collective-permute-done.11.got_ref = f32[224,512]{1,0:T(8,128)S(1)} collective-permute-done((f32[224,512]{1,0:T(8,128)S(1)}, f32[224,512]{1,0:T(8,128)S(1)}, u32[]{:S(2)}, u32[]{:S(2)}) %collective-permute-start.11) | collective-permute-done | bytes 458784 | tf_op jit(solution)/shard_map/ppermute | solution.py:391
  49.3 0.1 join.3.own_ref
  49.3 0.0 collective-permute-done.13.refs_3_
  49.3 0.5 collective-permute-done.12.refs_1_
  49.8 0.0 collective-permute-start.14
  49.8 1.3 %collective-permute-start.15 = (f32[256,512]{1,0:T(8,128)S(1)}, f32[256,512]{1,0:T(8,128)S(1)}, u32[]{:S(2)}, u32[]{:S(2)}) collective-permute-start(f32[256,512]{1,0:T(8,128)S(1)} %slice.3.lead_ref.refs_0_), channel_id=1, source_target_pairs={{0,2},{4,6},{8,10},{12,14},{16,18},{20,22},{24,26},{28,30},{32,34}... | collective-permute-start | bytes 1572872 | tf_op jit(solution)/shard_map/ppermute | solution.py:390
  51.1 7.7 %collective-permute-done.14.got_ref = f32[288,512]{1,0:T(8,128)S(1)} collective-permute-done((f32[288,512]{1,0:T(8,128)S(1)}, f32[288,512]{1,0:T(8,128)S(1)}, u32[]{:S(2)}, u32[]{:S(2)}) %collective-permute-start.14) | collective-permute-done | bytes 589856 | tf_op jit(solution)/shard_map/ppermute | solution.py:393
  58.8 0.1 join.4.own_ref
  58.9 1.6 %collective-permute-done.15.refs_2_ = f32[256,512]{1,0:T(8,128)S(1)} collective-permute-done((f32[256,512]{1,0:T(8,128)S(1)}, f32[256,512]{1,0:T(8,128)S(1)}, u32[]{:S(2)}, u32[]{:S(2)}) %collective-permute-start.15) | collective-permute-done | bytes 524320 | tf_op jit(solution)/shard_map/ppermute | solution.py:390
  60.5 0.0 collective-permute-start.16
  60.5 0.8 collective-permute-start.17
  61.3 1.9 %collective-permute-start.18 = (f32[256,512]{1,0:T(8,128)S(1)}, f32[256,512]{1,0:T(8,128)S(1)}, u32[]{:S(2)}, u32[]{:S(2)}) collective-permute-start(f32[256,512]{1,0:T(8,128)S(1)} %get-tuple-element.108), channel_id=1, source_target_pairs={{0,3},{1,0},{2,1},{3,2},{4,7},{5,4},{6,5},{7,6},{8,11},{9,8},{10,9... | collective-permute-start | bytes 1572872 | tf_op jit(solution)/shard_map/ppermute | solution.py:397
  63.2 10.4 %collective-permute-done.16.got_ref = f32[416,512]{1,0:T(8,128)S(1)} collective-permute-done((f32[416,512]{1,0:T(8,128)S(1)}, f32[416,512]{1,0:T(8,128)S(1)}, u32[]{:S(2)}, u32[]{:S(2)}) %collective-permute-start.16) | collective-permute-done | bytes 852000 | tf_op jit(solution)/shard_map/ppermute | solution.py:395
  73.5 0.1 join.5
  73.6 0.0 collective-permute-done.17.refs_2_
  73.6 0.0 collective-permute-done.18.refs_4_
  73.7 5.5 %collective-permute-start.20 = (f32[160,512]{1,0:T(8,128)S(1)}, f32[160,512]{1,0:T(8,128)S(1)}, u32[]{:S(2)}, u32[]{:S(2)}) collective-permute-start(f32[160,512]{1,0:T(8,128)S(1)} %get-tuple-element.110.own_ref), channel_id=1, source_target_pairs={{0,4},{4,0},{8,12},{12,8},{16,20},{20,16},{24,28},{28,24},{32,36},... | collective-permute-start | bytes 983048 | tf_op jit(solution)/shard_map/ppermute | solution.py:399
  79.2 3.7 %collective-permute-start.21 = (f32[256,512]{1,0:T(8,128)S(1)}, f32[256,512]{1,0:T(8,128)S(1)}, u32[]{:S(2)}, u32[]{:S(2)}) collective-permute-start(f32[256,512]{1,0:T(8,128)S(1)} %get-tuple-element.116), channel_id=1, source_target_pairs={{0,2},{1,3},{2,0},{3,1},{4,6},{5,7},{6,4},{7,5},{8,10},{9,11},{10,... | collective-permute-start | bytes 1572872 | tf_op jit(solution)/shard_map/ppermute | solution.py:401
  82.9 1.8 %collective-permute-start.19 = (f32[512,512]{1,0:T(8,128)S(1)}, f32[512,512]{1,0:T(8,128)S(1)}, u32[]{:S(2)}, u32[]{:S(2)}) collective-permute-start(f32[512,512]{1,0:T(8,128)S(1)} %get-tuple-element.128.refs_5_), channel_id=1, source_target_pairs={{0,8},{4,36},{8,0},{12,44},{16,24},{20,52},{24,16},{28,60},{32,40}... | collective-permute-start | bytes 3145736 | tf_op jit(solution)/shard_map/ppermute | solution.py:400
  84.7 0.0 collective-permute-done.20.other_ref
  84.7 18.2 %factor.1 = (f32[256,256]{1,0:T(8,128)S(1)}, f32[256,256]{1,0:T(8,128)S(1)}, f32[256,256]{1,0:T(8,128)S(1)}) custom-call(f32[160,512]{1,0:T(8,128)S(1)} %get-tuple-element.110.own_ref, f32[160,512]{1,0:T(8,128)S(1)} %collective-permute-done.20.other_ref), custom_call_target="tpu_custom_call" | custom-call | flops 21474836480 | bytes 1048576 | tf_op jit(solution)/shard_map/factor/pallas_call | solution.py:106
  102.9 0.0 copy-start.1
  102.9 0.0 collective-permute-done.21.refs_3_
  102.9 0.0 collective-permute-done.19.refs_6_
  102.9 0.1 collective-permute-start.22
  103.0 0.5 collective-permute-start.23
  103.5 2.9 %weigh.1 = (f32[256,512]{1,0:T(8,128)}, f32[256,512]{1,0:T(8,128)S(1)}) custom-call(f32[256,512]{1,0:T(8,128)S(1)} %slice.3.lead_ref.refs_0_, f32[256,512]{1,0:T(8,128)S(1)} %collective-permute-done.12.refs_1_, f32[256,512]{1,0:T(8,128)S(1)} %collective-permute-done.15.refs_2_, f32[256,512]{1,0:T(8,128)S(1)} %collective-permute-done.13.refs_3_, ...), custom_call_target="tpu_custom_call" | custom-call | flops 1024 | bytes 1024 | tf_op jit(solution)/shard_map/weigh/pallas_call | solution.py:282
  106.5 0.0 collective-permute-done.22.refs_7_
  106.5 0.7 collective-permute-done.23.refs_8_
  107.2 8.6 %update.1 = f32[256,2048]{1,0:T(8,128)} custom-call(s32[4,8]{1,0:T(4,128)S(1)} %get-tuple-element.122.plan, f32[256,512]{1,0:T(8,128)S(1)} %get-tuple-element.123.refs_0_, f32[256,512]{1,0:T(8,128)S(1)} %get-tuple-element.124.refs_1_, f32[256,512]{1,0:T(8,128)S(1)} %collective-permute-done.17.refs_2_, f32[256,512]{1,0:T(8,128)S(1)} %collective-permute-done.21.refs_3_, ...), custom_call_target="tpu_custom_call" | custom-call | tf_op jit(solution)/shard_map/update/pallas_call | solution.py:330
  (3 shorter events, 0.0 us)
Async XLA Ops:
  0.6 23.5 %copy-start.2 = (s32[32]{0:T(128)S(1)}, s32[32]{0:T(128)}, u32[]{:S(2)}) copy-start(s32[32]{0:T(128)} %map_ref.3) | copy-start | bytes 388
  1.7 8.9 %collective-permute-start.3 = (f32[256,512]{1,0:T(8,128)S(1)}, f32[256,512]{1,0:T(8,128)S(1)}, u32[]{:S(2)}, u32[]{:S(2)}) collective-permute-start(f32[256,512]{1,0:T(8,128)S(1)} %slice.3.lead_ref.refs_0_), channel_id=1, source_target_pairs={{0,4},{4,0},{8,12},{12,8},{16,20},{20,16},{24,28},{28,24},{32,36},... | collective-permute-start | bytes 1572872 | tf_op jit(solution)/shard_map/ppermute | solution.py:371
  3.3 21.8 %collective-permute-start.2 = (f32[160,512]{1,0:T(8,128)S(1)}, f32[160,512]{1,0:T(8,128)S(1)}, u32[]{:S(2)}, u32[]{:S(2)}) collective-permute-start(f32[160,512]{1,0:T(8,128)S(1)} %corner.1), channel_id=1, source_target_pairs={{0,3},{4,7}} | collective-permute-start | bytes 983048 | tf_op jit(solution)/shard_map/ppermute | solution.py:369
  8.0 17.1 %collective-permute-start.1 = (f32[160,512]{1,0:T(8,128)S(1)}, f32[160,512]{1,0:T(8,128)S(1)}, u32[]{:S(2)}, u32[]{:S(2)}) collective-permute-start(f32[160,512]{1,0:T(8,128)S(1)} %corner.1), channel_id=1, source_target_pairs={{0,2},{4,6}} | collective-permute-start | bytes 983048 | tf_op jit(solution)/shard_map/ppermute | solution.py:369
  9.3 15.8 %collective-permute-start = (f32[160,512]{1,0:T(8,128)S(1)}, f32[160,512]{1,0:T(8,128)S(1)}, u32[]{:S(2)}, u32[]{:S(2)}) collective-permute-start(f32[160,512]{1,0:T(8,128)S(1)} %corner.1), channel_id=1, source_target_pairs={{0,1},{4,5}} | collective-permute-start | bytes 983048 | tf_op jit(solution)/shard_map/ppermute | solution.py:369
  10.8 29.7 %copy-start = (f32[256,2048]{1,0:T(8,128)S(1)}, f32[256,2048]{1,0:T(8,128)}, u32[]{:S(2)}) copy-start(f32[256,2048]{1,0:T(8,128)} %front_ref.1) | copy-start | bytes 6291460
  10.8 9.2 %collective-permute-start.4 = (f32[2,32,512]{2,1,0:T(8,128)S(1)}, f32[2,32,512]{2,1,0:T(8,128)S(1)}, u32[]{:S(2)}, u32[]{:S(2)}) collective-permute-start(f32[2,32,512]{2,1,0:T(8,128)S(1)} %get-tuple-element.67), channel_id=1, source_target_pairs={{0,8},{4,12},{8,16},{12,20},{16,24},{20,28},{24,0},{28,4},{32,40},... | collective-permute-start | bytes 393224 | tf_op jit(solution)/shard_map/ppermute | solution.py:375
  10.9 9.1 %collective-permute-start.5 = (f32[2,32,512]{2,1,0:T(8,128)S(1)}, f32[2,32,512]{2,1,0:T(8,128)S(1)}, u32[]{:S(2)}, u32[]{:S(2)}) collective-permute-start(f32[2,32,512]{2,1,0:T(8,128)S(1)} %get-tuple-element.68), channel_id=1, source_target_pairs={{0,16},{4,20},{8,24},{12,28},{16,0},{20,4},{24,8},{28,12},{32,48},... | collective-permute-start | bytes 393224 | tf_op jit(solution)/shard_map/ppermute | solution.py:375
  19.9 4.2 %collective-permute-start.6 = (f32[2,32,512]{2,1,0:T(8,128)S(1)}, f32[2,32,512]{2,1,0:T(8,128)S(1)}, u32[]{:S(2)}, u32[]{:S(2)}) collective-permute-start(f32[2,32,512]{2,1,0:T(8,128)S(1)} %get-tuple-element.69), channel_id=1, source_target_pairs={{0,24},{4,28},{8,0},{12,4},{16,8},{20,12},{24,16},{28,20},{32,56},... | collective-permute-start | bytes 393224 | tf_op jit(solution)/shard_map/ppermute | solution.py:375
  25.3 8.6 %collective-permute-start.7 = (f32[160,512]{1,0:T(8,128)S(1)}, f32[160,512]{1,0:T(8,128)S(1)}, u32[]{:S(2)}, u32[]{:S(2)}) collective-permute-start(f32[160,512]{1,0:T(8,128)S(1)} %add_add_fusion.refs_4_), channel_id=1, source_target_pairs={{0,8},{4,36},{1,9},{5,37},{2,10},{6,38},{3,11},{7,39}} | collective-permute-start | bytes 983048 | tf_op jit(solution)/shard_map/ppermute | solution.py:383
  26.6 5.0 %collective-permute-start.8 = (f32[2,32,512]{2,1,0:T(8,128)S(1)}, f32[2,32,512]{2,1,0:T(8,128)S(1)}, u32[]{:S(2)}, u32[]{:S(2)}) collective-permute-start(f32[2,32,512]{2,1,0:T(8,128)S(1)} %get-tuple-element.79), channel_id=1, source_target_pairs={{0,1},{4,5},{8,9},{12,13},{16,17},{20,21},{24,25},{28,29},{32,33},... | collective-permute-start | bytes 393224 | tf_op jit(solution)/shard_map/ppermute | solution.py:381
  29.0 4.8 %collective-permute-start.9 = (f32[2,32,512]{2,1,0:T(8,128)S(1)}, f32[2,32,512]{2,1,0:T(8,128)S(1)}, u32[]{:S(2)}, u32[]{:S(2)}) collective-permute-start(f32[2,32,512]{2,1,0:T(8,128)S(1)} %get-tuple-element.80), channel_id=1, source_target_pairs={{0,2},{4,6},{8,10},{12,14},{16,18},{20,22},{24,26},{28,30},{32,34}... | collective-permute-start | bytes 393224 | tf_op jit(solution)/shard_map/ppermute | solution.py:381
  30.3 3.5 %collective-permute-start.10 = (f32[2,32,512]{2,1,0:T(8,128)S(1)}, f32[2,32,512]{2,1,0:T(8,128)S(1)}, u32[]{:S(2)}, u32[]{:S(2)}) collective-permute-start(f32[2,32,512]{2,1,0:T(8,128)S(1)} %get-tuple-element.81), channel_id=1, source_target_pairs={{0,3},{4,7},{8,11},{12,15},{16,19},{20,23},{24,27},{28,31},{32,35}... | collective-permute-start | bytes 393224 | tf_op jit(solution)/shard_map/ppermute | solution.py:381
  33.9 15.5 %collective-permute-start.13 = (f32[256,512]{1,0:T(8,128)S(1)}, f32[256,512]{1,0:T(8,128)S(1)}, u32[]{:S(2)}, u32[]{:S(2)}) collective-permute-start(f32[256,512]{1,0:T(8,128)S(1)} %slice.3.lead_ref.refs_0_), channel_id=1, source_target_pairs={{0,3},{4,7},{8,11},{12,15},{16,19},{20,23},{24,27},{28,31},{32,35}... | collective-permute-start | bytes 1572872 | tf_op jit(solution)/shard_map/ppermute | solution.py:390
  39.0 10.8 %collective-permute-start.12 = (f32[256,512]{1,0:T(8,128)S(1)}, f32[256,512]{1,0:T(8,128)S(1)}, u32[]{:S(2)}, u32[]{:S(2)}) collective-permute-start(f32[256,512]{1,0:T(8,128)S(1)} %slice.3.lead_ref.refs_0_), channel_id=1, source_target_pairs={{0,1},{4,5},{8,9},{12,13},{16,17},{20,21},{24,25},{28,29},{32,33},... | collective-permute-start | bytes 1572872 | tf_op jit(solution)/shard_map/ppermute | solution.py:390
  40.3 8.9 %collective-permute-start.11 = (f32[224,512]{1,0:T(8,128)S(1)}, f32[224,512]{1,0:T(8,128)S(1)}, u32[]{:S(2)}, u32[]{:S(2)}) collective-permute-start(f32[224,512]{1,0:T(8,128)S(1)} %merge.1.own_ref), channel_id=1, source_target_pairs={{0,24},{4,100},{8,16},{12,108},{16,8},{20,116},{24,0},{28,124},{32... | collective-permute-start | bytes 1376264 | tf_op jit(solution)/shard_map/ppermute | solution.py:391
  49.8 9.0 %collective-permute-start.14 = (f32[288,512]{1,0:T(8,128)S(1)}, f32[288,512]{1,0:T(8,128)S(1)}, u32[]{:S(2)}, u32[]{:S(2)}) collective-permute-start(f32[288,512]{1,0:T(8,128)S(1)} %join.3.own_ref), channel_id=1, source_target_pairs={{0,32},{4,12},{8,40},{12,4},{16,48},{20,28},{24,56},{28,20},{32,0}... | collective-permute-start | bytes 1769480 | tf_op jit(solution)/shard_map/ppermute | solution.py:393
  49.8 10.7 %collective-permute-start.15 = (f32[256,512]{1,0:T(8,128)S(1)}, f32[256,512]{1,0:T(8,128)S(1)}, u32[]{:S(2)}, u32[]{:S(2)}) collective-permute-start(f32[256,512]{1,0:T(8,128)S(1)} %slice.3.lead_ref.refs_0_), channel_id=1, source_target_pairs={{0,2},{4,6},{8,10},{12,14},{16,18},{20,22},{24,26},{28,30},{32,34}... | collective-permute-start | bytes 1572872 | tf_op jit(solution)/shard_map/ppermute | solution.py:390
  60.5 13.0 %collective-permute-start.16 = (f32[416,512]{1,0:T(8,128)S(1)}, f32[416,512]{1,0:T(8,128)S(1)}, u32[]{:S(2)}, u32[]{:S(2)}) collective-permute-start(f32[416,512]{1,0:T(8,128)S(1)} %join.4.own_ref), channel_id=1, source_target_pairs={{0,96},{4,28},{8,104},{12,20},{16,112},{20,12},{24,120},{28,4},{32... | collective-permute-start | bytes 2555912 | tf_op jit(solution)/shard_map/ppermute | solution.py:395
  60.5 13.2 %collective-permute-start.17 = (f32[256,512]{1,0:T(8,128)S(1)}, f32[256,512]{1,0:T(8,128)S(1)}, u32[]{:S(2)}, u32[]{:S(2)}) collective-permute-start(f32[256,512]{1,0:T(8,128)S(1)} %get-tuple-element.106), channel_id=1, source_target_pairs={{0,1},{1,2},{2,3},{3,0},{4,5},{5,6},{6,7},{7,4},{8,9},{9,10},{10,1... | collective-permute-start | bytes 1572872 | tf_op jit(solution)/shard_map/ppermute | solution.py:397
  61.3 12.4 %collective-permute-start.18 = (f32[256,512]{1,0:T(8,128)S(1)}, f32[256,512]{1,0:T(8,128)S(1)}, u32[]{:S(2)}, u32[]{:S(2)}) collective-permute-start(f32[256,512]{1,0:T(8,128)S(1)} %get-tuple-element.108), channel_id=1, source_target_pairs={{0,3},{1,0},{2,1},{3,2},{4,7},{5,4},{6,5},{7,6},{8,11},{9,8},{10,9... | collective-permute-start | bytes 1572872 | tf_op jit(solution)/shard_map/ppermute | solution.py:397
  73.7 11.0 %collective-permute-start.20 = (f32[160,512]{1,0:T(8,128)S(1)}, f32[160,512]{1,0:T(8,128)S(1)}, u32[]{:S(2)}, u32[]{:S(2)}) collective-permute-start(f32[160,512]{1,0:T(8,128)S(1)} %get-tuple-element.110.own_ref), channel_id=1, source_target_pairs={{0,4},{4,0},{8,12},{12,8},{16,20},{20,16},{24,28},{28,24},{32,36},... | collective-permute-start | bytes 983048 | tf_op jit(solution)/shard_map/ppermute | solution.py:399
  79.2 23.7 %collective-permute-start.21 = (f32[256,512]{1,0:T(8,128)S(1)}, f32[256,512]{1,0:T(8,128)S(1)}, u32[]{:S(2)}, u32[]{:S(2)}) collective-permute-start(f32[256,512]{1,0:T(8,128)S(1)} %get-tuple-element.116), channel_id=1, source_target_pairs={{0,2},{1,3},{2,0},{3,1},{4,6},{5,7},{6,4},{7,5},{8,10},{9,11},{10,... | collective-permute-start | bytes 1572872 | tf_op jit(solution)/shard_map/ppermute | solution.py:401
  82.9 20.0 %collective-permute-start.19 = (f32[512,512]{1,0:T(8,128)S(1)}, f32[512,512]{1,0:T(8,128)S(1)}, u32[]{:S(2)}, u32[]{:S(2)}) collective-permute-start(f32[512,512]{1,0:T(8,128)S(1)} %get-tuple-element.128.refs_5_), channel_id=1, source_target_pairs={{0,8},{4,36},{8,0},{12,44},{16,24},{20,52},{24,16},{28,60},{32,40}... | collective-permute-start | bytes 3145736 | tf_op jit(solution)/shard_map/ppermute | solution.py:400
  102.9 4.3 %copy-start.1 = (f32[256,2048]{1,0:T(8,128)S(1)}, f32[256,2048]{1,0:T(8,128)}, u32[]{:S(2)}) copy-start(f32[256,2048]{1,0:T(8,128)} %refs_9_.1) | copy-start | bytes 6291460
  102.9 3.5 %collective-permute-start.22 = (f32[512,512]{1,0:T(8,128)S(1)}, f32[512,512]{1,0:T(8,128)S(1)}, u32[]{:S(2)}, u32[]{:S(2)}) collective-permute-start(f32[512,512]{1,0:T(8,128)S(1)} %get-tuple-element.128.refs_5_), channel_id=1, source_target_pairs={{0,4},{4,0},{8,12},{12,8},{16,20},{20,16},{24,28},{28,24},{32,36},... | collective-permute-start | bytes 3145736 | tf_op jit(solution)/shard_map/ppermute | solution.py:406
  103.0 4.1 %collective-permute-start.23 = (f32[512,512]{1,0:T(8,128)S(1)}, f32[512,512]{1,0:T(8,128)S(1)}, u32[]{:S(2)}, u32[]{:S(2)}) collective-permute-start(f32[512,512]{1,0:T(8,128)S(1)} %collective-permute-done.19.refs_6_), channel_id=1, source_target_pairs={{0,4},{4,0},{8,12},{12,8},{16,20},{20,16},{24,28},{28,24},{32,36},... | collective-permute-start | bytes 3145736 | tf_op jit(solution)/shard_map/ppermute | solution.py:405

commit v9 on v8

--- a/solution.py
+++ b/solution.py
@@ -1,3 +1,5 @@
+from functools import partial
+
 import jax
 import jax.numpy as jnp
 from jax import lax
@@ -11,6 +13,7 @@
 STEP = 8
 TURN = 2
 BLOCK = 160
+PAD = 40
 LARGE = pl.CostEstimate(flops=20 << 30, bytes_accessed=1 << 20, transcendentals=0)
 SMALL = pl.CostEstimate(flops=1 << 10, bytes_accessed=1 << 10, transcendentals=0)
 HIGHEST = lax.Precision.HIGHEST
@@ -215,14 +218,14 @@
             out_ref[:32] = ref[0]
             out_ref[32:64] = ref[1]
 
-    out_ref[64:] = block_ref[...] + got_ref[...]
-
-
-def join_kernel(own_ref, got_ref, *outs):
-    rows = own_ref.shape[0] - BLOCK
+    out_ref[64 : 64 + BLOCK] = block_ref[...] + got_ref[...]
+    out_ref[64 + BLOCK :] = jnp.zeros((PAD, LEAD), jnp.float32)
+
+
+def join_kernel(rows, own_ref, got_ref, *outs):
     outs[0][:rows] = own_ref[:rows]
     outs[0][rows : 2 * rows] = got_ref[:rows]
-    block = own_ref[rows:] + got_ref[rows:]
+    block = own_ref[rows : rows + BLOCK] + got_ref[rows : rows + BLOCK]
     if len(outs) == 1:
         outs[0][2 * rows :] = block
     else:
@@ -258,11 +261,11 @@
 
 
 def weight_kernel(*refs):
-    rows, inverse = refs[:4], refs[4:7]
-    panel_ref, weight_ref, rows_ref = refs[7:]
+    rows, inverse = refs[:3], refs[3:6]
+    panel_ref, weight_ref, rows_ref = refs[6:]
     for index, ref in enumerate(rows):
 
-        @pl.when(lax.axis_index("col") == index)
+        @pl.when(jnp.minimum(lax.axis_index("col"), 2) == index)
         def _():
             rows_ref[...] = ref[...]
 
@@ -282,7 +285,7 @@
     return pl.pallas_call(
         weight_kernel,
         out_shape=[jax.ShapeDtypeStruct(shape, jnp.float32)] * 2,
-        in_specs=[whole] * 7,
+        in_specs=[whole] * 6,
         out_specs=[whole] * 2,
         scratch_shapes=[pltpu.VMEM(shape, jnp.float32)],
         compiler_params=pltpu.CompilerParams(vmem_limit_bytes=16 << 20),
@@ -371,7 +374,7 @@
     mate = lax.ppermute(lead, "row", swap)
     parts = list(local_call(share_kernel, "share", [part] * 4)(lead, mate))
     for hop in range(1, 4):
-        pairs = [(z * 8 + x * 2 + k, z * 8 + (x + hop) % 4 * 2 + k) for z in range(4) for x in range(4) for k in range(2)]
+        pairs = [(i, i // 8 * 8 + (i + 2 * hop) % 8) for i in range(2, 32)]
         parts[hop] = lax.ppermute(parts[hop], "row", pairs)
     parts = list(local_call(sort_kernel, "sort", [part] * 4, 1)(tile_map, *parts))
     blocks, parts = lax.optimization_barrier((blocks, parts))
@@ -382,17 +385,20 @@
     block = (blocks[0] + blocks[1]) + (blocks[2] + blocks[3])
     got = lax.ppermute(block, "row", spread)
     block, got, parts = lax.optimization_barrier((block, got, parts))
-    load = local_call(merge_kernel, "merge", [(64 + BLOCK, LEAD)])(*parts, block, got)[0]
+    load = local_call(merge_kernel, "merge", [(64 + BLOCK + PAD, LEAD)])(*parts, block, got)[0]
 
     *pieces, plan = local_call(pick_kernel, "pick", [(height, 2 * PW)] * 4, 1, [(4, 8)])(tile_map, front)
 
     load, lead = lax.optimization_barrier((load, lead))
-    copies = [lax.ppermute(lead, "col", [(0, to)]) for to in (1, 2, 3)]
-    load = local_call(join_kernel, "join", [(128 + BLOCK, LEAD)])(load, lax.ppermute(load, "row", every[1]))[0]
-    load, copies[0], copies[2], *pieces = lax.optimization_barrier((load, copies[0], copies[2], *pieces))
-    load = local_call(join_kernel, "join", [(256 + BLOCK, LEAD)])(load, lax.ppermute(load, "row", every[2]))[0]
-    load, copies[1], *pieces = lax.optimization_barrier((load, copies[1], *pieces))
-    gathered, block = local_call(join_kernel, "join", [(512, LEAD), (BLOCK, LEAD)])(load, lax.ppermute(load, "row", every[3]))
+    near = lax.ppermute(lead, "col", [(0, 1)])
+    load = local_call(partial(join_kernel, 64), "join", [(128 + BLOCK, LEAD)])(load, lax.ppermute(load, "row", every[1]))[0]
+    load, near, *pieces = lax.optimization_barrier((load, near, *pieces))
+    far = lax.ppermute(jnp.where(lax.axis_index("col") == 1, near, lead), "col", [(0, 3), (1, 2)])
+    load = local_call(partial(join_kernel, 128), "join", [(256 + BLOCK, LEAD)])(load, lax.ppermute(load, "row", every[2]))[0]
+    load, far, *pieces = lax.optimization_barrier((load, far, *pieces))
+    gathered, block = local_call(partial(join_kernel, 256), "join", [(512, LEAD), (BLOCK, LEAD)])(
+        load, lax.ppermute(load, "row", every[3])
+    )
     for hop in (1, 3):
         pieces[hop] = lax.ppermute(pieces[hop], "col", ring[hop])
     block, gathered, *pieces = lax.optimization_barrier((block, gathered, *pieces))
@@ -404,7 +410,7 @@
     late, gathered, inverse, pieces = lax.optimization_barrier((late, gathered, inverse, pieces))
     other_late = lax.ppermute(late, "row", swap)
     other_gathered = lax.ppermute(gathered, "row", swap)
-    panel, weight = weigh([lead, *copies], inverse)
+    panel, weight = weigh([lead, near, far], inverse)
     updated = update(plan, weight, pieces, [gathered, late, other_gathered, other_late], ancestor)
     return panel, updated
 

time: 116 us -> 114 us (0.983)
  waiting for transfers between devices: 43 us -> 36.4 us
  starting transfers between devices: 37.5 us -> 39.4 us
  local copies, waits for them, and re-layouts: 1.1 us -> 2.69 us
    ppermute x1, waiting for transfers between devices: 7.71 us -> 3.78 us  [shards(): lax.ppermute(load, 'row', every[2])]
    ppermute x3, starting transfers between devices: 0.16 us -> 4 us  [shards(): parts[hop] = lax.ppermute(parts[hop], 'row', pairs)]
    ppermute x1, waiting for transfers between devices: 6.8 us -> 4.76 us  [shards(): lax.ppermute(load, 'row', every[1])]
    unnamed x6 -> x14, local copies, waits for them, and re-layouts: 0.02 us -> 1.61 us
    ppermute x3 -> x2, starting transfers between devices: 7.76 us -> 6.46 us  [the longest x1 5.14 us: shards(): lax.ppermute(jnp.where(lax.axis_index('col') == 1, near, lead), 'col', [(...]
    ppermute x1, starting transfers between devices: 5.52 us -> 6.72 us  [shards(): other = lax.ppermute(block, 'row', swap)]
    ppermute x3 -> x2, waiting for transfers between devices: 2.05 us -> 3.11 us  [the longest x1 3.1 us: shards(): lax.ppermute(jnp.where(lax.axis_index('col') == 1, near, lead), 'col', [(...]
  transfers between devices with their start and end apart: 24 -> 23, of which waited for: 9 -> 9; matrix products, arithmetic and copies ran while one was open for 0% -> 0% of each run, Pallas kernels for 21% -> 22%
where the time goes in v9:
time: 114 us; the launch traced here: 113 us
  starting transfers between devices  39.4 us (35%)
  waiting for transfers between devices  36.4 us (32%)
  Pallas kernels  33.1 us (29%)
  local copies, waits for them, and re-layouts  2.69 us (2%)
    pallas_call x9, Pallas kernels, call(): pl.pallas_call(kernel, out_shape=[jax.ShapeDtypeStruct(shape, jnp.float32...  21.6 us
    ppermute x3, waiting for transfers between devices, shards(): parts[hop] = lax.ppermute(parts[hop], 'row', pairs)  12.5 us
    ppermute x1, waiting for transfers between devices, shards(): lax.ppermute(load, 'row', every[3])  9.54 us
    pallas_call x1, Pallas kernels, update(): pl.pallas_call(update_kernel, out_shape=jax.ShapeDtypeStruct(base.shape,...  8.58 us
    ppermute x3, starting transfers between devices, shards(): lax.ppermute(blocks[0], ('row', 'col'), [(4 * core, 4 * core + to) for co...  7.34 us
    ppermute x1, starting transfers between devices, shards(): other = lax.ppermute(block, 'row', swap)  6.72 us
    ppermute x1, starting transfers between devices, shards(): lax.ppermute(jnp.where(lax.axis_index('col') == 1, near, lead), 'col', [(...  5.14 us
    ppermute x1, waiting for transfers between devices, shards(): lax.ppermute(load, 'row', every[1])  4.76 us
  transfers between devices with their start and end apart: 23, of which 9 were waited for; matrix products, arithmetic and copies ran while one was open for 0% of the time, Pallas kernels for 22%

profile of v9, /device:TPU:1, one launch (start us, length us, event | category | flops | bytes accessed | tf_op | source)
XLA Modules:
  0.0 112.9 jit_solution(4398187293439404042)
XLA Ops:
  0.6 1.1 slice.3.lead_ref.refs_0_
  1.7 1.5 %collective-permute-start.3 = (f32[256,512]{1,0:T(8,128)S(1)}, f32[256,512]{1,0:T(8,128)S(1)}, u32[]{:S(2)}, u32[]{:S(2)}) collective-permute-start(f32[256,512]{1,0:T(8,128)S(1)} %slice.3.lead_ref.refs_0_), channel_id=1, source_target_pairs={{0,4},{4,0},{8,12},{12,8},{16,20},{20,16},{24,28},{28,24},{32,36},... | collective-permute-start | bytes 1572872 | tf_op jit(solution)/shard_map/ppermute | solution.py:374
  3.2 0.1 corner.1
  3.3 4.7 %collective-permute-start.2 = (f32[160,512]{1,0:T(8,128)S(1)}, f32[160,512]{1,0:T(8,128)S(1)}, u32[]{:S(2)}, u32[]{:S(2)}) collective-permute-start(f32[160,512]{1,0:T(8,128)S(1)} %corner.1), channel_id=1, source_target_pairs={{0,3},{4,7}} | collective-permute-start | bytes 983048 | tf_op jit(solution)/shard_map/ppermute | solution.py:372
  8.0 1.3 %collective-permute-start.1 = (f32[160,512]{1,0:T(8,128)S(1)}, f32[160,512]{1,0:T(8,128)S(1)}, u32[]{:S(2)}, u32[]{:S(2)}) collective-permute-start(f32[160,512]{1,0:T(8,128)S(1)} %corner.1), channel_id=1, source_target_pairs={{0,2},{4,6}} | collective-permute-start | bytes 983048 | tf_op jit(solution)/shard_map/ppermute | solution.py:372
  9.3 1.3 %collective-permute-start = (f32[160,512]{1,0:T(8,128)S(1)}, f32[160,512]{1,0:T(8,128)S(1)}, u32[]{:S(2)}, u32[]{:S(2)}) collective-permute-start(f32[160,512]{1,0:T(8,128)S(1)} %corner.1), channel_id=1, source_target_pairs={{0,1},{4,5}} | collective-permute-start | bytes 983048 | tf_op jit(solution)/shard_map/ppermute | solution.py:372
  10.6 0.0 collective-permute-done.3.mate_ref
  10.7 0.1 share.1
  10.8 0.0 copy-start
  10.8 1.4 %collective-permute-start.4 = (f32[2,32,512]{2,1,0:T(8,128)S(1)}, f32[2,32,512]{2,1,0:T(8,128)S(1)}, u32[]{:S(2)}, u32[]{:S(2)}) collective-permute-start(f32[2,32,512]{2,1,0:T(8,128)S(1)} %get-tuple-element.66), channel_id=1, source_target_pairs={{8,16},{12,20},{16,24},{20,28},{24,0},{28,4},{32,40},{36,44},{40,4... | collective-permute-start | bytes 393224 | tf_op jit(solution)/shard_map/ppermute | solution.py:378
  12.2 1.3 %collective-permute-start.5 = (f32[2,32,512]{2,1,0:T(8,128)S(1)}, f32[2,32,512]{2,1,0:T(8,128)S(1)}, u32[]{:S(2)}, u32[]{:S(2)}) collective-permute-start(f32[2,32,512]{2,1,0:T(8,128)S(1)} %get-tuple-element.67), channel_id=1, source_target_pairs={{8,24},{12,28},{16,0},{20,4},{24,8},{28,12},{32,48},{36,52},{40,56... | collective-permute-start | bytes 393224 | tf_op jit(solution)/shard_map/ppermute | solution.py:378
  13.5 8.1 %collective-permute-done.4.refs_1_ = f32[2,32,512]{2,1,0:T(8,128)S(1)} collective-permute-done((f32[2,32,512]{2,1,0:T(8,128)S(1)}, f32[2,32,512]{2,1,0:T(8,128)S(1)}, u32[]{:S(2)}, u32[]{:S(2)}) %collective-permute-start.4) | collective-permute-done | bytes 131104 | tf_op jit(solution)/shard_map/ppermute | solution.py:378
  21.6 1.3 %collective-permute-start.6 = (f32[2,32,512]{2,1,0:T(8,128)S(1)}, f32[2,32,512]{2,1,0:T(8,128)S(1)}, u32[]{:S(2)}, u32[]{:S(2)}) collective-permute-start(f32[2,32,512]{2,1,0:T(8,128)S(1)} %get-tuple-element.68), channel_id=1, source_target_pairs={{8,0},{12,4},{16,8},{20,12},{24,16},{28,20},{32,56},{36,60},{40,32... | collective-permute-start | bytes 393224 | tf_op jit(solution)/shard_map/ppermute | solution.py:378
  22.9 0.0 collective-permute-done.5.refs_2_
  22.9 4.4 %collective-permute-done.6.refs_3_ = f32[2,32,512]{2,1,0:T(8,128)S(1)} collective-permute-done((f32[2,32,512]{2,1,0:T(8,128)S(1)}, f32[2,32,512]{2,1,0:T(8,128)S(1)}, u32[]{:S(2)}, u32[]{:S(2)}) %collective-permute-start.6) | collective-permute-done | bytes 131104 | tf_op jit(solution)/shard_map/ppermute | solution.py:378
  27.3 1.0 sort.1
  28.3 0.0 collective-permute-done.2
  28.3 0.0 collective-permute-done.1
  28.3 0.0 collective-permute-done
  28.3 0.1 add_add_fusion.refs_4_
  28.5 1.3 %collective-permute-start.7 = (f32[160,512]{1,0:T(8,128)S(1)}, f32[160,512]{1,0:T(8,128)S(1)}, u32[]{:S(2)}, u32[]{:S(2)}) collective-permute-start(f32[160,512]{1,0:T(8,128)S(1)} %add_add_fusion.refs_4_), channel_id=1, source_target_pairs={{0,8},{4,36},{1,9},{5,37},{2,10},{6,38},{3,11},{7,39}} | collective-permute-start | bytes 983048 | tf_op jit(solution)/shard_map/ppermute | solution.py:386
  29.8 1.3 %collective-permute-start.8 = (f32[2,32,512]{2,1,0:T(8,128)S(1)}, f32[2,32,512]{2,1,0:T(8,128)S(1)}, u32[]{:S(2)}, u32[]{:S(2)}) collective-permute-start(f32[2,32,512]{2,1,0:T(8,128)S(1)} %get-tuple-element.78), channel_id=1, source_target_pairs={{0,1},{4,5},{8,9},{12,13},{16,17},{20,21},{24,25},{28,29},{32,33},... | collective-permute-start | bytes 393224 | tf_op jit(solution)/shard_map/ppermute | solution.py:384
  31.1 1.3 %collective-permute-start.9 = (f32[2,32,512]{2,1,0:T(8,128)S(1)}, f32[2,32,512]{2,1,0:T(8,128)S(1)}, u32[]{:S(2)}, u32[]{:S(2)}) collective-permute-start(f32[2,32,512]{2,1,0:T(8,128)S(1)} %get-tuple-element.79), channel_id=1, source_target_pairs={{0,2},{4,6},{8,10},{12,14},{16,18},{20,22},{24,26},{28,30},{32,34}... | collective-permute-start | bytes 393224 | tf_op jit(solution)/shard_map/ppermute | solution.py:384
  32.4 1.3 %collective-permute-start.10 = (f32[2,32,512]{2,1,0:T(8,128)S(1)}, f32[2,32,512]{2,1,0:T(8,128)S(1)}, u32[]{:S(2)}, u32[]{:S(2)}) collective-permute-start(f32[2,32,512]{2,1,0:T(8,128)S(1)} %get-tuple-element.80), channel_id=1, source_target_pairs={{0,3},{4,7},{8,11},{12,15},{16,19},{20,23},{24,27},{28,31},{32,35}... | collective-permute-start | bytes 393224 | tf_op jit(solution)/shard_map/ppermute | solution.py:384
  33.7 0.0 collective-permute-done.8.refs_1_
  33.7 0.7 collective-permute-done.9.refs_2_
  34.4 1.2 %collective-permute-done.10.refs_3_ = f32[2,32,512]{2,1,0:T(8,128)S(1)} collective-permute-done((f32[2,32,512]{2,1,0:T(8,128)S(1)}, f32[2,32,512]{2,1,0:T(8,128)S(1)}, u32[]{:S(2)}, u32[]{:S(2)}) %collective-permute-start.10) | collective-permute-done | bytes 131104 | tf_op jit(solution)/shard_map/ppermute | solution.py:384
  35.6 0.0 collective-permute-done.7.refs_5_
  35.6 0.1 merge.1.own_ref
  35.7 0.1 collective-permute-start.11
  35.8 1.3 %collective-permute-start.12 = (f32[256,512]{1,0:T(8,128)S(1)}, f32[256,512]{1,0:T(8,128)S(1)}, u32[]{:S(2)}, u32[]{:S(2)}) collective-permute-start(f32[256,512]{1,0:T(8,128)S(1)} %slice.3.lead_ref.refs_0_), channel_id=1, source_target_pairs={{0,1},{4,5},{8,9},{12,13},{16,17},{20,21},{24,25},{28,29},{32,33},... | collective-permute-start | bytes 1572872 | tf_op jit(solution)/shard_map/ppermute | solution.py:393
  37.1 2.0 %pick.1 = (f32[256,512]{1,0:T(8,128)S(1)}, f32[256,512]{1,0:T(8,128)S(1)}, f32[256,512]{1,0:T(8,128)S(1)}, f32[256,512]{1,0:T(8,128)S(1)}, s32[4,8]{1,0:T(4,128)S(1)}) custom-call(s32[32]{0:T(128)S(1)} %copy-done.2, f32[256,2048]{1,0:T(8,128)S(1)} %copy-done), custom_call_target="tpu_custom_call" | custom-call | flops 1024 | bytes 1024 | tf_op jit(solution)/shard_map/pick/pallas_call | solution.py:109
  39.1 0.0 copy-start.3
  39.1 0.8 copy-done.3
  39.9 0.8 copy-done.5
  40.7 4.8 %collective-permute-done.11.got_ref = f32[264,512]{1,0:T(8,128)S(1)} collective-permute-done((f32[264,512]{1,0:T(8,128)S(1)}, f32[264,512]{1,0:T(8,128)S(1)}, u32[]{:S(2)}, u32[]{:S(2)}) %collective-permute-start.11) | collective-permute-done | bytes 540704 | tf_op jit(solution)/shard_map/ppermute | solution.py:394
  45.5 0.1 join.3.own_ref
  45.5 0.0 copy-start.6
  45.5 0.0 copy-start.4
  45.6 0.0 collective-permute-done.12.refs_1_
  45.6 0.1 collective-permute-start.13
  45.7 0.1 broadcast_select_fusion
  45.7 5.1 %collective-permute-start.14 = (f32[256,512]{1,0:T(8,128)S(1)}, f32[256,512]{1,0:T(8,128)S(1)}, u32[]{:S(2)}, u32[]{:S(2)}) collective-permute-start(f32[256,512]{1,0:T(8,128)S(1)} %broadcast_select_fusion), channel_id=1, source_target_pairs={{0,3},{1,2},{4,7},{5,6},{8,11},{9,10},{12,15},{13,14},{16,19},{17,... | collective-permute-start | bytes 1572872 | tf_op jit(solution)/shard_map/ppermute | solution.py:396
  50.9 3.8 %collective-permute-done.13.got_ref = f32[288,512]{1,0:T(8,128)S(1)} collective-permute-done((f32[288,512]{1,0:T(8,128)S(1)}, f32[288,512]{1,0:T(8,128)S(1)}, u32[]{:S(2)}, u32[]{:S(2)}) %collective-permute-start.13) | collective-permute-done | bytes 589856 | tf_op jit(solution)/shard_map/ppermute | solution.py:397
  54.7 0.1 join.4.own_ref
  54.7 3.1 %collective-permute-done.14.refs_2_ = f32[256,512]{1,0:T(8,128)S(1)} collective-permute-done((f32[256,512]{1,0:T(8,128)S(1)}, f32[256,512]{1,0:T(8,128)S(1)}, u32[]{:S(2)}, u32[]{:S(2)}) %collective-permute-start.14) | collective-permute-done | bytes 524320 | tf_op jit(solution)/shard_map/ppermute | solution.py:396
  57.8 0.0 collective-permute-start.15
  57.9 0.0 collective-permute-start.16
  57.9 3.5 %collective-permute-start.17 = (f32[256,512]{1,0:T(8,128)S(1)}, f32[256,512]{1,0:T(8,128)S(1)}, u32[]{:S(2)}, u32[]{:S(2)}) collective-permute-start(f32[256,512]{1,0:T(8,128)S(1)} %copy-done.4), channel_id=1, source_target_pairs={{0,3},{1,0},{2,1},{3,2},{4,7},{5,4},{6,5},{7,6},{8,11},{9,8},{10,9... | collective-permute-start | bytes 1572872 | tf_op jit(solution)/shard_map/ppermute | solution.py:403
  61.4 9.5 %collective-permute-done.15.got_ref = f32[416,512]{1,0:T(8,128)S(1)} collective-permute-done((f32[416,512]{1,0:T(8,128)S(1)}, f32[416,512]{1,0:T(8,128)S(1)}, u32[]{:S(2)}, u32[]{:S(2)}) %collective-permute-start.15) | collective-permute-done | bytes 852000 | tf_op jit(solution)/shard_map/ppermute | solution.py:400
  70.9 0.1 join.5
  71.0 0.0 collective-permute-done.16.refs_2_
  71.0 0.0 collective-permute-done.17.refs_4_
  71.0 6.7 %collective-permute-start.19 = (f32[160,512]{1,0:T(8,128)S(1)}, f32[160,512]{1,0:T(8,128)S(1)}, u32[]{:S(2)}, u32[]{:S(2)}) collective-permute-start(f32[160,512]{1,0:T(8,128)S(1)} %get-tuple-element.108.own_ref), channel_id=1, source_target_pairs={{0,4},{4,0},{8,12},{12,8},{16,20},{20,16},{24,28},{28,24},{32,36},... | collective-permute-start | bytes 983048 | tf_op jit(solution)/shard_map/ppermute | solution.py:405
  77.7 2.8 %collective-permute-start.20 = (f32[256,512]{1,0:T(8,128)S(1)}, f32[256,512]{1,0:T(8,128)S(1)}, u32[]{:S(2)}, u32[]{:S(2)}) collective-permute-start(f32[256,512]{1,0:T(8,128)S(1)} %get-tuple-element.114), channel_id=1, source_target_pairs={{0,2},{1,3},{2,0},{3,1},{4,6},{5,7},{6,4},{7,5},{8,10},{9,11},{10,... | collective-permute-start | bytes 1572872 | tf_op jit(solution)/shard_map/ppermute | solution.py:407
  80.5 1.1 collective-permute-start.18
  81.6 0.0 collective-permute-done.19.other_ref
  81.6 18.2 %factor.1 = (f32[256,256]{1,0:T(8,128)S(1)}, f32[256,256]{1,0:T(8,128)S(1)}, f32[256,256]{1,0:T(8,128)S(1)}) custom-call(f32[160,512]{1,0:T(8,128)S(1)} %get-tuple-element.108.own_ref, f32[160,512]{1,0:T(8,128)S(1)} %collective-permute-done.19.other_ref), custom_call_target="tpu_custom_call" | custom-call | flops 21474836480 | bytes 1048576 | tf_op jit(solution)/shard_map/factor/pallas_call | solution.py:109
  99.8 0.0 copy-start.1
  99.9 0.6 collective-permute-start.21
  100.5 0.1 collective-permute-start.22
  100.6 2.9 %weigh.1 = (f32[256,512]{1,0:T(8,128)}, f32[256,512]{1,0:T(8,128)S(1)}) custom-call(f32[256,512]{1,0:T(8,128)S(1)} %slice.3.lead_ref.refs_0_, f32[256,512]{1,0:T(8,128)S(1)} %collective-permute-done.12.refs_1_, f32[256,512]{1,0:T(8,128)S(1)} %collective-permute-done.14.refs_2_, f32[256,256]{1,0:T(8,128)S(1)} %get-tuple-element.116.refs_3_, ...), custom_call_target="tpu_custom_call" | custom-call | flops 1024 | bytes 1024 | tf_op jit(solution)/shard_map/weigh/pallas_call | solution.py:285
  103.5 0.7 collective-permute-done.22.refs_8_
  104.3 8.6 %update.1 = f32[256,2048]{1,0:T(8,128)} custom-call(s32[4,8]{1,0:T(4,128)S(1)} %get-tuple-element.120.plan, f32[256,512]{1,0:T(8,128)S(1)} %get-tuple-element.121.refs_0_, f32[256,512]{1,0:T(8,128)S(1)} %get-tuple-element.122.refs_1_, f32[256,512]{1,0:T(8,128)S(1)} %collective-permute-done.16.refs_2_, f32[256,512]{1,0:T(8,128)S(1)} %collective-permute-done.20.refs_3_, ...), custom_call_target="tpu_custom_call" | custom-call | tf_op jit(solution)/shard_map/update/pallas_call | solution.py:333
  (10 shorter events, 0.0 us)
Async XLA Ops:
  0.6 26.7 %copy-start.2 = (s32[32]{0:T(128)S(1)}, s32[32]{0:T(128)}, u32[]{:S(2)}) copy-start(s32[32]{0:T(128)} %map_ref.3) | copy-start | bytes 388
  1.7 8.9 %collective-permute-start.3 = (f32[256,512]{1,0:T(8,128)S(1)}, f32[256,512]{1,0:T(8,128)S(1)}, u32[]{:S(2)}, u32[]{:S(2)}) collective-permute-start(f32[256,512]{1,0:T(8,128)S(1)} %slice.3.lead_ref.refs_0_), channel_id=1, source_target_pairs={{0,4},{4,0},{8,12},{12,8},{16,20},{20,16},{24,28},{28,24},{32,36},... | collective-permute-start | bytes 1572872 | tf_op jit(solution)/shard_map/ppermute | solution.py:374
  3.3 25.0 %collective-permute-start.2 = (f32[160,512]{1,0:T(8,128)S(1)}, f32[160,512]{1,0:T(8,128)S(1)}, u32[]{:S(2)}, u32[]{:S(2)}) collective-permute-start(f32[160,512]{1,0:T(8,128)S(1)} %corner.1), channel_id=1, source_target_pairs={{0,3},{4,7}} | collective-permute-start | bytes 983048 | tf_op jit(solution)/shard_map/ppermute | solution.py:372
  8.0 20.3 %collective-permute-start.1 = (f32[160,512]{1,0:T(8,128)S(1)}, f32[160,512]{1,0:T(8,128)S(1)}, u32[]{:S(2)}, u32[]{:S(2)}) collective-permute-start(f32[160,512]{1,0:T(8,128)S(1)} %corner.1), channel_id=1, source_target_pairs={{0,2},{4,6}} | collective-permute-start | bytes 983048 | tf_op jit(solution)/shard_map/ppermute | solution.py:372
  9.3 19.0 %collective-permute-start = (f32[160,512]{1,0:T(8,128)S(1)}, f32[160,512]{1,0:T(8,128)S(1)}, u32[]{:S(2)}, u32[]{:S(2)}) collective-permute-start(f32[160,512]{1,0:T(8,128)S(1)} %corner.1), channel_id=1, source_target_pairs={{0,1},{4,5}} | collective-permute-start | bytes 983048 | tf_op jit(solution)/shard_map/ppermute | solution.py:372
  10.8 26.3 %copy-start = (f32[256,2048]{1,0:T(8,128)S(1)}, f32[256,2048]{1,0:T(8,128)}, u32[]{:S(2)}) copy-start(f32[256,2048]{1,0:T(8,128)} %front_ref.1) | copy-start | bytes 6291460
  10.8 10.8 %collective-permute-start.4 = (f32[2,32,512]{2,1,0:T(8,128)S(1)}, f32[2,32,512]{2,1,0:T(8,128)S(1)}, u32[]{:S(2)}, u32[]{:S(2)}) collective-permute-start(f32[2,32,512]{2,1,0:T(8,128)S(1)} %get-tuple-element.66), channel_id=1, source_target_pairs={{8,16},{12,20},{16,24},{20,28},{24,0},{28,4},{32,40},{36,44},{40,4... | collective-permute-start | bytes 393224 | tf_op jit(solution)/shard_map/ppermute | solution.py:378
  12.2 10.7 %collective-permute-start.5 = (f32[2,32,512]{2,1,0:T(8,128)S(1)}, f32[2,32,512]{2,1,0:T(8,128)S(1)}, u32[]{:S(2)}, u32[]{:S(2)}) collective-permute-start(f32[2,32,512]{2,1,0:T(8,128)S(1)} %get-tuple-element.67), channel_id=1, source_target_pairs={{8,24},{12,28},{16,0},{20,4},{24,8},{28,12},{32,48},{36,52},{40,56... | collective-permute-start | bytes 393224 | tf_op jit(solution)/shard_map/ppermute | solution.py:378
  21.6 5.7 %collective-permute-start.6 = (f32[2,32,512]{2,1,0:T(8,128)S(1)}, f32[2,32,512]{2,1,0:T(8,128)S(1)}, u32[]{:S(2)}, u32[]{:S(2)}) collective-permute-start(f32[2,32,512]{2,1,0:T(8,128)S(1)} %get-tuple-element.68), channel_id=1, source_target_pairs={{8,0},{12,4},{16,8},{20,12},{24,16},{28,20},{32,56},{36,60},{40,32... | collective-permute-start | bytes 393224 | tf_op jit(solution)/shard_map/ppermute | solution.py:378
  28.5 7.2 %collective-permute-start.7 = (f32[160,512]{1,0:T(8,128)S(1)}, f32[160,512]{1,0:T(8,128)S(1)}, u32[]{:S(2)}, u32[]{:S(2)}) collective-permute-start(f32[160,512]{1,0:T(8,128)S(1)} %add_add_fusion.refs_4_), channel_id=1, source_target_pairs={{0,8},{4,36},{1,9},{5,37},{2,10},{6,38},{3,11},{7,39}} | collective-permute-start | bytes 983048 | tf_op jit(solution)/shard_map/ppermute | solution.py:386
  29.8 3.9 %collective-permute-start.8 = (f32[2,32,512]{2,1,0:T(8,128)S(1)}, f32[2,32,512]{2,1,0:T(8,128)S(1)}, u32[]{:S(2)}, u32[]{:S(2)}) collective-permute-start(f32[2,32,512]{2,1,0:T(8,128)S(1)} %get-tuple-element.78), channel_id=1, source_target_pairs={{0,1},{4,5},{8,9},{12,13},{16,17},{20,21},{24,25},{28,29},{32,33},... | collective-permute-start | bytes 393224 | tf_op jit(solution)/shard_map/ppermute | solution.py:384
  31.1 3.3 %collective-permute-start.9 = (f32[2,32,512]{2,1,0:T(8,128)S(1)}, f32[2,32,512]{2,1,0:T(8,128)S(1)}, u32[]{:S(2)}, u32[]{:S(2)}) collective-permute-start(f32[2,32,512]{2,1,0:T(8,128)S(1)} %get-tuple-element.79), channel_id=1, source_target_pairs={{0,2},{4,6},{8,10},{12,14},{16,18},{20,22},{24,26},{28,30},{32,34}... | collective-permute-start | bytes 393224 | tf_op jit(solution)/shard_map/ppermute | solution.py:384
  32.4 3.2 %collective-permute-start.10 = (f32[2,32,512]{2,1,0:T(8,128)S(1)}, f32[2,32,512]{2,1,0:T(8,128)S(1)}, u32[]{:S(2)}, u32[]{:S(2)}) collective-permute-start(f32[2,32,512]{2,1,0:T(8,128)S(1)} %get-tuple-element.80), channel_id=1, source_target_pairs={{0,3},{4,7},{8,11},{12,15},{16,19},{20,23},{24,27},{28,31},{32,35}... | collective-permute-start | bytes 393224 | tf_op jit(solution)/shard_map/ppermute | solution.py:384
  35.7 9.8 %collective-permute-start.11 = (f32[264,512]{1,0:T(8,128)S(1)}, f32[264,512]{1,0:T(8,128)S(1)}, u32[]{:S(2)}, u32[]{:S(2)}) collective-permute-start(f32[264,512]{1,0:T(8,128)S(1)} %merge.1.own_ref), channel_id=1, source_target_pairs={{0,24},{4,100},{8,16},{12,108},{16,8},{20,116},{24,0},{28,124},{32... | collective-permute-start | bytes 1622024 | tf_op jit(solution)/shard_map/ppermute | solution.py:394
  35.8 9.8 %collective-permute-start.12 = (f32[256,512]{1,0:T(8,128)S(1)}, f32[256,512]{1,0:T(8,128)S(1)}, u32[]{:S(2)}, u32[]{:S(2)}) collective-permute-start(f32[256,512]{1,0:T(8,128)S(1)} %slice.3.lead_ref.refs_0_), channel_id=1, source_target_pairs={{0,1},{4,5},{8,9},{12,13},{16,17},{20,21},{24,25},{28,29},{32,33},... | collective-permute-start | bytes 1572872 | tf_op jit(solution)/shard_map/ppermute | solution.py:393
  39.1 0.8 copy-start.3
  39.9 0.8 copy-start.5
  45.5 12.3 %copy-start.6 = (f32[256,512]{1,0:T(8,128)S(1)}, f32[256,512]{1,0:T(8,128)}, u32[]{:S(2)}) copy-start(f32[256,512]{1,0:T(8,128)} %copy-done.5) | copy-start | bytes 1572868
  45.5 12.3 %copy-start.4 = (f32[256,512]{1,0:T(8,128)S(1)}, f32[256,512]{1,0:T(8,128)}, u32[]{:S(2)}) copy-start(f32[256,512]{1,0:T(8,128)} %copy-done.3) | copy-start | bytes 1572868
  45.6 9.1 %collective-permute-start.13 = (f32[288,512]{1,0:T(8,128)S(1)}, f32[288,512]{1,0:T(8,128)S(1)}, u32[]{:S(2)}, u32[]{:S(2)}) collective-permute-start(f32[288,512]{1,0:T(8,128)S(1)} %join.3.own_ref), channel_id=1, source_target_pairs={{0,32},{4,12},{8,40},{12,4},{16,48},{20,28},{24,56},{28,20},{32,0}... | collective-permute-start | bytes 1769480 | tf_op jit(solution)/shard_map/ppermute | solution.py:397
  45.7 12.1 %collective-permute-start.14 = (f32[256,512]{1,0:T(8,128)S(1)}, f32[256,512]{1,0:T(8,128)S(1)}, u32[]{:S(2)}, u32[]{:S(2)}) collective-permute-start(f32[256,512]{1,0:T(8,128)S(1)} %broadcast_select_fusion), channel_id=1, source_target_pairs={{0,3},{1,2},{4,7},{5,6},{8,11},{9,10},{12,15},{13,14},{16,19},{17,... | collective-permute-start | bytes 1572872 | tf_op jit(solution)/shard_map/ppermute | solution.py:396
  57.8 13.0 %collective-permute-start.15 = (f32[416,512]{1,0:T(8,128)S(1)}, f32[416,512]{1,0:T(8,128)S(1)}, u32[]{:S(2)}, u32[]{:S(2)}) collective-permute-start(f32[416,512]{1,0:T(8,128)S(1)} %join.4.own_ref), channel_id=1, source_target_pairs={{0,96},{4,28},{8,104},{12,20},{16,112},{20,12},{24,120},{28,4},{32... | collective-permute-start | bytes 2555912 | tf_op jit(solution)/shard_map/ppermute | solution.py:400
  57.9 13.2 %collective-permute-start.16 = (f32[256,512]{1,0:T(8,128)S(1)}, f32[256,512]{1,0:T(8,128)S(1)}, u32[]{:S(2)}, u32[]{:S(2)}) collective-permute-start(f32[256,512]{1,0:T(8,128)S(1)} %copy-done.6), channel_id=1, source_target_pairs={{0,1},{1,2},{2,3},{3,0},{4,5},{5,6},{6,7},{7,4},{8,9},{9,10},{10,1... | collective-permute-start | bytes 1572872 | tf_op jit(solution)/shard_map/ppermute | solution.py:403
  57.9 13.1 %collective-permute-start.17 = (f32[256,512]{1,0:T(8,128)S(1)}, f32[256,512]{1,0:T(8,128)S(1)}, u32[]{:S(2)}, u32[]{:S(2)}) collective-permute-start(f32[256,512]{1,0:T(8,128)S(1)} %copy-done.4), channel_id=1, source_target_pairs={{0,3},{1,0},{2,1},{3,2},{4,7},{5,4},{6,5},{7,6},{8,11},{9,8},{10,9... | collective-permute-start | bytes 1572872 | tf_op jit(solution)/shard_map/ppermute | solution.py:403
  71.0 10.6 %collective-permute-start.19 = (f32[160,512]{1,0:T(8,128)S(1)}, f32[160,512]{1,0:T(8,128)S(1)}, u32[]{:S(2)}, u32[]{:S(2)}) collective-permute-start(f32[160,512]{1,0:T(8,128)S(1)} %get-tuple-element.108.own_ref), channel_id=1, source_target_pairs={{0,4},{4,0},{8,12},{12,8},{16,20},{20,16},{24,28},{28,24},{32,36},... | collective-permute-start | bytes 983048 | tf_op jit(solution)/shard_map/ppermute | solution.py:405
  77.7 22.1 %collective-permute-start.20 = (f32[256,512]{1,0:T(8,128)S(1)}, f32[256,512]{1,0:T(8,128)S(1)}, u32[]{:S(2)}, u32[]{:S(2)}) collective-permute-start(f32[256,512]{1,0:T(8,128)S(1)} %get-tuple-element.114), channel_id=1, source_target_pairs={{0,2},{1,3},{2,0},{3,1},{4,6},{5,7},{6,4},{7,5},{8,10},{9,11},{10,... | collective-permute-start | bytes 1572872 | tf_op jit(solution)/shard_map/ppermute | solution.py:407
  80.5 19.4 %collective-permute-start.18 = (f32[512,512]{1,0:T(8,128)S(1)}, f32[512,512]{1,0:T(8,128)S(1)}, u32[]{:S(2)}, u32[]{:S(2)}) collective-permute-start(f32[512,512]{1,0:T(8,128)S(1)} %get-tuple-element.126.refs_5_), channel_id=1, source_target_pairs={{0,8},{4,36},{8,0},{12,44},{16,24},{20,52},{24,16},{28,60},{32,40}... | collective-permute-start | bytes 3145736 | tf_op jit(solution)/shard_map/ppermute | solution.py:406
  99.8 4.4 %copy-start.1 = (f32[256,2048]{1,0:T(8,128)S(1)}, f32[256,2048]{1,0:T(8,128)}, u32[]{:S(2)}) copy-start(f32[256,2048]{1,0:T(8,128)} %refs_9_.1) | copy-start | bytes 6291460
  99.9 3.6 %collective-permute-start.21 = (f32[512,512]{1,0:T(8,128)S(1)}, f32[512,512]{1,0:T(8,128)S(1)}, u32[]{:S(2)}, u32[]{:S(2)}) collective-permute-start(f32[512,512]{1,0:T(8,128)S(1)} %get-tuple-element.126.refs_5_), channel_id=1, source_target_pairs={{0,4},{4,0},{8,12},{12,8},{16,20},{20,16},{24,28},{28,24},{32,36},... | collective-permute-start | bytes 3145736 | tf_op jit(solution)/shard_map/ppermute | solution.py:412
  100.5 3.8 %collective-permute-start.22 = (f32[512,512]{1,0:T(8,128)S(1)}, f32[512,512]{1,0:T(8,128)S(1)}, u32[]{:S(2)}, u32[]{:S(2)}) collective-permute-start(f32[512,512]{1,0:T(8,128)S(1)} %collective-permute-done.18.refs_6_), channel_id=1, source_target_pairs={{0,4},{4,0},{8,12},{12,8},{16,20},{20,16},{24,28},{28,24},{32,36},... | collective-permute-start | bytes 3145736 | tf_op jit(solution)/shard_map/ppermute | solution.py:411

commit v10 on v9

--- a/solution.py
+++ b/solution.py
@@ -13,7 +13,6 @@
 STEP = 8
 TURN = 2
 BLOCK = 160
-PAD = 40
 LARGE = pl.CostEstimate(flops=20 << 30, bytes_accessed=1 << 20, transcendentals=0)
 SMALL = pl.CostEstimate(flops=1 << 10, bytes_accessed=1 << 10, transcendentals=0)
 HIGHEST = lax.Precision.HIGHEST
@@ -210,16 +209,20 @@
 
 
 def merge_kernel(*refs):
-    parts, block_ref, got_ref, out_ref = refs[:4], refs[4], refs[5], refs[6]
+    parts, out_ref = refs[:4], refs[4]
     for index, ref in enumerate(parts):
 
         @pl.when(lax.axis_index("col") == index)
         def _():
             out_ref[:32] = ref[0]
-            out_ref[32:64] = ref[1]
-
-    out_ref[64 : 64 + BLOCK] = block_ref[...] + got_ref[...]
-    out_ref[64 + BLOCK :] = jnp.zeros((PAD, LEAD), jnp.float32)
+            out_ref[32:] = ref[1]
+
+
+def load_kernel(own_ref, got_ref, *refs):
+    blocks, out_ref = refs[:4], refs[4]
+    out_ref[:64] = own_ref[...]
+    out_ref[64:128] = got_ref[...]
+    out_ref[128:] = (blocks[0][...] + blocks[1][...]) + (blocks[2][...] + blocks[3][...])
 
 
 def join_kernel(rows, own_ref, got_ref, *outs):
@@ -306,12 +309,12 @@
             off_z, off_x = plane ^ group, line ^ x
             first = jnp.where(holder == 0, off_x, off_z)
             second = jnp.where(holder == 0, off_z, off_x)
-            index = (first >> 1) + 2 * ((second & 1) ^ (second >> 1)) + 4 * (second >> 1)
+            index = ((first & 1) ^ (first >> 1)) + 2 * ((second & 1) ^ (second >> 1)) + 4 * (second >> 1)
             rows = pl.ds(pl.multiple_of(index * 64 + place * 32, 32), 32)
             into = pl.ds(pl.multiple_of((2 * x + holder) * 32, 32), 32)
             for late in range(2):
 
-                @pl.when(((first & 1) ^ (first >> 1)) == late)
+                @pl.when((first >> 1) == late)
                 def _():
                     ahead_ref[into, :] = gathered[2 * parity + late][rows, :]
 
@@ -349,14 +352,14 @@
     every = []
     for step in range(4):
         flip = 1 if step % 2 == 0 else 3
-        pairs = []
+        pairs = {}
         for z in range(4):
             for x in range(4):
                 for core in range(2):
                     to = (z, x ^ flip) if step // 2 == core else (z ^ flip, x)
-                    pairs.append(((z * 4 + x) * 2 + core, (to[0] * 4 + to[1]) * 2 + core))
+                    pairs[(z * 4 + x) * 2 + core] = (to[0] * 4 + to[1]) * 2 + core
         every.append(pairs)
-    return every, [pair for pair in every[0] if pair[0] < 2]
+    return every
 
 
 def shards(front, ancestor, tile_map):
@@ -367,9 +370,13 @@
 
     ring = [[(i, (i + hop) % 4) for i in range(4)] for hop in range(4)]
 
-    blocks = [local_call(corner_kernel, "corner", [(BLOCK, LEAD)])(lead)[0]]
-    for to in range(1, 4):
-        blocks.append(lax.ppermute(blocks[0], ("row", "col"), [(4 * core, 4 * core + to) for core in range(2)]))
+    steps = doubling_steps()
+    every = [list(step.items()) for step in steps]
+
+    have = [0, 1]
+    block = local_call(corner_kernel, "corner", [(BLOCK, LEAD)])(lead)[0]
+    got = lax.ppermute(block, ("row", "col"), [(4 * i, 4 * steps[0][i]) for i in have])
+    have += [steps[0][i] for i in have]
 
     mate = lax.ppermute(lead, "row", swap)
     parts = list(local_call(share_kernel, "share", [part] * 4)(lead, mate))
@@ -377,34 +384,38 @@
         pairs = [(i, i // 8 * 8 + (i + 2 * hop) % 8) for i in range(2, 32)]
         parts[hop] = lax.ppermute(parts[hop], "row", pairs)
     parts = list(local_call(sort_kernel, "sort", [part] * 4, 1)(tile_map, *parts))
-    blocks, parts = lax.optimization_barrier((blocks, parts))
-
-    every, spread = doubling_steps()
+    block, got, parts = lax.optimization_barrier((block, got, parts))
+
     for to in range(1, 4):
         parts[to] = lax.ppermute(parts[to], "col", [(0, to)])
-    block = (blocks[0] + blocks[1]) + (blocks[2] + blocks[3])
-    got = lax.ppermute(block, "row", spread)
+    block = block + got
+    got = lax.ppermute(block, ("row", "col"), [(4 * i, 4 * steps[1][i]) for i in have])
+    have += [steps[1][i] for i in have]
     block, got, parts = lax.optimization_barrier((block, got, parts))
-    load = local_call(merge_kernel, "merge", [(64 + BLOCK + PAD, LEAD)])(*parts, block, got)[0]
+
+    part = local_call(merge_kernel, "merge", [(64, LEAD)])(*parts)[0]
+    beside = lax.ppermute(part, "row", every[0])
+    blocks = [block + got]
+    for to in range(1, 4):
+        blocks.append(lax.ppermute(blocks[0], ("row", "col"), [(4 * i, 4 * i + to) for i in have]))
 
     *pieces, plan = local_call(pick_kernel, "pick", [(height, 2 * PW)] * 4, 1, [(4, 8)])(tile_map, front)
 
-    load, lead = lax.optimization_barrier((load, lead))
+    load = local_call(load_kernel, "load", [(128 + BLOCK, LEAD)])(part, beside, *blocks)[0]
+    load, lead, *pieces = lax.optimization_barrier((load, lead, *pieces))
     near = lax.ppermute(lead, "col", [(0, 1)])
-    load = local_call(partial(join_kernel, 64), "join", [(128 + BLOCK, LEAD)])(load, lax.ppermute(load, "row", every[1]))[0]
+    pieces[3] = lax.ppermute(pieces[3], "col", ring[3])
+    load = local_call(partial(join_kernel, 128), "join", [(256 + BLOCK, LEAD)])(load, lax.ppermute(load, "row", every[2]))[0]
     load, near, *pieces = lax.optimization_barrier((load, near, *pieces))
     far = lax.ppermute(jnp.where(lax.axis_index("col") == 1, near, lead), "col", [(0, 3), (1, 2)])
-    load = local_call(partial(join_kernel, 128), "join", [(256 + BLOCK, LEAD)])(load, lax.ppermute(load, "row", every[2]))[0]
-    load, far, *pieces = lax.optimization_barrier((load, far, *pieces))
     gathered, block = local_call(partial(join_kernel, 256), "join", [(512, LEAD), (BLOCK, LEAD)])(
         load, lax.ppermute(load, "row", every[3])
     )
-    for hop in (1, 3):
+    block, gathered, far, *pieces = lax.optimization_barrier((block, gathered, far, *pieces))
+    other = lax.ppermute(block, "row", swap)
+    late = lax.ppermute(gathered, "row", every[1])
+    for hop in (1, 2):
         pieces[hop] = lax.ppermute(pieces[hop], "col", ring[hop])
-    block, gathered, *pieces = lax.optimization_barrier((block, gathered, *pieces))
-    other = lax.ppermute(block, "row", swap)
-    late = lax.ppermute(gathered, "row", every[0])
-    pieces[2] = lax.ppermute(pieces[2], "col", ring[2])
 
     inverse = factor(block, other)
     late, gathered, inverse, pieces = lax.optimization_barrier((late, gathered, inverse, pieces))

time: 114 us -> 122 us (1.070)
  waiting for transfers between devices: 36.4 us -> 47.8 us
  starting transfers between devices: 39.4 us -> 37.8 us
    ppermute x7 -> x8, waiting for transfers between devices: 4.78 us -> 13.8 us  [the longest x3 7.86 us: shards(): lax.ppermute(blocks[0], ('row', 'col'), [(4 * i, 4 * i + to) for i in have])]
    ppermute x2, waiting for transfers between devices: 0.01 us -> 5.05 us  [shards(): pieces[hop] = lax.ppermute(pieces[hop], 'col', ring[hop])]
    ppermute x1, starting transfers between devices: 6.72 us -> 3.35 us  [shards(): other = lax.ppermute(block, 'row', swap)]
    ppermute x1, waiting for transfers between devices: 3.1 us -> 0.01 us  [shards(): lax.ppermute(jnp.where(lax.axis_index('col') == 1, near, lead), 'col', [(...]
    ppermute x3, waiting for transfers between devices: 12.5 us -> 9.45 us  [shards(): parts[hop] = lax.ppermute(parts[hop], 'row', pairs)]
    ppermute x1, starting transfers between devices: 1.32 us -> 4.14 us  [shards(): near = lax.ppermute(lead, 'col', [(0, 1)])]
    ppermute x1, starting transfers between devices: 5.14 us -> 2.47 us  [shards(): lax.ppermute(jnp.where(lax.axis_index('col') == 1, near, lead), 'col', [(...]
    ppermute x7 -> x8, starting transfers between devices: 12.6 us -> 15 us  [the longest x3 7.75 us: shards(): lax.ppermute(blocks[0], ('row', 'col'), [(4 * i, 4 * i + to) for i in have])]
  transfers between devices with their start and end apart: 23 -> 24, of which waited for: 9 -> 13; matrix products, arithmetic and copies ran while one was open for 0% -> 0% of each run, Pallas kernels for 22% -> 20%
where the time goes in v10:
time: 122 us
  waiting for transfers between devices  47.8 us (39%)
  starting transfers between devices  37.8 us (31%)
  Pallas kernels  33.2 us (27%)
  local copies, waits for them, and re-layouts  1.92 us (2%)
    pallas_call x9, Pallas kernels, call(): pl.pallas_call(kernel, out_shape=[jax.ShapeDtypeStruct(shape, jnp.float32...  21.7 us
    ppermute x1, waiting for transfers between devices, shards(): lax.ppermute(load, 'row', every[3])  10.5 us
    ppermute x3, waiting for transfers between devices, shards(): parts[hop] = lax.ppermute(parts[hop], 'row', pairs)  9.45 us
    pallas_call x1, Pallas kernels, update(): pl.pallas_call(update_kernel, out_shape=jax.ShapeDtypeStruct(base.shape,...  8.56 us
    ppermute x3, waiting for transfers between devices, shards(): lax.ppermute(blocks[0], ('row', 'col'), [(4 * i, 4 * i + to) for i in have])  7.86 us
    ppermute x3, starting transfers between devices, shards(): lax.ppermute(blocks[0], ('row', 'col'), [(4 * i, 4 * i + to) for i in have])  7.75 us
    ppermute x2, waiting for transfers between devices, shards(): pieces[hop] = lax.ppermute(pieces[hop], 'col', ring[hop])  5.05 us
    ppermute x1, waiting for transfers between devices, shards(): lax.ppermute(load, 'row', every[2])  4.79 us
  transfers between devices with their start and end apart: 24, of which 13 were waited for; matrix products, arithmetic and copies ran while one was open for 0% of the time, Pallas kernels for 20%

profile of v10, /device:TPU:1, one launch (start us, length us, event | category | flops | bytes accessed | tf_op | source)
XLA Modules:
  0.0 121.8 jit_solution(3744014163660777318)
XLA Ops:
  0.6 1.1 slice.3.lead_ref.refs_0_
  1.7 1.5 %collective-permute-start.1 = (f32[256,512]{1,0:T(8,128)S(1)}, f32[256,512]{1,0:T(8,128)S(1)}, u32[]{:S(2)}, u32[]{:S(2)}) collective-permute-start(f32[256,512]{1,0:T(8,128)S(1)} %slice.3.lead_ref.refs_0_), channel_id=1, source_target_pairs={{0,4},{4,0},{8,12},{12,8},{16,20},{20,16},{24,28},{28,24},{32,36},... | collective-permute-start | bytes 1572872 | tf_op jit(solution)/shard_map/ppermute | solution.py:381
  3.2 0.1 corner.1
  3.3 0.0 copy-start
  3.3 3.8 %collective-permute-start = (f32[160,512]{1,0:T(8,128)S(1)}, f32[160,512]{1,0:T(8,128)S(1)}, u32[]{:S(2)}, u32[]{:S(2)}) collective-permute-start(f32[160,512]{1,0:T(8,128)S(1)} %corner.1), channel_id=1, source_target_pairs={{0,8},{4,36}} | collective-permute-start | bytes 983048 | tf_op jit(solution)/shard_map/ppermute | solution.py:378
  7.1 0.0 collective-permute-done.1.mate_ref
  7.1 0.1 share.1
  7.2 1.3 %collective-permute-start.2 = (f32[2,32,512]{2,1,0:T(8,128)S(1)}, f32[2,32,512]{2,1,0:T(8,128)S(1)}, u32[]{:S(2)}, u32[]{:S(2)}) collective-permute-start(f32[2,32,512]{2,1,0:T(8,128)S(1)} %get-tuple-element.63), channel_id=1, source_target_pairs={{8,16},{12,20},{16,24},{20,28},{24,0},{28,4},{32,40},{36,44},{40,4... | collective-permute-start | bytes 393224 | tf_op jit(solution)/shard_map/ppermute | solution.py:385
  8.5 1.3 %collective-permute-start.3 = (f32[2,32,512]{2,1,0:T(8,128)S(1)}, f32[2,32,512]{2,1,0:T(8,128)S(1)}, u32[]{:S(2)}, u32[]{:S(2)}) collective-permute-start(f32[2,32,512]{2,1,0:T(8,128)S(1)} %get-tuple-element.64), channel_id=1, source_target_pairs={{8,24},{12,28},{16,0},{20,4},{24,8},{28,12},{32,48},{36,52},{40,56... | collective-permute-start | bytes 393224 | tf_op jit(solution)/shard_map/ppermute | solution.py:385
  9.8 1.3 %collective-permute-start.4 = (f32[2,32,512]{2,1,0:T(8,128)S(1)}, f32[2,32,512]{2,1,0:T(8,128)S(1)}, u32[]{:S(2)}, u32[]{:S(2)}) collective-permute-start(f32[2,32,512]{2,1,0:T(8,128)S(1)} %get-tuple-element.65), channel_id=1, source_target_pairs={{8,0},{12,4},{16,8},{20,12},{24,16},{28,20},{32,56},{36,60},{40,32... | collective-permute-start | bytes 393224 | tf_op jit(solution)/shard_map/ppermute | solution.py:385
  11.1 7.3 %collective-permute-done.2.refs_1_ = f32[2,32,512]{2,1,0:T(8,128)S(1)} collective-permute-done((f32[2,32,512]{2,1,0:T(8,128)S(1)}, f32[2,32,512]{2,1,0:T(8,128)S(1)}, u32[]{:S(2)}, u32[]{:S(2)}) %collective-permute-start.2) | collective-permute-done | bytes 131104 | tf_op jit(solution)/shard_map/ppermute | solution.py:385
  18.3 0.0 collective-permute-done.3.refs_2_
  18.3 2.2 %collective-permute-done.4.refs_3_ = f32[2,32,512]{2,1,0:T(8,128)S(1)} collective-permute-done((f32[2,32,512]{2,1,0:T(8,128)S(1)}, f32[2,32,512]{2,1,0:T(8,128)S(1)}, u32[]{:S(2)}, u32[]{:S(2)}) %collective-permute-start.4) | collective-permute-done | bytes 131104 | tf_op jit(solution)/shard_map/ppermute | solution.py:385
  20.5 1.0 sort.1
  21.5 0.0 collective-permute-done
  21.6 3.3 %collective-permute-start.5 = (f32[160,512]{1,0:T(8,128)S(1)}, f32[160,512]{1,0:T(8,128)S(1)}, u32[]{:S(2)}, u32[]{:S(2)}) collective-permute-start(f32[160,512]{1,0:T(8,128)S(1)} %add.6), channel_id=1, source_target_pairs={{0,24},{4,100},{8,16},{36,68}} | collective-permute-start | bytes 983048 | tf_op jit(solution)/shard_map/ppermute | solution.py:392
  24.9 1.3 %collective-permute-start.6 = (f32[2,32,512]{2,1,0:T(8,128)S(1)}, f32[2,32,512]{2,1,0:T(8,128)S(1)}, u32[]{:S(2)}, u32[]{:S(2)}) collective-permute-start(f32[2,32,512]{2,1,0:T(8,128)S(1)} %get-tuple-element.73), channel_id=1, source_target_pairs={{0,1},{4,5},{8,9},{12,13},{16,17},{20,21},{24,25},{28,29},{32,33},... | collective-permute-start | bytes 393224 | tf_op jit(solution)/shard_map/ppermute | solution.py:390
  26.2 1.3 %collective-permute-start.7 = (f32[2,32,512]{2,1,0:T(8,128)S(1)}, f32[2,32,512]{2,1,0:T(8,128)S(1)}, u32[]{:S(2)}, u32[]{:S(2)}) collective-permute-start(f32[2,32,512]{2,1,0:T(8,128)S(1)} %get-tuple-element.74), channel_id=1, source_target_pairs={{0,2},{4,6},{8,10},{12,14},{16,18},{20,22},{24,26},{28,30},{32,34}... | collective-permute-start | bytes 393224 | tf_op jit(solution)/shard_map/ppermute | solution.py:390
  27.5 1.3 %collective-permute-start.8 = (f32[2,32,512]{2,1,0:T(8,128)S(1)}, f32[2,32,512]{2,1,0:T(8,128)S(1)}, u32[]{:S(2)}, u32[]{:S(2)}) collective-permute-start(f32[2,32,512]{2,1,0:T(8,128)S(1)} %get-tuple-element.75), channel_id=1, source_target_pairs={{0,3},{4,7},{8,11},{12,15},{16,19},{20,23},{24,27},{28,31},{32,35}... | collective-permute-start | bytes 393224 | tf_op jit(solution)/shard_map/ppermute | solution.py:390
  28.8 0.4 collective-permute-done.6.refs_1_
  29.2 2.8 %collective-permute-done.7.refs_2_ = f32[2,32,512]{2,1,0:T(8,128)S(1)} collective-permute-done((f32[2,32,512]{2,1,0:T(8,128)S(1)}, f32[2,32,512]{2,1,0:T(8,128)S(1)}, u32[]{:S(2)}, u32[]{:S(2)}) %collective-permute-start.7) | collective-permute-done | bytes 131104 | tf_op jit(solution)/shard_map/ppermute | solution.py:390
  32.0 0.0 collective-permute-done.8.refs_3_
  32.1 0.0 collective-permute-done.5
  32.1 5.1 %collective-permute-start.12 = (f32[160,512]{1,0:T(8,128)S(1)}, f32[160,512]{1,0:T(8,128)S(1)}, u32[]{:S(2)}, u32[]{:S(2)}) collective-permute-start(f32[160,512]{1,0:T(8,128)S(1)} %add.7.refs_0_), channel_id=1, source_target_pairs={{0,3},{4,7},{8,11},{36,39},{24,27},{100,103},{16,19},{68,71}} | collective-permute-start | bytes 983048 | tf_op jit(solution)/shard_map/ppermute | solution.py:400
  37.2 1.3 %collective-permute-start.11 = (f32[160,512]{1,0:T(8,128)S(1)}, f32[160,512]{1,0:T(8,128)S(1)}, u32[]{:S(2)}, u32[]{:S(2)}) collective-permute-start(f32[160,512]{1,0:T(8,128)S(1)} %add.7.refs_0_), channel_id=1, source_target_pairs={{0,2},{4,6},{8,10},{36,38},{24,26},{100,102},{16,18},{68,70}} | collective-permute-start | bytes 983048 | tf_op jit(solution)/shard_map/ppermute | solution.py:400
  38.6 1.3 %collective-permute-start.10 = (f32[160,512]{1,0:T(8,128)S(1)}, f32[160,512]{1,0:T(8,128)S(1)}, u32[]{:S(2)}, u32[]{:S(2)}) collective-permute-start(f32[160,512]{1,0:T(8,128)S(1)} %add.7.refs_0_), channel_id=1, source_target_pairs={{0,1},{4,5},{8,9},{36,37},{24,25},{100,101},{16,17},{68,69}} | collective-permute-start | bytes 983048 | tf_op jit(solution)/shard_map/ppermute | solution.py:400
  39.9 0.1 collective-permute-start.9
  40.0 2.0 %pick.1 = (f32[256,512]{1,0:T(8,128)S(1)}, f32[256,512]{1,0:T(8,128)S(1)}, f32[256,512]{1,0:T(8,128)S(1)}, f32[256,512]{1,0:T(8,128)S(1)}, s32[4,8]{1,0:T(4,128)S(1)}) custom-call(s32[32]{0:T(128)S(1)} %copy-done.4, f32[256,2048]{1,0:T(8,128)S(1)} %copy-done), custom_call_target="tpu_custom_call" | custom-call | flops 1024 | bytes 1024 | tf_op jit(solution)/shard_map/pick/pallas_call | solution.py:108
  42.0 0.0 copy-start.5
  42.0 0.0 copy-start.7
  42.1 2.1 %collective-permute-done.9.got_ref = f32[64,512]{1,0:T(8,128)S(1)} collective-permute-done((f32[64,512]{1,0:T(8,128)S(1)}, f32[64,512]{1,0:T(8,128)S(1)}, u32[]{:S(2)}, u32[]{:S(2)}) %collective-permute-start.9) | collective-permute-done | bytes 131104 | tf_op jit(solution)/shard_map/ppermute | solution.py:397
  44.1 0.0 collective-permute-done.12.refs_3_
  44.1 0.8 collective-permute-done.11.refs_2_
  45.0 7.0 %collective-permute-done.10.refs_1_ = f32[160,512]{1,0:T(8,128)S(1)} collective-permute-done((f32[160,512]{1,0:T(8,128)S(1)}, f32[160,512]{1,0:T(8,128)S(1)}, u32[]{:S(2)}, u32[]{:S(2)}) %collective-permute-start.10) | collective-permute-done | bytes 327712 | tf_op jit(solution)/shard_map/ppermute | solution.py:400
  52.0 0.1 load.1.own_ref
  52.1 0.1 collective-permute-start.13
  52.2 0.1 collective-permute-start.15
  52.3 4.1 %collective-permute-start.14 = (f32[256,512]{1,0:T(8,128)S(1)}, f32[256,512]{1,0:T(8,128)S(1)}, u32[]{:S(2)}, u32[]{:S(2)}) collective-permute-start(f32[256,512]{1,0:T(8,128)S(1)} %slice.3.lead_ref.refs_0_), channel_id=1, source_target_pairs={{0,1},{4,5},{8,9},{12,13},{16,17},{20,21},{24,25},{28,29},{32,33},... | collective-permute-start | bytes 1572872 | tf_op jit(solution)/shard_map/ppermute | solution.py:406
  56.4 4.8 %collective-permute-done.13.got_ref = f32[288,512]{1,0:T(8,128)S(1)} collective-permute-done((f32[288,512]{1,0:T(8,128)S(1)}, f32[288,512]{1,0:T(8,128)S(1)}, u32[]{:S(2)}, u32[]{:S(2)}) %collective-permute-start.13) | collective-permute-done | bytes 589856 | tf_op jit(solution)/shard_map/ppermute | solution.py:408
  61.2 0.1 join.2.own_ref
  61.3 3.9 %collective-permute-done.15.refs_4_ = f32[256,512]{1,0:T(8,128)S(1)} collective-permute-done((f32[256,512]{1,0:T(8,128)S(1)}, f32[256,512]{1,0:T(8,128)S(1)}, u32[]{:S(2)}, u32[]{:S(2)}) %collective-permute-start.15) | collective-permute-done | bytes 524320 | tf_op jit(solution)/shard_map/ppermute | solution.py:407
  65.2 0.8 copy-done.2
  66.0 0.1 collective-permute-done.14.refs_1_
  66.1 0.0 collective-permute-start.16
  66.1 0.1 broadcast_select_fusion
  66.2 2.5 %collective-permute-start.17 = (f32[256,512]{1,0:T(8,128)S(1)}, f32[256,512]{1,0:T(8,128)S(1)}, u32[]{:S(2)}, u32[]{:S(2)}) collective-permute-start(f32[256,512]{1,0:T(8,128)S(1)} %broadcast_select_fusion), channel_id=1, source_target_pairs={{0,3},{1,2},{4,7},{5,6},{8,11},{9,10},{12,15},{13,14},{16,19},{17,... | collective-permute-start | bytes 1572872 | tf_op jit(solution)/shard_map/ppermute | solution.py:410
  68.7 10.5 %collective-permute-done.16.got_ref = f32[416,512]{1,0:T(8,128)S(1)} collective-permute-done((f32[416,512]{1,0:T(8,128)S(1)}, f32[416,512]{1,0:T(8,128)S(1)}, u32[]{:S(2)}, u32[]{:S(2)}) %collective-permute-start.16) | collective-permute-done | bytes 852000 | tf_op jit(solution)/shard_map/ppermute | solution.py:412
  79.1 0.1 join.3
  79.2 0.0 collective-permute-done.17.refs_2_
  79.2 3.4 %collective-permute-start.19 = (f32[160,512]{1,0:T(8,128)S(1)}, f32[160,512]{1,0:T(8,128)S(1)}, u32[]{:S(2)}, u32[]{:S(2)}) collective-permute-start(f32[160,512]{1,0:T(8,128)S(1)} %get-tuple-element.102.own_ref), channel_id=1, source_target_pairs={{0,4},{4,0},{8,12},{12,8},{16,20},{20,16},{24,28},{28,24},{32,36},... | collective-permute-start | bytes 983048 | tf_op jit(solution)/shard_map/ppermute | solution.py:415
  82.6 2.2 %collective-permute-start.20 = (f32[256,512]{1,0:T(8,128)S(1)}, f32[256,512]{1,0:T(8,128)S(1)}, u32[]{:S(2)}, u32[]{:S(2)}) collective-permute-start(f32[256,512]{1,0:T(8,128)S(1)} %copy-done.8), channel_id=1, source_target_pairs={{0,1},{1,2},{2,3},{3,0},{4,5},{5,6},{6,7},{7,4},{8,9},{9,10},{10,1... | collective-permute-start | bytes 1572872 | tf_op jit(solution)/shard_map/ppermute | solution.py:418
  84.8 0.5 collective-permute-start.21
  85.3 0.0 collective-permute-start.18
  85.3 0.0 collective-permute-done.19.other_ref
  85.4 18.2 %factor.1 = (f32[256,256]{1,0:T(8,128)S(1)}, f32[256,256]{1,0:T(8,128)S(1)}, f32[256,256]{1,0:T(8,128)S(1)}) custom-call(f32[160,512]{1,0:T(8,128)S(1)} %get-tuple-element.102.own_ref, f32[160,512]{1,0:T(8,128)S(1)} %collective-permute-done.19.other_ref), custom_call_target="tpu_custom_call" | custom-call | flops 21474836480 | bytes 1048576 | tf_op jit(solution)/shard_map/factor/pallas_call | solution.py:108
  103.6 0.0 copy-start.1
  103.6 0.0 collective-permute-done.20.refs_2_
  103.6 5.0 %collective-permute-done.21.refs_3_ = f32[256,512]{1,0:T(8,128)S(1)} collective-permute-done((f32[256,512]{1,0:T(8,128)S(1)}, f32[256,512]{1,0:T(8,128)S(1)}, u32[]{:S(2)}, u32[]{:S(2)}) %collective-permute-start.21) | collective-permute-done | bytes 524320 | tf_op jit(solution)/shard_map/ppermute | solution.py:418
  108.7 0.0 collective-permute-done.18.refs_6_
  108.7 0.8 collective-permute-start.22
  109.5 0.0 collective-permute-start.23
  109.5 2.9 %weigh.1 = (f32[256,512]{1,0:T(8,128)}, f32[256,512]{1,0:T(8,128)S(1)}) custom-call(f32[256,512]{1,0:T(8,128)S(1)} %slice.3.lead_ref.refs_0_, f32[256,512]{1,0:T(8,128)S(1)} %collective-permute-done.14.refs_1_, f32[256,512]{1,0:T(8,128)S(1)} %collective-permute-done.17.refs_2_, f32[256,256]{1,0:T(8,128)S(1)} %get-tuple-element.110.refs_3_, ...), custom_call_target="tpu_custom_call" | custom-call | flops 1024 | bytes 1024 | tf_op jit(solution)/shard_map/weigh/pallas_call | solution.py:288
  112.4 0.8 collective-permute-done.23.refs_8_
  113.2 8.6 %update.1 = f32[256,2048]{1,0:T(8,128)} custom-call(s32[4,8]{1,0:T(4,128)S(1)} %get-tuple-element.114.plan, f32[256,512]{1,0:T(8,128)S(1)} %get-tuple-element.115.refs_0_, f32[256,512]{1,0:T(8,128)S(1)} %get-tuple-element.116.refs_1_, f32[256,512]{1,0:T(8,128)S(1)} %collective-permute-done.20.refs_2_, f32[256,512]{1,0:T(8,128)S(1)} %collective-permute-done.21.refs_3_, ...), custom_call_target="tpu_custom_call" | custom-call | tf_op jit(solution)/shard_map/update/pallas_call | solution.py:336
  (17 shorter events, 0.2 us)
Async XLA Ops:
  0.6 19.9 %copy-start.4 = (s32[32]{0:T(128)S(1)}, s32[32]{0:T(128)}, u32[]{:S(2)}) copy-start(s32[32]{0:T(128)} %map_ref.3) | copy-start | bytes 388
  1.7 5.3 %collective-permute-start.1 = (f32[256,512]{1,0:T(8,128)S(1)}, f32[256,512]{1,0:T(8,128)S(1)}, u32[]{:S(2)}, u32[]{:S(2)}) collective-permute-start(f32[256,512]{1,0:T(8,128)S(1)} %slice.3.lead_ref.refs_0_), channel_id=1, source_target_pairs={{0,4},{4,0},{8,12},{12,8},{16,20},{20,16},{24,28},{28,24},{32,36},... | collective-permute-start | bytes 1572872 | tf_op jit(solution)/shard_map/ppermute | solution.py:381
  3.3 36.7 %copy-start = (f32[256,2048]{1,0:T(8,128)S(1)}, f32[256,2048]{1,0:T(8,128)}, u32[]{:S(2)}) copy-start(f32[256,2048]{1,0:T(8,128)} %front_ref.1) | copy-start | bytes 6291460
  3.3 18.2 %collective-permute-start = (f32[160,512]{1,0:T(8,128)S(1)}, f32[160,512]{1,0:T(8,128)S(1)}, u32[]{:S(2)}, u32[]{:S(2)}) collective-permute-start(f32[160,512]{1,0:T(8,128)S(1)} %corner.1), channel_id=1, source_target_pairs={{0,8},{4,36}} | collective-permute-start | bytes 983048 | tf_op jit(solution)/shard_map/ppermute | solution.py:378
  7.2 11.2 %collective-permute-start.2 = (f32[2,32,512]{2,1,0:T(8,128)S(1)}, f32[2,32,512]{2,1,0:T(8,128)S(1)}, u32[]{:S(2)}, u32[]{:S(2)}) collective-permute-start(f32[2,32,512]{2,1,0:T(8,128)S(1)} %get-tuple-element.63), channel_id=1, source_target_pairs={{8,16},{12,20},{16,24},{20,28},{24,0},{28,4},{32,40},{36,44},{40,4... | collective-permute-start | bytes 393224 | tf_op jit(solution)/shard_map/ppermute | solution.py:385
  8.5 9.9 %collective-permute-start.3 = (f32[2,32,512]{2,1,0:T(8,128)S(1)}, f32[2,32,512]{2,1,0:T(8,128)S(1)}, u32[]{:S(2)}, u32[]{:S(2)}) collective-permute-start(f32[2,32,512]{2,1,0:T(8,128)S(1)} %get-tuple-element.64), channel_id=1, source_target_pairs={{8,24},{12,28},{16,0},{20,4},{24,8},{28,12},{32,48},{36,52},{40,56... | collective-permute-start | bytes 393224 | tf_op jit(solution)/shard_map/ppermute | solution.py:385
  9.8 10.7 %collective-permute-start.4 = (f32[2,32,512]{2,1,0:T(8,128)S(1)}, f32[2,32,512]{2,1,0:T(8,128)S(1)}, u32[]{:S(2)}, u32[]{:S(2)}) collective-permute-start(f32[2,32,512]{2,1,0:T(8,128)S(1)} %get-tuple-element.65), channel_id=1, source_target_pairs={{8,0},{12,4},{16,8},{20,12},{24,16},{28,20},{32,56},{36,60},{40,32... | collective-permute-start | bytes 393224 | tf_op jit(solution)/shard_map/ppermute | solution.py:385
  21.6 10.5 %collective-permute-start.5 = (f32[160,512]{1,0:T(8,128)S(1)}, f32[160,512]{1,0:T(8,128)S(1)}, u32[]{:S(2)}, u32[]{:S(2)}) collective-permute-start(f32[160,512]{1,0:T(8,128)S(1)} %add.6), channel_id=1, source_target_pairs={{0,24},{4,100},{8,16},{36,68}} | collective-permute-start | bytes 983048 | tf_op jit(solution)/shard_map/ppermute | solution.py:392
  24.9 4.4 %collective-permute-start.6 = (f32[2,32,512]{2,1,0:T(8,128)S(1)}, f32[2,32,512]{2,1,0:T(8,128)S(1)}, u32[]{:S(2)}, u32[]{:S(2)}) collective-permute-start(f32[2,32,512]{2,1,0:T(8,128)S(1)} %get-tuple-element.73), channel_id=1, source_target_pairs={{0,1},{4,5},{8,9},{12,13},{16,17},{20,21},{24,25},{28,29},{32,33},... | collective-permute-start | bytes 393224 | tf_op jit(solution)/shard_map/ppermute | solution.py:390
  26.2 5.9 %collective-permute-start.7 = (f32[2,32,512]{2,1,0:T(8,128)S(1)}, f32[2,32,512]{2,1,0:T(8,128)S(1)}, u32[]{:S(2)}, u32[]{:S(2)}) collective-permute-start(f32[2,32,512]{2,1,0:T(8,128)S(1)} %get-tuple-element.74), channel_id=1, source_target_pairs={{0,2},{4,6},{8,10},{12,14},{16,18},{20,22},{24,26},{28,30},{32,34}... | collective-permute-start | bytes 393224 | tf_op jit(solution)/shard_map/ppermute | solution.py:390
  27.5 4.6 %collective-permute-start.8 = (f32[2,32,512]{2,1,0:T(8,128)S(1)}, f32[2,32,512]{2,1,0:T(8,128)S(1)}, u32[]{:S(2)}, u32[]{:S(2)}) collective-permute-start(f32[2,32,512]{2,1,0:T(8,128)S(1)} %get-tuple-element.75), channel_id=1, source_target_pairs={{0,3},{4,7},{8,11},{12,15},{16,19},{20,23},{24,27},{28,31},{32,35}... | collective-permute-start | bytes 393224 | tf_op jit(solution)/shard_map/ppermute | solution.py:390
  32.1 12.0 %collective-permute-start.12 = (f32[160,512]{1,0:T(8,128)S(1)}, f32[160,512]{1,0:T(8,128)S(1)}, u32[]{:S(2)}, u32[]{:S(2)}) collective-permute-start(f32[160,512]{1,0:T(8,128)S(1)} %add.7.refs_0_), channel_id=1, source_target_pairs={{0,3},{4,7},{8,11},{36,39},{24,27},{100,103},{16,19},{68,71}} | collective-permute-start | bytes 983048 | tf_op jit(solution)/shard_map/ppermute | solution.py:400
  37.2 7.7 %collective-permute-start.11 = (f32[160,512]{1,0:T(8,128)S(1)}, f32[160,512]{1,0:T(8,128)S(1)}, u32[]{:S(2)}, u32[]{:S(2)}) collective-permute-start(f32[160,512]{1,0:T(8,128)S(1)} %add.7.refs_0_), channel_id=1, source_target_pairs={{0,2},{4,6},{8,10},{36,38},{24,26},{100,102},{16,18},{68,70}} | collective-permute-start | bytes 983048 | tf_op jit(solution)/shard_map/ppermute | solution.py:400
  38.6 13.4 %collective-permute-start.10 = (f32[160,512]{1,0:T(8,128)S(1)}, f32[160,512]{1,0:T(8,128)S(1)}, u32[]{:S(2)}, u32[]{:S(2)}) collective-permute-start(f32[160,512]{1,0:T(8,128)S(1)} %add.7.refs_0_), channel_id=1, source_target_pairs={{0,1},{4,5},{8,9},{36,37},{24,25},{100,101},{16,17},{68,69}} | collective-permute-start | bytes 983048 | tf_op jit(solution)/shard_map/ppermute | solution.py:400
  39.9 4.2 %collective-permute-start.9 = (f32[64,512]{1,0:T(8,128)S(1)}, f32[64,512]{1,0:T(8,128)S(1)}, u32[]{:S(2)}, u32[]{:S(2)}) collective-permute-start(f32[64,512]{1,0:T(8,128)S(1)} %merge.1.own_ref), channel_id=1, source_target_pairs={{0,8},{4,36},{8,0},{12,44},{16,24},{20,52},{24,16},{28,60},{32,40}... | collective-permute-start | bytes 393224 | tf_op jit(solution)/shard_map/ppermute | solution.py:397
  42.0 19.2 %copy-start.5 = (f32[256,512]{1,0:T(8,128)}, f32[256,512]{1,0:T(8,128)S(1)}, u32[]{:S(2)}) copy-start(f32[256,512]{1,0:T(8,128)S(1)} %get-tuple-element.108) | copy-start | bytes 1572868
  42.0 19.2 %copy-start.7 = (f32[256,512]{1,0:T(8,128)}, f32[256,512]{1,0:T(8,128)S(1)}, u32[]{:S(2)}) copy-start(f32[256,512]{1,0:T(8,128)S(1)} %get-tuple-element.107) | copy-start | bytes 1572868
  52.1 9.1 %collective-permute-start.13 = (f32[288,512]{1,0:T(8,128)S(1)}, f32[288,512]{1,0:T(8,128)S(1)}, u32[]{:S(2)}, u32[]{:S(2)}) collective-permute-start(f32[288,512]{1,0:T(8,128)S(1)} %load.1.own_ref), channel_id=1, source_target_pairs={{0,32},{4,12},{8,40},{12,4},{16,48},{20,28},{24,56},{28,20},{32,0}... | collective-permute-start | bytes 1769480 | tf_op jit(solution)/shard_map/ppermute | solution.py:408
  52.2 13.0 %collective-permute-start.15 = (f32[256,512]{1,0:T(8,128)S(1)}, f32[256,512]{1,0:T(8,128)S(1)}, u32[]{:S(2)}, u32[]{:S(2)}) collective-permute-start(f32[256,512]{1,0:T(8,128)S(1)} %get-tuple-element.91), channel_id=1, source_target_pairs={{0,3},{1,0},{2,1},{3,2},{4,7},{5,4},{6,5},{7,6},{8,11},{9,8},{10,9... | collective-permute-start | bytes 1572872 | tf_op jit(solution)/shard_map/ppermute | solution.py:407
  52.3 13.8 %collective-permute-start.14 = (f32[256,512]{1,0:T(8,128)S(1)}, f32[256,512]{1,0:T(8,128)S(1)}, u32[]{:S(2)}, u32[]{:S(2)}) collective-permute-start(f32[256,512]{1,0:T(8,128)S(1)} %slice.3.lead_ref.refs_0_), channel_id=1, source_target_pairs={{0,1},{4,5},{8,9},{12,13},{16,17},{20,21},{24,25},{28,29},{32,33},... | collective-permute-start | bytes 1572872 | tf_op jit(solution)/shard_map/ppermute | solution.py:406
  65.2 0.8 copy-start.2
  66.1 13.0 %collective-permute-start.16 = (f32[416,512]{1,0:T(8,128)S(1)}, f32[416,512]{1,0:T(8,128)S(1)}, u32[]{:S(2)}, u32[]{:S(2)}) collective-permute-start(f32[416,512]{1,0:T(8,128)S(1)} %join.2.own_ref), channel_id=1, source_target_pairs={{0,96},{4,28},{8,104},{12,20},{16,112},{20,12},{24,120},{28,4},{32... | collective-permute-start | bytes 2555912 | tf_op jit(solution)/shard_map/ppermute | solution.py:412
  66.1 16.5 %copy-start.8 = (f32[256,512]{1,0:T(8,128)S(1)}, f32[256,512]{1,0:T(8,128)}, u32[]{:S(2)}) copy-start(f32[256,512]{1,0:T(8,128)} %copy-done.7) | copy-start | bytes 1572868
  66.1 18.7 %copy-start.6 = (f32[256,512]{1,0:T(8,128)S(1)}, f32[256,512]{1,0:T(8,128)}, u32[]{:S(2)}) copy-start(f32[256,512]{1,0:T(8,128)} %copy-done.5) | copy-start | bytes 1572868
  66.2 13.1 %collective-permute-start.17 = (f32[256,512]{1,0:T(8,128)S(1)}, f32[256,512]{1,0:T(8,128)S(1)}, u32[]{:S(2)}, u32[]{:S(2)}) collective-permute-start(f32[256,512]{1,0:T(8,128)S(1)} %broadcast_select_fusion), channel_id=1, source_target_pairs={{0,3},{1,2},{4,7},{5,6},{8,11},{9,10},{12,15},{13,14},{16,19},{17,... | collective-permute-start | bytes 1572872 | tf_op jit(solution)/shard_map/ppermute | solution.py:410
  79.2 6.1 %collective-permute-start.19 = (f32[160,512]{1,0:T(8,128)S(1)}, f32[160,512]{1,0:T(8,128)S(1)}, u32[]{:S(2)}, u32[]{:S(2)}) collective-permute-start(f32[160,512]{1,0:T(8,128)S(1)} %get-tuple-element.102.own_ref), channel_id=1, source_target_pairs={{0,4},{4,0},{8,12},{12,8},{16,20},{20,16},{24,28},{28,24},{32,36},... | collective-permute-start | bytes 983048 | tf_op jit(solution)/shard_map/ppermute | solution.py:415
  82.6 21.0 %collective-permute-start.20 = (f32[256,512]{1,0:T(8,128)S(1)}, f32[256,512]{1,0:T(8,128)S(1)}, u32[]{:S(2)}, u32[]{:S(2)}) collective-permute-start(f32[256,512]{1,0:T(8,128)S(1)} %copy-done.8), channel_id=1, source_target_pairs={{0,1},{1,2},{2,3},{3,0},{4,5},{5,6},{6,7},{7,4},{8,9},{9,10},{10,1... | collective-permute-start | bytes 1572872 | tf_op jit(solution)/shard_map/ppermute | solution.py:418
  84.8 23.8 %collective-permute-start.21 = (f32[256,512]{1,0:T(8,128)S(1)}, f32[256,512]{1,0:T(8,128)S(1)}, u32[]{:S(2)}, u32[]{:S(2)}) collective-permute-start(f32[256,512]{1,0:T(8,128)S(1)} %copy-done.6), channel_id=1, source_target_pairs={{0,2},{1,3},{2,0},{3,1},{4,6},{5,7},{6,4},{7,5},{8,10},{9,11},{10,... | collective-permute-start | bytes 1572872 | tf_op jit(solution)/shard_map/ppermute | solution.py:418
  85.3 23.3 %collective-permute-start.18 = (f32[512,512]{1,0:T(8,128)S(1)}, f32[512,512]{1,0:T(8,128)S(1)}, u32[]{:S(2)}, u32[]{:S(2)}) collective-permute-start(f32[512,512]{1,0:T(8,128)S(1)} %get-tuple-element.120.refs_5_), channel_id=1, source_target_pairs={{0,24},{4,100},{8,16},{12,108},{16,8},{20,116},{24,0},{28,124},{32... | collective-permute-start | bytes 3145736 | tf_op jit(solution)/shard_map/ppermute | solution.py:416
  85.3 27.9 %copy-start.3 = (f32[256,512]{1,0:T(8,128)S(1)}, f32[256,512]{1,0:T(8,128)}, u32[]{:S(2)}) copy-start(f32[256,512]{1,0:T(8,128)} %copy-done.2) | copy-start | bytes 1572868
  103.6 9.7 %copy-start.1 = (f32[256,2048]{1,0:T(8,128)S(1)}, f32[256,2048]{1,0:T(8,128)}, u32[]{:S(2)}) copy-start(f32[256,2048]{1,0:T(8,128)} %refs_9_.1) | copy-start | bytes 6291460
  108.7 3.7 %collective-permute-start.22 = (f32[512,512]{1,0:T(8,128)S(1)}, f32[512,512]{1,0:T(8,128)S(1)}, u32[]{:S(2)}, u32[]{:S(2)}) collective-permute-start(f32[512,512]{1,0:T(8,128)S(1)} %get-tuple-element.120.refs_5_), channel_id=1, source_target_pairs={{0,4},{4,0},{8,12},{12,8},{16,20},{20,16},{24,28},{28,24},{32,36},... | collective-permute-start | bytes 3145736 | tf_op jit(solution)/shard_map/ppermute | solution.py:423
  109.5 3.8 %collective-permute-start.23 = (f32[512,512]{1,0:T(8,128)S(1)}, f32[512,512]{1,0:T(8,128)S(1)}, u32[]{:S(2)}, u32[]{:S(2)}) collective-permute-start(f32[512,512]{1,0:T(8,128)S(1)} %collective-permute-done.18.refs_6_), channel_id=1, source_target_pairs={{0,4},{4,0},{8,12},{12,8},{16,20},{20,16},{24,28},{28,24},{32,36},... | collective-permute-start | bytes 3145736 | tf_op jit(solution)/shard_map/ppermute | solution.py:422

commit v11 on v9

--- a/solution.py
+++ b/solution.py
@@ -1,5 +1,3 @@
-from functools import partial
-
 import jax
 import jax.numpy as jnp
 from jax import lax
@@ -222,14 +220,13 @@
     out_ref[64 + BLOCK :] = jnp.zeros((PAD, LEAD), jnp.float32)
 
 
-def join_kernel(rows, own_ref, got_ref, *outs):
-    outs[0][:rows] = own_ref[:rows]
-    outs[0][rows : 2 * rows] = got_ref[:rows]
-    block = own_ref[rows : rows + BLOCK] + got_ref[rows : rows + BLOCK]
+def join_kernel(own_ref, got_ref, *outs):
     if len(outs) == 1:
-        outs[0][2 * rows :] = block
+        outs[0][:128] = jnp.concatenate([own_ref[:64], got_ref[:64]], 0)
+        outs[0][128:] = own_ref[64 : 64 + BLOCK] + got_ref[64 : 64 + BLOCK]
     else:
-        outs[1][...] = block
+        outs[0][...] = jnp.concatenate([own_ref[:128], got_ref[:128]], 0)
+        outs[1][...] = own_ref[128:] + got_ref[128:]
 
 
 def pick_kernel(map_ref, front_ref, *refs):
@@ -306,12 +303,12 @@
             off_z, off_x = plane ^ group, line ^ x
             first = jnp.where(holder == 0, off_x, off_z)
             second = jnp.where(holder == 0, off_z, off_x)
-            index = (first >> 1) + 2 * ((second & 1) ^ (second >> 1)) + 4 * (second >> 1)
+            index = ((first & 1) ^ (first >> 1)) + 2 * (first >> 1) + 4 * ((second & 1) ^ (second >> 1))
             rows = pl.ds(pl.multiple_of(index * 64 + place * 32, 32), 32)
             into = pl.ds(pl.multiple_of((2 * x + holder) * 32, 32), 32)
             for late in range(2):
 
-                @pl.when(((first & 1) ^ (first >> 1)) == late)
+                @pl.when((second >> 1) == late)
                 def _():
                     ahead_ref[into, :] = gathered[2 * parity + late][rows, :]
 
@@ -346,7 +343,8 @@
 
 
 def doubling_steps():
-    every = []
+    every, spread = [], []
+    have = {0, 1}
     for step in range(4):
         flip = 1 if step % 2 == 0 else 3
         pairs = []
@@ -356,7 +354,9 @@
                     to = (z, x ^ flip) if step // 2 == core else (z ^ flip, x)
                     pairs.append(((z * 4 + x) * 2 + core, (to[0] * 4 + to[1]) * 2 + core))
         every.append(pairs)
-    return every, [pair for pair in every[0] if pair[0] < 2]
+        spread.append([pair for pair in pairs if pair[0] in have])
+        have |= {pair[1] for pair in spread[-1]}
+    return every, spread
 
 
 def shards(front, ancestor, tile_map):
@@ -367,9 +367,8 @@
 
     ring = [[(i, (i + hop) % 4) for i in range(4)] for hop in range(4)]
 
-    blocks = [local_call(corner_kernel, "corner", [(BLOCK, LEAD)])(lead)[0]]
-    for to in range(1, 4):
-        blocks.append(lax.ppermute(blocks[0], ("row", "col"), [(4 * core, 4 * core + to) for core in range(2)]))
+    block = local_call(corner_kernel, "corner", [(BLOCK, LEAD)])(lead)[0]
+    got = lax.ppermute(block, ("row", "col"), [(4 * i, 4 * i + 1) for i in (0, 1)])
 
     mate = lax.ppermute(lead, "row", swap)
     parts = list(local_call(share_kernel, "share", [part] * 4)(lead, mate))
@@ -377,13 +376,13 @@
         pairs = [(i, i // 8 * 8 + (i + 2 * hop) % 8) for i in range(2, 32)]
         parts[hop] = lax.ppermute(parts[hop], "row", pairs)
     parts = list(local_call(sort_kernel, "sort", [part] * 4, 1)(tile_map, *parts))
-    blocks, parts = lax.optimization_barrier((blocks, parts))
+    block, got, parts = lax.optimization_barrier((block, got, parts))
 
     every, spread = doubling_steps()
     for to in range(1, 4):
         parts[to] = lax.ppermute(parts[to], "col", [(0, to)])
-    block = (blocks[0] + blocks[1]) + (blocks[2] + blocks[3])
-    got = lax.ppermute(block, "row", spread)
+    block = block + got
+    got = lax.ppermute(block, ("row", "col"), [(4 * i + y, 4 * i + to) for i in (0, 1) for y, to in ((0, 3), (1, 2))])
     block, got, parts = lax.optimization_barrier((block, got, parts))
     load = local_call(merge_kernel, "merge", [(64 + BLOCK + PAD, LEAD)])(*parts, block, got)[0]
 
@@ -391,20 +390,22 @@
 
     load, lead = lax.optimization_barrier((load, lead))
     near = lax.ppermute(lead, "col", [(0, 1)])
-    load = local_call(partial(join_kernel, 64), "join", [(128 + BLOCK, LEAD)])(load, lax.ppermute(load, "row", every[1]))[0]
+    load = local_call(join_kernel, "join", [(128 + BLOCK, LEAD)])(load, lax.ppermute(load, "row", every[0]))[0]
     load, near, *pieces = lax.optimization_barrier((load, near, *pieces))
     far = lax.ppermute(jnp.where(lax.axis_index("col") == 1, near, lead), "col", [(0, 3), (1, 2)])
-    load = local_call(partial(join_kernel, 128), "join", [(256 + BLOCK, LEAD)])(load, lax.ppermute(load, "row", every[2]))[0]
-    load, far, *pieces = lax.optimization_barrier((load, far, *pieces))
-    gathered, block = local_call(partial(join_kernel, 256), "join", [(512, LEAD), (BLOCK, LEAD)])(
-        load, lax.ppermute(load, "row", every[3])
-    )
-    for hop in (1, 3):
-        pieces[hop] = lax.ppermute(pieces[hop], "col", ring[hop])
+    gathered, block = local_call(join_kernel, "join", [(256, LEAD), (BLOCK, LEAD)])(load, lax.ppermute(load, "row", every[1]))
+    block, gathered, far, *pieces = lax.optimization_barrier((block, gathered, far, *pieces))
+
+    block = block + lax.ppermute(block, "row", spread[2])
+    block, gathered = lax.optimization_barrier((block, gathered))
+    pieces[3] = lax.ppermute(pieces[3], "col", ring[3])
+    block = block + lax.ppermute(block, "row", spread[3])
+    gathered = jnp.concatenate([gathered, lax.ppermute(gathered, "row", every[2])], 0)
     block, gathered, *pieces = lax.optimization_barrier((block, gathered, *pieces))
     other = lax.ppermute(block, "row", swap)
-    late = lax.ppermute(gathered, "row", every[0])
-    pieces[2] = lax.ppermute(pieces[2], "col", ring[2])
+    late = lax.ppermute(gathered, "row", every[3])
+    for hop in (1, 2):
+        pieces[hop] = lax.ppermute(pieces[hop], "col", ring[hop])
 
     inverse = factor(block, other)
     late, gathered, inverse, pieces = lax.optimization_barrier((late, gathered, inverse, pieces))

time: 114 us -> 125 us (1.096)
  waiting for transfers between devices: 36.4 us -> 45.8 us
  starting transfers between devices: 39.4 us -> 42.1 us
    ppermute x8, starting transfers between devices: 12.6 us -> 20.7 us  [the longest x1 7.78 us: shards(): block = block + lax.ppermute(block, 'row', spread[2])]
    ppermute x1, starting transfers between devices: 6.72 us -> 0.74 us  [shards(): other = lax.ppermute(block, 'row', swap)]
    ppermute x2, waiting for transfers between devices: 0.01 us -> 5.07 us  [shards(): pieces[hop] = lax.ppermute(pieces[hop], 'col', ring[hop])]
    ppermute x8, waiting for transfers between devices: 13.3 us -> 17.5 us  [the longest x1 5.97 us: shards(): pieces[3] = lax.ppermute(pieces[3], 'col', ring[3])]
    ppermute x3, waiting for transfers between devices: 12.5 us -> 9.12 us  [shards(): parts[hop] = lax.ppermute(parts[hop], 'row', pairs)]
    ppermute x3, waiting for transfers between devices: 1.91 us -> 4.07 us  [shards(): parts[to] = lax.ppermute(parts[to], 'col', [(0, to)])]
    pallas_call x9 -> x8, Pallas kernels: 21.6 us -> 21.5 us  [call(): pl.pallas_call(kernel, out_shape=[jax.ShapeDtypeStruct(shape, jnp.float32...]
  transfers between devices with their start and end apart: 23 -> 23, of which waited for: 9 -> 13; matrix products, arithmetic and copies ran while one was open for 0% -> 0% of each run, Pallas kernels for 22% -> 20%
where the time goes in v11:
time: 125 us
  waiting for transfers between devices  45.8 us (37%)
  starting transfers between devices  42.1 us (34%)
  Pallas kernels  33 us (26%)
  local copies, waits for them, and re-layouts  2.69 us (2%)
    pallas_call x8, Pallas kernels, call(): pl.pallas_call(kernel, out_shape=[jax.ShapeDtypeStruct(shape, jnp.float32...  21.5 us
    ppermute x3, waiting for transfers between devices, shards(): parts[hop] = lax.ppermute(parts[hop], 'row', pairs)  9.12 us
    pallas_call x1, Pallas kernels, update(): pl.pallas_call(update_kernel, out_shape=jax.ShapeDtypeStruct(base.shape,...  8.59 us
    ppermute x1, starting transfers between devices, shards(): block = block + lax.ppermute(block, 'row', spread[2])  7.78 us
    ppermute x1, waiting for transfers between devices, shards(): pieces[3] = lax.ppermute(pieces[3], 'col', ring[3])  5.97 us
    ppermute x1, waiting for transfers between devices, shards(): lax.ppermute(load, 'row', every[1])  5.95 us
    ppermute x2, waiting for transfers between devices, shards(): pieces[hop] = lax.ppermute(pieces[hop], 'col', ring[hop])  5.07 us
    ppermute x2, starting transfers between devices, shards(): pieces[hop] = lax.ppermute(pieces[hop], 'col', ring[hop])  4.59 us
  transfers between devices with their start and end apart: 23, of which 13 were waited for; matrix products, arithmetic and copies ran while one was open for 0% of the time, Pallas kernels for 20%

profile of v11, /device:TPU:1, one launch (start us, length us, event | category | flops | bytes accessed | tf_op | source)
XLA Modules:
  0.0 124.9 jit_solution(15751585229742914091)
XLA Ops:
  0.6 1.1 slice.3.lead_ref.refs_0_
  1.7 1.5 %collective-permute-start.1 = (f32[256,512]{1,0:T(8,128)S(1)}, f32[256,512]{1,0:T(8,128)S(1)}, u32[]{:S(2)}, u32[]{:S(2)}) collective-permute-start(f32[256,512]{1,0:T(8,128)S(1)} %slice.3.lead_ref.refs_0_), channel_id=1, source_target_pairs={{0,4},{4,0},{8,12},{12,8},{16,20},{20,16},{24,28},{28,24},{32,36},... | collective-permute-start | bytes 1572872 | tf_op jit(solution)/shard_map/ppermute | solution.py:373
  3.2 0.1 corner.1
  3.3 0.0 copy-start
  3.3 3.4 %collective-permute-start = (f32[160,512]{1,0:T(8,128)S(1)}, f32[160,512]{1,0:T(8,128)S(1)}, u32[]{:S(2)}, u32[]{:S(2)}) collective-permute-start(f32[160,512]{1,0:T(8,128)S(1)} %corner.1), channel_id=1, source_target_pairs={{0,1},{4,5}} | collective-permute-start | bytes 983048 | tf_op jit(solution)/shard_map/ppermute | solution.py:371
  6.7 0.0 collective-permute-done.1.mate_ref
  6.7 0.1 share.1
  6.8 1.3 %collective-permute-start.2 = (f32[2,32,512]{2,1,0:T(8,128)S(1)}, f32[2,32,512]{2,1,0:T(8,128)S(1)}, u32[]{:S(2)}, u32[]{:S(2)}) collective-permute-start(f32[2,32,512]{2,1,0:T(8,128)S(1)} %get-tuple-element.67), channel_id=1, source_target_pairs={{8,16},{12,20},{16,24},{20,28},{24,0},{28,4},{32,40},{36,44},{40,4... | collective-permute-start | bytes 393224 | tf_op jit(solution)/shard_map/ppermute | solution.py:377
  8.1 1.3 %collective-permute-start.3 = (f32[2,32,512]{2,1,0:T(8,128)S(1)}, f32[2,32,512]{2,1,0:T(8,128)S(1)}, u32[]{:S(2)}, u32[]{:S(2)}) collective-permute-start(f32[2,32,512]{2,1,0:T(8,128)S(1)} %get-tuple-element.68), channel_id=1, source_target_pairs={{8,24},{12,28},{16,0},{20,4},{24,8},{28,12},{32,48},{36,52},{40,56... | collective-permute-start | bytes 393224 | tf_op jit(solution)/shard_map/ppermute | solution.py:377
  9.4 1.3 %collective-permute-start.4 = (f32[2,32,512]{2,1,0:T(8,128)S(1)}, f32[2,32,512]{2,1,0:T(8,128)S(1)}, u32[]{:S(2)}, u32[]{:S(2)}) collective-permute-start(f32[2,32,512]{2,1,0:T(8,128)S(1)} %get-tuple-element.69), channel_id=1, source_target_pairs={{8,0},{12,4},{16,8},{20,12},{24,16},{28,20},{32,56},{36,60},{40,32... | collective-permute-start | bytes 393224 | tf_op jit(solution)/shard_map/ppermute | solution.py:377
  10.7 6.8 %collective-permute-done.2.refs_1_ = f32[2,32,512]{2,1,0:T(8,128)S(1)} collective-permute-done((f32[2,32,512]{2,1,0:T(8,128)S(1)}, f32[2,32,512]{2,1,0:T(8,128)S(1)}, u32[]{:S(2)}, u32[]{:S(2)}) %collective-permute-start.2) | collective-permute-done | bytes 131104 | tf_op jit(solution)/shard_map/ppermute | solution.py:377
  17.5 0.0 collective-permute-done.3.refs_2_
  17.5 2.3 %collective-permute-done.4.refs_3_ = f32[2,32,512]{2,1,0:T(8,128)S(1)} collective-permute-done((f32[2,32,512]{2,1,0:T(8,128)S(1)}, f32[2,32,512]{2,1,0:T(8,128)S(1)}, u32[]{:S(2)}, u32[]{:S(2)}) %collective-permute-start.4) | collective-permute-done | bytes 131104 | tf_op jit(solution)/shard_map/ppermute | solution.py:377
  19.8 1.0 sort.1
  20.9 0.0 collective-permute-done
  20.9 2.7 %collective-permute-start.5 = (f32[160,512]{1,0:T(8,128)S(1)}, f32[160,512]{1,0:T(8,128)S(1)}, u32[]{:S(2)}, u32[]{:S(2)}) collective-permute-start(f32[160,512]{1,0:T(8,128)S(1)} %add.9.refs_4_), channel_id=1, source_target_pairs={{0,3},{1,2},{4,7},{5,6}} | collective-permute-start | bytes 983048 | tf_op jit(solution)/shard_map/ppermute | solution.py:385
  23.7 1.8 %collective-permute-start.6 = (f32[2,32,512]{2,1,0:T(8,128)S(1)}, f32[2,32,512]{2,1,0:T(8,128)S(1)}, u32[]{:S(2)}, u32[]{:S(2)}) collective-permute-start(f32[2,32,512]{2,1,0:T(8,128)S(1)} %get-tuple-element.77), channel_id=1, source_target_pairs={{0,1},{4,5},{8,9},{12,13},{16,17},{20,21},{24,25},{28,29},{32,33},... | collective-permute-start | bytes 393224 | tf_op jit(solution)/shard_map/ppermute | solution.py:383
  25.4 1.3 %collective-permute-start.7 = (f32[2,32,512]{2,1,0:T(8,128)S(1)}, f32[2,32,512]{2,1,0:T(8,128)S(1)}, u32[]{:S(2)}, u32[]{:S(2)}) collective-permute-start(f32[2,32,512]{2,1,0:T(8,128)S(1)} %get-tuple-element.78), channel_id=1, source_target_pairs={{0,2},{4,6},{8,10},{12,14},{16,18},{20,22},{24,26},{28,30},{32,34}... | collective-permute-start | bytes 393224 | tf_op jit(solution)/shard_map/ppermute | solution.py:383
  26.7 1.3 %collective-permute-start.8 = (f32[2,32,512]{2,1,0:T(8,128)S(1)}, f32[2,32,512]{2,1,0:T(8,128)S(1)}, u32[]{:S(2)}, u32[]{:S(2)}) collective-permute-start(f32[2,32,512]{2,1,0:T(8,128)S(1)} %get-tuple-element.79), channel_id=1, source_target_pairs={{0,3},{4,7},{8,11},{12,15},{16,19},{20,23},{24,27},{28,31},{32,35}... | collective-permute-start | bytes 393224 | tf_op jit(solution)/shard_map/ppermute | solution.py:383
  28.0 0.0 collective-permute-done.6.refs_1_
  28.1 1.4 %collective-permute-done.7.refs_2_ = f32[2,32,512]{2,1,0:T(8,128)S(1)} collective-permute-done((f32[2,32,512]{2,1,0:T(8,128)S(1)}, f32[2,32,512]{2,1,0:T(8,128)S(1)}, u32[]{:S(2)}, u32[]{:S(2)}) %collective-permute-start.7) | collective-permute-done | bytes 131104 | tf_op jit(solution)/shard_map/ppermute | solution.py:383
  29.4 2.7 %collective-permute-done.8.refs_3_ = f32[2,32,512]{2,1,0:T(8,128)S(1)} collective-permute-done((f32[2,32,512]{2,1,0:T(8,128)S(1)}, f32[2,32,512]{2,1,0:T(8,128)S(1)}, u32[]{:S(2)}, u32[]{:S(2)}) %collective-permute-start.8) | collective-permute-done | bytes 131104 | tf_op jit(solution)/shard_map/ppermute | solution.py:383
  32.1 0.0 collective-permute-done.5.refs_5_
  32.1 0.1 merge.1.own_ref
  32.2 0.1 collective-permute-start.9
  32.3 1.3 %collective-permute-start.10 = (f32[256,512]{1,0:T(8,128)S(1)}, f32[256,512]{1,0:T(8,128)S(1)}, u32[]{:S(2)}, u32[]{:S(2)}) collective-permute-start(f32[256,512]{1,0:T(8,128)S(1)} %slice.3.lead_ref.refs_0_), channel_id=1, source_target_pairs={{0,1},{4,5},{8,9},{12,13},{16,17},{20,21},{24,25},{28,29},{32,33},... | collective-permute-start | bytes 1572872 | tf_op jit(solution)/shard_map/ppermute | solution.py:392
  33.6 2.0 %pick.1 = (f32[256,512]{1,0:T(8,128)S(1)}, f32[256,512]{1,0:T(8,128)S(1)}, f32[256,512]{1,0:T(8,128)S(1)}, f32[256,512]{1,0:T(8,128)S(1)}, s32[4,8]{1,0:T(4,128)S(1)}) custom-call(s32[32]{0:T(128)S(1)} %copy-done.2, f32[256,2048]{1,0:T(8,128)S(1)} %copy-done), custom_call_target="tpu_custom_call" | custom-call | flops 1024 | bytes 1024 | tf_op jit(solution)/shard_map/pick/pallas_call | solution.py:107
  35.6 0.0 copy-start.3
  35.6 0.8 copy-done.3
  36.4 0.8 copy-done.5
  37.2 3.6 %collective-permute-done.9.got_ref = f32[264,512]{1,0:T(8,128)S(1)} collective-permute-done((f32[264,512]{1,0:T(8,128)S(1)}, f32[264,512]{1,0:T(8,128)S(1)}, u32[]{:S(2)}, u32[]{:S(2)}) %collective-permute-start.9) | collective-permute-done | bytes 540704 | tf_op jit(solution)/shard_map/ppermute | solution.py:393
  40.8 0.1 join.2.own_ref
  40.8 0.0 copy-start.6
  40.8 1.2 collective-permute-done.10.refs_1_
  42.1 0.0 collective-permute-start.11
  42.1 0.1 broadcast_select_fusion
  42.2 4.2 %collective-permute-start.12 = (f32[256,512]{1,0:T(8,128)S(1)}, f32[256,512]{1,0:T(8,128)S(1)}, u32[]{:S(2)}, u32[]{:S(2)}) collective-permute-start(f32[256,512]{1,0:T(8,128)S(1)} %broadcast_select_fusion), channel_id=1, source_target_pairs={{0,3},{1,2},{4,7},{5,6},{8,11},{9,10},{12,15},{13,14},{16,19},{17,... | collective-permute-start | bytes 1572872 | tf_op jit(solution)/shard_map/ppermute | solution.py:395
  46.4 5.9 %collective-permute-done.11.got_ref = f32[288,512]{1,0:T(8,128)S(1)} collective-permute-done((f32[288,512]{1,0:T(8,128)S(1)}, f32[288,512]{1,0:T(8,128)S(1)}, u32[]{:S(2)}, u32[]{:S(2)}) %collective-permute-start.11) | collective-permute-done | bytes 589856 | tf_op jit(solution)/shard_map/ppermute | solution.py:396
  52.3 0.1 join.3
  52.4 0.0 copy-start.4
  52.4 2.0 %collective-permute-done.12.refs_2_ = f32[256,512]{1,0:T(8,128)S(1)} collective-permute-done((f32[256,512]{1,0:T(8,128)S(1)}, f32[256,512]{1,0:T(8,128)S(1)}, u32[]{:S(2)}, u32[]{:S(2)}) %collective-permute-start.12) | collective-permute-done | bytes 524320 | tf_op jit(solution)/shard_map/ppermute | solution.py:395
  54.5 7.8 %collective-permute-start.13 = (f32[160,512]{1,0:T(8,128)S(1)}, f32[160,512]{1,0:T(8,128)S(1)}, u32[]{:S(2)}, u32[]{:S(2)}) collective-permute-start(f32[160,512]{1,0:T(8,128)S(1)} %get-tuple-element.101), channel_id=1, source_target_pairs={{0,32},{4,12},{8,40},{16,48},{24,56},{36,44},{68,76},{100,108},{1,... | collective-permute-start | bytes 983048 | tf_op jit(solution)/shard_map/ppermute | solution.py:399
  62.2 4.0 %collective-permute-done.13 = f32[160,512]{1,0:T(8,128)S(1)} collective-permute-done((f32[160,512]{1,0:T(8,128)S(1)}, f32[160,512]{1,0:T(8,128)S(1)}, u32[]{:S(2)}, u32[]{:S(2)}) %collective-permute-start.13) | collective-permute-done | bytes 327712 | tf_op jit(solution)/shard_map/ppermute | solution.py:399
  66.3 2.0 %collective-permute-start.15 = (f32[256,512]{1,0:T(8,128)S(1)}, f32[256,512]{1,0:T(8,128)S(1)}, u32[]{:S(2)}, u32[]{:S(2)}) collective-permute-start(f32[256,512]{1,0:T(8,128)S(1)} %get-tuple-element.104), channel_id=1, source_target_pairs={{0,32},{4,12},{8,40},{12,4},{16,48},{20,28},{24,56},{28,20},{32,0}... | collective-permute-start | bytes 1572872 | tf_op jit(solution)/shard_map/ppermute | solution.py:403
  68.3 3.4 %collective-permute-start.16 = (f32[256,512]{1,0:T(8,128)S(1)}, f32[256,512]{1,0:T(8,128)S(1)}, u32[]{:S(2)}, u32[]{:S(2)}) collective-permute-start(f32[256,512]{1,0:T(8,128)S(1)} %copy-done.6), channel_id=1, source_target_pairs={{0,3},{1,0},{2,1},{3,2},{4,7},{5,4},{6,5},{7,6},{8,11},{9,8},{10,9... | collective-permute-start | bytes 1572872 | tf_op jit(solution)/shard_map/ppermute | solution.py:401
  71.7 1.3 %collective-permute-start.14 = (f32[160,512]{1,0:T(8,128)S(1)}, f32[160,512]{1,0:T(8,128)S(1)}, u32[]{:S(2)}, u32[]{:S(2)}) collective-permute-start(f32[160,512]{1,0:T(8,128)S(1)} %add.10), channel_id=1, source_target_pairs={{0,96},{4,28},{8,104},{12,20},{16,112},{24,120},{32,64},{36,60},{4... | collective-permute-start | bytes 983048 | tf_op jit(solution)/shard_map/ppermute | solution.py:402
  73.0 4.0 %collective-permute-done.14 = f32[160,512]{1,0:T(8,128)S(1)} collective-permute-done((f32[160,512]{1,0:T(8,128)S(1)}, f32[160,512]{1,0:T(8,128)S(1)}, u32[]{:S(2)}, u32[]{:S(2)}) %collective-permute-start.14) | collective-permute-done | bytes 327712 | tf_op jit(solution)/shard_map/ppermute | solution.py:402
  77.0 0.0 collective-permute-done.15
  77.0 0.1 pad_maximum_fusion.refs_5_
  77.1 6.0 %collective-permute-done.16.refs_4_ = f32[256,512]{1,0:T(8,128)S(1)} collective-permute-done((f32[256,512]{1,0:T(8,128)S(1)}, f32[256,512]{1,0:T(8,128)S(1)}, u32[]{:S(2)}, u32[]{:S(2)}) %collective-permute-start.16) | collective-permute-done | bytes 524320 | tf_op jit(solution)/shard_map/ppermute | solution.py:401
  83.1 0.7 collective-permute-start.18
  83.8 0.0 collective-permute-start.19
  83.8 4.6 %collective-permute-start.20 = (f32[256,512]{1,0:T(8,128)S(1)}, f32[256,512]{1,0:T(8,128)S(1)}, u32[]{:S(2)}, u32[]{:S(2)}) collective-permute-start(f32[256,512]{1,0:T(8,128)S(1)} %get-tuple-element.116), channel_id=1, source_target_pairs={{0,2},{1,3},{2,0},{3,1},{4,6},{5,7},{6,4},{7,5},{8,10},{9,11},{10,... | collective-permute-start | bytes 1572872 | tf_op jit(solution)/shard_map/ppermute | solution.py:408
  88.4 0.0 collective-permute-start.17
  88.4 18.2 %factor.1 = (f32[256,256]{1,0:T(8,128)S(1)}, f32[256,256]{1,0:T(8,128)S(1)}, f32[256,256]{1,0:T(8,128)S(1)}) custom-call(f32[160,512]{1,0:T(8,128)S(1)} %add.11.own_ref, f32[160,512]{1,0:T(8,128)S(1)} %collective-permute-done.18.other_ref), custom_call_target="tpu_custom_call" | custom-call | flops 21474836480 | bytes 1048576 | tf_op jit(solution)/shard_map/factor/pallas_call | solution.py:107
  106.6 0.0 copy-start.1
  106.7 0.0 collective-permute-done.19.refs_2_
  106.7 5.1 %collective-permute-done.20.refs_3_ = f32[256,512]{1,0:T(8,128)S(1)} collective-permute-done((f32[256,512]{1,0:T(8,128)S(1)}, f32[256,512]{1,0:T(8,128)S(1)}, u32[]{:S(2)}, u32[]{:S(2)}) %collective-permute-start.20) | collective-permute-done | bytes 524320 | tf_op jit(solution)/shard_map/ppermute | solution.py:408
  111.7 0.8 collective-permute-start.21
  112.5 0.0 collective-permute-start.22
  112.5 2.9 %weigh.1 = (f32[256,512]{1,0:T(8,128)}, f32[256,512]{1,0:T(8,128)S(1)}) custom-call(f32[256,512]{1,0:T(8,128)S(1)} %slice.3.lead_ref.refs_0_, f32[256,512]{1,0:T(8,128)S(1)} %collective-permute-done.10.refs_1_, f32[256,512]{1,0:T(8,128)S(1)} %collective-permute-done.12.refs_2_, f32[256,256]{1,0:T(8,128)S(1)} %get-tuple-element.118.refs_3_, ...), custom_call_target="tpu_custom_call" | custom-call | flops 1024 | bytes 1024 | tf_op jit(solution)/shard_map/weigh/pallas_call | solution.py:282
  115.5 0.0 collective-permute-done.21.refs_7_
  115.5 0.8 collective-permute-done.22.refs_8_
  116.3 8.6 %update.1 = f32[256,2048]{1,0:T(8,128)} custom-call(s32[4,8]{1,0:T(4,128)S(1)} %get-tuple-element.122.plan, f32[256,512]{1,0:T(8,128)S(1)} %get-tuple-element.123.refs_0_, f32[256,512]{1,0:T(8,128)S(1)} %get-tuple-element.124.refs_1_, f32[256,512]{1,0:T(8,128)S(1)} %collective-permute-done.19.refs_2_, f32[256,512]{1,0:T(8,128)S(1)} %collective-permute-done.20.refs_3_, ...), custom_call_target="tpu_custom_call" | custom-call | tf_op jit(solution)/shard_map/update/pallas_call | solution.py:330
  (12 shorter events, 0.2 us)
Async XLA Ops:
  0.6 19.2 %copy-start.2 = (s32[32]{0:T(128)S(1)}, s32[32]{0:T(128)}, u32[]{:S(2)}) copy-start(s32[32]{0:T(128)} %map_ref.3) | copy-start | bytes 388
  1.7 5.0 %collective-permute-start.1 = (f32[256,512]{1,0:T(8,128)S(1)}, f32[256,512]{1,0:T(8,128)S(1)}, u32[]{:S(2)}, u32[]{:S(2)}) collective-permute-start(f32[256,512]{1,0:T(8,128)S(1)} %slice.3.lead_ref.refs_0_), channel_id=1, source_target_pairs={{0,4},{4,0},{8,12},{12,8},{16,20},{20,16},{24,28},{28,24},{32,36},... | collective-permute-start | bytes 1572872 | tf_op jit(solution)/shard_map/ppermute | solution.py:373
  3.3 30.3 %copy-start = (f32[256,2048]{1,0:T(8,128)S(1)}, f32[256,2048]{1,0:T(8,128)}, u32[]{:S(2)}) copy-start(f32[256,2048]{1,0:T(8,128)} %front_ref.1) | copy-start | bytes 6291460
  3.3 17.6 %collective-permute-start = (f32[160,512]{1,0:T(8,128)S(1)}, f32[160,512]{1,0:T(8,128)S(1)}, u32[]{:S(2)}, u32[]{:S(2)}) collective-permute-start(f32[160,512]{1,0:T(8,128)S(1)} %corner.1), channel_id=1, source_target_pairs={{0,1},{4,5}} | collective-permute-start | bytes 983048 | tf_op jit(solution)/shard_map/ppermute | solution.py:371
  6.8 10.7 %collective-permute-start.2 = (f32[2,32,512]{2,1,0:T(8,128)S(1)}, f32[2,32,512]{2,1,0:T(8,128)S(1)}, u32[]{:S(2)}, u32[]{:S(2)}) collective-permute-start(f32[2,32,512]{2,1,0:T(8,128)S(1)} %get-tuple-element.67), channel_id=1, source_target_pairs={{8,16},{12,20},{16,24},{20,28},{24,0},{28,4},{32,40},{36,44},{40,4... | collective-permute-start | bytes 393224 | tf_op jit(solution)/shard_map/ppermute | solution.py:377
  8.1 9.4 %collective-permute-start.3 = (f32[2,32,512]{2,1,0:T(8,128)S(1)}, f32[2,32,512]{2,1,0:T(8,128)S(1)}, u32[]{:S(2)}, u32[]{:S(2)}) collective-permute-start(f32[2,32,512]{2,1,0:T(8,128)S(1)} %get-tuple-element.68), channel_id=1, source_target_pairs={{8,24},{12,28},{16,0},{20,4},{24,8},{28,12},{32,48},{36,52},{40,56... | collective-permute-start | bytes 393224 | tf_op jit(solution)/shard_map/ppermute | solution.py:377
  9.4 10.4 %collective-permute-start.4 = (f32[2,32,512]{2,1,0:T(8,128)S(1)}, f32[2,32,512]{2,1,0:T(8,128)S(1)}, u32[]{:S(2)}, u32[]{:S(2)}) collective-permute-start(f32[2,32,512]{2,1,0:T(8,128)S(1)} %get-tuple-element.69), channel_id=1, source_target_pairs={{8,0},{12,4},{16,8},{20,12},{24,16},{28,20},{32,56},{36,60},{40,32... | collective-permute-start | bytes 393224 | tf_op jit(solution)/shard_map/ppermute | solution.py:377
  20.9 11.2 %collective-permute-start.5 = (f32[160,512]{1,0:T(8,128)S(1)}, f32[160,512]{1,0:T(8,128)S(1)}, u32[]{:S(2)}, u32[]{:S(2)}) collective-permute-start(f32[160,512]{1,0:T(8,128)S(1)} %add.9.refs_4_), channel_id=1, source_target_pairs={{0,3},{1,2},{4,7},{5,6}} | collective-permute-start | bytes 983048 | tf_op jit(solution)/shard_map/ppermute | solution.py:385
  23.7 4.4 %collective-permute-start.6 = (f32[2,32,512]{2,1,0:T(8,128)S(1)}, f32[2,32,512]{2,1,0:T(8,128)S(1)}, u32[]{:S(2)}, u32[]{:S(2)}) collective-permute-start(f32[2,32,512]{2,1,0:T(8,128)S(1)} %get-tuple-element.77), channel_id=1, source_target_pairs={{0,1},{4,5},{8,9},{12,13},{16,17},{20,21},{24,25},{28,29},{32,33},... | collective-permute-start | bytes 393224 | tf_op jit(solution)/shard_map/ppermute | solution.py:383
  25.4 4.0 %collective-permute-start.7 = (f32[2,32,512]{2,1,0:T(8,128)S(1)}, f32[2,32,512]{2,1,0:T(8,128)S(1)}, u32[]{:S(2)}, u32[]{:S(2)}) collective-permute-start(f32[2,32,512]{2,1,0:T(8,128)S(1)} %get-tuple-element.78), channel_id=1, source_target_pairs={{0,2},{4,6},{8,10},{12,14},{16,18},{20,22},{24,26},{28,30},{32,34}... | collective-permute-start | bytes 393224 | tf_op jit(solution)/shard_map/ppermute | solution.py:383
  26.7 5.4 %collective-permute-start.8 = (f32[2,32,512]{2,1,0:T(8,128)S(1)}, f32[2,32,512]{2,1,0:T(8,128)S(1)}, u32[]{:S(2)}, u32[]{:S(2)}) collective-permute-start(f32[2,32,512]{2,1,0:T(8,128)S(1)} %get-tuple-element.79), channel_id=1, source_target_pairs={{0,3},{4,7},{8,11},{12,15},{16,19},{20,23},{24,27},{28,31},{32,35}... | collective-permute-start | bytes 393224 | tf_op jit(solution)/shard_map/ppermute | solution.py:383
  32.2 8.6 %collective-permute-start.9 = (f32[264,512]{1,0:T(8,128)S(1)}, f32[264,512]{1,0:T(8,128)S(1)}, u32[]{:S(2)}, u32[]{:S(2)}) collective-permute-start(f32[264,512]{1,0:T(8,128)S(1)} %merge.1.own_ref), channel_id=1, source_target_pairs={{0,8},{4,36},{8,0},{12,44},{16,24},{20,52},{24,16},{28,60},{32,40}... | collective-permute-start | bytes 1622024 | tf_op jit(solution)/shard_map/ppermute | solution.py:393
  32.3 9.8 %collective-permute-start.10 = (f32[256,512]{1,0:T(8,128)S(1)}, f32[256,512]{1,0:T(8,128)S(1)}, u32[]{:S(2)}, u32[]{:S(2)}) collective-permute-start(f32[256,512]{1,0:T(8,128)S(1)} %slice.3.lead_ref.refs_0_), channel_id=1, source_target_pairs={{0,1},{4,5},{8,9},{12,13},{16,17},{20,21},{24,25},{28,29},{32,33},... | collective-permute-start | bytes 1572872 | tf_op jit(solution)/shard_map/ppermute | solution.py:392
  35.6 0.8 copy-start.3
  36.4 0.8 copy-start.5
  40.8 27.4 %copy-start.6 = (f32[256,512]{1,0:T(8,128)S(1)}, f32[256,512]{1,0:T(8,128)}, u32[]{:S(2)}) copy-start(f32[256,512]{1,0:T(8,128)} %copy-done.5) | copy-start | bytes 1572868
  42.1 10.2 %collective-permute-start.11 = (f32[288,512]{1,0:T(8,128)S(1)}, f32[288,512]{1,0:T(8,128)S(1)}, u32[]{:S(2)}, u32[]{:S(2)}) collective-permute-start(f32[288,512]{1,0:T(8,128)S(1)} %join.2.own_ref), channel_id=1, source_target_pairs={{0,24},{4,100},{8,16},{12,108},{16,8},{20,116},{24,0},{28,124},{32... | collective-permute-start | bytes 1769480 | tf_op jit(solution)/shard_map/ppermute | solution.py:396
  42.2 12.3 %collective-permute-start.12 = (f32[256,512]{1,0:T(8,128)S(1)}, f32[256,512]{1,0:T(8,128)S(1)}, u32[]{:S(2)}, u32[]{:S(2)}) collective-permute-start(f32[256,512]{1,0:T(8,128)S(1)} %broadcast_select_fusion), channel_id=1, source_target_pairs={{0,3},{1,2},{4,7},{5,6},{8,11},{9,10},{12,15},{13,14},{16,19},{17,... | collective-permute-start | bytes 1572872 | tf_op jit(solution)/shard_map/ppermute | solution.py:395
  52.4 31.4 %copy-start.4 = (f32[256,512]{1,0:T(8,128)S(1)}, f32[256,512]{1,0:T(8,128)}, u32[]{:S(2)}) copy-start(f32[256,512]{1,0:T(8,128)} %copy-done.3) | copy-start | bytes 1572868
  54.5 11.8 %collective-permute-start.13 = (f32[160,512]{1,0:T(8,128)S(1)}, f32[160,512]{1,0:T(8,128)S(1)}, u32[]{:S(2)}, u32[]{:S(2)}) collective-permute-start(f32[160,512]{1,0:T(8,128)S(1)} %get-tuple-element.101), channel_id=1, source_target_pairs={{0,32},{4,12},{8,40},{16,48},{24,56},{36,44},{68,76},{100,108},{1,... | collective-permute-start | bytes 983048 | tf_op jit(solution)/shard_map/ppermute | solution.py:399
  66.3 10.7 %collective-permute-start.15 = (f32[256,512]{1,0:T(8,128)S(1)}, f32[256,512]{1,0:T(8,128)S(1)}, u32[]{:S(2)}, u32[]{:S(2)}) collective-permute-start(f32[256,512]{1,0:T(8,128)S(1)} %get-tuple-element.104), channel_id=1, source_target_pairs={{0,32},{4,12},{8,40},{12,4},{16,48},{20,28},{24,56},{28,20},{32,0}... | collective-permute-start | bytes 1572872 | tf_op jit(solution)/shard_map/ppermute | solution.py:403
  68.3 14.8 %collective-permute-start.16 = (f32[256,512]{1,0:T(8,128)S(1)}, f32[256,512]{1,0:T(8,128)S(1)}, u32[]{:S(2)}, u32[]{:S(2)}) collective-permute-start(f32[256,512]{1,0:T(8,128)S(1)} %copy-done.6), channel_id=1, source_target_pairs={{0,3},{1,0},{2,1},{3,2},{4,7},{5,4},{6,5},{7,6},{8,11},{9,8},{10,9... | collective-permute-start | bytes 1572872 | tf_op jit(solution)/shard_map/ppermute | solution.py:401
  71.7 5.3 %collective-permute-start.14 = (f32[160,512]{1,0:T(8,128)S(1)}, f32[160,512]{1,0:T(8,128)S(1)}, u32[]{:S(2)}, u32[]{:S(2)}) collective-permute-start(f32[160,512]{1,0:T(8,128)S(1)} %add.10), channel_id=1, source_target_pairs={{0,96},{4,28},{8,104},{12,20},{16,112},{24,120},{32,64},{36,60},{4... | collective-permute-start | bytes 983048 | tf_op jit(solution)/shard_map/ppermute | solution.py:402
  83.1 5.3 %collective-permute-start.18 = (f32[160,512]{1,0:T(8,128)S(1)}, f32[160,512]{1,0:T(8,128)S(1)}, u32[]{:S(2)}, u32[]{:S(2)}) collective-permute-start(f32[160,512]{1,0:T(8,128)S(1)} %add.11.own_ref), channel_id=1, source_target_pairs={{0,4},{4,0},{8,12},{12,8},{16,20},{20,16},{24,28},{28,24},{32,36},... | collective-permute-start | bytes 983048 | tf_op jit(solution)/shard_map/ppermute | solution.py:405
  83.8 22.8 %collective-permute-start.19 = (f32[256,512]{1,0:T(8,128)S(1)}, f32[256,512]{1,0:T(8,128)S(1)}, u32[]{:S(2)}, u32[]{:S(2)}) collective-permute-start(f32[256,512]{1,0:T(8,128)S(1)} %copy-done.4), channel_id=1, source_target_pairs={{0,1},{1,2},{2,3},{3,0},{4,5},{5,6},{6,7},{7,4},{8,9},{9,10},{10,1... | collective-permute-start | bytes 1572872 | tf_op jit(solution)/shard_map/ppermute | solution.py:408
  83.8 27.9 %collective-permute-start.20 = (f32[256,512]{1,0:T(8,128)S(1)}, f32[256,512]{1,0:T(8,128)S(1)}, u32[]{:S(2)}, u32[]{:S(2)}) collective-permute-start(f32[256,512]{1,0:T(8,128)S(1)} %get-tuple-element.116), channel_id=1, source_target_pairs={{0,2},{1,3},{2,0},{3,1},{4,6},{5,7},{6,4},{7,5},{8,10},{9,11},{10,... | collective-permute-start | bytes 1572872 | tf_op jit(solution)/shard_map/ppermute | solution.py:408
  88.4 23.3 %collective-permute-start.17 = (f32[512,512]{1,0:T(8,128)S(1)}, f32[512,512]{1,0:T(8,128)S(1)}, u32[]{:S(2)}, u32[]{:S(2)}) collective-permute-start(f32[512,512]{1,0:T(8,128)S(1)} %pad_maximum_fusion.refs_5_), channel_id=1, source_target_pairs={{0,96},{4,28},{8,104},{12,20},{16,112},{20,12},{24,120},{28,4},{32... | collective-permute-start | bytes 3145736 | tf_op jit(solution)/shard_map/ppermute | solution.py:406
  106.6 9.7 %copy-start.1 = (f32[256,2048]{1,0:T(8,128)S(1)}, f32[256,2048]{1,0:T(8,128)}, u32[]{:S(2)}) copy-start(f32[256,2048]{1,0:T(8,128)} %refs_9_.1) | copy-start | bytes 6291460
  111.7 3.7 %collective-permute-start.21 = (f32[512,512]{1,0:T(8,128)S(1)}, f32[512,512]{1,0:T(8,128)S(1)}, u32[]{:S(2)}, u32[]{:S(2)}) collective-permute-start(f32[512,512]{1,0:T(8,128)S(1)} %pad_maximum_fusion.refs_5_), channel_id=1, source_target_pairs={{0,4},{4,0},{8,12},{12,8},{16,20},{20,16},{24,28},{28,24},{32,36},... | collective-permute-start | bytes 3145736 | tf_op jit(solution)/shard_map/ppermute | solution.py:413
  112.5 3.8 %collective-permute-start.22 = (f32[512,512]{1,0:T(8,128)S(1)}, f32[512,512]{1,0:T(8,128)S(1)}, u32[]{:S(2)}, u32[]{:S(2)}) collective-permute-start(f32[512,512]{1,0:T(8,128)S(1)} %collective-permute-done.17.refs_6_), channel_id=1, source_target_pairs={{0,4},{4,0},{8,12},{12,8},{16,20},{20,16},{24,28},{28,24},{32,36},... | collective-permute-start | bytes 3145736 | tf_op jit(solution)/shard_map/ppermute | solution.py:412

commit v12 on v9

--- a/solution.py
+++ b/solution.py
@@ -297,48 +297,53 @@
 def update_kernel(plan, *refs):
     weight_ref, pieces, gathered = refs[0], refs[1:5], refs[5:9]
     base_ref, out_ref, ahead_ref = refs[9:]
-    slot = pl.program_id(0)
     plane, line, core, _ = position()
-    group, place = plan[1, slot], plan[2, slot]
-    for parity in range(2):
-        holder = core if parity == 0 else 1 - core
-        for x in range(4):
-            off_z, off_x = plane ^ group, line ^ x
-            first = jnp.where(holder == 0, off_x, off_z)
-            second = jnp.where(holder == 0, off_z, off_x)
-            index = (first >> 1) + 2 * ((second & 1) ^ (second >> 1)) + 4 * (second >> 1)
-            rows = pl.ds(pl.multiple_of(index * 64 + place * 32, 32), 32)
-            into = pl.ds(pl.multiple_of((2 * x + holder) * 32, 32), 32)
-            for late in range(2):
-
-                @pl.when(((first & 1) ^ (first >> 1)) == late)
-                def _():
-                    ahead_ref[into, :] = gathered[2 * parity + late][rows, :]
-
-    product = dot(weight_ref[...], ahead_ref[...], 1, 1)
-    column = pl.multiple_of(place * PW, PW)
-    base = base_ref[...]
-    out_ref[...] = base
-    for index, ref in enumerate(pieces):
-
-        @pl.when((plan[0, slot] == index) & (plan[3, slot] == 1))
+    for half in range(2):
+        slot = 2 * pl.program_id(0) + half
+        group, place = plan[1, slot], plan[2, slot]
+        for parity in range(2):
+            holder = core if parity == 0 else 1 - core
+            for x in range(4):
+                off_z, off_x = plane ^ group, line ^ x
+                first = jnp.where(holder == 0, off_x, off_z)
+                second = jnp.where(holder == 0, off_z, off_x)
+                index = (first >> 1) + 2 * ((second & 1) ^ (second >> 1)) + 4 * (second >> 1)
+                rows = pl.ds(pl.multiple_of(index * 64 + place * 32, 32), 32)
+                into = pl.ds(pl.multiple_of((2 * x + holder) * 32, 32), 32)
+                for late in range(2):
+
+                    @pl.when(((first & 1) ^ (first >> 1)) == late)
+                    def _():
+                        ahead_ref[half, into, :] = gathered[2 * parity + late][rows, :]
+
+        product = dot(weight_ref[...], ahead_ref[half], 1, 1)
+        column = pl.multiple_of(place * PW, PW)
+        here = slice(half * PW, half * PW + PW)
+
+        @pl.when(plan[3, slot] == 0)
         def _():
-            out_ref[...] = base + (ref[:, pl.ds(column, PW)] - product)
+            out_ref[:, here] = base_ref[:, here]
+
+        for index, ref in enumerate(pieces):
+
+            @pl.when((plan[0, slot] == index) & (plan[3, slot] == 1))
+            def _():
+                out_ref[:, here] = base_ref[:, here] + (ref[:, pl.ds(column, PW)] - product)
 
 
 def update(plan, weight, pieces, gathered, base):
     height, width = base.shape
     whole = pl.BlockSpec(memory_space=pltpu.VMEM)
-    tile = pl.BlockSpec((height, PW), lambda u, plan: (0, u))
+    tile = pl.BlockSpec((height, 2 * PW), lambda u, plan: (0, u))
     return pl.pallas_call(
         update_kernel,
         out_shape=jax.ShapeDtypeStruct(base.shape, jnp.float32),
         grid_spec=pltpu.PrefetchScalarGridSpec(
             num_scalar_prefetch=1,
-            grid=(width // PW,),
+            grid=(width // (2 * PW),),
             in_specs=[whole] * 9 + [tile],
             out_specs=tile,
-            scratch_shapes=[pltpu.VMEM((PW, LEAD), jnp.float32)],
+            scratch_shapes=[pltpu.VMEM((2, PW, LEAD), jnp.float32)],
         ),
         compiler_params=pltpu.CompilerParams(vmem_limit_bytes=16 << 20),
         name="update",
@@ -393,18 +398,18 @@
     near = lax.ppermute(lead, "col", [(0, 1)])
     load = local_call(partial(join_kernel, 64), "join", [(128 + BLOCK, LEAD)])(load, lax.ppermute(load, "row", every[1]))[0]
     load, near, *pieces = lax.optimization_barrier((load, near, *pieces))
+    load = local_call(partial(join_kernel, 128), "join", [(256 + BLOCK, LEAD)])(load, lax.ppermute(load, "row", every[2]))[0]
+    load, near, lead, *pieces = lax.optimization_barrier((load, near, lead, *pieces))
     far = lax.ppermute(jnp.where(lax.axis_index("col") == 1, near, lead), "col", [(0, 3), (1, 2)])
-    load = local_call(partial(join_kernel, 128), "join", [(256 + BLOCK, LEAD)])(load, lax.ppermute(load, "row", every[2]))[0]
-    load, far, *pieces = lax.optimization_barrier((load, far, *pieces))
+    pieces[3] = lax.ppermute(pieces[3], "col", ring[3])
     gathered, block = local_call(partial(join_kernel, 256), "join", [(512, LEAD), (BLOCK, LEAD)])(
         load, lax.ppermute(load, "row", every[3])
     )
-    for hop in (1, 3):
-        pieces[hop] = lax.ppermute(pieces[hop], "col", ring[hop])
-    block, gathered, *pieces = lax.optimization_barrier((block, gathered, *pieces))
+    block, gathered, far, *pieces = lax.optimization_barrier((block, gathered, far, *pieces))
     other = lax.ppermute(block, "row", swap)
     late = lax.ppermute(gathered, "row", every[0])
-    pieces[2] = lax.ppermute(pieces[2], "col", ring[2])
+    for hop in (1, 2):
+        pieces[hop] = lax.ppermute(pieces[hop], "col", ring[hop])
 
     inverse = factor(block, other)
     late, gathered, inverse, pieces = lax.optimization_barrier((late, gathered, inverse, pieces))

time: 114 us -> 128 us (1.12)
  waiting for transfers between devices: 36.4 us -> 52.9 us
  starting transfers between devices: 39.4 us -> 36.1 us
  Pallas kernels: 33.1 us -> 36 us
  local copies, waits for them, and re-layouts: 2.69 us -> 1.13 us
    ppermute x1, waiting for transfers between devices: 0.01 us -> 9.57 us  [shards(): pieces[3] = lax.ppermute(pieces[3], 'col', ring[3])]
    ppermute x1, waiting for transfers between devices: 3.78 us -> 9.01 us  [shards(): lax.ppermute(load, 'row', every[2])]
    ppermute x2, waiting for transfers between devices: 0.01 us -> 5.06 us  [shards(): pieces[hop] = lax.ppermute(pieces[hop], 'col', ring[hop])]
    ppermute x1, waiting for transfers between devices: 3.1 us -> 0.01 us  [shards(): lax.ppermute(jnp.where(lax.axis_index('col') == 1, near, lead), 'col', [(...]
    pallas_call x1, Pallas kernels: 8.58 us -> 11.4 us  [update(): pl.pallas_call(update_kernel, out_shape=jax.ShapeDtypeStruct(base.shape,...]
    ppermute x1, starting transfers between devices: 2.75 us -> 0.07 us  [shards(): pieces[3] = lax.ppermute(pieces[3], 'col', ring[3])]
    ppermute x1, waiting for transfers between devices: 9.54 us -> 7.68 us  [shards(): lax.ppermute(load, 'row', every[3])]
    unnamed x14 -> x16, local copies, waits for them, and re-layouts: 1.61 us -> 0.05 us
  transfers between devices with their start and end apart: 23 -> 23, of which waited for: 9 -> 10; matrix products, arithmetic and copies ran while one was open for 0% -> 0% of each run, Pallas kernels for 22% -> 19%
where the time goes in v12:
time: 128 us; the launch traced here: 127 us
  waiting for transfers between devices  52.9 us (41%)
  starting transfers between devices  36.1 us (28%)
  Pallas kernels  36 us (28%)
    pallas_call x9, Pallas kernels, call(): pl.pallas_call(kernel, out_shape=[jax.ShapeDtypeStruct(shape, jnp.float32...  21.7 us
    ppermute x3, waiting for transfers between devices, shards(): parts[hop] = lax.ppermute(parts[hop], 'row', pairs)  12.5 us
    pallas_call x1, Pallas kernels, update(): pl.pallas_call(update_kernel, out_shape=jax.ShapeDtypeStruct(base.shape,...  11.4 us
    ppermute x1, waiting for transfers between devices, shards(): pieces[3] = lax.ppermute(pieces[3], 'col', ring[3])  9.57 us
    ppermute x1, waiting for transfers between devices, shards(): lax.ppermute(load, 'row', every[2])  9.01 us
    ppermute x1, waiting for transfers between devices, shards(): lax.ppermute(load, 'row', every[3])  7.68 us
    ppermute x3, starting transfers between devices, shards(): lax.ppermute(blocks[0], ('row', 'col'), [(4 * core, 4 * core + to) for co...  7.34 us
    ppermute x1, waiting for transfers between devices, shards(): lax.ppermute(load, 'row', every[1])  6.32 us
  transfers between devices with their start and end apart: 23, of which 10 were waited for; matrix products, arithmetic and copies ran while one was open for 0% of the time, Pallas kernels for 19%

profile of v12, /device:TPU:1, one launch (start us, length us, event | category | flops | bytes accessed | tf_op | source)
XLA Modules:
  0.0 127.3 jit_solution(14007161205984106766)
XLA Ops:
  0.6 1.1 slice.3.lead_ref.refs_0_
  1.7 1.5 %collective-permute-start.3 = (f32[256,512]{1,0:T(8,128)S(1)}, f32[256,512]{1,0:T(8,128)S(1)}, u32[]{:S(2)}, u32[]{:S(2)}) collective-permute-start(f32[256,512]{1,0:T(8,128)S(1)} %slice.3.lead_ref.refs_0_), channel_id=1, source_target_pairs={{0,4},{4,0},{8,12},{12,8},{16,20},{20,16},{24,28},{28,24},{32,36},... | collective-permute-start | bytes 1572872 | tf_op jit(solution)/shard_map/ppermute | solution.py:379
  3.2 0.1 corner.1
  3.3 4.7 %collective-permute-start.2 = (f32[160,512]{1,0:T(8,128)S(1)}, f32[160,512]{1,0:T(8,128)S(1)}, u32[]{:S(2)}, u32[]{:S(2)}) collective-permute-start(f32[160,512]{1,0:T(8,128)S(1)} %corner.1), channel_id=1, source_target_pairs={{0,3},{4,7}} | collective-permute-start | bytes 983048 | tf_op jit(solution)/shard_map/ppermute | solution.py:377
  8.0 1.3 %collective-permute-start.1 = (f32[160,512]{1,0:T(8,128)S(1)}, f32[160,512]{1,0:T(8,128)S(1)}, u32[]{:S(2)}, u32[]{:S(2)}) collective-permute-start(f32[160,512]{1,0:T(8,128)S(1)} %corner.1), channel_id=1, source_target_pairs={{0,2},{4,6}} | collective-permute-start | bytes 983048 | tf_op jit(solution)/shard_map/ppermute | solution.py:377
  9.3 1.3 %collective-permute-start = (f32[160,512]{1,0:T(8,128)S(1)}, f32[160,512]{1,0:T(8,128)S(1)}, u32[]{:S(2)}, u32[]{:S(2)}) collective-permute-start(f32[160,512]{1,0:T(8,128)S(1)} %corner.1), channel_id=1, source_target_pairs={{0,1},{4,5}} | collective-permute-start | bytes 983048 | tf_op jit(solution)/shard_map/ppermute | solution.py:377
  10.6 0.0 collective-permute-done.3.mate_ref
  10.7 0.1 share.1
  10.8 0.0 copy-start
  10.8 1.4 %collective-permute-start.4 = (f32[2,32,512]{2,1,0:T(8,128)S(1)}, f32[2,32,512]{2,1,0:T(8,128)S(1)}, u32[]{:S(2)}, u32[]{:S(2)}) collective-permute-start(f32[2,32,512]{2,1,0:T(8,128)S(1)} %get-tuple-element.68), channel_id=1, source_target_pairs={{8,16},{12,20},{16,24},{20,28},{24,0},{28,4},{32,40},{36,44},{40,4... | collective-permute-start | bytes 393224 | tf_op jit(solution)/shard_map/ppermute | solution.py:383
  12.2 1.3 %collective-permute-start.5 = (f32[2,32,512]{2,1,0:T(8,128)S(1)}, f32[2,32,512]{2,1,0:T(8,128)S(1)}, u32[]{:S(2)}, u32[]{:S(2)}) collective-permute-start(f32[2,32,512]{2,1,0:T(8,128)S(1)} %get-tuple-element.69), channel_id=1, source_target_pairs={{8,24},{12,28},{16,0},{20,4},{24,8},{28,12},{32,48},{36,52},{40,56... | collective-permute-start | bytes 393224 | tf_op jit(solution)/shard_map/ppermute | solution.py:383
  13.5 8.1 %collective-permute-done.4.refs_1_ = f32[2,32,512]{2,1,0:T(8,128)S(1)} collective-permute-done((f32[2,32,512]{2,1,0:T(8,128)S(1)}, f32[2,32,512]{2,1,0:T(8,128)S(1)}, u32[]{:S(2)}, u32[]{:S(2)}) %collective-permute-start.4) | collective-permute-done | bytes 131104 | tf_op jit(solution)/shard_map/ppermute | solution.py:383
  21.6 1.3 %collective-permute-start.6 = (f32[2,32,512]{2,1,0:T(8,128)S(1)}, f32[2,32,512]{2,1,0:T(8,128)S(1)}, u32[]{:S(2)}, u32[]{:S(2)}) collective-permute-start(f32[2,32,512]{2,1,0:T(8,128)S(1)} %get-tuple-element.70), channel_id=1, source_target_pairs={{8,0},{12,4},{16,8},{20,12},{24,16},{28,20},{32,56},{36,60},{40,32... | collective-permute-start | bytes 393224 | tf_op jit(solution)/shard_map/ppermute | solution.py:383
  22.9 0.0 collective-permute-done.5.refs_2_
  22.9 4.4 %collective-permute-done.6.refs_3_ = f32[2,32,512]{2,1,0:T(8,128)S(1)} collective-permute-done((f32[2,32,512]{2,1,0:T(8,128)S(1)}, f32[2,32,512]{2,1,0:T(8,128)S(1)}, u32[]{:S(2)}, u32[]{:S(2)}) %collective-permute-start.6) | collective-permute-done | bytes 131104 | tf_op jit(solution)/shard_map/ppermute | solution.py:383
  27.3 1.0 sort.1
  28.3 0.0 collective-permute-done.2
  28.3 0.0 collective-permute-done.1
  28.3 0.0 collective-permute-done
  28.3 0.1 add_add_fusion.refs_4_
  28.5 1.3 %collective-permute-start.7 = (f32[160,512]{1,0:T(8,128)S(1)}, f32[160,512]{1,0:T(8,128)S(1)}, u32[]{:S(2)}, u32[]{:S(2)}) collective-permute-start(f32[160,512]{1,0:T(8,128)S(1)} %add_add_fusion.refs_4_), channel_id=1, source_target_pairs={{0,8},{4,36},{1,9},{5,37},{2,10},{6,38},{3,11},{7,39}} | collective-permute-start | bytes 983048 | tf_op jit(solution)/shard_map/ppermute | solution.py:391
  29.8 1.3 %collective-permute-start.8 = (f32[2,32,512]{2,1,0:T(8,128)S(1)}, f32[2,32,512]{2,1,0:T(8,128)S(1)}, u32[]{:S(2)}, u32[]{:S(2)}) collective-permute-start(f32[2,32,512]{2,1,0:T(8,128)S(1)} %get-tuple-element.80), channel_id=1, source_target_pairs={{0,1},{4,5},{8,9},{12,13},{16,17},{20,21},{24,25},{28,29},{32,33},... | collective-permute-start | bytes 393224 | tf_op jit(solution)/shard_map/ppermute | solution.py:389
  31.1 1.3 %collective-permute-start.9 = (f32[2,32,512]{2,1,0:T(8,128)S(1)}, f32[2,32,512]{2,1,0:T(8,128)S(1)}, u32[]{:S(2)}, u32[]{:S(2)}) collective-permute-start(f32[2,32,512]{2,1,0:T(8,128)S(1)} %get-tuple-element.81), channel_id=1, source_target_pairs={{0,2},{4,6},{8,10},{12,14},{16,18},{20,22},{24,26},{28,30},{32,34}... | collective-permute-start | bytes 393224 | tf_op jit(solution)/shard_map/ppermute | solution.py:389
  32.4 1.3 %collective-permute-start.10 = (f32[2,32,512]{2,1,0:T(8,128)S(1)}, f32[2,32,512]{2,1,0:T(8,128)S(1)}, u32[]{:S(2)}, u32[]{:S(2)}) collective-permute-start(f32[2,32,512]{2,1,0:T(8,128)S(1)} %get-tuple-element.82), channel_id=1, source_target_pairs={{0,3},{4,7},{8,11},{12,15},{16,19},{20,23},{24,27},{28,31},{32,35}... | collective-permute-start | bytes 393224 | tf_op jit(solution)/shard_map/ppermute | solution.py:389
  33.7 0.0 collective-permute-done.8.refs_1_
  33.7 0.7 collective-permute-done.9.refs_2_
  34.4 1.2 collective-permute-done.10.refs_3_
  35.6 0.0 collective-permute-done.7.refs_5_
  35.6 0.1 merge.1.own_ref
  35.7 0.1 collective-permute-start.11
  35.8 1.3 %collective-permute-start.12 = (f32[256,512]{1,0:T(8,128)S(1)}, f32[256,512]{1,0:T(8,128)S(1)}, u32[]{:S(2)}, u32[]{:S(2)}) collective-permute-start(f32[256,512]{1,0:T(8,128)S(1)} %slice.3.lead_ref.refs_0_), channel_id=1, source_target_pairs={{0,1},{4,5},{8,9},{12,13},{16,17},{20,21},{24,25},{28,29},{32,33},... | collective-permute-start | bytes 1572872 | tf_op jit(solution)/shard_map/ppermute | solution.py:398
  37.1 2.0 %pick.1 = (f32[256,512]{1,0:T(8,128)S(1)}, f32[256,512]{1,0:T(8,128)S(1)}, f32[256,512]{1,0:T(8,128)S(1)}, f32[256,512]{1,0:T(8,128)S(1)}, s32[4,8]{1,0:T(4,128)S(1)}) custom-call(s32[32]{0:T(128)S(1)} %copy-done.2, f32[256,2048]{1,0:T(8,128)S(1)} %copy-done), custom_call_target="tpu_custom_call" | custom-call | flops 1024 | bytes 1024 | tf_op jit(solution)/shard_map/pick/pallas_call | solution.py:109
  39.1 0.0 copy-start.5
  39.1 0.0 copy-start.3
  39.2 6.3 %collective-permute-done.11.got_ref = f32[264,512]{1,0:T(8,128)S(1)} collective-permute-done((f32[264,512]{1,0:T(8,128)S(1)}, f32[264,512]{1,0:T(8,128)S(1)}, u32[]{:S(2)}, u32[]{:S(2)}) %collective-permute-start.11) | collective-permute-done | bytes 540704 | tf_op jit(solution)/shard_map/ppermute | solution.py:399
  45.5 0.1 join.3.own_ref
  45.5 0.0 collective-permute-done.12.refs_1_
  45.5 0.1 collective-permute-start.13
  45.6 9.0 %collective-permute-done.13.got_ref = f32[288,512]{1,0:T(8,128)S(1)} collective-permute-done((f32[288,512]{1,0:T(8,128)S(1)}, f32[288,512]{1,0:T(8,128)S(1)}, u32[]{:S(2)}, u32[]{:S(2)}) %collective-permute-start.13) | collective-permute-done | bytes 589856 | tf_op jit(solution)/shard_map/ppermute | solution.py:401
  54.6 0.1 join.4.own_ref
  54.7 0.1 collective-permute-start.14
  54.8 0.0 copy-start.6
  54.9 0.0 copy-start.4
  54.9 0.1 broadcast_select_fusion
  55.0 5.1 %collective-permute-start.15 = (f32[256,512]{1,0:T(8,128)S(1)}, f32[256,512]{1,0:T(8,128)S(1)}, u32[]{:S(2)}, u32[]{:S(2)}) collective-permute-start(f32[256,512]{1,0:T(8,128)S(1)} %broadcast_select_fusion), channel_id=1, source_target_pairs={{0,3},{1,2},{4,7},{5,6},{8,11},{9,10},{12,15},{13,14},{16,19},{17,... | collective-permute-start | bytes 1572872 | tf_op jit(solution)/shard_map/ppermute | solution.py:403
  60.1 0.1 collective-permute-start.16
  60.2 7.7 %collective-permute-done.14.got_ref = f32[416,512]{1,0:T(8,128)S(1)} collective-permute-done((f32[416,512]{1,0:T(8,128)S(1)}, f32[416,512]{1,0:T(8,128)S(1)}, u32[]{:S(2)}, u32[]{:S(2)}) %collective-permute-start.14) | collective-permute-done | bytes 852000 | tf_op jit(solution)/shard_map/ppermute | solution.py:406
  67.9 0.1 join.5
  68.0 0.0 collective-permute-done.15.refs_2_
  68.0 9.6 %collective-permute-done.16.refs_4_ = f32[256,512]{1,0:T(8,128)S(1)} collective-permute-done((f32[256,512]{1,0:T(8,128)}, f32[256,512]{1,0:T(8,128)S(1)}, u32[]{:S(2)}, u32[]{:S(2)}) %collective-permute-start.16) | collective-permute-done | bytes 524320 | tf_op jit(solution)/shard_map/ppermute | solution.py:404
  77.5 6.0 %collective-permute-start.18 = (f32[160,512]{1,0:T(8,128)S(1)}, f32[160,512]{1,0:T(8,128)S(1)}, u32[]{:S(2)}, u32[]{:S(2)}) collective-permute-start(f32[160,512]{1,0:T(8,128)S(1)} %get-tuple-element.112.own_ref), channel_id=1, source_target_pairs={{0,4},{4,0},{8,12},{12,8},{16,20},{20,16},{24,28},{28,24},{32,36},... | collective-permute-start | bytes 983048 | tf_op jit(solution)/shard_map/ppermute | solution.py:409
  83.5 4.5 %collective-permute-start.20 = (f32[256,512]{1,0:T(8,128)S(1)}, f32[256,512]{1,0:T(8,128)S(1)}, u32[]{:S(2)}, u32[]{:S(2)}) collective-permute-start(f32[256,512]{1,0:T(8,128)S(1)} %copy-done.4), channel_id=1, source_target_pairs={{0,2},{1,3},{2,0},{3,1},{4,6},{5,7},{6,4},{7,5},{8,10},{9,11},{10,... | collective-permute-start | bytes 1572872 | tf_op jit(solution)/shard_map/ppermute | solution.py:412
  88.0 0.0 collective-permute-start.17
  88.0 0.0 collective-permute-done.18.other_ref
  88.0 18.2 %factor.1 = (f32[256,256]{1,0:T(8,128)S(1)}, f32[256,256]{1,0:T(8,128)S(1)}, f32[256,256]{1,0:T(8,128)S(1)}) custom-call(f32[160,512]{1,0:T(8,128)S(1)} %get-tuple-element.112.own_ref, f32[160,512]{1,0:T(8,128)S(1)} %collective-permute-done.18.other_ref), custom_call_target="tpu_custom_call" | custom-call | flops 21474836480 | bytes 1048576 | tf_op jit(solution)/shard_map/factor/pallas_call | solution.py:109
  106.3 0.0 copy-start.1
  106.3 0.0 collective-permute-done.19.refs_2_
  106.3 5.1 %collective-permute-done.20.refs_3_ = f32[256,512]{1,0:T(8,128)S(1)} collective-permute-done((f32[256,512]{1,0:T(8,128)S(1)}, f32[256,512]{1,0:T(8,128)S(1)}, u32[]{:S(2)}, u32[]{:S(2)}) %collective-permute-start.20) | collective-permute-done | bytes 524320 | tf_op jit(solution)/shard_map/ppermute | solution.py:412
  111.3 0.8 collective-permute-start.21
  112.1 0.0 collective-permute-start.22
  112.1 2.9 %weigh.1 = (f32[256,512]{1,0:T(8,128)}, f32[256,512]{1,0:T(8,128)S(1)}) custom-call(f32[256,512]{1,0:T(8,128)S(1)} %slice.3.lead_ref.refs_0_, f32[256,512]{1,0:T(8,128)S(1)} %collective-permute-done.12.refs_1_, f32[256,512]{1,0:T(8,128)S(1)} %collective-permute-done.15.refs_2_, f32[256,256]{1,0:T(8,128)S(1)} %get-tuple-element.120.refs_3_, ...), custom_call_target="tpu_custom_call" | custom-call | flops 1024 | bytes 1024 | tf_op jit(solution)/shard_map/weigh/pallas_call | solution.py:285
  115.1 0.0 collective-permute-done.21.refs_7_
  115.1 0.8 collective-permute-done.22.refs_8_
  115.9 11.4 %update.1 = f32[256,2048]{1,0:T(8,128)} custom-call(s32[4,8]{1,0:T(4,128)S(1)} %get-tuple-element.124.plan, f32[256,512]{1,0:T(8,128)S(1)} %get-tuple-element.125.refs_0_, f32[256,512]{1,0:T(8,128)S(1)} %get-tuple-element.126.refs_1_, f32[256,512]{1,0:T(8,128)S(1)} %collective-permute-done.19.refs_2_, f32[256,512]{1,0:T(8,128)S(1)} %collective-permute-done.20.refs_3_, ...), custom_call_target="tpu_custom_call" | custom-call | tf_op jit(solution)/shard_map/update/pallas_call | solution.py:338
  (12 shorter events, 0.0 us)
Async XLA Ops:
  0.6 26.7 %copy-start.2 = (s32[32]{0:T(128)S(1)}, s32[32]{0:T(128)}, u32[]{:S(2)}) copy-start(s32[32]{0:T(128)} %map_ref.3) | copy-start | bytes 388
  1.7 8.9 %collective-permute-start.3 = (f32[256,512]{1,0:T(8,128)S(1)}, f32[256,512]{1,0:T(8,128)S(1)}, u32[]{:S(2)}, u32[]{:S(2)}) collective-permute-start(f32[256,512]{1,0:T(8,128)S(1)} %slice.3.lead_ref.refs_0_), channel_id=1, source_target_pairs={{0,4},{4,0},{8,12},{12,8},{16,20},{20,16},{24,28},{28,24},{32,36},... | collective-permute-start | bytes 1572872 | tf_op jit(solution)/shard_map/ppermute | solution.py:379
  3.3 25.0 %collective-permute-start.2 = (f32[160,512]{1,0:T(8,128)S(1)}, f32[160,512]{1,0:T(8,128)S(1)}, u32[]{:S(2)}, u32[]{:S(2)}) collective-permute-start(f32[160,512]{1,0:T(8,128)S(1)} %corner.1), channel_id=1, source_target_pairs={{0,3},{4,7}} | collective-permute-start | bytes 983048 | tf_op jit(solution)/shard_map/ppermute | solution.py:377
  8.0 20.3 %collective-permute-start.1 = (f32[160,512]{1,0:T(8,128)S(1)}, f32[160,512]{1,0:T(8,128)S(1)}, u32[]{:S(2)}, u32[]{:S(2)}) collective-permute-start(f32[160,512]{1,0:T(8,128)S(1)} %corner.1), channel_id=1, source_target_pairs={{0,2},{4,6}} | collective-permute-start | bytes 983048 | tf_op jit(solution)/shard_map/ppermute | solution.py:377
  9.3 19.0 %collective-permute-start = (f32[160,512]{1,0:T(8,128)S(1)}, f32[160,512]{1,0:T(8,128)S(1)}, u32[]{:S(2)}, u32[]{:S(2)}) collective-permute-start(f32[160,512]{1,0:T(8,128)S(1)} %corner.1), channel_id=1, source_target_pairs={{0,1},{4,5}} | collective-permute-start | bytes 983048 | tf_op jit(solution)/shard_map/ppermute | solution.py:377
  10.8 26.3 %copy-start = (f32[256,2048]{1,0:T(8,128)S(1)}, f32[256,2048]{1,0:T(8,128)}, u32[]{:S(2)}) copy-start(f32[256,2048]{1,0:T(8,128)} %front_ref.1) | copy-start | bytes 6291460
  10.8 10.8 %collective-permute-start.4 = (f32[2,32,512]{2,1,0:T(8,128)S(1)}, f32[2,32,512]{2,1,0:T(8,128)S(1)}, u32[]{:S(2)}, u32[]{:S(2)}) collective-permute-start(f32[2,32,512]{2,1,0:T(8,128)S(1)} %get-tuple-element.68), channel_id=1, source_target_pairs={{8,16},{12,20},{16,24},{20,28},{24,0},{28,4},{32,40},{36,44},{40,4... | collective-permute-start | bytes 393224 | tf_op jit(solution)/shard_map/ppermute | solution.py:383
  12.2 10.7 %collective-permute-start.5 = (f32[2,32,512]{2,1,0:T(8,128)S(1)}, f32[2,32,512]{2,1,0:T(8,128)S(1)}, u32[]{:S(2)}, u32[]{:S(2)}) collective-permute-start(f32[2,32,512]{2,1,0:T(8,128)S(1)} %get-tuple-element.69), channel_id=1, source_target_pairs={{8,24},{12,28},{16,0},{20,4},{24,8},{28,12},{32,48},{36,52},{40,56... | collective-permute-start | bytes 393224 | tf_op jit(solution)/shard_map/ppermute | solution.py:383
  21.6 5.7 %collective-permute-start.6 = (f32[2,32,512]{2,1,0:T(8,128)S(1)}, f32[2,32,512]{2,1,0:T(8,128)S(1)}, u32[]{:S(2)}, u32[]{:S(2)}) collective-permute-start(f32[2,32,512]{2,1,0:T(8,128)S(1)} %get-tuple-element.70), channel_id=1, source_target_pairs={{8,0},{12,4},{16,8},{20,12},{24,16},{28,20},{32,56},{36,60},{40,32... | collective-permute-start | bytes 393224 | tf_op jit(solution)/shard_map/ppermute | solution.py:383
  28.5 7.2 %collective-permute-start.7 = (f32[160,512]{1,0:T(8,128)S(1)}, f32[160,512]{1,0:T(8,128)S(1)}, u32[]{:S(2)}, u32[]{:S(2)}) collective-permute-start(f32[160,512]{1,0:T(8,128)S(1)} %add_add_fusion.refs_4_), channel_id=1, source_target_pairs={{0,8},{4,36},{1,9},{5,37},{2,10},{6,38},{3,11},{7,39}} | collective-permute-start | bytes 983048 | tf_op jit(solution)/shard_map/ppermute | solution.py:391
  29.8 3.9 %collective-permute-start.8 = (f32[2,32,512]{2,1,0:T(8,128)S(1)}, f32[2,32,512]{2,1,0:T(8,128)S(1)}, u32[]{:S(2)}, u32[]{:S(2)}) collective-permute-start(f32[2,32,512]{2,1,0:T(8,128)S(1)} %get-tuple-element.80), channel_id=1, source_target_pairs={{0,1},{4,5},{8,9},{12,13},{16,17},{20,21},{24,25},{28,29},{32,33},... | collective-permute-start | bytes 393224 | tf_op jit(solution)/shard_map/ppermute | solution.py:389
  31.1 3.3 %collective-permute-start.9 = (f32[2,32,512]{2,1,0:T(8,128)S(1)}, f32[2,32,512]{2,1,0:T(8,128)S(1)}, u32[]{:S(2)}, u32[]{:S(2)}) collective-permute-start(f32[2,32,512]{2,1,0:T(8,128)S(1)} %get-tuple-element.81), channel_id=1, source_target_pairs={{0,2},{4,6},{8,10},{12,14},{16,18},{20,22},{24,26},{28,30},{32,34}... | collective-permute-start | bytes 393224 | tf_op jit(solution)/shard_map/ppermute | solution.py:389
  32.4 3.2 %collective-permute-start.10 = (f32[2,32,512]{2,1,0:T(8,128)S(1)}, f32[2,32,512]{2,1,0:T(8,128)S(1)}, u32[]{:S(2)}, u32[]{:S(2)}) collective-permute-start(f32[2,32,512]{2,1,0:T(8,128)S(1)} %get-tuple-element.82), channel_id=1, source_target_pairs={{0,3},{4,7},{8,11},{12,15},{16,19},{20,23},{24,27},{28,31},{32,35}... | collective-permute-start | bytes 393224 | tf_op jit(solution)/shard_map/ppermute | solution.py:389
  35.7 9.8 %collective-permute-start.11 = (f32[264,512]{1,0:T(8,128)S(1)}, f32[264,512]{1,0:T(8,128)S(1)}, u32[]{:S(2)}, u32[]{:S(2)}) collective-permute-start(f32[264,512]{1,0:T(8,128)S(1)} %merge.1.own_ref), channel_id=1, source_target_pairs={{0,24},{4,100},{8,16},{12,108},{16,8},{20,116},{24,0},{28,124},{32... | collective-permute-start | bytes 1622024 | tf_op jit(solution)/shard_map/ppermute | solution.py:399
  35.8 9.8 %collective-permute-start.12 = (f32[256,512]{1,0:T(8,128)S(1)}, f32[256,512]{1,0:T(8,128)S(1)}, u32[]{:S(2)}, u32[]{:S(2)}) collective-permute-start(f32[256,512]{1,0:T(8,128)S(1)} %slice.3.lead_ref.refs_0_), channel_id=1, source_target_pairs={{0,1},{4,5},{8,9},{12,13},{16,17},{20,21},{24,25},{28,29},{32,33},... | collective-permute-start | bytes 1572872 | tf_op jit(solution)/shard_map/ppermute | solution.py:398
  39.1 15.5 %copy-start.5 = (f32[256,512]{1,0:T(8,128)}, f32[256,512]{1,0:T(8,128)S(1)}, u32[]{:S(2)}) copy-start(f32[256,512]{1,0:T(8,128)S(1)} %get-tuple-element.117) | copy-start | bytes 1572868
  39.1 15.6 %copy-start.3 = (f32[256,512]{1,0:T(8,128)}, f32[256,512]{1,0:T(8,128)S(1)}, u32[]{:S(2)}) copy-start(f32[256,512]{1,0:T(8,128)S(1)} %get-tuple-element.118) | copy-start | bytes 1572868
  39.1 15.7 %copy-start.7 = (f32[256,512]{1,0:T(8,128)}, f32[256,512]{1,0:T(8,128)S(1)}, u32[]{:S(2)}) copy-start(f32[256,512]{1,0:T(8,128)S(1)} %get-tuple-element.109) | copy-start | bytes 1572868
  45.5 9.1 %collective-permute-start.13 = (f32[288,512]{1,0:T(8,128)S(1)}, f32[288,512]{1,0:T(8,128)S(1)}, u32[]{:S(2)}, u32[]{:S(2)}) collective-permute-start(f32[288,512]{1,0:T(8,128)S(1)} %join.3.own_ref), channel_id=1, source_target_pairs={{0,32},{4,12},{8,40},{12,4},{16,48},{20,28},{24,56},{28,20},{32,0}... | collective-permute-start | bytes 1769480 | tf_op jit(solution)/shard_map/ppermute | solution.py:401
  54.7 13.1 %collective-permute-start.14 = (f32[416,512]{1,0:T(8,128)S(1)}, f32[416,512]{1,0:T(8,128)S(1)}, u32[]{:S(2)}, u32[]{:S(2)}) collective-permute-start(f32[416,512]{1,0:T(8,128)S(1)} %join.4.own_ref), channel_id=1, source_target_pairs={{0,96},{4,28},{8,104},{12,20},{16,112},{20,12},{24,120},{28,4},{32... | collective-permute-start | bytes 2555912 | tf_op jit(solution)/shard_map/ppermute | solution.py:406
  54.8 28.7 %copy-start.6 = (f32[256,512]{1,0:T(8,128)S(1)}, f32[256,512]{1,0:T(8,128)}, u32[]{:S(2)}) copy-start(f32[256,512]{1,0:T(8,128)} %copy-done.5) | copy-start | bytes 1572868
  54.9 28.7 %copy-start.4 = (f32[256,512]{1,0:T(8,128)S(1)}, f32[256,512]{1,0:T(8,128)}, u32[]{:S(2)}) copy-start(f32[256,512]{1,0:T(8,128)} %copy-done.3) | copy-start | bytes 1572868
  55.0 13.0 %collective-permute-start.15 = (f32[256,512]{1,0:T(8,128)S(1)}, f32[256,512]{1,0:T(8,128)S(1)}, u32[]{:S(2)}, u32[]{:S(2)}) collective-permute-start(f32[256,512]{1,0:T(8,128)S(1)} %broadcast_select_fusion), channel_id=1, source_target_pairs={{0,3},{1,2},{4,7},{5,6},{8,11},{9,10},{12,15},{13,14},{16,19},{17,... | collective-permute-start | bytes 1572872 | tf_op jit(solution)/shard_map/ppermute | solution.py:403
  60.1 17.4 %collective-permute-start.16 = (f32[256,512]{1,0:T(8,128)}, f32[256,512]{1,0:T(8,128)S(1)}, u32[]{:S(2)}, u32[]{:S(2)}) collective-permute-start(f32[256,512]{1,0:T(8,128)} %copy-done.7), channel_id=1, source_target_pairs={{0,3},{1,0},{2,1},{3,2},{4,7},{5,4},{6,5},{7,6},{8,11},{9,8},{10,9... | collective-permute-start | bytes 1572872 | tf_op jit(solution)/shard_map/ppermute | solution.py:404
  77.5 10.5 %collective-permute-start.18 = (f32[160,512]{1,0:T(8,128)S(1)}, f32[160,512]{1,0:T(8,128)S(1)}, u32[]{:S(2)}, u32[]{:S(2)}) collective-permute-start(f32[160,512]{1,0:T(8,128)S(1)} %get-tuple-element.112.own_ref), channel_id=1, source_target_pairs={{0,4},{4,0},{8,12},{12,8},{16,20},{20,16},{24,28},{28,24},{32,36},... | collective-permute-start | bytes 983048 | tf_op jit(solution)/shard_map/ppermute | solution.py:409
  83.5 22.8 %collective-permute-start.19 = (f32[256,512]{1,0:T(8,128)S(1)}, f32[256,512]{1,0:T(8,128)S(1)}, u32[]{:S(2)}, u32[]{:S(2)}) collective-permute-start(f32[256,512]{1,0:T(8,128)S(1)} %copy-done.6), channel_id=1, source_target_pairs={{0,1},{1,2},{2,3},{3,0},{4,5},{5,6},{6,7},{7,4},{8,9},{9,10},{10,1... | collective-permute-start | bytes 1572872 | tf_op jit(solution)/shard_map/ppermute | solution.py:412
  83.5 27.8 %collective-permute-start.20 = (f32[256,512]{1,0:T(8,128)S(1)}, f32[256,512]{1,0:T(8,128)S(1)}, u32[]{:S(2)}, u32[]{:S(2)}) collective-permute-start(f32[256,512]{1,0:T(8,128)S(1)} %copy-done.4), channel_id=1, source_target_pairs={{0,2},{1,3},{2,0},{3,1},{4,6},{5,7},{6,4},{7,5},{8,10},{9,11},{10,... | collective-permute-start | bytes 1572872 | tf_op jit(solution)/shard_map/ppermute | solution.py:412
  88.0 23.3 %collective-permute-start.17 = (f32[512,512]{1,0:T(8,128)S(1)}, f32[512,512]{1,0:T(8,128)S(1)}, u32[]{:S(2)}, u32[]{:S(2)}) collective-permute-start(f32[512,512]{1,0:T(8,128)S(1)} %get-tuple-element.130.refs_5_), channel_id=1, source_target_pairs={{0,8},{4,36},{8,0},{12,44},{16,24},{20,52},{24,16},{28,60},{32,40}... | collective-permute-start | bytes 3145736 | tf_op jit(solution)/shard_map/ppermute | solution.py:410
  106.3 9.7 %copy-start.1 = (f32[256,2048]{1,0:T(8,128)S(1)}, f32[256,2048]{1,0:T(8,128)}, u32[]{:S(2)}) copy-start(f32[256,2048]{1,0:T(8,128)} %refs_9_.1) | copy-start | bytes 6291460
  111.3 3.7 %collective-permute-start.21 = (f32[512,512]{1,0:T(8,128)S(1)}, f32[512,512]{1,0:T(8,128)S(1)}, u32[]{:S(2)}, u32[]{:S(2)}) collective-permute-start(f32[512,512]{1,0:T(8,128)S(1)} %get-tuple-element.130.refs_5_), channel_id=1, source_target_pairs={{0,4},{4,0},{8,12},{12,8},{16,20},{20,16},{24,28},{28,24},{32,36},... | collective-permute-start | bytes 3145736 | tf_op jit(solution)/shard_map/ppermute | solution.py:417
  112.1 3.8 %collective-permute-start.22 = (f32[512,512]{1,0:T(8,128)S(1)}, f32[512,512]{1,0:T(8,128)S(1)}, u32[]{:S(2)}, u32[]{:S(2)}) collective-permute-start(f32[512,512]{1,0:T(8,128)S(1)} %collective-permute-done.17.refs_6_), channel_id=1, source_target_pairs={{0,4},{4,0},{8,12},{12,8},{16,20},{20,16},{24,28},{28,24},{32,36},... | collective-permute-start | bytes 3145736 | tf_op jit(solution)/shard_map/ppermute | solution.py:416

commit v13 on v9

--- a/solution.py
+++ b/solution.py
@@ -12,8 +12,8 @@
 HALF = 128
 STEP = 8
 TURN = 2
-BLOCK = 160
-PAD = 40
+BLOCK = 136
+PAD = 64
 LARGE = pl.CostEstimate(flops=20 << 30, bytes_accessed=1 << 20, transcendentals=0)
 SMALL = pl.CostEstimate(flops=1 << 10, bytes_accessed=1 << 10, transcendentals=0)
 HIGHEST = lax.Precision.HIGHEST
@@ -130,24 +130,37 @@
     own, other = own_ref[...], other_ref[...]
     zero = jnp.where(even, own, other)
     one = jnp.where(even, other, own)
+    down = lax.broadcasted_iota(jnp.int32, (HALF, HALF), 0)
+    right = lax.broadcasted_iota(jnp.int32, (HALF, HALF), 1)
 
     def piece(blocks, index):
         rows = blocks[index * 32 : (index + 1) * 32]
         return jnp.concatenate([rows[:, part * HALF : (part + 1) * HALF] for part in range(4)], 0)
 
-    inv_a = inverse_factor_256(piece(zero, 0), piece(zero, 1), piece(zero, 2))
+    def diagonal(blocks):
+        packed = piece(blocks, 0)
+        low = jnp.where(down > right, packed, 0.0)
+        high = jnp.where(down < right, packed, 0.0)
+        edge = jnp.broadcast_to(blocks[128:129, :HALF], (HALF, HALF))
+        first = jnp.where(down >= right, packed, jnp.transpose(low))
+        second = jnp.where(down < right, packed, jnp.where(down == right, edge, jnp.transpose(high)))
+        return first, second
+
+    top, bottom = diagonal(zero)
+    inv_a = inverse_factor_256(top, piece(zero, 1), bottom)
     across = jnp.concatenate(
         [
-            dot(jnp.concatenate([piece(zero, 3), piece(zero, 4)], 0), inv_a, 0, 1),
-            dot(jnp.concatenate([piece(one, 3), piece(one, 4)], 1), inv_a, 1, 1),
+            dot(jnp.concatenate([piece(zero, 2), piece(zero, 3)], 0), inv_a, 0, 1),
+            dot(jnp.concatenate([piece(one, 2), piece(one, 3)], 1), inv_a, 1, 1),
         ],
         0,
     )
     square = dot(across, across, 1, 1)
+    top, bottom = diagonal(one)
     inv_b = inverse_factor_256(
-        piece(one, 0) - square[:HALF, :HALF],
+        top - square[:HALF, :HALF],
         piece(one, 1) - square[HALF:, :HALF],
-        piece(one, 2) - square[HALF:, HALF:],
+        bottom - square[HALF:, HALF:],
     )
     inv_a_ref[...] = inv_a
     across_ref[...] = across
@@ -196,17 +209,20 @@
 def corner_kernel(lead_ref, out_ref):
     plane, line, core, col = position()
     out_ref[...] = jnp.zeros_like(out_ref)
-    places = [[(0, 0), (1, 0), (1, 1), (0, 2), (1, 2)], [(0, 2), (1, 2), (1, 3), (1, 0), (1, 1)]]
+    down = lax.broadcasted_iota(jnp.int32, (HALF, HALF), 0)
+    right = lax.broadcasted_iota(jnp.int32, (HALF, HALF), 1)
+    places = [[(0, 0), (1, 1), (1, 0), (0, 2), (1, 2)], [(0, 2), (1, 3), (1, 2), (1, 0), (1, 1)]]
     for holder in range(2):
 
         @pl.when((col == 0) & (plane == 0) & (line == 0) & (core == holder))
         def _():
-            for index, (down, right) in enumerate(places[holder]):
+            blocks = [lead_ref[i * HALF : i * HALF + HALF, j * HALF : j * HALF + HALF] for i, j in places[holder]]
+            first, second = blocks[:2]
+            for index, block in enumerate([jnp.where(down >= right, first, second)] + blocks[2:]):
                 for part in range(4):
-                    rows = slice(down * HALF + part * 32, down * HALF + part * 32 + 32)
-                    out_ref[index * 32 : index * 32 + 32, part * HALF : part * HALF + HALF] = lead_ref[
-                        rows, right * HALF : right * HALF + HALF
-                    ]
+                    out_ref[index * 32 : index * 32 + 32, part * HALF : part * HALF + HALF] = block[part * 32 : part * 32 + 32]
+            diagonal = jnp.sum(jnp.where(down == right, second, 0.0), axis=0, keepdims=True)
+            out_ref[128:, :HALF] = jnp.broadcast_to(diagonal, (8, HALF))
 
 
 def merge_kernel(*refs):
@@ -309,16 +325,17 @@
             index = (first >> 1) + 2 * ((second & 1) ^ (second >> 1)) + 4 * (second >> 1)
             rows = pl.ds(pl.multiple_of(index * 64 + place * 32, 32), 32)
             into = pl.ds(pl.multiple_of((2 * x + holder) * 32, 32), 32)
-            for late in range(2):
-
-                @pl.when(((first & 1) ^ (first >> 1)) == late)
-                def _():
-                    ahead_ref[into, :] = gathered[2 * parity + late][rows, :]
+            late = ((first & 1) ^ (first >> 1)) == 1
+            ahead_ref[into, :] = jnp.where(late, gathered[2 * parity + 1][rows, :], gathered[2 * parity][rows, :])
 
     product = dot(weight_ref[...], ahead_ref[...], 1, 1)
     column = pl.multiple_of(place * PW, PW)
     base = base_ref[...]
-    out_ref[...] = base
+
+    @pl.when(plan[3, slot] == 0)
+    def _():
+        out_ref[...] = base
+
     for index, ref in enumerate(pieces):
 
         @pl.when((plan[0, slot] == index) & (plan[3, slot] == 1))

time: 114 us -> 113 us (level)
  no operation moved by 1% of the time
where the time goes in v13:
time: 113 us
  starting transfers between devices  40.4 us (36%)
  waiting for transfers between devices  35.8 us (32%)
  Pallas kernels  32.8 us (29%)
  local copies, waits for them, and re-layouts  2.69 us (2%)
    pallas_call x9, Pallas kernels, call(): pl.pallas_call(kernel, out_shape=[jax.ShapeDtypeStruct(shape, jnp.float32...  21.8 us
    ppermute x3, waiting for transfers between devices, shards(): parts[hop] = lax.ppermute(parts[hop], 'row', pairs)  12.5 us
    ppermute x1, waiting for transfers between devices, shards(): lax.ppermute(load, 'row', every[3])  9.02 us
    pallas_call x1, Pallas kernels, update(): pl.pallas_call(update_kernel, out_shape=jax.ShapeDtypeStruct(base.shape,...  8.1 us
    ppermute x3, starting transfers between devices, shards(): lax.ppermute(blocks[0], ('row', 'col'), [(4 * core, 4 * core + to) for co...  7.47 us
    ppermute x1, starting transfers between devices, shards(): other = lax.ppermute(block, 'row', swap)  6.72 us
    ppermute x1, starting transfers between devices, shards(): lax.ppermute(jnp.where(lax.axis_index('col') == 1, near, lead), 'col', [(...  5.14 us
    ppermute x1, waiting for transfers between devices, shards(): lax.ppermute(load, 'row', every[1])  4.76 us
  transfers between devices with their start and end apart: 23, of which 9 were waited for; matrix products, arithmetic and copies ran while one was open for 0% of the time, Pallas kernels for 22%

profile of v13, /device:TPU:1, one launch (start us, length us, event | category | flops | bytes accessed | tf_op | source)
XLA Modules:
  0.0 112.9 jit_solution(13480797172712434538)
XLA Ops:
  0.6 1.1 slice.3.lead_ref.refs_0_
  1.7 1.5 %collective-permute-start.3 = (f32[256,512]{1,0:T(8,128)S(1)}, f32[256,512]{1,0:T(8,128)S(1)}, u32[]{:S(2)}, u32[]{:S(2)}) collective-permute-start(f32[256,512]{1,0:T(8,128)S(1)} %slice.3.lead_ref.refs_0_), channel_id=1, source_target_pairs={{0,4},{4,0},{8,12},{12,8},{16,20},{20,16},{24,28},{28,24},{32,36},... | collective-permute-start | bytes 1572872 | tf_op jit(solution)/shard_map/ppermute | solution.py:391
  3.3 0.0 copy-start
  3.3 4.9 %collective-permute-start.2 = (f32[136,512]{1,0:T(8,128)S(1)}, f32[136,512]{1,0:T(8,128)S(1)}, u32[]{:S(2)}, u32[]{:S(2)}) collective-permute-start(f32[136,512]{1,0:T(8,128)S(1)} %corner.1), channel_id=1, source_target_pairs={{0,3},{4,7}} | collective-permute-start | bytes 835592 | tf_op jit(solution)/shard_map/ppermute | solution.py:389
  8.2 1.3 %collective-permute-start.1 = (f32[136,512]{1,0:T(8,128)S(1)}, f32[136,512]{1,0:T(8,128)S(1)}, u32[]{:S(2)}, u32[]{:S(2)}) collective-permute-start(f32[136,512]{1,0:T(8,128)S(1)} %corner.1), channel_id=1, source_target_pairs={{0,2},{4,6}} | collective-permute-start | bytes 835592 | tf_op jit(solution)/shard_map/ppermute | solution.py:389
  9.5 1.3 %collective-permute-start = (f32[136,512]{1,0:T(8,128)S(1)}, f32[136,512]{1,0:T(8,128)S(1)}, u32[]{:S(2)}, u32[]{:S(2)}) collective-permute-start(f32[136,512]{1,0:T(8,128)S(1)} %corner.1), channel_id=1, source_target_pairs={{0,1},{4,5}} | collective-permute-start | bytes 835592 | tf_op jit(solution)/shard_map/ppermute | solution.py:389
  10.8 0.0 collective-permute-done.3.mate_ref
  10.8 0.1 share.1
  10.9 1.3 %collective-permute-start.4 = (f32[2,32,512]{2,1,0:T(8,128)S(1)}, f32[2,32,512]{2,1,0:T(8,128)S(1)}, u32[]{:S(2)}, u32[]{:S(2)}) collective-permute-start(f32[2,32,512]{2,1,0:T(8,128)S(1)} %get-tuple-element.66), channel_id=1, source_target_pairs={{8,16},{12,20},{16,24},{20,28},{24,0},{28,4},{32,40},{36,44},{40,4... | collective-permute-start | bytes 393224 | tf_op jit(solution)/shard_map/ppermute | solution.py:395
  12.2 1.3 %collective-permute-start.5 = (f32[2,32,512]{2,1,0:T(8,128)S(1)}, f32[2,32,512]{2,1,0:T(8,128)S(1)}, u32[]{:S(2)}, u32[]{:S(2)}) collective-permute-start(f32[2,32,512]{2,1,0:T(8,128)S(1)} %get-tuple-element.67), channel_id=1, source_target_pairs={{8,24},{12,28},{16,0},{20,4},{24,8},{28,12},{32,48},{36,52},{40,56... | collective-permute-start | bytes 393224 | tf_op jit(solution)/shard_map/ppermute | solution.py:395
  13.5 8.1 %collective-permute-done.4.refs_1_ = f32[2,32,512]{2,1,0:T(8,128)S(1)} collective-permute-done((f32[2,32,512]{2,1,0:T(8,128)S(1)}, f32[2,32,512]{2,1,0:T(8,128)S(1)}, u32[]{:S(2)}, u32[]{:S(2)}) %collective-permute-start.4) | collective-permute-done | bytes 131104 | tf_op jit(solution)/shard_map/ppermute | solution.py:395
  21.6 1.3 %collective-permute-start.6 = (f32[2,32,512]{2,1,0:T(8,128)S(1)}, f32[2,32,512]{2,1,0:T(8,128)S(1)}, u32[]{:S(2)}, u32[]{:S(2)}) collective-permute-start(f32[2,32,512]{2,1,0:T(8,128)S(1)} %get-tuple-element.68), channel_id=1, source_target_pairs={{8,0},{12,4},{16,8},{20,12},{24,16},{28,20},{32,56},{36,60},{40,32... | collective-permute-start | bytes 393224 | tf_op jit(solution)/shard_map/ppermute | solution.py:395
  22.9 0.0 collective-permute-done.5.refs_2_
  22.9 4.4 %collective-permute-done.6.refs_3_ = f32[2,32,512]{2,1,0:T(8,128)S(1)} collective-permute-done((f32[2,32,512]{2,1,0:T(8,128)S(1)}, f32[2,32,512]{2,1,0:T(8,128)S(1)}, u32[]{:S(2)}, u32[]{:S(2)}) %collective-permute-start.6) | collective-permute-done | bytes 131104 | tf_op jit(solution)/shard_map/ppermute | solution.py:395
  27.3 1.0 sort.1
  28.3 0.0 collective-permute-done.2
  28.3 0.0 collective-permute-done.1
  28.3 0.0 collective-permute-done
  28.3 0.1 add_add_fusion.refs_4_
  28.4 1.3 %collective-permute-start.7 = (f32[136,512]{1,0:T(8,128)S(1)}, f32[136,512]{1,0:T(8,128)S(1)}, u32[]{:S(2)}, u32[]{:S(2)}) collective-permute-start(f32[136,512]{1,0:T(8,128)S(1)} %add_add_fusion.refs_4_), channel_id=1, source_target_pairs={{0,8},{4,36},{1,9},{5,37},{2,10},{6,38},{3,11},{7,39}} | collective-permute-start | bytes 835592 | tf_op jit(solution)/shard_map/ppermute | solution.py:403
  29.7 1.3 %collective-permute-start.8 = (f32[2,32,512]{2,1,0:T(8,128)S(1)}, f32[2,32,512]{2,1,0:T(8,128)S(1)}, u32[]{:S(2)}, u32[]{:S(2)}) collective-permute-start(f32[2,32,512]{2,1,0:T(8,128)S(1)} %get-tuple-element.78), channel_id=1, source_target_pairs={{0,1},{4,5},{8,9},{12,13},{16,17},{20,21},{24,25},{28,29},{32,33},... | collective-permute-start | bytes 393224 | tf_op jit(solution)/shard_map/ppermute | solution.py:401
  31.0 1.3 %collective-permute-start.9 = (f32[2,32,512]{2,1,0:T(8,128)S(1)}, f32[2,32,512]{2,1,0:T(8,128)S(1)}, u32[]{:S(2)}, u32[]{:S(2)}) collective-permute-start(f32[2,32,512]{2,1,0:T(8,128)S(1)} %get-tuple-element.79), channel_id=1, source_target_pairs={{0,2},{4,6},{8,10},{12,14},{16,18},{20,22},{24,26},{28,30},{32,34}... | collective-permute-start | bytes 393224 | tf_op jit(solution)/shard_map/ppermute | solution.py:401
  32.3 1.3 %collective-permute-start.10 = (f32[2,32,512]{2,1,0:T(8,128)S(1)}, f32[2,32,512]{2,1,0:T(8,128)S(1)}, u32[]{:S(2)}, u32[]{:S(2)}) collective-permute-start(f32[2,32,512]{2,1,0:T(8,128)S(1)} %get-tuple-element.80), channel_id=1, source_target_pairs={{0,3},{4,7},{8,11},{12,15},{16,19},{20,23},{24,27},{28,31},{32,35}... | collective-permute-start | bytes 393224 | tf_op jit(solution)/shard_map/ppermute | solution.py:401
  33.6 0.0 collective-permute-done.8.refs_1_
  33.7 0.7 collective-permute-done.9.refs_2_
  34.3 1.2 %collective-permute-done.10.refs_3_ = f32[2,32,512]{2,1,0:T(8,128)S(1)} collective-permute-done((f32[2,32,512]{2,1,0:T(8,128)S(1)}, f32[2,32,512]{2,1,0:T(8,128)S(1)}, u32[]{:S(2)}, u32[]{:S(2)}) %collective-permute-start.10) | collective-permute-done | bytes 131104 | tf_op jit(solution)/shard_map/ppermute | solution.py:401
  35.6 0.0 collective-permute-done.7.refs_5_
  35.6 0.1 merge.1.own_ref
  35.6 0.1 collective-permute-start.11
  35.7 1.3 %collective-permute-start.12 = (f32[256,512]{1,0:T(8,128)S(1)}, f32[256,512]{1,0:T(8,128)S(1)}, u32[]{:S(2)}, u32[]{:S(2)}) collective-permute-start(f32[256,512]{1,0:T(8,128)S(1)} %slice.3.lead_ref.refs_0_), channel_id=1, source_target_pairs={{0,1},{4,5},{8,9},{12,13},{16,17},{20,21},{24,25},{28,29},{32,33},... | collective-permute-start | bytes 1572872 | tf_op jit(solution)/shard_map/ppermute | solution.py:410
  37.1 2.0 %pick.1 = (f32[256,512]{1,0:T(8,128)S(1)}, f32[256,512]{1,0:T(8,128)S(1)}, f32[256,512]{1,0:T(8,128)S(1)}, f32[256,512]{1,0:T(8,128)S(1)}, s32[4,8]{1,0:T(4,128)S(1)}) custom-call(s32[32]{0:T(128)S(1)} %copy-done.2, f32[256,2048]{1,0:T(8,128)S(1)} %copy-done), custom_call_target="tpu_custom_call" | custom-call | flops 1024 | bytes 1024 | tf_op jit(solution)/shard_map/pick/pallas_call | solution.py:109
  39.1 0.0 copy-start.3
  39.1 0.8 copy-done.3
  39.9 0.8 copy-done.5
  40.7 4.8 %collective-permute-done.11.got_ref = f32[264,512]{1,0:T(8,128)S(1)} collective-permute-done((f32[264,512]{1,0:T(8,128)S(1)}, f32[264,512]{1,0:T(8,128)S(1)}, u32[]{:S(2)}, u32[]{:S(2)}) %collective-permute-start.11) | collective-permute-done | bytes 540704 | tf_op jit(solution)/shard_map/ppermute | solution.py:411
  45.5 0.0 copy-start.6
  45.5 0.0 copy-start.4
  45.5 0.0 collective-permute-done.12.refs_1_
  45.5 0.1 collective-permute-start.13
  45.6 0.1 broadcast_select_fusion
  45.7 5.1 %collective-permute-start.14 = (f32[256,512]{1,0:T(8,128)S(1)}, f32[256,512]{1,0:T(8,128)S(1)}, u32[]{:S(2)}, u32[]{:S(2)}) collective-permute-start(f32[256,512]{1,0:T(8,128)S(1)} %broadcast_select_fusion), channel_id=1, source_target_pairs={{0,3},{1,2},{4,7},{5,6},{8,11},{9,10},{12,15},{13,14},{16,19},{17,... | collective-permute-start | bytes 1572872 | tf_op jit(solution)/shard_map/ppermute | solution.py:413
  50.8 3.3 %collective-permute-done.13.got_ref = f32[264,512]{1,0:T(8,128)S(1)} collective-permute-done((f32[264,512]{1,0:T(8,128)S(1)}, f32[264,512]{1,0:T(8,128)S(1)}, u32[]{:S(2)}, u32[]{:S(2)}) %collective-permute-start.13) | collective-permute-done | bytes 540704 | tf_op jit(solution)/shard_map/ppermute | solution.py:414
  54.1 0.1 join.4.own_ref
  54.2 3.6 %collective-permute-done.14.refs_2_ = f32[256,512]{1,0:T(8,128)S(1)} collective-permute-done((f32[256,512]{1,0:T(8,128)S(1)}, f32[256,512]{1,0:T(8,128)S(1)}, u32[]{:S(2)}, u32[]{:S(2)}) %collective-permute-start.14) | collective-permute-done | bytes 524320 | tf_op jit(solution)/shard_map/ppermute | solution.py:413
  57.8 0.0 collective-permute-start.15
  57.8 0.0 collective-permute-start.16
  57.8 3.5 %collective-permute-start.17 = (f32[256,512]{1,0:T(8,128)S(1)}, f32[256,512]{1,0:T(8,128)S(1)}, u32[]{:S(2)}, u32[]{:S(2)}) collective-permute-start(f32[256,512]{1,0:T(8,128)S(1)} %copy-done.4), channel_id=1, source_target_pairs={{0,3},{1,0},{2,1},{3,2},{4,7},{5,4},{6,5},{7,6},{8,11},{9,8},{10,9... | collective-permute-start | bytes 1572872 | tf_op jit(solution)/shard_map/ppermute | solution.py:420
  61.3 9.0 %collective-permute-done.15.got_ref = f32[392,512]{1,0:T(8,128)S(1)} collective-permute-done((f32[392,512]{1,0:T(8,128)S(1)}, f32[392,512]{1,0:T(8,128)S(1)}, u32[]{:S(2)}, u32[]{:S(2)}) %collective-permute-start.15) | collective-permute-done | bytes 802848 | tf_op jit(solution)/shard_map/ppermute | solution.py:417
  70.3 0.1 join.5
  70.4 0.0 collective-permute-done.16.refs_2_
  70.4 0.0 collective-permute-done.17.refs_4_
  70.4 6.7 %collective-permute-start.19 = (f32[136,512]{1,0:T(8,128)S(1)}, f32[136,512]{1,0:T(8,128)S(1)}, u32[]{:S(2)}, u32[]{:S(2)}) collective-permute-start(f32[136,512]{1,0:T(8,128)S(1)} %get-tuple-element.108.own_ref), channel_id=1, source_target_pairs={{0,4},{4,0},{8,12},{12,8},{16,20},{20,16},{24,28},{28,24},{32,36},... | collective-permute-start | bytes 835592 | tf_op jit(solution)/shard_map/ppermute | solution.py:422
  77.2 2.8 %collective-permute-start.20 = (f32[256,512]{1,0:T(8,128)S(1)}, f32[256,512]{1,0:T(8,128)S(1)}, u32[]{:S(2)}, u32[]{:S(2)}) collective-permute-start(f32[256,512]{1,0:T(8,128)S(1)} %get-tuple-element.114), channel_id=1, source_target_pairs={{0,2},{1,3},{2,0},{3,1},{4,6},{5,7},{6,4},{7,5},{8,10},{9,11},{10,... | collective-permute-start | bytes 1572872 | tf_op jit(solution)/shard_map/ppermute | solution.py:424
  79.9 2.2 %collective-permute-start.18 = (f32[512,512]{1,0:T(8,128)S(1)}, f32[512,512]{1,0:T(8,128)S(1)}, u32[]{:S(2)}, u32[]{:S(2)}) collective-permute-start(f32[512,512]{1,0:T(8,128)S(1)} %get-tuple-element.126.refs_5_), channel_id=1, source_target_pairs={{0,8},{4,36},{8,0},{12,44},{16,24},{20,52},{24,16},{28,60},{32,40}... | collective-permute-start | bytes 3145736 | tf_op jit(solution)/shard_map/ppermute | solution.py:423
  82.1 0.0 collective-permute-done.19.other_ref
  82.1 18.4 %factor.1 = (f32[256,256]{1,0:T(8,128)S(1)}, f32[256,256]{1,0:T(8,128)S(1)}, f32[256,256]{1,0:T(8,128)S(1)}) custom-call(f32[136,512]{1,0:T(8,128)S(1)} %get-tuple-element.108.own_ref, f32[136,512]{1,0:T(8,128)S(1)} %collective-permute-done.19.other_ref), custom_call_target="tpu_custom_call" | custom-call | flops 21474836480 | bytes 1048576 | tf_op jit(solution)/shard_map/factor/pallas_call | solution.py:109
  100.6 0.0 copy-start.1
  100.6 0.0 collective-permute-done.20.refs_3_
  100.6 0.0 collective-permute-done.18.refs_6_
  100.6 0.1 collective-permute-start.21
  100.7 0.5 collective-permute-start.22
  101.2 2.9 %weigh.1 = (f32[256,512]{1,0:T(8,128)}, f32[256,512]{1,0:T(8,128)S(1)}) custom-call(f32[256,512]{1,0:T(8,128)S(1)} %slice.3.lead_ref.refs_0_, f32[256,512]{1,0:T(8,128)S(1)} %collective-permute-done.12.refs_1_, f32[256,512]{1,0:T(8,128)S(1)} %collective-permute-done.14.refs_2_, f32[256,256]{1,0:T(8,128)S(1)} %get-tuple-element.116.refs_3_, ...), custom_call_target="tpu_custom_call" | custom-call | flops 1024 | bytes 1024 | tf_op jit(solution)/shard_map/weigh/pallas_call | solution.py:301
  104.1 0.7 collective-permute-done.22.refs_8_
  104.8 8.1 %update.1 = f32[256,2048]{1,0:T(8,128)} custom-call(s32[4,8]{1,0:T(4,128)S(1)} %get-tuple-element.120.plan, f32[256,512]{1,0:T(8,128)S(1)} %get-tuple-element.121.refs_0_, f32[256,512]{1,0:T(8,128)S(1)} %get-tuple-element.122.refs_1_, f32[256,512]{1,0:T(8,128)S(1)} %collective-permute-done.16.refs_2_, f32[256,512]{1,0:T(8,128)S(1)} %collective-permute-done.20.refs_3_, ...), custom_call_target="tpu_custom_call" | custom-call | tf_op jit(solution)/shard_map/update/pallas_call | solution.py:350
  (10 shorter events, 0.1 us)
Async XLA Ops:
  0.6 26.7 %copy-start.2 = (s32[32]{0:T(128)S(1)}, s32[32]{0:T(128)}, u32[]{:S(2)}) copy-start(s32[32]{0:T(128)} %map_ref.3) | copy-start | bytes 388
  1.7 9.1 %collective-permute-start.3 = (f32[256,512]{1,0:T(8,128)S(1)}, f32[256,512]{1,0:T(8,128)S(1)}, u32[]{:S(2)}, u32[]{:S(2)}) collective-permute-start(f32[256,512]{1,0:T(8,128)S(1)} %slice.3.lead_ref.refs_0_), channel_id=1, source_target_pairs={{0,4},{4,0},{8,12},{12,8},{16,20},{20,16},{24,28},{28,24},{32,36},... | collective-permute-start | bytes 1572872 | tf_op jit(solution)/shard_map/ppermute | solution.py:391
  3.3 33.8 %copy-start = (f32[256,2048]{1,0:T(8,128)S(1)}, f32[256,2048]{1,0:T(8,128)}, u32[]{:S(2)}) copy-start(f32[256,2048]{1,0:T(8,128)} %front_ref.1) | copy-start | bytes 6291460
  3.3 25.0 %collective-permute-start.2 = (f32[136,512]{1,0:T(8,128)S(1)}, f32[136,512]{1,0:T(8,128)S(1)}, u32[]{:S(2)}, u32[]{:S(2)}) collective-permute-start(f32[136,512]{1,0:T(8,128)S(1)} %corner.1), channel_id=1, source_target_pairs={{0,3},{4,7}} | collective-permute-start | bytes 835592 | tf_op jit(solution)/shard_map/ppermute | solution.py:389
  8.2 20.1 %collective-permute-start.1 = (f32[136,512]{1,0:T(8,128)S(1)}, f32[136,512]{1,0:T(8,128)S(1)}, u32[]{:S(2)}, u32[]{:S(2)}) collective-permute-start(f32[136,512]{1,0:T(8,128)S(1)} %corner.1), channel_id=1, source_target_pairs={{0,2},{4,6}} | collective-permute-start | bytes 835592 | tf_op jit(solution)/shard_map/ppermute | solution.py:389
  9.5 18.8 %collective-permute-start = (f32[136,512]{1,0:T(8,128)S(1)}, f32[136,512]{1,0:T(8,128)S(1)}, u32[]{:S(2)}, u32[]{:S(2)}) collective-permute-start(f32[136,512]{1,0:T(8,128)S(1)} %corner.1), channel_id=1, source_target_pairs={{0,1},{4,5}} | collective-permute-start | bytes 835592 | tf_op jit(solution)/shard_map/ppermute | solution.py:389
  10.9 10.7 %collective-permute-start.4 = (f32[2,32,512]{2,1,0:T(8,128)S(1)}, f32[2,32,512]{2,1,0:T(8,128)S(1)}, u32[]{:S(2)}, u32[]{:S(2)}) collective-permute-start(f32[2,32,512]{2,1,0:T(8,128)S(1)} %get-tuple-element.66), channel_id=1, source_target_pairs={{8,16},{12,20},{16,24},{20,28},{24,0},{28,4},{32,40},{36,44},{40,4... | collective-permute-start | bytes 393224 | tf_op jit(solution)/shard_map/ppermute | solution.py:395
  12.2 10.7 %collective-permute-start.5 = (f32[2,32,512]{2,1,0:T(8,128)S(1)}, f32[2,32,512]{2,1,0:T(8,128)S(1)}, u32[]{:S(2)}, u32[]{:S(2)}) collective-permute-start(f32[2,32,512]{2,1,0:T(8,128)S(1)} %get-tuple-element.67), channel_id=1, source_target_pairs={{8,24},{12,28},{16,0},{20,4},{24,8},{28,12},{32,48},{36,52},{40,56... | collective-permute-start | bytes 393224 | tf_op jit(solution)/shard_map/ppermute | solution.py:395
  21.6 5.7 %collective-permute-start.6 = (f32[2,32,512]{2,1,0:T(8,128)S(1)}, f32[2,32,512]{2,1,0:T(8,128)S(1)}, u32[]{:S(2)}, u32[]{:S(2)}) collective-permute-start(f32[2,32,512]{2,1,0:T(8,128)S(1)} %get-tuple-element.68), channel_id=1, source_target_pairs={{8,0},{12,4},{16,8},{20,12},{24,16},{28,20},{32,56},{36,60},{40,32... | collective-permute-start | bytes 393224 | tf_op jit(solution)/shard_map/ppermute | solution.py:395
  28.4 7.2 %collective-permute-start.7 = (f32[136,512]{1,0:T(8,128)S(1)}, f32[136,512]{1,0:T(8,128)S(1)}, u32[]{:S(2)}, u32[]{:S(2)}) collective-permute-start(f32[136,512]{1,0:T(8,128)S(1)} %add_add_fusion.refs_4_), channel_id=1, source_target_pairs={{0,8},{4,36},{1,9},{5,37},{2,10},{6,38},{3,11},{7,39}} | collective-permute-start | bytes 835592 | tf_op jit(solution)/shard_map/ppermute | solution.py:403
  29.7 3.9 %collective-permute-start.8 = (f32[2,32,512]{2,1,0:T(8,128)S(1)}, f32[2,32,512]{2,1,0:T(8,128)S(1)}, u32[]{:S(2)}, u32[]{:S(2)}) collective-permute-start(f32[2,32,512]{2,1,0:T(8,128)S(1)} %get-tuple-element.78), channel_id=1, source_target_pairs={{0,1},{4,5},{8,9},{12,13},{16,17},{20,21},{24,25},{28,29},{32,33},... | collective-permute-start | bytes 393224 | tf_op jit(solution)/shard_map/ppermute | solution.py:401
  31.0 3.3 %collective-permute-start.9 = (f32[2,32,512]{2,1,0:T(8,128)S(1)}, f32[2,32,512]{2,1,0:T(8,128)S(1)}, u32[]{:S(2)}, u32[]{:S(2)}) collective-permute-start(f32[2,32,512]{2,1,0:T(8,128)S(1)} %get-tuple-element.79), channel_id=1, source_target_pairs={{0,2},{4,6},{8,10},{12,14},{16,18},{20,22},{24,26},{28,30},{32,34}... | collective-permute-start | bytes 393224 | tf_op jit(solution)/shard_map/ppermute | solution.py:401
  32.3 3.2 %collective-permute-start.10 = (f32[2,32,512]{2,1,0:T(8,128)S(1)}, f32[2,32,512]{2,1,0:T(8,128)S(1)}, u32[]{:S(2)}, u32[]{:S(2)}) collective-permute-start(f32[2,32,512]{2,1,0:T(8,128)S(1)} %get-tuple-element.80), channel_id=1, source_target_pairs={{0,3},{4,7},{8,11},{12,15},{16,19},{20,23},{24,27},{28,31},{32,35}... | collective-permute-start | bytes 393224 | tf_op jit(solution)/shard_map/ppermute | solution.py:401
  35.6 9.8 %collective-permute-start.11 = (f32[264,512]{1,0:T(8,128)S(1)}, f32[264,512]{1,0:T(8,128)S(1)}, u32[]{:S(2)}, u32[]{:S(2)}) collective-permute-start(f32[264,512]{1,0:T(8,128)S(1)} %merge.1.own_ref), channel_id=1, source_target_pairs={{0,24},{4,100},{8,16},{12,108},{16,8},{20,116},{24,0},{28,124},{32... | collective-permute-start | bytes 1622024 | tf_op jit(solution)/shard_map/ppermute | solution.py:411
  35.7 9.8 %collective-permute-start.12 = (f32[256,512]{1,0:T(8,128)S(1)}, f32[256,512]{1,0:T(8,128)S(1)}, u32[]{:S(2)}, u32[]{:S(2)}) collective-permute-start(f32[256,512]{1,0:T(8,128)S(1)} %slice.3.lead_ref.refs_0_), channel_id=1, source_target_pairs={{0,1},{4,5},{8,9},{12,13},{16,17},{20,21},{24,25},{28,29},{32,33},... | collective-permute-start | bytes 1572872 | tf_op jit(solution)/shard_map/ppermute | solution.py:410
  39.1 0.8 copy-start.3
  39.9 0.8 copy-start.5
  45.5 12.3 %copy-start.6 = (f32[256,512]{1,0:T(8,128)S(1)}, f32[256,512]{1,0:T(8,128)}, u32[]{:S(2)}) copy-start(f32[256,512]{1,0:T(8,128)} %copy-done.5) | copy-start | bytes 1572868
  45.5 12.3 %copy-start.4 = (f32[256,512]{1,0:T(8,128)S(1)}, f32[256,512]{1,0:T(8,128)}, u32[]{:S(2)}) copy-start(f32[256,512]{1,0:T(8,128)} %copy-done.3) | copy-start | bytes 1572868
  45.5 8.6 %collective-permute-start.13 = (f32[264,512]{1,0:T(8,128)S(1)}, f32[264,512]{1,0:T(8,128)S(1)}, u32[]{:S(2)}, u32[]{:S(2)}) collective-permute-start(f32[264,512]{1,0:T(8,128)S(1)} %join.3.own_ref), channel_id=1, source_target_pairs={{0,32},{4,12},{8,40},{12,4},{16,48},{20,28},{24,56},{28,20},{32,0}... | collective-permute-start | bytes 1622024 | tf_op jit(solution)/shard_map/ppermute | solution.py:414
  45.7 12.1 %collective-permute-start.14 = (f32[256,512]{1,0:T(8,128)S(1)}, f32[256,512]{1,0:T(8,128)S(1)}, u32[]{:S(2)}, u32[]{:S(2)}) collective-permute-start(f32[256,512]{1,0:T(8,128)S(1)} %broadcast_select_fusion), channel_id=1, source_target_pairs={{0,3},{1,2},{4,7},{5,6},{8,11},{9,10},{12,15},{13,14},{16,19},{17,... | collective-permute-start | bytes 1572872 | tf_op jit(solution)/shard_map/ppermute | solution.py:413
  57.8 12.5 %collective-permute-start.15 = (f32[392,512]{1,0:T(8,128)S(1)}, f32[392,512]{1,0:T(8,128)S(1)}, u32[]{:S(2)}, u32[]{:S(2)}) collective-permute-start(f32[392,512]{1,0:T(8,128)S(1)} %join.4.own_ref), channel_id=1, source_target_pairs={{0,96},{4,28},{8,104},{12,20},{16,112},{20,12},{24,120},{28,4},{32... | collective-permute-start | bytes 2408456 | tf_op jit(solution)/shard_map/ppermute | solution.py:417
  57.8 12.6 %collective-permute-start.16 = (f32[256,512]{1,0:T(8,128)S(1)}, f32[256,512]{1,0:T(8,128)S(1)}, u32[]{:S(2)}, u32[]{:S(2)}) collective-permute-start(f32[256,512]{1,0:T(8,128)S(1)} %copy-done.6), channel_id=1, source_target_pairs={{0,1},{1,2},{2,3},{3,0},{4,5},{5,6},{6,7},{7,4},{8,9},{9,10},{10,1... | collective-permute-start | bytes 1572872 | tf_op jit(solution)/shard_map/ppermute | solution.py:420
  57.8 12.6 %collective-permute-start.17 = (f32[256,512]{1,0:T(8,128)S(1)}, f32[256,512]{1,0:T(8,128)S(1)}, u32[]{:S(2)}, u32[]{:S(2)}) collective-permute-start(f32[256,512]{1,0:T(8,128)S(1)} %copy-done.4), channel_id=1, source_target_pairs={{0,3},{1,0},{2,1},{3,2},{4,7},{5,4},{6,5},{7,6},{8,11},{9,8},{10,9... | collective-permute-start | bytes 1572872 | tf_op jit(solution)/shard_map/ppermute | solution.py:420
  70.4 11.7 %collective-permute-start.19 = (f32[136,512]{1,0:T(8,128)S(1)}, f32[136,512]{1,0:T(8,128)S(1)}, u32[]{:S(2)}, u32[]{:S(2)}) collective-permute-start(f32[136,512]{1,0:T(8,128)S(1)} %get-tuple-element.108.own_ref), channel_id=1, source_target_pairs={{0,4},{4,0},{8,12},{12,8},{16,20},{20,16},{24,28},{28,24},{32,36},... | collective-permute-start | bytes 835592 | tf_op jit(solution)/shard_map/ppermute | solution.py:422
  77.2 23.4 %collective-permute-start.20 = (f32[256,512]{1,0:T(8,128)S(1)}, f32[256,512]{1,0:T(8,128)S(1)}, u32[]{:S(2)}, u32[]{:S(2)}) collective-permute-start(f32[256,512]{1,0:T(8,128)S(1)} %get-tuple-element.114), channel_id=1, source_target_pairs={{0,2},{1,3},{2,0},{3,1},{4,6},{5,7},{6,4},{7,5},{8,10},{9,11},{10,... | collective-permute-start | bytes 1572872 | tf_op jit(solution)/shard_map/ppermute | solution.py:424
  79.9 20.7 %collective-permute-start.18 = (f32[512,512]{1,0:T(8,128)S(1)}, f32[512,512]{1,0:T(8,128)S(1)}, u32[]{:S(2)}, u32[]{:S(2)}) collective-permute-start(f32[512,512]{1,0:T(8,128)S(1)} %get-tuple-element.126.refs_5_), channel_id=1, source_target_pairs={{0,8},{4,36},{8,0},{12,44},{16,24},{20,52},{24,16},{28,60},{32,40}... | collective-permute-start | bytes 3145736 | tf_op jit(solution)/shard_map/ppermute | solution.py:423
  100.6 4.3 %copy-start.1 = (f32[256,2048]{1,0:T(8,128)S(1)}, f32[256,2048]{1,0:T(8,128)}, u32[]{:S(2)}) copy-start(f32[256,2048]{1,0:T(8,128)} %refs_9_.1) | copy-start | bytes 6291460
  100.6 3.5 %collective-permute-start.21 = (f32[512,512]{1,0:T(8,128)S(1)}, f32[512,512]{1,0:T(8,128)S(1)}, u32[]{:S(2)}, u32[]{:S(2)}) collective-permute-start(f32[512,512]{1,0:T(8,128)S(1)} %get-tuple-element.126.refs_5_), channel_id=1, source_target_pairs={{0,4},{4,0},{8,12},{12,8},{16,20},{20,16},{24,28},{28,24},{32,36},... | collective-permute-start | bytes 3145736 | tf_op jit(solution)/shard_map/ppermute | solution.py:429
  100.7 4.1 %collective-permute-start.22 = (f32[512,512]{1,0:T(8,128)S(1)}, f32[512,512]{1,0:T(8,128)S(1)}, u32[]{:S(2)}, u32[]{:S(2)}) collective-permute-start(f32[512,512]{1,0:T(8,128)S(1)} %collective-permute-done.18.refs_6_), channel_id=1, source_target_pairs={{0,4},{4,0},{8,12},{12,8},{16,20},{20,16},{24,28},{28,24},{32,36},... | collective-permute-start | bytes 3145736 | tf_op jit(solution)/shard_map/ppermute | solution.py:428

commit v14 on v13

--- a/solution.py
+++ b/solution.py
@@ -277,11 +277,11 @@
 
 
 def weight_kernel(*refs):
-    rows, inverse = refs[:3], refs[3:6]
-    panel_ref, weight_ref, rows_ref = refs[6:]
+    rows, inverse = refs[:4], refs[4:7]
+    panel_ref, weight_ref, rows_ref = refs[7:]
     for index, ref in enumerate(rows):
 
-        @pl.when(jnp.minimum(lax.axis_index("col"), 2) == index)
+        @pl.when(lax.axis_index("col") == index)
         def _():
             rows_ref[...] = ref[...]
 
@@ -301,7 +301,7 @@
     return pl.pallas_call(
         weight_kernel,
         out_shape=[jax.ShapeDtypeStruct(shape, jnp.float32)] * 2,
-        in_specs=[whole] * 6,
+        in_specs=[whole] * 7,
         out_specs=[whole] * 2,
         scratch_shapes=[pltpu.VMEM(shape, jnp.float32)],
         compiler_params=pltpu.CompilerParams(vmem_limit_bytes=16 << 20),
@@ -407,12 +407,11 @@
     *pieces, plan = local_call(pick_kernel, "pick", [(height, 2 * PW)] * 4, 1, [(4, 8)])(tile_map, front)
 
     load, lead = lax.optimization_barrier((load, lead))
-    near = lax.ppermute(lead, "col", [(0, 1)])
+    copies = [lax.ppermute(lead, "col", [(0, to)]) for to in (1, 2, 3)]
     load = local_call(partial(join_kernel, 64), "join", [(128 + BLOCK, LEAD)])(load, lax.ppermute(load, "row", every[1]))[0]
-    load, near, *pieces = lax.optimization_barrier((load, near, *pieces))
-    far = lax.ppermute(jnp.where(lax.axis_index("col") == 1, near, lead), "col", [(0, 3), (1, 2)])
+    load, copies[0], copies[2], *pieces = lax.optimization_barrier((load, copies[0], copies[2], *pieces))
     load = local_call(partial(join_kernel, 128), "join", [(256 + BLOCK, LEAD)])(load, lax.ppermute(load, "row", every[2]))[0]
-    load, far, *pieces = lax.optimization_barrier((load, far, *pieces))
+    load, copies[1], *pieces = lax.optimization_barrier((load, copies[1], *pieces))
     gathered, block = local_call(partial(join_kernel, 256), "join", [(512, LEAD), (BLOCK, LEAD)])(
         load, lax.ppermute(load, "row", every[3])
     )
@@ -422,12 +421,12 @@
     other = lax.ppermute(block, "row", swap)
     late = lax.ppermute(gathered, "row", every[0])
     pieces[2] = lax.ppermute(pieces[2], "col", ring[2])
+    other_gathered = lax.ppermute(gathered, "row", swap)
 
     inverse = factor(block, other)
-    late, gathered, inverse, pieces = lax.optimization_barrier((late, gathered, inverse, pieces))
+    late, other_gathered, inverse, pieces = lax.optimization_barrier((late, other_gathered, inverse, pieces))
     other_late = lax.ppermute(late, "row", swap)
-    other_gathered = lax.ppermute(gathered, "row", swap)
-    panel, weight = weigh([lead, near, far], inverse)
+    panel, weight = weigh([lead, *copies], inverse)
     updated = update(plan, weight, pieces, [gathered, late, other_gathered, other_late], ancestor)
     return panel, updated
 

time: 113 us -> 117 us (1.035)
  waiting for transfers between devices: 35.8 us -> 39 us
  starting transfers between devices: 40.4 us -> 42.9 us
  local copies, waits for them, and re-layouts: 2.69 us -> 1.1 us
    ppermute x1, waiting for transfers between devices: 3.26 us -> 6.8 us  [shards(): lax.ppermute(load, 'row', every[2])]
    ppermute x1, waiting for transfers between devices: 4.76 us -> 1.34 us  [shards(): lax.ppermute(load, 'row', every[1])]
    ppermute x2 -> x3, waiting for transfers between devices: 3.64 us -> 6.87 us  [shards(): copies = [lax.ppermute(lead, 'col', [(0, to)]) for to in (1, 2, 3)]]
    ppermute x1, starting transfers between devices: 6.72 us -> 9.79 us  [shards(): other = lax.ppermute(block, 'row', swap)]
    ppermute x1, starting transfers between devices: 2.22 us -> 0.09 us  [shards(): late = lax.ppermute(gathered, 'row', every[0])]
    unnamed x14 -> x6, local copies, waits for them, and re-layouts: 1.61 us -> 0.02 us
    ppermute x2 -> x3, starting transfers between devices: 6.46 us -> 7.64 us  [shards(): copies = [lax.ppermute(lead, 'col', [(0, to)]) for to in (1, 2, 3)]]
  transfers between devices with their start and end apart: 23 -> 24, of which waited for: 9 -> 10; matrix products, arithmetic and copies ran while one was open for 0% -> 0% of each run, Pallas kernels for 22% -> 21%
where the time goes in v14:
time: 117 us
  starting transfers between devices  42.9 us (37%)
  waiting for transfers between devices  39 us (33%)
  Pallas kernels  32.9 us (28%)
    pallas_call x9, Pallas kernels, call(): pl.pallas_call(kernel, out_shape=[jax.ShapeDtypeStruct(shape, jnp.float32...  21.8 us
    ppermute x3, waiting for transfers between devices, shards(): parts[hop] = lax.ppermute(parts[hop], 'row', pairs)  12.5 us
    ppermute x1, starting transfers between devices, shards(): other = lax.ppermute(block, 'row', swap)  9.79 us
    ppermute x1, waiting for transfers between devices, shards(): lax.ppermute(load, 'row', every[3])  9.55 us
    pallas_call x1, Pallas kernels, update(): pl.pallas_call(update_kernel, out_shape=jax.ShapeDtypeStruct(base.shape,...  8.11 us
    ppermute x3, starting transfers between devices, shards(): copies = [lax.ppermute(lead, 'col', [(0, to)]) for to in (1, 2, 3)]  7.64 us
    ppermute x3, starting transfers between devices, shards(): lax.ppermute(blocks[0], ('row', 'col'), [(4 * core, 4 * core + to) for co...  7.47 us
    ppermute x3, waiting for transfers between devices, shards(): copies = [lax.ppermute(lead, 'col', [(0, to)]) for to in (1, 2, 3)]  6.87 us
  transfers between devices with their start and end apart: 24, of which 10 were waited for; matrix products, arithmetic and copies ran while one was open for 0% of the time, Pallas kernels for 21%

profile of v14, /device:TPU:1, one launch (start us, length us, event | category | flops | bytes accessed | tf_op | source)
XLA Modules:
  0.0 116.9 jit_solution(10866896255832204477)
XLA Ops:
  0.6 0.0 copy-start.2
  0.6 1.1 slice.3.lead_ref.refs_0_
  1.7 1.5 %collective-permute-start.3 = (f32[256,512]{1,0:T(8,128)S(1)}, f32[256,512]{1,0:T(8,128)S(1)}, u32[]{:S(2)}, u32[]{:S(2)}) collective-permute-start(f32[256,512]{1,0:T(8,128)S(1)} %slice.3.lead_ref.refs_0_), channel_id=1, source_target_pairs={{0,4},{4,0},{8,12},{12,8},{16,20},{20,16},{24,28},{28,24},{32,36},... | collective-permute-start | bytes 1572872 | tf_op jit(solution)/shard_map/ppermute | solution.py:391
  3.3 0.0 copy-start
  3.3 4.9 %collective-permute-start.2 = (f32[136,512]{1,0:T(8,128)S(1)}, f32[136,512]{1,0:T(8,128)S(1)}, u32[]{:S(2)}, u32[]{:S(2)}) collective-permute-start(f32[136,512]{1,0:T(8,128)S(1)} %corner.1), channel_id=1, source_target_pairs={{0,3},{4,7}} | collective-permute-start | bytes 835592 | tf_op jit(solution)/shard_map/ppermute | solution.py:389
  8.2 1.3 %collective-permute-start.1 = (f32[136,512]{1,0:T(8,128)S(1)}, f32[136,512]{1,0:T(8,128)S(1)}, u32[]{:S(2)}, u32[]{:S(2)}) collective-permute-start(f32[136,512]{1,0:T(8,128)S(1)} %corner.1), channel_id=1, source_target_pairs={{0,2},{4,6}} | collective-permute-start | bytes 835592 | tf_op jit(solution)/shard_map/ppermute | solution.py:389
  9.5 1.3 %collective-permute-start = (f32[136,512]{1,0:T(8,128)S(1)}, f32[136,512]{1,0:T(8,128)S(1)}, u32[]{:S(2)}, u32[]{:S(2)}) collective-permute-start(f32[136,512]{1,0:T(8,128)S(1)} %corner.1), channel_id=1, source_target_pairs={{0,1},{4,5}} | collective-permute-start | bytes 835592 | tf_op jit(solution)/shard_map/ppermute | solution.py:389
  10.8 0.0 collective-permute-done.3.mate_ref
  10.8 0.1 share.1
  10.9 1.3 %collective-permute-start.4 = (f32[2,32,512]{2,1,0:T(8,128)S(1)}, f32[2,32,512]{2,1,0:T(8,128)S(1)}, u32[]{:S(2)}, u32[]{:S(2)}) collective-permute-start(f32[2,32,512]{2,1,0:T(8,128)S(1)} %get-tuple-element.67), channel_id=1, source_target_pairs={{8,16},{12,20},{16,24},{20,28},{24,0},{28,4},{32,40},{36,44},{40,4... | collective-permute-start | bytes 393224 | tf_op jit(solution)/shard_map/ppermute | solution.py:395
  12.2 1.3 %collective-permute-start.5 = (f32[2,32,512]{2,1,0:T(8,128)S(1)}, f32[2,32,512]{2,1,0:T(8,128)S(1)}, u32[]{:S(2)}, u32[]{:S(2)}) collective-permute-start(f32[2,32,512]{2,1,0:T(8,128)S(1)} %get-tuple-element.68), channel_id=1, source_target_pairs={{8,24},{12,28},{16,0},{20,4},{24,8},{28,12},{32,48},{36,52},{40,56... | collective-permute-start | bytes 393224 | tf_op jit(solution)/shard_map/ppermute | solution.py:395
  13.5 8.1 %collective-permute-done.4.refs_1_ = f32[2,32,512]{2,1,0:T(8,128)S(1)} collective-permute-done((f32[2,32,512]{2,1,0:T(8,128)S(1)}, f32[2,32,512]{2,1,0:T(8,128)S(1)}, u32[]{:S(2)}, u32[]{:S(2)}) %collective-permute-start.4) | collective-permute-done | bytes 131104 | tf_op jit(solution)/shard_map/ppermute | solution.py:395
  21.6 1.3 %collective-permute-start.6 = (f32[2,32,512]{2,1,0:T(8,128)S(1)}, f32[2,32,512]{2,1,0:T(8,128)S(1)}, u32[]{:S(2)}, u32[]{:S(2)}) collective-permute-start(f32[2,32,512]{2,1,0:T(8,128)S(1)} %get-tuple-element.69), channel_id=1, source_target_pairs={{8,0},{12,4},{16,8},{20,12},{24,16},{28,20},{32,56},{36,60},{40,32... | collective-permute-start | bytes 393224 | tf_op jit(solution)/shard_map/ppermute | solution.py:395
  22.9 0.0 collective-permute-done.5.refs_2_
  22.9 4.4 %collective-permute-done.6.refs_3_ = f32[2,32,512]{2,1,0:T(8,128)S(1)} collective-permute-done((f32[2,32,512]{2,1,0:T(8,128)S(1)}, f32[2,32,512]{2,1,0:T(8,128)S(1)}, u32[]{:S(2)}, u32[]{:S(2)}) %collective-permute-start.6) | collective-permute-done | bytes 131104 | tf_op jit(solution)/shard_map/ppermute | solution.py:395
  27.3 0.0 copy-done.2
  27.3 1.0 sort.1
  28.3 0.0 collective-permute-done.2
  28.3 0.0 collective-permute-done.1
  28.3 0.0 collective-permute-done
  28.3 0.1 add_add_fusion.refs_4_
  28.4 1.3 %collective-permute-start.7 = (f32[136,512]{1,0:T(8,128)S(1)}, f32[136,512]{1,0:T(8,128)S(1)}, u32[]{:S(2)}, u32[]{:S(2)}) collective-permute-start(f32[136,512]{1,0:T(8,128)S(1)} %add_add_fusion.refs_4_), channel_id=1, source_target_pairs={{0,8},{4,36},{1,9},{5,37},{2,10},{6,38},{3,11},{7,39}} | collective-permute-start | bytes 835592 | tf_op jit(solution)/shard_map/ppermute | solution.py:403
  29.7 1.3 %collective-permute-start.8 = (f32[2,32,512]{2,1,0:T(8,128)S(1)}, f32[2,32,512]{2,1,0:T(8,128)S(1)}, u32[]{:S(2)}, u32[]{:S(2)}) collective-permute-start(f32[2,32,512]{2,1,0:T(8,128)S(1)} %get-tuple-element.79), channel_id=1, source_target_pairs={{0,1},{4,5},{8,9},{12,13},{16,17},{20,21},{24,25},{28,29},{32,33},... | collective-permute-start | bytes 393224 | tf_op jit(solution)/shard_map/ppermute | solution.py:401
  31.0 1.3 %collective-permute-start.9 = (f32[2,32,512]{2,1,0:T(8,128)S(1)}, f32[2,32,512]{2,1,0:T(8,128)S(1)}, u32[]{:S(2)}, u32[]{:S(2)}) collective-permute-start(f32[2,32,512]{2,1,0:T(8,128)S(1)} %get-tuple-element.80), channel_id=1, source_target_pairs={{0,2},{4,6},{8,10},{12,14},{16,18},{20,22},{24,26},{28,30},{32,34}... | collective-permute-start | bytes 393224 | tf_op jit(solution)/shard_map/ppermute | solution.py:401
  32.3 1.3 %collective-permute-start.10 = (f32[2,32,512]{2,1,0:T(8,128)S(1)}, f32[2,32,512]{2,1,0:T(8,128)S(1)}, u32[]{:S(2)}, u32[]{:S(2)}) collective-permute-start(f32[2,32,512]{2,1,0:T(8,128)S(1)} %get-tuple-element.81), channel_id=1, source_target_pairs={{0,3},{4,7},{8,11},{12,15},{16,19},{20,23},{24,27},{28,31},{32,35}... | collective-permute-start | bytes 393224 | tf_op jit(solution)/shard_map/ppermute | solution.py:401
  33.7 0.0 collective-permute-done.8.refs_1_
  33.7 0.7 collective-permute-done.9.refs_2_
  34.3 1.2 %collective-permute-done.10.refs_3_ = f32[2,32,512]{2,1,0:T(8,128)S(1)} collective-permute-done((f32[2,32,512]{2,1,0:T(8,128)S(1)}, f32[2,32,512]{2,1,0:T(8,128)S(1)}, u32[]{:S(2)}, u32[]{:S(2)}) %collective-permute-start.10) | collective-permute-done | bytes 131104 | tf_op jit(solution)/shard_map/ppermute | solution.py:401
  35.6 0.0 collective-permute-done.7.refs_5_
  35.6 0.1 merge.1.own_ref
  35.6 0.1 collective-permute-start.11
  35.7 5.0 %collective-permute-start.13 = (f32[256,512]{1,0:T(8,128)S(1)}, f32[256,512]{1,0:T(8,128)S(1)}, u32[]{:S(2)}, u32[]{:S(2)}) collective-permute-start(f32[256,512]{1,0:T(8,128)S(1)} %slice.3.lead_ref.refs_0_), channel_id=1, source_target_pairs={{0,3},{4,7},{8,11},{12,15},{16,19},{20,23},{24,27},{28,31},{32,35}... | collective-permute-start | bytes 1572872 | tf_op jit(solution)/shard_map/ppermute | solution.py:410
  40.7 1.3 %collective-permute-start.12 = (f32[256,512]{1,0:T(8,128)S(1)}, f32[256,512]{1,0:T(8,128)S(1)}, u32[]{:S(2)}, u32[]{:S(2)}) collective-permute-start(f32[256,512]{1,0:T(8,128)S(1)} %slice.3.lead_ref.refs_0_), channel_id=1, source_target_pairs={{0,1},{4,5},{8,9},{12,13},{16,17},{20,21},{24,25},{28,29},{32,33},... | collective-permute-start | bytes 1572872 | tf_op jit(solution)/shard_map/ppermute | solution.py:410
  42.1 2.0 %pick.1 = (f32[256,512]{1,0:T(8,128)S(1)}, f32[256,512]{1,0:T(8,128)S(1)}, f32[256,512]{1,0:T(8,128)S(1)}, f32[256,512]{1,0:T(8,128)S(1)}, s32[4,8]{1,0:T(4,128)S(1)}) custom-call(s32[32]{0:T(128)S(1)} %copy-done.2, f32[256,2048]{1,0:T(8,128)S(1)} %copy-done), custom_call_target="tpu_custom_call" | custom-call | flops 1024 | bytes 1024 | tf_op jit(solution)/shard_map/pick/pallas_call | solution.py:109
  44.1 1.3 %collective-permute-done.11.got_ref = f32[264,512]{1,0:T(8,128)S(1)} collective-permute-done((f32[264,512]{1,0:T(8,128)S(1)}, f32[264,512]{1,0:T(8,128)S(1)}, u32[]{:S(2)}, u32[]{:S(2)}) %collective-permute-start.11) | collective-permute-done | bytes 540704 | tf_op jit(solution)/shard_map/ppermute | solution.py:411
  45.5 3.1 %collective-permute-done.13.refs_3_ = f32[256,512]{1,0:T(8,128)S(1)} collective-permute-done((f32[256,512]{1,0:T(8,128)S(1)}, f32[256,512]{1,0:T(8,128)S(1)}, u32[]{:S(2)}, u32[]{:S(2)}) %collective-permute-start.13) | collective-permute-done | bytes 524320 | tf_op jit(solution)/shard_map/ppermute | solution.py:410
  48.6 1.3 %collective-permute-done.12.refs_1_ = f32[256,512]{1,0:T(8,128)S(1)} collective-permute-done((f32[256,512]{1,0:T(8,128)S(1)}, f32[256,512]{1,0:T(8,128)S(1)}, u32[]{:S(2)}, u32[]{:S(2)}) %collective-permute-start.12) | collective-permute-done | bytes 524320 | tf_op jit(solution)/shard_map/ppermute | solution.py:410
  49.9 0.1 collective-permute-start.14
  50.0 1.3 %collective-permute-start.15 = (f32[256,512]{1,0:T(8,128)S(1)}, f32[256,512]{1,0:T(8,128)S(1)}, u32[]{:S(2)}, u32[]{:S(2)}) collective-permute-start(f32[256,512]{1,0:T(8,128)S(1)} %slice.3.lead_ref.refs_0_), channel_id=1, source_target_pairs={{0,2},{4,6},{8,10},{12,14},{16,18},{20,22},{24,26},{28,30},{32,34}... | collective-permute-start | bytes 1572872 | tf_op jit(solution)/shard_map/ppermute | solution.py:410
  51.3 6.8 %collective-permute-done.14.got_ref = f32[264,512]{1,0:T(8,128)S(1)} collective-permute-done((f32[264,512]{1,0:T(8,128)S(1)}, f32[264,512]{1,0:T(8,128)S(1)}, u32[]{:S(2)}, u32[]{:S(2)}) %collective-permute-start.14) | collective-permute-done | bytes 540704 | tf_op jit(solution)/shard_map/ppermute | solution.py:413
  58.1 0.1 join.4.own_ref
  58.2 2.5 %collective-permute-done.15.refs_2_ = f32[256,512]{1,0:T(8,128)S(1)} collective-permute-done((f32[256,512]{1,0:T(8,128)S(1)}, f32[256,512]{1,0:T(8,128)S(1)}, u32[]{:S(2)}, u32[]{:S(2)}) %collective-permute-start.15) | collective-permute-done | bytes 524320 | tf_op jit(solution)/shard_map/ppermute | solution.py:410
  60.6 0.0 collective-permute-start.16
  60.6 0.0 collective-permute-start.17
  60.6 2.7 %collective-permute-start.18 = (f32[256,512]{1,0:T(8,128)S(1)}, f32[256,512]{1,0:T(8,128)S(1)}, u32[]{:S(2)}, u32[]{:S(2)}) collective-permute-start(f32[256,512]{1,0:T(8,128)S(1)} %get-tuple-element.108), channel_id=1, source_target_pairs={{0,3},{1,0},{2,1},{3,2},{4,7},{5,4},{6,5},{7,6},{8,11},{9,8},{10,9... | collective-permute-start | bytes 1572872 | tf_op jit(solution)/shard_map/ppermute | solution.py:419
  63.3 9.5 %collective-permute-done.16.got_ref = f32[392,512]{1,0:T(8,128)S(1)} collective-permute-done((f32[392,512]{1,0:T(8,128)S(1)}, f32[392,512]{1,0:T(8,128)S(1)}, u32[]{:S(2)}, u32[]{:S(2)}) %collective-permute-start.16) | collective-permute-done | bytes 802848 | tf_op jit(solution)/shard_map/ppermute | solution.py:416
  72.9 0.1 join.5
  73.0 0.0 collective-permute-done.17.refs_2_
  73.0 0.0 collective-permute-done.18.refs_4_
  73.0 9.8 %collective-permute-start.21 = (f32[136,512]{1,0:T(8,128)S(1)}, f32[136,512]{1,0:T(8,128)S(1)}, u32[]{:S(2)}, u32[]{:S(2)}) collective-permute-start(f32[136,512]{1,0:T(8,128)S(1)} %get-tuple-element.110.own_ref), channel_id=1, source_target_pairs={{0,4},{4,0},{8,12},{12,8},{16,20},{20,16},{24,28},{28,24},{32,36},... | collective-permute-start | bytes 835592 | tf_op jit(solution)/shard_map/ppermute | solution.py:421
  82.8 0.1 collective-permute-start.20
  82.9 0.1 collective-permute-start.19
  83.0 3.6 %collective-permute-start.22 = (f32[256,512]{1,0:T(8,128)S(1)}, f32[256,512]{1,0:T(8,128)S(1)}, u32[]{:S(2)}, u32[]{:S(2)}) collective-permute-start(f32[256,512]{1,0:T(8,128)S(1)} %get-tuple-element.116), channel_id=1, source_target_pairs={{0,2},{1,3},{2,0},{3,1},{4,6},{5,7},{6,4},{7,5},{8,10},{9,11},{10,... | collective-permute-start | bytes 1572872 | tf_op jit(solution)/shard_map/ppermute | solution.py:423
  86.6 0.0 collective-permute-done.21.other_ref
  86.6 18.4 %factor.1 = (f32[256,256]{1,0:T(8,128)S(1)}, f32[256,256]{1,0:T(8,128)S(1)}, f32[256,256]{1,0:T(8,128)S(1)}) custom-call(f32[136,512]{1,0:T(8,128)S(1)} %get-tuple-element.110.own_ref, f32[136,512]{1,0:T(8,128)S(1)} %collective-permute-done.21.other_ref), custom_call_target="tpu_custom_call" | custom-call | flops 21474836480 | bytes 1048576 | tf_op jit(solution)/shard_map/factor/pallas_call | solution.py:109
  105.0 0.0 copy-start.1
  105.0 0.0 collective-permute-done.22.refs_3_
  105.0 0.0 collective-permute-done.20.refs_7_
  105.0 0.0 collective-permute-done.19.refs_6_
  105.0 0.8 collective-permute-start.23
  105.8 2.9 %weigh.1 = (f32[256,512]{1,0:T(8,128)}, f32[256,512]{1,0:T(8,128)S(1)}) custom-call(f32[256,512]{1,0:T(8,128)S(1)} %slice.3.lead_ref.refs_0_, f32[256,512]{1,0:T(8,128)S(1)} %collective-permute-done.12.refs_1_, f32[256,512]{1,0:T(8,128)S(1)} %collective-permute-done.15.refs_2_, f32[256,512]{1,0:T(8,128)S(1)} %collective-permute-done.13.refs_3_, ...), custom_call_target="tpu_custom_call" | custom-call | flops 1024 | bytes 1024 | tf_op jit(solution)/shard_map/weigh/pallas_call | solution.py:301
  108.8 0.0 collective-permute-done.23.refs_8_
  108.8 0.0 copy-done.1
  108.8 8.1 %update.1 = f32[256,2048]{1,0:T(8,128)} custom-call(s32[4,8]{1,0:T(4,128)S(1)} %get-tuple-element.122.plan, f32[256,512]{1,0:T(8,128)S(1)} %get-tuple-element.123.refs_0_, f32[256,512]{1,0:T(8,128)S(1)} %get-tuple-element.124.refs_1_, f32[256,512]{1,0:T(8,128)S(1)} %collective-permute-done.17.refs_2_, f32[256,512]{1,0:T(8,128)S(1)} %collective-permute-done.22.refs_3_, ...), custom_call_target="tpu_custom_call" | custom-call | tf_op jit(solution)/shard_map/update/pallas_call | solution.py:350
  (3 shorter events, 0.1 us)
Async XLA Ops:
  0.6 26.7 %copy-start.2 = (s32[32]{0:T(128)S(1)}, s32[32]{0:T(128)}, u32[]{:S(2)}) copy-start(s32[32]{0:T(128)} %map_ref.3) | copy-start | bytes 388
  1.7 9.1 %collective-permute-start.3 = (f32[256,512]{1,0:T(8,128)S(1)}, f32[256,512]{1,0:T(8,128)S(1)}, u32[]{:S(2)}, u32[]{:S(2)}) collective-permute-start(f32[256,512]{1,0:T(8,128)S(1)} %slice.3.lead_ref.refs_0_), channel_id=1, source_target_pairs={{0,4},{4,0},{8,12},{12,8},{16,20},{20,16},{24,28},{28,24},{32,36},... | collective-permute-start | bytes 1572872 | tf_op jit(solution)/shard_map/ppermute | solution.py:391
  3.3 38.8 %copy-start = (f32[256,2048]{1,0:T(8,128)S(1)}, f32[256,2048]{1,0:T(8,128)}, u32[]{:S(2)}) copy-start(f32[256,2048]{1,0:T(8,128)} %front_ref.1) | copy-start | bytes 6291460
  3.3 25.0 %collective-permute-start.2 = (f32[136,512]{1,0:T(8,128)S(1)}, f32[136,512]{1,0:T(8,128)S(1)}, u32[]{:S(2)}, u32[]{:S(2)}) collective-permute-start(f32[136,512]{1,0:T(8,128)S(1)} %corner.1), channel_id=1, source_target_pairs={{0,3},{4,7}} | collective-permute-start | bytes 835592 | tf_op jit(solution)/shard_map/ppermute | solution.py:389
  8.2 20.1 %collective-permute-start.1 = (f32[136,512]{1,0:T(8,128)S(1)}, f32[136,512]{1,0:T(8,128)S(1)}, u32[]{:S(2)}, u32[]{:S(2)}) collective-permute-start(f32[136,512]{1,0:T(8,128)S(1)} %corner.1), channel_id=1, source_target_pairs={{0,2},{4,6}} | collective-permute-start | bytes 835592 | tf_op jit(solution)/shard_map/ppermute | solution.py:389
  9.5 18.8 %collective-permute-start = (f32[136,512]{1,0:T(8,128)S(1)}, f32[136,512]{1,0:T(8,128)S(1)}, u32[]{:S(2)}, u32[]{:S(2)}) collective-permute-start(f32[136,512]{1,0:T(8,128)S(1)} %corner.1), channel_id=1, source_target_pairs={{0,1},{4,5}} | collective-permute-start | bytes 835592 | tf_op jit(solution)/shard_map/ppermute | solution.py:389
  10.9 10.7 %collective-permute-start.4 = (f32[2,32,512]{2,1,0:T(8,128)S(1)}, f32[2,32,512]{2,1,0:T(8,128)S(1)}, u32[]{:S(2)}, u32[]{:S(2)}) collective-permute-start(f32[2,32,512]{2,1,0:T(8,128)S(1)} %get-tuple-element.67), channel_id=1, source_target_pairs={{8,16},{12,20},{16,24},{20,28},{24,0},{28,4},{32,40},{36,44},{40,4... | collective-permute-start | bytes 393224 | tf_op jit(solution)/shard_map/ppermute | solution.py:395
  12.2 10.7 %collective-permute-start.5 = (f32[2,32,512]{2,1,0:T(8,128)S(1)}, f32[2,32,512]{2,1,0:T(8,128)S(1)}, u32[]{:S(2)}, u32[]{:S(2)}) collective-permute-start(f32[2,32,512]{2,1,0:T(8,128)S(1)} %get-tuple-element.68), channel_id=1, source_target_pairs={{8,24},{12,28},{16,0},{20,4},{24,8},{28,12},{32,48},{36,52},{40,56... | collective-permute-start | bytes 393224 | tf_op jit(solution)/shard_map/ppermute | solution.py:395
  21.6 5.7 %collective-permute-start.6 = (f32[2,32,512]{2,1,0:T(8,128)S(1)}, f32[2,32,512]{2,1,0:T(8,128)S(1)}, u32[]{:S(2)}, u32[]{:S(2)}) collective-permute-start(f32[2,32,512]{2,1,0:T(8,128)S(1)} %get-tuple-element.69), channel_id=1, source_target_pairs={{8,0},{12,4},{16,8},{20,12},{24,16},{28,20},{32,56},{36,60},{40,32... | collective-permute-start | bytes 393224 | tf_op jit(solution)/shard_map/ppermute | solution.py:395
  28.4 7.2 %collective-permute-start.7 = (f32[136,512]{1,0:T(8,128)S(1)}, f32[136,512]{1,0:T(8,128)S(1)}, u32[]{:S(2)}, u32[]{:S(2)}) collective-permute-start(f32[136,512]{1,0:T(8,128)S(1)} %add_add_fusion.refs_4_), channel_id=1, source_target_pairs={{0,8},{4,36},{1,9},{5,37},{2,10},{6,38},{3,11},{7,39}} | collective-permute-start | bytes 835592 | tf_op jit(solution)/shard_map/ppermute | solution.py:403
  29.7 3.9 %collective-permute-start.8 = (f32[2,32,512]{2,1,0:T(8,128)S(1)}, f32[2,32,512]{2,1,0:T(8,128)S(1)}, u32[]{:S(2)}, u32[]{:S(2)}) collective-permute-start(f32[2,32,512]{2,1,0:T(8,128)S(1)} %get-tuple-element.79), channel_id=1, source_target_pairs={{0,1},{4,5},{8,9},{12,13},{16,17},{20,21},{24,25},{28,29},{32,33},... | collective-permute-start | bytes 393224 | tf_op jit(solution)/shard_map/ppermute | solution.py:401
  31.0 3.3 %collective-permute-start.9 = (f32[2,32,512]{2,1,0:T(8,128)S(1)}, f32[2,32,512]{2,1,0:T(8,128)S(1)}, u32[]{:S(2)}, u32[]{:S(2)}) collective-permute-start(f32[2,32,512]{2,1,0:T(8,128)S(1)} %get-tuple-element.80), channel_id=1, source_target_pairs={{0,2},{4,6},{8,10},{12,14},{16,18},{20,22},{24,26},{28,30},{32,34}... | collective-permute-start | bytes 393224 | tf_op jit(solution)/shard_map/ppermute | solution.py:401
  32.3 3.2 %collective-permute-start.10 = (f32[2,32,512]{2,1,0:T(8,128)S(1)}, f32[2,32,512]{2,1,0:T(8,128)S(1)}, u32[]{:S(2)}, u32[]{:S(2)}) collective-permute-start(f32[2,32,512]{2,1,0:T(8,128)S(1)} %get-tuple-element.81), channel_id=1, source_target_pairs={{0,3},{4,7},{8,11},{12,15},{16,19},{20,23},{24,27},{28,31},{32,35}... | collective-permute-start | bytes 393224 | tf_op jit(solution)/shard_map/ppermute | solution.py:401
  35.6 9.8 %collective-permute-start.11 = (f32[264,512]{1,0:T(8,128)S(1)}, f32[264,512]{1,0:T(8,128)S(1)}, u32[]{:S(2)}, u32[]{:S(2)}) collective-permute-start(f32[264,512]{1,0:T(8,128)S(1)} %merge.1.own_ref), channel_id=1, source_target_pairs={{0,24},{4,100},{8,16},{12,108},{16,8},{20,116},{24,0},{28,124},{32... | collective-permute-start | bytes 1622024 | tf_op jit(solution)/shard_map/ppermute | solution.py:411
  35.7 12.8 %collective-permute-start.13 = (f32[256,512]{1,0:T(8,128)S(1)}, f32[256,512]{1,0:T(8,128)S(1)}, u32[]{:S(2)}, u32[]{:S(2)}) collective-permute-start(f32[256,512]{1,0:T(8,128)S(1)} %slice.3.lead_ref.refs_0_), channel_id=1, source_target_pairs={{0,3},{4,7},{8,11},{12,15},{16,19},{20,23},{24,27},{28,31},{32,35}... | collective-permute-start | bytes 1572872 | tf_op jit(solution)/shard_map/ppermute | solution.py:410
  40.7 9.1 %collective-permute-start.12 = (f32[256,512]{1,0:T(8,128)S(1)}, f32[256,512]{1,0:T(8,128)S(1)}, u32[]{:S(2)}, u32[]{:S(2)}) collective-permute-start(f32[256,512]{1,0:T(8,128)S(1)} %slice.3.lead_ref.refs_0_), channel_id=1, source_target_pairs={{0,1},{4,5},{8,9},{12,13},{16,17},{20,21},{24,25},{28,29},{32,33},... | collective-permute-start | bytes 1572872 | tf_op jit(solution)/shard_map/ppermute | solution.py:410
  49.9 8.2 %collective-permute-start.14 = (f32[264,512]{1,0:T(8,128)S(1)}, f32[264,512]{1,0:T(8,128)S(1)}, u32[]{:S(2)}, u32[]{:S(2)}) collective-permute-start(f32[264,512]{1,0:T(8,128)S(1)} %join.3.own_ref), channel_id=1, source_target_pairs={{0,32},{4,12},{8,40},{12,4},{16,48},{20,28},{24,56},{28,20},{32,0}... | collective-permute-start | bytes 1622024 | tf_op jit(solution)/shard_map/ppermute | solution.py:413
  50.0 10.7 %collective-permute-start.15 = (f32[256,512]{1,0:T(8,128)S(1)}, f32[256,512]{1,0:T(8,128)S(1)}, u32[]{:S(2)}, u32[]{:S(2)}) collective-permute-start(f32[256,512]{1,0:T(8,128)S(1)} %slice.3.lead_ref.refs_0_), channel_id=1, source_target_pairs={{0,2},{4,6},{8,10},{12,14},{16,18},{20,22},{24,26},{28,30},{32,34}... | collective-permute-start | bytes 1572872 | tf_op jit(solution)/shard_map/ppermute | solution.py:410
  60.6 12.2 %collective-permute-start.16 = (f32[392,512]{1,0:T(8,128)S(1)}, f32[392,512]{1,0:T(8,128)S(1)}, u32[]{:S(2)}, u32[]{:S(2)}) collective-permute-start(f32[392,512]{1,0:T(8,128)S(1)} %join.4.own_ref), channel_id=1, source_target_pairs={{0,96},{4,28},{8,104},{12,20},{16,112},{20,12},{24,120},{28,4},{32... | collective-permute-start | bytes 2408456 | tf_op jit(solution)/shard_map/ppermute | solution.py:416
  60.6 12.3 %collective-permute-start.17 = (f32[256,512]{1,0:T(8,128)S(1)}, f32[256,512]{1,0:T(8,128)S(1)}, u32[]{:S(2)}, u32[]{:S(2)}) collective-permute-start(f32[256,512]{1,0:T(8,128)S(1)} %get-tuple-element.106), channel_id=1, source_target_pairs={{0,1},{1,2},{2,3},{3,0},{4,5},{5,6},{6,7},{7,4},{8,9},{9,10},{10,1... | collective-permute-start | bytes 1572872 | tf_op jit(solution)/shard_map/ppermute | solution.py:419
  60.6 12.3 %collective-permute-start.18 = (f32[256,512]{1,0:T(8,128)S(1)}, f32[256,512]{1,0:T(8,128)S(1)}, u32[]{:S(2)}, u32[]{:S(2)}) collective-permute-start(f32[256,512]{1,0:T(8,128)S(1)} %get-tuple-element.108), channel_id=1, source_target_pairs={{0,3},{1,0},{2,1},{3,2},{4,7},{5,4},{6,5},{7,6},{8,11},{9,8},{10,9... | collective-permute-start | bytes 1572872 | tf_op jit(solution)/shard_map/ppermute | solution.py:419
  73.0 13.6 %collective-permute-start.21 = (f32[136,512]{1,0:T(8,128)S(1)}, f32[136,512]{1,0:T(8,128)S(1)}, u32[]{:S(2)}, u32[]{:S(2)}) collective-permute-start(f32[136,512]{1,0:T(8,128)S(1)} %get-tuple-element.110.own_ref), channel_id=1, source_target_pairs={{0,4},{4,0},{8,12},{12,8},{16,20},{20,16},{24,28},{28,24},{32,36},... | collective-permute-start | bytes 835592 | tf_op jit(solution)/shard_map/ppermute | solution.py:421
  82.8 22.3 %collective-permute-start.20 = (f32[512,512]{1,0:T(8,128)S(1)}, f32[512,512]{1,0:T(8,128)S(1)}, u32[]{:S(2)}, u32[]{:S(2)}) collective-permute-start(f32[512,512]{1,0:T(8,128)S(1)} %get-tuple-element.109.refs_5_), channel_id=1, source_target_pairs={{0,4},{4,0},{8,12},{12,8},{16,20},{20,16},{24,28},{28,24},{32,36},... | collective-permute-start | bytes 3145736 | tf_op jit(solution)/shard_map/ppermute | solution.py:424
  82.9 22.2 %collective-permute-start.19 = (f32[512,512]{1,0:T(8,128)S(1)}, f32[512,512]{1,0:T(8,128)S(1)}, u32[]{:S(2)}, u32[]{:S(2)}) collective-permute-start(f32[512,512]{1,0:T(8,128)S(1)} %get-tuple-element.109.refs_5_), channel_id=1, source_target_pairs={{0,8},{4,36},{8,0},{12,44},{16,24},{20,52},{24,16},{28,60},{32,40}... | collective-permute-start | bytes 3145736 | tf_op jit(solution)/shard_map/ppermute | solution.py:422
  83.0 22.1 %collective-permute-start.22 = (f32[256,512]{1,0:T(8,128)S(1)}, f32[256,512]{1,0:T(8,128)S(1)}, u32[]{:S(2)}, u32[]{:S(2)}) collective-permute-start(f32[256,512]{1,0:T(8,128)S(1)} %get-tuple-element.116), channel_id=1, source_target_pairs={{0,2},{1,3},{2,0},{3,1},{4,6},{5,7},{6,4},{7,5},{8,10},{9,11},{10,... | collective-permute-start | bytes 1572872 | tf_op jit(solution)/shard_map/ppermute | solution.py:423
  105.0 3.8 %copy-start.1 = (f32[256,2048]{1,0:T(8,128)S(1)}, f32[256,2048]{1,0:T(8,128)}, u32[]{:S(2)}) copy-start(f32[256,2048]{1,0:T(8,128)} %refs_9_.1) | copy-start | bytes 6291460
  105.0 3.7 %collective-permute-start.23 = (f32[512,512]{1,0:T(8,128)S(1)}, f32[512,512]{1,0:T(8,128)S(1)}, u32[]{:S(2)}, u32[]{:S(2)}) collective-permute-start(f32[512,512]{1,0:T(8,128)S(1)} %collective-permute-done.19.refs_6_), channel_id=1, source_target_pairs={{0,4},{4,0},{8,12},{12,8},{16,20},{20,16},{24,28},{28,24},{32,36},... | collective-permute-start | bytes 3145736 | tf_op jit(solution)/shard_map/ppermute | solution.py:428

commit v15 on v13

--- a/solution.py
+++ b/solution.py
@@ -422,11 +422,11 @@
     other = lax.ppermute(block, "row", swap)
     late = lax.ppermute(gathered, "row", every[0])
     pieces[2] = lax.ppermute(pieces[2], "col", ring[2])
+    other_gathered = lax.ppermute(gathered, "row", swap)
 
     inverse = factor(block, other)
-    late, gathered, inverse, pieces = lax.optimization_barrier((late, gathered, inverse, pieces))
+    late, other_gathered, inverse, pieces = lax.optimization_barrier((late, other_gathered, inverse, pieces))
     other_late = lax.ppermute(late, "row", swap)
-    other_gathered = lax.ppermute(gathered, "row", swap)
     panel, weight = weigh([lead, near, far], inverse)
     updated = update(plan, weight, pieces, [gathered, late, other_gathered, other_late], ancestor)
     return panel, updated

time: 113 us -> 113 us (level)
    ppermute x1, starting transfers between devices: 2.75 us -> 1.61 us  [shards(): pieces[2] = lax.ppermute(pieces[2], 'col', ring[2])]
  transfers between devices with their start and end apart: 23 -> 23, of which waited for: 9 -> 8; matrix products, arithmetic and copies ran while one was open for 0% -> 0% of each run, Pallas kernels for 22% -> 22%
where the time goes in v15:
time: 113 us; the launch traced here: 112 us
  starting transfers between devices  40.4 us (36%)
  waiting for transfers between devices  35.1 us (31%)
  Pallas kernels  32.8 us (29%)
  local copies, waits for them, and re-layouts  2.69 us (2%)
    pallas_call x9, Pallas kernels, call(): pl.pallas_call(kernel, out_shape=[jax.ShapeDtypeStruct(shape, jnp.float32...  21.8 us
    ppermute x3, waiting for transfers between devices, shards(): parts[hop] = lax.ppermute(parts[hop], 'row', pairs)  12.5 us
    ppermute x1, waiting for transfers between devices, shards(): lax.ppermute(load, 'row', every[3])  9.02 us
    pallas_call x1, Pallas kernels, update(): pl.pallas_call(update_kernel, out_shape=jax.ShapeDtypeStruct(base.shape,...  8.11 us
    ppermute x3, starting transfers between devices, shards(): lax.ppermute(blocks[0], ('row', 'col'), [(4 * core, 4 * core + to) for co...  7.47 us
    ppermute x1, starting transfers between devices, shards(): other = lax.ppermute(block, 'row', swap)  6.72 us
    ppermute x1, starting transfers between devices, shards(): lax.ppermute(jnp.where(lax.axis_index('col') == 1, near, lead), 'col', [(...  5.14 us
    ppermute x1, waiting for transfers between devices, shards(): lax.ppermute(load, 'row', every[1])  4.76 us
  transfers between devices with their start and end apart: 23, of which 8 were waited for; matrix products, arithmetic and copies ran while one was open for 0% of the time, Pallas kernels for 22%

profile of v15, /device:TPU:1, one launch (start us, length us, event | category | flops | bytes accessed | tf_op | source)
XLA Modules:
  0.0 112.2 jit_solution(13645965402912945614)
XLA Ops:
  0.6 1.1 slice.3.lead_ref.refs_0_
  1.7 1.5 %collective-permute-start.3 = (f32[256,512]{1,0:T(8,128)S(1)}, f32[256,512]{1,0:T(8,128)S(1)}, u32[]{:S(2)}, u32[]{:S(2)}) collective-permute-start(f32[256,512]{1,0:T(8,128)S(1)} %slice.3.lead_ref.refs_0_), channel_id=1, source_target_pairs={{0,4},{4,0},{8,12},{12,8},{16,20},{20,16},{24,28},{28,24},{32,36},... | collective-permute-start | bytes 1572872 | tf_op jit(solution)/shard_map/ppermute | solution.py:391
  3.3 0.0 copy-start
  3.3 4.9 %collective-permute-start.2 = (f32[136,512]{1,0:T(8,128)S(1)}, f32[136,512]{1,0:T(8,128)S(1)}, u32[]{:S(2)}, u32[]{:S(2)}) collective-permute-start(f32[136,512]{1,0:T(8,128)S(1)} %corner.1), channel_id=1, source_target_pairs={{0,3},{4,7}} | collective-permute-start | bytes 835592 | tf_op jit(solution)/shard_map/ppermute | solution.py:389
  8.2 1.3 %collective-permute-start.1 = (f32[136,512]{1,0:T(8,128)S(1)}, f32[136,512]{1,0:T(8,128)S(1)}, u32[]{:S(2)}, u32[]{:S(2)}) collective-permute-start(f32[136,512]{1,0:T(8,128)S(1)} %corner.1), channel_id=1, source_target_pairs={{0,2},{4,6}} | collective-permute-start | bytes 835592 | tf_op jit(solution)/shard_map/ppermute | solution.py:389
  9.5 1.3 %collective-permute-start = (f32[136,512]{1,0:T(8,128)S(1)}, f32[136,512]{1,0:T(8,128)S(1)}, u32[]{:S(2)}, u32[]{:S(2)}) collective-permute-start(f32[136,512]{1,0:T(8,128)S(1)} %corner.1), channel_id=1, source_target_pairs={{0,1},{4,5}} | collective-permute-start | bytes 835592 | tf_op jit(solution)/shard_map/ppermute | solution.py:389
  10.8 0.0 collective-permute-done.3.mate_ref
  10.8 0.1 share.1
  10.9 1.3 %collective-permute-start.4 = (f32[2,32,512]{2,1,0:T(8,128)S(1)}, f32[2,32,512]{2,1,0:T(8,128)S(1)}, u32[]{:S(2)}, u32[]{:S(2)}) collective-permute-start(f32[2,32,512]{2,1,0:T(8,128)S(1)} %get-tuple-element.66), channel_id=1, source_target_pairs={{8,16},{12,20},{16,24},{20,28},{24,0},{28,4},{32,40},{36,44},{40,4... | collective-permute-start | bytes 393224 | tf_op jit(solution)/shard_map/ppermute | solution.py:395
  12.2 1.3 %collective-permute-start.5 = (f32[2,32,512]{2,1,0:T(8,128)S(1)}, f32[2,32,512]{2,1,0:T(8,128)S(1)}, u32[]{:S(2)}, u32[]{:S(2)}) collective-permute-start(f32[2,32,512]{2,1,0:T(8,128)S(1)} %get-tuple-element.67), channel_id=1, source_target_pairs={{8,24},{12,28},{16,0},{20,4},{24,8},{28,12},{32,48},{36,52},{40,56... | collective-permute-start | bytes 393224 | tf_op jit(solution)/shard_map/ppermute | solution.py:395
  13.5 8.1 %collective-permute-done.4.refs_1_ = f32[2,32,512]{2,1,0:T(8,128)S(1)} collective-permute-done((f32[2,32,512]{2,1,0:T(8,128)S(1)}, f32[2,32,512]{2,1,0:T(8,128)S(1)}, u32[]{:S(2)}, u32[]{:S(2)}) %collective-permute-start.4) | collective-permute-done | bytes 131104 | tf_op jit(solution)/shard_map/ppermute | solution.py:395
  21.6 1.3 %collective-permute-start.6 = (f32[2,32,512]{2,1,0:T(8,128)S(1)}, f32[2,32,512]{2,1,0:T(8,128)S(1)}, u32[]{:S(2)}, u32[]{:S(2)}) collective-permute-start(f32[2,32,512]{2,1,0:T(8,128)S(1)} %get-tuple-element.68), channel_id=1, source_target_pairs={{8,0},{12,4},{16,8},{20,12},{24,16},{28,20},{32,56},{36,60},{40,32... | collective-permute-start | bytes 393224 | tf_op jit(solution)/shard_map/ppermute | solution.py:395
  22.9 0.0 collective-permute-done.5.refs_2_
  22.9 4.4 %collective-permute-done.6.refs_3_ = f32[2,32,512]{2,1,0:T(8,128)S(1)} collective-permute-done((f32[2,32,512]{2,1,0:T(8,128)S(1)}, f32[2,32,512]{2,1,0:T(8,128)S(1)}, u32[]{:S(2)}, u32[]{:S(2)}) %collective-permute-start.6) | collective-permute-done | bytes 131104 | tf_op jit(solution)/shard_map/ppermute | solution.py:395
  27.3 1.0 sort.1
  28.3 0.0 collective-permute-done.2
  28.3 0.0 collective-permute-done.1
  28.3 0.0 collective-permute-done
  28.3 0.1 add_add_fusion.refs_4_
  28.4 1.3 %collective-permute-start.7 = (f32[136,512]{1,0:T(8,128)S(1)}, f32[136,512]{1,0:T(8,128)S(1)}, u32[]{:S(2)}, u32[]{:S(2)}) collective-permute-start(f32[136,512]{1,0:T(8,128)S(1)} %add_add_fusion.refs_4_), channel_id=1, source_target_pairs={{0,8},{4,36},{1,9},{5,37},{2,10},{6,38},{3,11},{7,39}} | collective-permute-start | bytes 835592 | tf_op jit(solution)/shard_map/ppermute | solution.py:403
  29.7 1.3 %collective-permute-start.8 = (f32[2,32,512]{2,1,0:T(8,128)S(1)}, f32[2,32,512]{2,1,0:T(8,128)S(1)}, u32[]{:S(2)}, u32[]{:S(2)}) collective-permute-start(f32[2,32,512]{2,1,0:T(8,128)S(1)} %get-tuple-element.78), channel_id=1, source_target_pairs={{0,1},{4,5},{8,9},{12,13},{16,17},{20,21},{24,25},{28,29},{32,33},... | collective-permute-start | bytes 393224 | tf_op jit(solution)/shard_map/ppermute | solution.py:401
  31.0 1.3 %collective-permute-start.9 = (f32[2,32,512]{2,1,0:T(8,128)S(1)}, f32[2,32,512]{2,1,0:T(8,128)S(1)}, u32[]{:S(2)}, u32[]{:S(2)}) collective-permute-start(f32[2,32,512]{2,1,0:T(8,128)S(1)} %get-tuple-element.79), channel_id=1, source_target_pairs={{0,2},{4,6},{8,10},{12,14},{16,18},{20,22},{24,26},{28,30},{32,34}... | collective-permute-start | bytes 393224 | tf_op jit(solution)/shard_map/ppermute | solution.py:401
  32.3 1.3 %collective-permute-start.10 = (f32[2,32,512]{2,1,0:T(8,128)S(1)}, f32[2,32,512]{2,1,0:T(8,128)S(1)}, u32[]{:S(2)}, u32[]{:S(2)}) collective-permute-start(f32[2,32,512]{2,1,0:T(8,128)S(1)} %get-tuple-element.80), channel_id=1, source_target_pairs={{0,3},{4,7},{8,11},{12,15},{16,19},{20,23},{24,27},{28,31},{32,35}... | collective-permute-start | bytes 393224 | tf_op jit(solution)/shard_map/ppermute | solution.py:401
  33.7 0.0 collective-permute-done.8.refs_1_
  33.7 0.7 collective-permute-done.9.refs_2_
  34.3 1.2 %collective-permute-done.10.refs_3_ = f32[2,32,512]{2,1,0:T(8,128)S(1)} collective-permute-done((f32[2,32,512]{2,1,0:T(8,128)S(1)}, f32[2,32,512]{2,1,0:T(8,128)S(1)}, u32[]{:S(2)}, u32[]{:S(2)}) %collective-permute-start.10) | collective-permute-done | bytes 131104 | tf_op jit(solution)/shard_map/ppermute | solution.py:401
  35.6 0.0 collective-permute-done.7.refs_5_
  35.6 0.1 merge.1.own_ref
  35.6 0.1 collective-permute-start.11
  35.7 1.3 %collective-permute-start.12 = (f32[256,512]{1,0:T(8,128)S(1)}, f32[256,512]{1,0:T(8,128)S(1)}, u32[]{:S(2)}, u32[]{:S(2)}) collective-permute-start(f32[256,512]{1,0:T(8,128)S(1)} %slice.3.lead_ref.refs_0_), channel_id=1, source_target_pairs={{0,1},{4,5},{8,9},{12,13},{16,17},{20,21},{24,25},{28,29},{32,33},... | collective-permute-start | bytes 1572872 | tf_op jit(solution)/shard_map/ppermute | solution.py:410
  37.1 2.0 %pick.1 = (f32[256,512]{1,0:T(8,128)S(1)}, f32[256,512]{1,0:T(8,128)S(1)}, f32[256,512]{1,0:T(8,128)S(1)}, f32[256,512]{1,0:T(8,128)S(1)}, s32[4,8]{1,0:T(4,128)S(1)}) custom-call(s32[32]{0:T(128)S(1)} %copy-done.2, f32[256,2048]{1,0:T(8,128)S(1)} %copy-done), custom_call_target="tpu_custom_call" | custom-call | flops 1024 | bytes 1024 | tf_op jit(solution)/shard_map/pick/pallas_call | solution.py:109
  39.1 0.0 copy-start.3
  39.1 0.8 copy-done.3
  39.9 0.8 copy-done.5
  40.7 4.8 %collective-permute-done.11.got_ref = f32[264,512]{1,0:T(8,128)S(1)} collective-permute-done((f32[264,512]{1,0:T(8,128)S(1)}, f32[264,512]{1,0:T(8,128)S(1)}, u32[]{:S(2)}, u32[]{:S(2)}) %collective-permute-start.11) | collective-permute-done | bytes 540704 | tf_op jit(solution)/shard_map/ppermute | solution.py:411
  45.5 0.0 copy-start.6
  45.5 0.0 copy-start.4
  45.5 0.0 collective-permute-done.12.refs_1_
  45.5 0.1 collective-permute-start.13
  45.6 0.1 broadcast_select_fusion
  45.7 5.1 %collective-permute-start.14 = (f32[256,512]{1,0:T(8,128)S(1)}, f32[256,512]{1,0:T(8,128)S(1)}, u32[]{:S(2)}, u32[]{:S(2)}) collective-permute-start(f32[256,512]{1,0:T(8,128)S(1)} %broadcast_select_fusion), channel_id=1, source_target_pairs={{0,3},{1,2},{4,7},{5,6},{8,11},{9,10},{12,15},{13,14},{16,19},{17,... | collective-permute-start | bytes 1572872 | tf_op jit(solution)/shard_map/ppermute | solution.py:413
  50.8 3.3 %collective-permute-done.13.got_ref = f32[264,512]{1,0:T(8,128)S(1)} collective-permute-done((f32[264,512]{1,0:T(8,128)S(1)}, f32[264,512]{1,0:T(8,128)S(1)}, u32[]{:S(2)}, u32[]{:S(2)}) %collective-permute-start.13) | collective-permute-done | bytes 540704 | tf_op jit(solution)/shard_map/ppermute | solution.py:414
  54.1 0.1 join.4.own_ref
  54.2 3.6 %collective-permute-done.14.refs_2_ = f32[256,512]{1,0:T(8,128)S(1)} collective-permute-done((f32[256,512]{1,0:T(8,128)S(1)}, f32[256,512]{1,0:T(8,128)S(1)}, u32[]{:S(2)}, u32[]{:S(2)}) %collective-permute-start.14) | collective-permute-done | bytes 524320 | tf_op jit(solution)/shard_map/ppermute | solution.py:413
  57.8 0.0 collective-permute-start.15
  57.8 0.0 collective-permute-start.16
  57.8 3.5 %collective-permute-start.17 = (f32[256,512]{1,0:T(8,128)S(1)}, f32[256,512]{1,0:T(8,128)S(1)}, u32[]{:S(2)}, u32[]{:S(2)}) collective-permute-start(f32[256,512]{1,0:T(8,128)S(1)} %copy-done.4), channel_id=1, source_target_pairs={{0,3},{1,0},{2,1},{3,2},{4,7},{5,4},{6,5},{7,6},{8,11},{9,8},{10,9... | collective-permute-start | bytes 1572872 | tf_op jit(solution)/shard_map/ppermute | solution.py:420
  61.3 9.0 %collective-permute-done.15.got_ref = f32[392,512]{1,0:T(8,128)S(1)} collective-permute-done((f32[392,512]{1,0:T(8,128)S(1)}, f32[392,512]{1,0:T(8,128)S(1)}, u32[]{:S(2)}, u32[]{:S(2)}) %collective-permute-start.15) | collective-permute-done | bytes 802848 | tf_op jit(solution)/shard_map/ppermute | solution.py:417
  70.3 0.1 join.5
  70.4 0.0 collective-permute-done.16.refs_2_
  70.4 0.0 collective-permute-done.17.refs_4_
  70.4 6.7 %collective-permute-start.20 = (f32[136,512]{1,0:T(8,128)S(1)}, f32[136,512]{1,0:T(8,128)S(1)}, u32[]{:S(2)}, u32[]{:S(2)}) collective-permute-start(f32[136,512]{1,0:T(8,128)S(1)} %get-tuple-element.108.own_ref), channel_id=1, source_target_pairs={{0,4},{4,0},{8,12},{12,8},{16,20},{20,16},{24,28},{28,24},{32,36},... | collective-permute-start | bytes 835592 | tf_op jit(solution)/shard_map/ppermute | solution.py:422
  77.2 0.1 collective-permute-start.19
  77.3 3.3 %collective-permute-start.18 = (f32[512,512]{1,0:T(8,128)S(1)}, f32[512,512]{1,0:T(8,128)S(1)}, u32[]{:S(2)}, u32[]{:S(2)}) collective-permute-start(f32[512,512]{1,0:T(8,128)S(1)} %get-tuple-element.107.refs_5_), channel_id=1, source_target_pairs={{0,8},{4,36},{8,0},{12,44},{16,24},{20,52},{24,16},{28,60},{32,40}... | collective-permute-start | bytes 3145736 | tf_op jit(solution)/shard_map/ppermute | solution.py:423
  80.5 1.6 %collective-permute-start.21 = (f32[256,512]{1,0:T(8,128)S(1)}, f32[256,512]{1,0:T(8,128)S(1)}, u32[]{:S(2)}, u32[]{:S(2)}) collective-permute-start(f32[256,512]{1,0:T(8,128)S(1)} %get-tuple-element.114), channel_id=1, source_target_pairs={{0,2},{1,3},{2,0},{3,1},{4,6},{5,7},{6,4},{7,5},{8,10},{9,11},{10,... | collective-permute-start | bytes 1572872 | tf_op jit(solution)/shard_map/ppermute | solution.py:424
  82.1 0.0 collective-permute-done.20.other_ref
  82.1 18.4 %factor.1 = (f32[256,256]{1,0:T(8,128)S(1)}, f32[256,256]{1,0:T(8,128)S(1)}, f32[256,256]{1,0:T(8,128)S(1)}) custom-call(f32[136,512]{1,0:T(8,128)S(1)} %get-tuple-element.108.own_ref, f32[136,512]{1,0:T(8,128)S(1)} %collective-permute-done.20.other_ref), custom_call_target="tpu_custom_call" | custom-call | flops 21474836480 | bytes 1048576 | tf_op jit(solution)/shard_map/factor/pallas_call | solution.py:109
  100.6 0.0 copy-start.1
  100.6 0.0 collective-permute-done.19.refs_7_
  100.6 0.0 collective-permute-done.18.refs_6_
  100.6 0.5 collective-permute-start.22
  101.1 2.9 %weigh.1 = (f32[256,512]{1,0:T(8,128)}, f32[256,512]{1,0:T(8,128)S(1)}) custom-call(f32[256,512]{1,0:T(8,128)S(1)} %slice.3.lead_ref.refs_0_, f32[256,512]{1,0:T(8,128)S(1)} %collective-permute-done.12.refs_1_, f32[256,512]{1,0:T(8,128)S(1)} %collective-permute-done.14.refs_2_, f32[256,256]{1,0:T(8,128)S(1)} %get-tuple-element.116.refs_3_, ...), custom_call_target="tpu_custom_call" | custom-call | flops 1024 | bytes 1024 | tf_op jit(solution)/shard_map/weigh/pallas_call | solution.py:301
  104.1 0.0 collective-permute-done.22.refs_8_
  104.1 8.1 %update.1 = f32[256,2048]{1,0:T(8,128)} custom-call(s32[4,8]{1,0:T(4,128)S(1)} %get-tuple-element.120.plan, f32[256,512]{1,0:T(8,128)S(1)} %get-tuple-element.121.refs_0_, f32[256,512]{1,0:T(8,128)S(1)} %get-tuple-element.122.refs_1_, f32[256,512]{1,0:T(8,128)S(1)} %collective-permute-done.16.refs_2_, f32[256,512]{1,0:T(8,128)S(1)} %collective-permute-done.21.refs_3_, ...), custom_call_target="tpu_custom_call" | custom-call | tf_op jit(solution)/shard_map/update/pallas_call | solution.py:350
  (10 shorter events, 0.1 us)
Async XLA Ops:
  0.6 26.7 %copy-start.2 = (s32[32]{0:T(128)S(1)}, s32[32]{0:T(128)}, u32[]{:S(2)}) copy-start(s32[32]{0:T(128)} %map_ref.3) | copy-start | bytes 388
  1.7 9.1 %collective-permute-start.3 = (f32[256,512]{1,0:T(8,128)S(1)}, f32[256,512]{1,0:T(8,128)S(1)}, u32[]{:S(2)}, u32[]{:S(2)}) collective-permute-start(f32[256,512]{1,0:T(8,128)S(1)} %slice.3.lead_ref.refs_0_), channel_id=1, source_target_pairs={{0,4},{4,0},{8,12},{12,8},{16,20},{20,16},{24,28},{28,24},{32,36},... | collective-permute-start | bytes 1572872 | tf_op jit(solution)/shard_map/ppermute | solution.py:391
  3.3 33.8 %copy-start = (f32[256,2048]{1,0:T(8,128)S(1)}, f32[256,2048]{1,0:T(8,128)}, u32[]{:S(2)}) copy-start(f32[256,2048]{1,0:T(8,128)} %front_ref.1) | copy-start | bytes 6291460
  3.3 25.0 %collective-permute-start.2 = (f32[136,512]{1,0:T(8,128)S(1)}, f32[136,512]{1,0:T(8,128)S(1)}, u32[]{:S(2)}, u32[]{:S(2)}) collective-permute-start(f32[136,512]{1,0:T(8,128)S(1)} %corner.1), channel_id=1, source_target_pairs={{0,3},{4,7}} | collective-permute-start | bytes 835592 | tf_op jit(solution)/shard_map/ppermute | solution.py:389
  8.2 20.1 %collective-permute-start.1 = (f32[136,512]{1,0:T(8,128)S(1)}, f32[136,512]{1,0:T(8,128)S(1)}, u32[]{:S(2)}, u32[]{:S(2)}) collective-permute-start(f32[136,512]{1,0:T(8,128)S(1)} %corner.1), channel_id=1, source_target_pairs={{0,2},{4,6}} | collective-permute-start | bytes 835592 | tf_op jit(solution)/shard_map/ppermute | solution.py:389
  9.5 18.8 %collective-permute-start = (f32[136,512]{1,0:T(8,128)S(1)}, f32[136,512]{1,0:T(8,128)S(1)}, u32[]{:S(2)}, u32[]{:S(2)}) collective-permute-start(f32[136,512]{1,0:T(8,128)S(1)} %corner.1), channel_id=1, source_target_pairs={{0,1},{4,5}} | collective-permute-start | bytes 835592 | tf_op jit(solution)/shard_map/ppermute | solution.py:389
  10.9 10.7 %collective-permute-start.4 = (f32[2,32,512]{2,1,0:T(8,128)S(1)}, f32[2,32,512]{2,1,0:T(8,128)S(1)}, u32[]{:S(2)}, u32[]{:S(2)}) collective-permute-start(f32[2,32,512]{2,1,0:T(8,128)S(1)} %get-tuple-element.66), channel_id=1, source_target_pairs={{8,16},{12,20},{16,24},{20,28},{24,0},{28,4},{32,40},{36,44},{40,4... | collective-permute-start | bytes 393224 | tf_op jit(solution)/shard_map/ppermute | solution.py:395
  12.2 10.7 %collective-permute-start.5 = (f32[2,32,512]{2,1,0:T(8,128)S(1)}, f32[2,32,512]{2,1,0:T(8,128)S(1)}, u32[]{:S(2)}, u32[]{:S(2)}) collective-permute-start(f32[2,32,512]{2,1,0:T(8,128)S(1)} %get-tuple-element.67), channel_id=1, source_target_pairs={{8,24},{12,28},{16,0},{20,4},{24,8},{28,12},{32,48},{36,52},{40,56... | collective-permute-start | bytes 393224 | tf_op jit(solution)/shard_map/ppermute | solution.py:395
  21.6 5.7 %collective-permute-start.6 = (f32[2,32,512]{2,1,0:T(8,128)S(1)}, f32[2,32,512]{2,1,0:T(8,128)S(1)}, u32[]{:S(2)}, u32[]{:S(2)}) collective-permute-start(f32[2,32,512]{2,1,0:T(8,128)S(1)} %get-tuple-element.68), channel_id=1, source_target_pairs={{8,0},{12,4},{16,8},{20,12},{24,16},{28,20},{32,56},{36,60},{40,32... | collective-permute-start | bytes 393224 | tf_op jit(solution)/shard_map/ppermute | solution.py:395
  28.4 7.2 %collective-permute-start.7 = (f32[136,512]{1,0:T(8,128)S(1)}, f32[136,512]{1,0:T(8,128)S(1)}, u32[]{:S(2)}, u32[]{:S(2)}) collective-permute-start(f32[136,512]{1,0:T(8,128)S(1)} %add_add_fusion.refs_4_), channel_id=1, source_target_pairs={{0,8},{4,36},{1,9},{5,37},{2,10},{6,38},{3,11},{7,39}} | collective-permute-start | bytes 835592 | tf_op jit(solution)/shard_map/ppermute | solution.py:403
  29.7 3.9 %collective-permute-start.8 = (f32[2,32,512]{2,1,0:T(8,128)S(1)}, f32[2,32,512]{2,1,0:T(8,128)S(1)}, u32[]{:S(2)}, u32[]{:S(2)}) collective-permute-start(f32[2,32,512]{2,1,0:T(8,128)S(1)} %get-tuple-element.78), channel_id=1, source_target_pairs={{0,1},{4,5},{8,9},{12,13},{16,17},{20,21},{24,25},{28,29},{32,33},... | collective-permute-start | bytes 393224 | tf_op jit(solution)/shard_map/ppermute | solution.py:401
  31.0 3.3 %collective-permute-start.9 = (f32[2,32,512]{2,1,0:T(8,128)S(1)}, f32[2,32,512]{2,1,0:T(8,128)S(1)}, u32[]{:S(2)}, u32[]{:S(2)}) collective-permute-start(f32[2,32,512]{2,1,0:T(8,128)S(1)} %get-tuple-element.79), channel_id=1, source_target_pairs={{0,2},{4,6},{8,10},{12,14},{16,18},{20,22},{24,26},{28,30},{32,34}... | collective-permute-start | bytes 393224 | tf_op jit(solution)/shard_map/ppermute | solution.py:401
  32.3 3.2 %collective-permute-start.10 = (f32[2,32,512]{2,1,0:T(8,128)S(1)}, f32[2,32,512]{2,1,0:T(8,128)S(1)}, u32[]{:S(2)}, u32[]{:S(2)}) collective-permute-start(f32[2,32,512]{2,1,0:T(8,128)S(1)} %get-tuple-element.80), channel_id=1, source_target_pairs={{0,3},{4,7},{8,11},{12,15},{16,19},{20,23},{24,27},{28,31},{32,35}... | collective-permute-start | bytes 393224 | tf_op jit(solution)/shard_map/ppermute | solution.py:401
  35.6 9.8 %collective-permute-start.11 = (f32[264,512]{1,0:T(8,128)S(1)}, f32[264,512]{1,0:T(8,128)S(1)}, u32[]{:S(2)}, u32[]{:S(2)}) collective-permute-start(f32[264,512]{1,0:T(8,128)S(1)} %merge.1.own_ref), channel_id=1, source_target_pairs={{0,24},{4,100},{8,16},{12,108},{16,8},{20,116},{24,0},{28,124},{32... | collective-permute-start | bytes 1622024 | tf_op jit(solution)/shard_map/ppermute | solution.py:411
  35.7 9.8 %collective-permute-start.12 = (f32[256,512]{1,0:T(8,128)S(1)}, f32[256,512]{1,0:T(8,128)S(1)}, u32[]{:S(2)}, u32[]{:S(2)}) collective-permute-start(f32[256,512]{1,0:T(8,128)S(1)} %slice.3.lead_ref.refs_0_), channel_id=1, source_target_pairs={{0,1},{4,5},{8,9},{12,13},{16,17},{20,21},{24,25},{28,29},{32,33},... | collective-permute-start | bytes 1572872 | tf_op jit(solution)/shard_map/ppermute | solution.py:410
  39.1 0.8 copy-start.3
  39.9 0.8 copy-start.5
  45.5 12.3 %copy-start.6 = (f32[256,512]{1,0:T(8,128)S(1)}, f32[256,512]{1,0:T(8,128)}, u32[]{:S(2)}) copy-start(f32[256,512]{1,0:T(8,128)} %copy-done.5) | copy-start | bytes 1572868
  45.5 12.3 %copy-start.4 = (f32[256,512]{1,0:T(8,128)S(1)}, f32[256,512]{1,0:T(8,128)}, u32[]{:S(2)}) copy-start(f32[256,512]{1,0:T(8,128)} %copy-done.3) | copy-start | bytes 1572868
  45.5 8.6 %collective-permute-start.13 = (f32[264,512]{1,0:T(8,128)S(1)}, f32[264,512]{1,0:T(8,128)S(1)}, u32[]{:S(2)}, u32[]{:S(2)}) collective-permute-start(f32[264,512]{1,0:T(8,128)S(1)} %join.3.own_ref), channel_id=1, source_target_pairs={{0,32},{4,12},{8,40},{12,4},{16,48},{20,28},{24,56},{28,20},{32,0}... | collective-permute-start | bytes 1622024 | tf_op jit(solution)/shard_map/ppermute | solution.py:414
  45.7 12.1 %collective-permute-start.14 = (f32[256,512]{1,0:T(8,128)S(1)}, f32[256,512]{1,0:T(8,128)S(1)}, u32[]{:S(2)}, u32[]{:S(2)}) collective-permute-start(f32[256,512]{1,0:T(8,128)S(1)} %broadcast_select_fusion), channel_id=1, source_target_pairs={{0,3},{1,2},{4,7},{5,6},{8,11},{9,10},{12,15},{13,14},{16,19},{17,... | collective-permute-start | bytes 1572872 | tf_op jit(solution)/shard_map/ppermute | solution.py:413
  57.8 12.5 %collective-permute-start.15 = (f32[392,512]{1,0:T(8,128)S(1)}, f32[392,512]{1,0:T(8,128)S(1)}, u32[]{:S(2)}, u32[]{:S(2)}) collective-permute-start(f32[392,512]{1,0:T(8,128)S(1)} %join.4.own_ref), channel_id=1, source_target_pairs={{0,96},{4,28},{8,104},{12,20},{16,112},{20,12},{24,120},{28,4},{32... | collective-permute-start | bytes 2408456 | tf_op jit(solution)/shard_map/ppermute | solution.py:417
  57.8 12.6 %collective-permute-start.16 = (f32[256,512]{1,0:T(8,128)S(1)}, f32[256,512]{1,0:T(8,128)S(1)}, u32[]{:S(2)}, u32[]{:S(2)}) collective-permute-start(f32[256,512]{1,0:T(8,128)S(1)} %copy-done.6), channel_id=1, source_target_pairs={{0,1},{1,2},{2,3},{3,0},{4,5},{5,6},{6,7},{7,4},{8,9},{9,10},{10,1... | collective-permute-start | bytes 1572872 | tf_op jit(solution)/shard_map/ppermute | solution.py:420
  57.8 12.6 %collective-permute-start.17 = (f32[256,512]{1,0:T(8,128)S(1)}, f32[256,512]{1,0:T(8,128)S(1)}, u32[]{:S(2)}, u32[]{:S(2)}) collective-permute-start(f32[256,512]{1,0:T(8,128)S(1)} %copy-done.4), channel_id=1, source_target_pairs={{0,3},{1,0},{2,1},{3,2},{4,7},{5,4},{6,5},{7,6},{8,11},{9,8},{10,9... | collective-permute-start | bytes 1572872 | tf_op jit(solution)/shard_map/ppermute | solution.py:420
  70.4 11.7 %collective-permute-start.20 = (f32[136,512]{1,0:T(8,128)S(1)}, f32[136,512]{1,0:T(8,128)S(1)}, u32[]{:S(2)}, u32[]{:S(2)}) collective-permute-start(f32[136,512]{1,0:T(8,128)S(1)} %get-tuple-element.108.own_ref), channel_id=1, source_target_pairs={{0,4},{4,0},{8,12},{12,8},{16,20},{20,16},{24,28},{28,24},{32,36},... | collective-permute-start | bytes 835592 | tf_op jit(solution)/shard_map/ppermute | solution.py:422
  77.2 23.4 %collective-permute-start.19 = (f32[512,512]{1,0:T(8,128)S(1)}, f32[512,512]{1,0:T(8,128)S(1)}, u32[]{:S(2)}, u32[]{:S(2)}) collective-permute-start(f32[512,512]{1,0:T(8,128)S(1)} %get-tuple-element.107.refs_5_), channel_id=1, source_target_pairs={{0,4},{4,0},{8,12},{12,8},{16,20},{20,16},{24,28},{28,24},{32,36},... | collective-permute-start | bytes 3145736 | tf_op jit(solution)/shard_map/ppermute | solution.py:425
  77.3 23.3 %collective-permute-start.18 = (f32[512,512]{1,0:T(8,128)S(1)}, f32[512,512]{1,0:T(8,128)S(1)}, u32[]{:S(2)}, u32[]{:S(2)}) collective-permute-start(f32[512,512]{1,0:T(8,128)S(1)} %get-tuple-element.107.refs_5_), channel_id=1, source_target_pairs={{0,8},{4,36},{8,0},{12,44},{16,24},{20,52},{24,16},{28,60},{32,40}... | collective-permute-start | bytes 3145736 | tf_op jit(solution)/shard_map/ppermute | solution.py:423
  80.5 20.0 %collective-permute-start.21 = (f32[256,512]{1,0:T(8,128)S(1)}, f32[256,512]{1,0:T(8,128)S(1)}, u32[]{:S(2)}, u32[]{:S(2)}) collective-permute-start(f32[256,512]{1,0:T(8,128)S(1)} %get-tuple-element.114), channel_id=1, source_target_pairs={{0,2},{1,3},{2,0},{3,1},{4,6},{5,7},{6,4},{7,5},{8,10},{9,11},{10,... | collective-permute-start | bytes 1572872 | tf_op jit(solution)/shard_map/ppermute | solution.py:424
  100.6 3.5 %copy-start.1 = (f32[256,2048]{1,0:T(8,128)S(1)}, f32[256,2048]{1,0:T(8,128)}, u32[]{:S(2)}) copy-start(f32[256,2048]{1,0:T(8,128)} %refs_9_.1) | copy-start | bytes 6291460
  100.6 3.5 %collective-permute-start.22 = (f32[512,512]{1,0:T(8,128)S(1)}, f32[512,512]{1,0:T(8,128)S(1)}, u32[]{:S(2)}, u32[]{:S(2)}) collective-permute-start(f32[512,512]{1,0:T(8,128)S(1)} %collective-permute-done.18.refs_6_), channel_id=1, source_target_pairs={{0,4},{4,0},{8,12},{12,8},{16,20},{20,16},{24,28},{28,24},{32,36},... | collective-permute-start | bytes 3145736 | tf_op jit(solution)/shard_map/ppermute | solution.py:429

commit v16 on v15

--- a/solution.py
+++ b/solution.py
@@ -330,7 +330,7 @@
 
     product = dot(weight_ref[...], ahead_ref[...], 1, 1)
     column = pl.multiple_of(place * PW, PW)
-    base = base_ref[...]
+    base = base_ref[:, pl.ds(pl.multiple_of(slot * PW, PW), PW)]
 
     @pl.when(plan[3, slot] == 0)
     def _():
@@ -353,7 +353,7 @@
         grid_spec=pltpu.PrefetchScalarGridSpec(
             num_scalar_prefetch=1,
             grid=(width // PW,),
-            in_specs=[whole] * 9 + [tile],
+            in_specs=[whole] * 10,
             out_specs=tile,
             scratch_shapes=[pltpu.VMEM((PW, LEAD), jnp.float32)],
         ),

time: 113 us -> 112 us (level)
  no operation moved by 1% of the time
where the time goes in v16:
time: 112 us
  starting transfers between devices  40.4 us (36%)
  waiting for transfers between devices  35.1 us (31%)
  Pallas kernels  32.7 us (29%)
  local copies, waits for them, and re-layouts  2.69 us (2%)
    pallas_call x9, Pallas kernels, call(): pl.pallas_call(kernel, out_shape=[jax.ShapeDtypeStruct(shape, jnp.float32...  21.8 us
    ppermute x3, waiting for transfers between devices, shards(): parts[hop] = lax.ppermute(parts[hop], 'row', pairs)  12.5 us
    ppermute x1, waiting for transfers between devices, shards(): lax.ppermute(load, 'row', every[3])  9.02 us
    pallas_call x1, Pallas kernels, update(): pl.pallas_call(update_kernel, out_shape=jax.ShapeDtypeStruct(base.shape,...  8 us
    ppermute x3, starting transfers between devices, shards(): lax.ppermute(blocks[0], ('row', 'col'), [(4 * core, 4 * core + to) for co...  7.47 us
    ppermute x1, starting transfers between devices, shards(): other = lax.ppermute(block, 'row', swap)  6.72 us
    ppermute x1, starting transfers between devices, shards(): lax.ppermute(jnp.where(lax.axis_index('col') == 1, near, lead), 'col', [(...  5.14 us
    ppermute x1, waiting for transfers between devices, shards(): lax.ppermute(load, 'row', every[1])  4.76 us
  transfers between devices with their start and end apart: 23, of which 8 were waited for; matrix products, arithmetic and copies ran while one was open for 0% of the time, Pallas kernels for 22%

profile of v16, /device:TPU:1, one launch (start us, length us, event | category | flops | bytes accessed | tf_op | source)
XLA Modules:
  0.0 112.1 jit_solution(5629573508020180264)
XLA Ops:
  0.6 1.1 slice.3.lead_ref.refs_0_
  1.7 1.5 %collective-permute-start.3 = (f32[256,512]{1,0:T(8,128)S(1)}, f32[256,512]{1,0:T(8,128)S(1)}, u32[]{:S(2)}, u32[]{:S(2)}) collective-permute-start(f32[256,512]{1,0:T(8,128)S(1)} %slice.3.lead_ref.refs_0_), channel_id=1, source_target_pairs={{0,4},{4,0},{8,12},{12,8},{16,20},{20,16},{24,28},{28,24},{32,36},... | collective-permute-start | bytes 1572872 | tf_op jit(solution)/shard_map/ppermute | solution.py:391
  3.3 0.0 copy-start
  3.3 4.9 %collective-permute-start.2 = (f32[136,512]{1,0:T(8,128)S(1)}, f32[136,512]{1,0:T(8,128)S(1)}, u32[]{:S(2)}, u32[]{:S(2)}) collective-permute-start(f32[136,512]{1,0:T(8,128)S(1)} %corner.1), channel_id=1, source_target_pairs={{0,3},{4,7}} | collective-permute-start | bytes 835592 | tf_op jit(solution)/shard_map/ppermute | solution.py:389
  8.2 1.3 %collective-permute-start.1 = (f32[136,512]{1,0:T(8,128)S(1)}, f32[136,512]{1,0:T(8,128)S(1)}, u32[]{:S(2)}, u32[]{:S(2)}) collective-permute-start(f32[136,512]{1,0:T(8,128)S(1)} %corner.1), channel_id=1, source_target_pairs={{0,2},{4,6}} | collective-permute-start | bytes 835592 | tf_op jit(solution)/shard_map/ppermute | solution.py:389
  9.5 1.3 %collective-permute-start = (f32[136,512]{1,0:T(8,128)S(1)}, f32[136,512]{1,0:T(8,128)S(1)}, u32[]{:S(2)}, u32[]{:S(2)}) collective-permute-start(f32[136,512]{1,0:T(8,128)S(1)} %corner.1), channel_id=1, source_target_pairs={{0,1},{4,5}} | collective-permute-start | bytes 835592 | tf_op jit(solution)/shard_map/ppermute | solution.py:389
  10.8 0.0 collective-permute-done.3.mate_ref
  10.8 0.1 share.1
  10.9 1.3 %collective-permute-start.4 = (f32[2,32,512]{2,1,0:T(8,128)S(1)}, f32[2,32,512]{2,1,0:T(8,128)S(1)}, u32[]{:S(2)}, u32[]{:S(2)}) collective-permute-start(f32[2,32,512]{2,1,0:T(8,128)S(1)} %get-tuple-element.66), channel_id=1, source_target_pairs={{8,16},{12,20},{16,24},{20,28},{24,0},{28,4},{32,40},{36,44},{40,4... | collective-permute-start | bytes 393224 | tf_op jit(solution)/shard_map/ppermute | solution.py:395
  12.2 1.3 %collective-permute-start.5 = (f32[2,32,512]{2,1,0:T(8,128)S(1)}, f32[2,32,512]{2,1,0:T(8,128)S(1)}, u32[]{:S(2)}, u32[]{:S(2)}) collective-permute-start(f32[2,32,512]{2,1,0:T(8,128)S(1)} %get-tuple-element.67), channel_id=1, source_target_pairs={{8,24},{12,28},{16,0},{20,4},{24,8},{28,12},{32,48},{36,52},{40,56... | collective-permute-start | bytes 393224 | tf_op jit(solution)/shard_map/ppermute | solution.py:395
  13.5 8.1 %collective-permute-done.4.refs_1_ = f32[2,32,512]{2,1,0:T(8,128)S(1)} collective-permute-done((f32[2,32,512]{2,1,0:T(8,128)S(1)}, f32[2,32,512]{2,1,0:T(8,128)S(1)}, u32[]{:S(2)}, u32[]{:S(2)}) %collective-permute-start.4) | collective-permute-done | bytes 131104 | tf_op jit(solution)/shard_map/ppermute | solution.py:395
  21.6 1.3 %collective-permute-start.6 = (f32[2,32,512]{2,1,0:T(8,128)S(1)}, f32[2,32,512]{2,1,0:T(8,128)S(1)}, u32[]{:S(2)}, u32[]{:S(2)}) collective-permute-start(f32[2,32,512]{2,1,0:T(8,128)S(1)} %get-tuple-element.68), channel_id=1, source_target_pairs={{8,0},{12,4},{16,8},{20,12},{24,16},{28,20},{32,56},{36,60},{40,32... | collective-permute-start | bytes 393224 | tf_op jit(solution)/shard_map/ppermute | solution.py:395
  22.9 0.0 collective-permute-done.5.refs_2_
  22.9 4.4 %collective-permute-done.6.refs_3_ = f32[2,32,512]{2,1,0:T(8,128)S(1)} collective-permute-done((f32[2,32,512]{2,1,0:T(8,128)S(1)}, f32[2,32,512]{2,1,0:T(8,128)S(1)}, u32[]{:S(2)}, u32[]{:S(2)}) %collective-permute-start.6) | collective-permute-done | bytes 131104 | tf_op jit(solution)/shard_map/ppermute | solution.py:395
  27.3 1.0 sort.1
  28.3 0.0 collective-permute-done.2
  28.3 0.0 collective-permute-done.1
  28.3 0.0 collective-permute-done
  28.3 0.1 add_add_fusion.refs_4_
  28.4 1.3 %collective-permute-start.7 = (f32[136,512]{1,0:T(8,128)S(1)}, f32[136,512]{1,0:T(8,128)S(1)}, u32[]{:S(2)}, u32[]{:S(2)}) collective-permute-start(f32[136,512]{1,0:T(8,128)S(1)} %add_add_fusion.refs_4_), channel_id=1, source_target_pairs={{0,8},{4,36},{1,9},{5,37},{2,10},{6,38},{3,11},{7,39}} | collective-permute-start | bytes 835592 | tf_op jit(solution)/shard_map/ppermute | solution.py:403
  29.7 1.3 %collective-permute-start.8 = (f32[2,32,512]{2,1,0:T(8,128)S(1)}, f32[2,32,512]{2,1,0:T(8,128)S(1)}, u32[]{:S(2)}, u32[]{:S(2)}) collective-permute-start(f32[2,32,512]{2,1,0:T(8,128)S(1)} %get-tuple-element.78), channel_id=1, source_target_pairs={{0,1},{4,5},{8,9},{12,13},{16,17},{20,21},{24,25},{28,29},{32,33},... | collective-permute-start | bytes 393224 | tf_op jit(solution)/shard_map/ppermute | solution.py:401
  31.0 1.3 %collective-permute-start.9 = (f32[2,32,512]{2,1,0:T(8,128)S(1)}, f32[2,32,512]{2,1,0:T(8,128)S(1)}, u32[]{:S(2)}, u32[]{:S(2)}) collective-permute-start(f32[2,32,512]{2,1,0:T(8,128)S(1)} %get-tuple-element.79), channel_id=1, source_target_pairs={{0,2},{4,6},{8,10},{12,14},{16,18},{20,22},{24,26},{28,30},{32,34}... | collective-permute-start | bytes 393224 | tf_op jit(solution)/shard_map/ppermute | solution.py:401
  32.3 1.3 %collective-permute-start.10 = (f32[2,32,512]{2,1,0:T(8,128)S(1)}, f32[2,32,512]{2,1,0:T(8,128)S(1)}, u32[]{:S(2)}, u32[]{:S(2)}) collective-permute-start(f32[2,32,512]{2,1,0:T(8,128)S(1)} %get-tuple-element.80), channel_id=1, source_target_pairs={{0,3},{4,7},{8,11},{12,15},{16,19},{20,23},{24,27},{28,31},{32,35}... | collective-permute-start | bytes 393224 | tf_op jit(solution)/shard_map/ppermute | solution.py:401
  33.7 0.0 collective-permute-done.8.refs_1_
  33.7 0.7 collective-permute-done.9.refs_2_
  34.3 1.2 %collective-permute-done.10.refs_3_ = f32[2,32,512]{2,1,0:T(8,128)S(1)} collective-permute-done((f32[2,32,512]{2,1,0:T(8,128)S(1)}, f32[2,32,512]{2,1,0:T(8,128)S(1)}, u32[]{:S(2)}, u32[]{:S(2)}) %collective-permute-start.10) | collective-permute-done | bytes 131104 | tf_op jit(solution)/shard_map/ppermute | solution.py:401
  35.6 0.0 collective-permute-done.7.refs_5_
  35.6 0.1 merge.1.own_ref
  35.6 0.1 collective-permute-start.11
  35.7 1.3 %collective-permute-start.12 = (f32[256,512]{1,0:T(8,128)S(1)}, f32[256,512]{1,0:T(8,128)S(1)}, u32[]{:S(2)}, u32[]{:S(2)}) collective-permute-start(f32[256,512]{1,0:T(8,128)S(1)} %slice.3.lead_ref.refs_0_), channel_id=1, source_target_pairs={{0,1},{4,5},{8,9},{12,13},{16,17},{20,21},{24,25},{28,29},{32,33},... | collective-permute-start | bytes 1572872 | tf_op jit(solution)/shard_map/ppermute | solution.py:410
  37.1 2.0 %pick.1 = (f32[256,512]{1,0:T(8,128)S(1)}, f32[256,512]{1,0:T(8,128)S(1)}, f32[256,512]{1,0:T(8,128)S(1)}, f32[256,512]{1,0:T(8,128)S(1)}, s32[4,8]{1,0:T(4,128)S(1)}) custom-call(s32[32]{0:T(128)S(1)} %copy-done.2, f32[256,2048]{1,0:T(8,128)S(1)} %copy-done), custom_call_target="tpu_custom_call" | custom-call | flops 1024 | bytes 1024 | tf_op jit(solution)/shard_map/pick/pallas_call | solution.py:109
  39.1 0.0 copy-start.3
  39.1 0.8 copy-done.3
  39.9 0.8 copy-done.5
  40.7 4.8 %collective-permute-done.11.got_ref = f32[264,512]{1,0:T(8,128)S(1)} collective-permute-done((f32[264,512]{1,0:T(8,128)S(1)}, f32[264,512]{1,0:T(8,128)S(1)}, u32[]{:S(2)}, u32[]{:S(2)}) %collective-permute-start.11) | collective-permute-done | bytes 540704 | tf_op jit(solution)/shard_map/ppermute | solution.py:411
  45.5 0.0 copy-start.6
  45.5 0.0 copy-start.4
  45.5 0.0 collective-permute-done.12.refs_1_
  45.5 0.1 collective-permute-start.13
  45.6 0.1 broadcast_select_fusion
  45.7 5.1 %collective-permute-start.14 = (f32[256,512]{1,0:T(8,128)S(1)}, f32[256,512]{1,0:T(8,128)S(1)}, u32[]{:S(2)}, u32[]{:S(2)}) collective-permute-start(f32[256,512]{1,0:T(8,128)S(1)} %broadcast_select_fusion), channel_id=1, source_target_pairs={{0,3},{1,2},{4,7},{5,6},{8,11},{9,10},{12,15},{13,14},{16,19},{17,... | collective-permute-start | bytes 1572872 | tf_op jit(solution)/shard_map/ppermute | solution.py:413
  50.8 3.3 %collective-permute-done.13.got_ref = f32[264,512]{1,0:T(8,128)S(1)} collective-permute-done((f32[264,512]{1,0:T(8,128)S(1)}, f32[264,512]{1,0:T(8,128)S(1)}, u32[]{:S(2)}, u32[]{:S(2)}) %collective-permute-start.13) | collective-permute-done | bytes 540704 | tf_op jit(solution)/shard_map/ppermute | solution.py:414
  54.1 0.1 join.4.own_ref
  54.2 3.6 %collective-permute-done.14.refs_2_ = f32[256,512]{1,0:T(8,128)S(1)} collective-permute-done((f32[256,512]{1,0:T(8,128)S(1)}, f32[256,512]{1,0:T(8,128)S(1)}, u32[]{:S(2)}, u32[]{:S(2)}) %collective-permute-start.14) | collective-permute-done | bytes 524320 | tf_op jit(solution)/shard_map/ppermute | solution.py:413
  57.8 0.0 collective-permute-start.15
  57.8 0.0 collective-permute-start.16
  57.8 3.5 %collective-permute-start.17 = (f32[256,512]{1,0:T(8,128)S(1)}, f32[256,512]{1,0:T(8,128)S(1)}, u32[]{:S(2)}, u32[]{:S(2)}) collective-permute-start(f32[256,512]{1,0:T(8,128)S(1)} %copy-done.4), channel_id=1, source_target_pairs={{0,3},{1,0},{2,1},{3,2},{4,7},{5,4},{6,5},{7,6},{8,11},{9,8},{10,9... | collective-permute-start | bytes 1572872 | tf_op jit(solution)/shard_map/ppermute | solution.py:420
  61.3 9.0 %collective-permute-done.15.got_ref = f32[392,512]{1,0:T(8,128)S(1)} collective-permute-done((f32[392,512]{1,0:T(8,128)S(1)}, f32[392,512]{1,0:T(8,128)S(1)}, u32[]{:S(2)}, u32[]{:S(2)}) %collective-permute-start.15) | collective-permute-done | bytes 802848 | tf_op jit(solution)/shard_map/ppermute | solution.py:417
  70.3 0.1 join.5
  70.4 0.0 collective-permute-done.16.refs_2_
  70.4 0.0 collective-permute-done.17.refs_4_
  70.4 6.7 %collective-permute-start.20 = (f32[136,512]{1,0:T(8,128)S(1)}, f32[136,512]{1,0:T(8,128)S(1)}, u32[]{:S(2)}, u32[]{:S(2)}) collective-permute-start(f32[136,512]{1,0:T(8,128)S(1)} %get-tuple-element.108.own_ref), channel_id=1, source_target_pairs={{0,4},{4,0},{8,12},{12,8},{16,20},{20,16},{24,28},{28,24},{32,36},... | collective-permute-start | bytes 835592 | tf_op jit(solution)/shard_map/ppermute | solution.py:422
  77.2 0.1 collective-permute-start.19
  77.3 3.3 %collective-permute-start.18 = (f32[512,512]{1,0:T(8,128)S(1)}, f32[512,512]{1,0:T(8,128)S(1)}, u32[]{:S(2)}, u32[]{:S(2)}) collective-permute-start(f32[512,512]{1,0:T(8,128)S(1)} %get-tuple-element.107.refs_5_), channel_id=1, source_target_pairs={{0,8},{4,36},{8,0},{12,44},{16,24},{20,52},{24,16},{28,60},{32,40}... | collective-permute-start | bytes 3145736 | tf_op jit(solution)/shard_map/ppermute | solution.py:423
  80.5 1.6 %collective-permute-start.21 = (f32[256,512]{1,0:T(8,128)S(1)}, f32[256,512]{1,0:T(8,128)S(1)}, u32[]{:S(2)}, u32[]{:S(2)}) collective-permute-start(f32[256,512]{1,0:T(8,128)S(1)} %get-tuple-element.114), channel_id=1, source_target_pairs={{0,2},{1,3},{2,0},{3,1},{4,6},{5,7},{6,4},{7,5},{8,10},{9,11},{10,... | collective-permute-start | bytes 1572872 | tf_op jit(solution)/shard_map/ppermute | solution.py:424
  82.1 0.0 collective-permute-done.20.other_ref
  82.1 18.4 %factor.1 = (f32[256,256]{1,0:T(8,128)S(1)}, f32[256,256]{1,0:T(8,128)S(1)}, f32[256,256]{1,0:T(8,128)S(1)}) custom-call(f32[136,512]{1,0:T(8,128)S(1)} %get-tuple-element.108.own_ref, f32[136,512]{1,0:T(8,128)S(1)} %collective-permute-done.20.other_ref), custom_call_target="tpu_custom_call" | custom-call | flops 21474836480 | bytes 1048576 | tf_op jit(solution)/shard_map/factor/pallas_call | solution.py:109
  100.6 0.0 copy-start.1
  100.6 0.0 collective-permute-done.21.refs_3_
  100.6 0.0 collective-permute-done.18.refs_6_
  100.6 0.5 collective-permute-start.22
  101.1 2.9 %weigh.1 = (f32[256,512]{1,0:T(8,128)}, f32[256,512]{1,0:T(8,128)S(1)}) custom-call(f32[256,512]{1,0:T(8,128)S(1)} %slice.3.lead_ref.refs_0_, f32[256,512]{1,0:T(8,128)S(1)} %collective-permute-done.12.refs_1_, f32[256,512]{1,0:T(8,128)S(1)} %collective-permute-done.14.refs_2_, f32[256,256]{1,0:T(8,128)S(1)} %get-tuple-element.116.refs_3_, ...), custom_call_target="tpu_custom_call" | custom-call | flops 1024 | bytes 1024 | tf_op jit(solution)/shard_map/weigh/pallas_call | solution.py:301
  104.1 0.0 collective-permute-done.22.refs_8_
  104.1 8.0 %update.1 = f32[256,2048]{1,0:T(8,128)} custom-call(s32[4,8]{1,0:T(4,128)S(1)} %get-tuple-element.120.plan, f32[256,512]{1,0:T(8,128)S(1)} %get-tuple-element.121.refs_0_, f32[256,512]{1,0:T(8,128)S(1)} %get-tuple-element.122.refs_1_, f32[256,512]{1,0:T(8,128)S(1)} %collective-permute-done.16.refs_2_, f32[256,512]{1,0:T(8,128)S(1)} %collective-permute-done.21.refs_3_, ...), custom_call_target="tpu_custom_call" | custom-call | tf_op jit(solution)/shard_map/update/pallas_call | solution.py:350
  (10 shorter events, 0.1 us)
Async XLA Ops:
  0.6 26.7 %copy-start.2 = (s32[32]{0:T(128)S(1)}, s32[32]{0:T(128)}, u32[]{:S(2)}) copy-start(s32[32]{0:T(128)} %map_ref.3) | copy-start | bytes 388
  1.7 9.1 %collective-permute-start.3 = (f32[256,512]{1,0:T(8,128)S(1)}, f32[256,512]{1,0:T(8,128)S(1)}, u32[]{:S(2)}, u32[]{:S(2)}) collective-permute-start(f32[256,512]{1,0:T(8,128)S(1)} %slice.3.lead_ref.refs_0_), channel_id=1, source_target_pairs={{0,4},{4,0},{8,12},{12,8},{16,20},{20,16},{24,28},{28,24},{32,36},... | collective-permute-start | bytes 1572872 | tf_op jit(solution)/shard_map/ppermute | solution.py:391
  3.3 33.8 %copy-start = (f32[256,2048]{1,0:T(8,128)S(1)}, f32[256,2048]{1,0:T(8,128)}, u32[]{:S(2)}) copy-start(f32[256,2048]{1,0:T(8,128)} %front_ref.1) | copy-start | bytes 6291460
  3.3 25.0 %collective-permute-start.2 = (f32[136,512]{1,0:T(8,128)S(1)}, f32[136,512]{1,0:T(8,128)S(1)}, u32[]{:S(2)}, u32[]{:S(2)}) collective-permute-start(f32[136,512]{1,0:T(8,128)S(1)} %corner.1), channel_id=1, source_target_pairs={{0,3},{4,7}} | collective-permute-start | bytes 835592 | tf_op jit(solution)/shard_map/ppermute | solution.py:389
  8.2 20.1 %collective-permute-start.1 = (f32[136,512]{1,0:T(8,128)S(1)}, f32[136,512]{1,0:T(8,128)S(1)}, u32[]{:S(2)}, u32[]{:S(2)}) collective-permute-start(f32[136,512]{1,0:T(8,128)S(1)} %corner.1), channel_id=1, source_target_pairs={{0,2},{4,6}} | collective-permute-start | bytes 835592 | tf_op jit(solution)/shard_map/ppermute | solution.py:389
  9.5 18.8 %collective-permute-start = (f32[136,512]{1,0:T(8,128)S(1)}, f32[136,512]{1,0:T(8,128)S(1)}, u32[]{:S(2)}, u32[]{:S(2)}) collective-permute-start(f32[136,512]{1,0:T(8,128)S(1)} %corner.1), channel_id=1, source_target_pairs={{0,1},{4,5}} | collective-permute-start | bytes 835592 | tf_op jit(solution)/shard_map/ppermute | solution.py:389
  10.9 10.7 %collective-permute-start.4 = (f32[2,32,512]{2,1,0:T(8,128)S(1)}, f32[2,32,512]{2,1,0:T(8,128)S(1)}, u32[]{:S(2)}, u32[]{:S(2)}) collective-permute-start(f32[2,32,512]{2,1,0:T(8,128)S(1)} %get-tuple-element.66), channel_id=1, source_target_pairs={{8,16},{12,20},{16,24},{20,28},{24,0},{28,4},{32,40},{36,44},{40,4... | collective-permute-start | bytes 393224 | tf_op jit(solution)/shard_map/ppermute | solution.py:395
  12.2 10.7 %collective-permute-start.5 = (f32[2,32,512]{2,1,0:T(8,128)S(1)}, f32[2,32,512]{2,1,0:T(8,128)S(1)}, u32[]{:S(2)}, u32[]{:S(2)}) collective-permute-start(f32[2,32,512]{2,1,0:T(8,128)S(1)} %get-tuple-element.67), channel_id=1, source_target_pairs={{8,24},{12,28},{16,0},{20,4},{24,8},{28,12},{32,48},{36,52},{40,56... | collective-permute-start | bytes 393224 | tf_op jit(solution)/shard_map/ppermute | solution.py:395
  21.6 5.7 %collective-permute-start.6 = (f32[2,32,512]{2,1,0:T(8,128)S(1)}, f32[2,32,512]{2,1,0:T(8,128)S(1)}, u32[]{:S(2)}, u32[]{:S(2)}) collective-permute-start(f32[2,32,512]{2,1,0:T(8,128)S(1)} %get-tuple-element.68), channel_id=1, source_target_pairs={{8,0},{12,4},{16,8},{20,12},{24,16},{28,20},{32,56},{36,60},{40,32... | collective-permute-start | bytes 393224 | tf_op jit(solution)/shard_map/ppermute | solution.py:395
  28.4 7.2 %collective-permute-start.7 = (f32[136,512]{1,0:T(8,128)S(1)}, f32[136,512]{1,0:T(8,128)S(1)}, u32[]{:S(2)}, u32[]{:S(2)}) collective-permute-start(f32[136,512]{1,0:T(8,128)S(1)} %add_add_fusion.refs_4_), channel_id=1, source_target_pairs={{0,8},{4,36},{1,9},{5,37},{2,10},{6,38},{3,11},{7,39}} | collective-permute-start | bytes 835592 | tf_op jit(solution)/shard_map/ppermute | solution.py:403
  29.7 3.9 %collective-permute-start.8 = (f32[2,32,512]{2,1,0:T(8,128)S(1)}, f32[2,32,512]{2,1,0:T(8,128)S(1)}, u32[]{:S(2)}, u32[]{:S(2)}) collective-permute-start(f32[2,32,512]{2,1,0:T(8,128)S(1)} %get-tuple-element.78), channel_id=1, source_target_pairs={{0,1},{4,5},{8,9},{12,13},{16,17},{20,21},{24,25},{28,29},{32,33},... | collective-permute-start | bytes 393224 | tf_op jit(solution)/shard_map/ppermute | solution.py:401
  31.0 3.3 %collective-permute-start.9 = (f32[2,32,512]{2,1,0:T(8,128)S(1)}, f32[2,32,512]{2,1,0:T(8,128)S(1)}, u32[]{:S(2)}, u32[]{:S(2)}) collective-permute-start(f32[2,32,512]{2,1,0:T(8,128)S(1)} %get-tuple-element.79), channel_id=1, source_target_pairs={{0,2},{4,6},{8,10},{12,14},{16,18},{20,22},{24,26},{28,30},{32,34}... | collective-permute-start | bytes 393224 | tf_op jit(solution)/shard_map/ppermute | solution.py:401
  32.3 3.2 %collective-permute-start.10 = (f32[2,32,512]{2,1,0:T(8,128)S(1)}, f32[2,32,512]{2,1,0:T(8,128)S(1)}, u32[]{:S(2)}, u32[]{:S(2)}) collective-permute-start(f32[2,32,512]{2,1,0:T(8,128)S(1)} %get-tuple-element.80), channel_id=1, source_target_pairs={{0,3},{4,7},{8,11},{12,15},{16,19},{20,23},{24,27},{28,31},{32,35}... | collective-permute-start | bytes 393224 | tf_op jit(solution)/shard_map/ppermute | solution.py:401
  35.6 9.8 %collective-permute-start.11 = (f32[264,512]{1,0:T(8,128)S(1)}, f32[264,512]{1,0:T(8,128)S(1)}, u32[]{:S(2)}, u32[]{:S(2)}) collective-permute-start(f32[264,512]{1,0:T(8,128)S(1)} %merge.1.own_ref), channel_id=1, source_target_pairs={{0,24},{4,100},{8,16},{12,108},{16,8},{20,116},{24,0},{28,124},{32... | collective-permute-start | bytes 1622024 | tf_op jit(solution)/shard_map/ppermute | solution.py:411
  35.7 9.8 %collective-permute-start.12 = (f32[256,512]{1,0:T(8,128)S(1)}, f32[256,512]{1,0:T(8,128)S(1)}, u32[]{:S(2)}, u32[]{:S(2)}) collective-permute-start(f32[256,512]{1,0:T(8,128)S(1)} %slice.3.lead_ref.refs_0_), channel_id=1, source_target_pairs={{0,1},{4,5},{8,9},{12,13},{16,17},{20,21},{24,25},{28,29},{32,33},... | collective-permute-start | bytes 1572872 | tf_op jit(solution)/shard_map/ppermute | solution.py:410
  39.1 0.8 copy-start.3
  39.9 0.8 copy-start.5
  45.5 12.3 %copy-start.6 = (f32[256,512]{1,0:T(8,128)S(1)}, f32[256,512]{1,0:T(8,128)}, u32[]{:S(2)}) copy-start(f32[256,512]{1,0:T(8,128)} %copy-done.5) | copy-start | bytes 1572868
  45.5 12.3 %copy-start.4 = (f32[256,512]{1,0:T(8,128)S(1)}, f32[256,512]{1,0:T(8,128)}, u32[]{:S(2)}) copy-start(f32[256,512]{1,0:T(8,128)} %copy-done.3) | copy-start | bytes 1572868
  45.5 8.6 %collective-permute-start.13 = (f32[264,512]{1,0:T(8,128)S(1)}, f32[264,512]{1,0:T(8,128)S(1)}, u32[]{:S(2)}, u32[]{:S(2)}) collective-permute-start(f32[264,512]{1,0:T(8,128)S(1)} %join.3.own_ref), channel_id=1, source_target_pairs={{0,32},{4,12},{8,40},{12,4},{16,48},{20,28},{24,56},{28,20},{32,0}... | collective-permute-start | bytes 1622024 | tf_op jit(solution)/shard_map/ppermute | solution.py:414
  45.7 12.1 %collective-permute-start.14 = (f32[256,512]{1,0:T(8,128)S(1)}, f32[256,512]{1,0:T(8,128)S(1)}, u32[]{:S(2)}, u32[]{:S(2)}) collective-permute-start(f32[256,512]{1,0:T(8,128)S(1)} %broadcast_select_fusion), channel_id=1, source_target_pairs={{0,3},{1,2},{4,7},{5,6},{8,11},{9,10},{12,15},{13,14},{16,19},{17,... | collective-permute-start | bytes 1572872 | tf_op jit(solution)/shard_map/ppermute | solution.py:413
  57.8 12.5 %collective-permute-start.15 = (f32[392,512]{1,0:T(8,128)S(1)}, f32[392,512]{1,0:T(8,128)S(1)}, u32[]{:S(2)}, u32[]{:S(2)}) collective-permute-start(f32[392,512]{1,0:T(8,128)S(1)} %join.4.own_ref), channel_id=1, source_target_pairs={{0,96},{4,28},{8,104},{12,20},{16,112},{20,12},{24,120},{28,4},{32... | collective-permute-start | bytes 2408456 | tf_op jit(solution)/shard_map/ppermute | solution.py:417
  57.8 12.6 %collective-permute-start.16 = (f32[256,512]{1,0:T(8,128)S(1)}, f32[256,512]{1,0:T(8,128)S(1)}, u32[]{:S(2)}, u32[]{:S(2)}) collective-permute-start(f32[256,512]{1,0:T(8,128)S(1)} %copy-done.6), channel_id=1, source_target_pairs={{0,1},{1,2},{2,3},{3,0},{4,5},{5,6},{6,7},{7,4},{8,9},{9,10},{10,1... | collective-permute-start | bytes 1572872 | tf_op jit(solution)/shard_map/ppermute | solution.py:420
  57.8 12.6 %collective-permute-start.17 = (f32[256,512]{1,0:T(8,128)S(1)}, f32[256,512]{1,0:T(8,128)S(1)}, u32[]{:S(2)}, u32[]{:S(2)}) collective-permute-start(f32[256,512]{1,0:T(8,128)S(1)} %copy-done.4), channel_id=1, source_target_pairs={{0,3},{1,0},{2,1},{3,2},{4,7},{5,4},{6,5},{7,6},{8,11},{9,8},{10,9... | collective-permute-start | bytes 1572872 | tf_op jit(solution)/shard_map/ppermute | solution.py:420
  70.4 11.7 %collective-permute-start.20 = (f32[136,512]{1,0:T(8,128)S(1)}, f32[136,512]{1,0:T(8,128)S(1)}, u32[]{:S(2)}, u32[]{:S(2)}) collective-permute-start(f32[136,512]{1,0:T(8,128)S(1)} %get-tuple-element.108.own_ref), channel_id=1, source_target_pairs={{0,4},{4,0},{8,12},{12,8},{16,20},{20,16},{24,28},{28,24},{32,36},... | collective-permute-start | bytes 835592 | tf_op jit(solution)/shard_map/ppermute | solution.py:422
  77.2 23.4 %collective-permute-start.19 = (f32[512,512]{1,0:T(8,128)S(1)}, f32[512,512]{1,0:T(8,128)S(1)}, u32[]{:S(2)}, u32[]{:S(2)}) collective-permute-start(f32[512,512]{1,0:T(8,128)S(1)} %get-tuple-element.107.refs_5_), channel_id=1, source_target_pairs={{0,4},{4,0},{8,12},{12,8},{16,20},{20,16},{24,28},{28,24},{32,36},... | collective-permute-start | bytes 3145736 | tf_op jit(solution)/shard_map/ppermute | solution.py:425
  77.3 23.3 %collective-permute-start.18 = (f32[512,512]{1,0:T(8,128)S(1)}, f32[512,512]{1,0:T(8,128)S(1)}, u32[]{:S(2)}, u32[]{:S(2)}) collective-permute-start(f32[512,512]{1,0:T(8,128)S(1)} %get-tuple-element.107.refs_5_), channel_id=1, source_target_pairs={{0,8},{4,36},{8,0},{12,44},{16,24},{20,52},{24,16},{28,60},{32,40}... | collective-permute-start | bytes 3145736 | tf_op jit(solution)/shard_map/ppermute | solution.py:423
  80.5 20.0 %collective-permute-start.21 = (f32[256,512]{1,0:T(8,128)S(1)}, f32[256,512]{1,0:T(8,128)S(1)}, u32[]{:S(2)}, u32[]{:S(2)}) collective-permute-start(f32[256,512]{1,0:T(8,128)S(1)} %get-tuple-element.114), channel_id=1, source_target_pairs={{0,2},{1,3},{2,0},{3,1},{4,6},{5,7},{6,4},{7,5},{8,10},{9,11},{10,... | collective-permute-start | bytes 1572872 | tf_op jit(solution)/shard_map/ppermute | solution.py:424
  100.6 3.5 %copy-start.1 = (f32[256,2048]{1,0:T(8,128)S(1)}, f32[256,2048]{1,0:T(8,128)}, u32[]{:S(2)}) copy-start(f32[256,2048]{1,0:T(8,128)} %refs_9_.1) | copy-start | bytes 6291460
  100.6 3.5 %collective-permute-start.22 = (f32[512,512]{1,0:T(8,128)S(1)}, f32[512,512]{1,0:T(8,128)S(1)}, u32[]{:S(2)}, u32[]{:S(2)}) collective-permute-start(f32[512,512]{1,0:T(8,128)S(1)} %collective-permute-done.18.refs_6_), channel_id=1, source_target_pairs={{0,4},{4,0},{8,12},{12,8},{16,20},{20,16},{24,28},{28,24},{32,36},... | collective-permute-start | bytes 3145736 | tf_op jit(solution)/shard_map/ppermute | solution.py:429

commit v17 on v14

--- a/solution.py
+++ b/solution.py
@@ -279,11 +279,17 @@
 def weight_kernel(*refs):
     rows, inverse = refs[:4], refs[4:7]
     panel_ref, weight_ref, rows_ref = refs[7:]
-    for index, ref in enumerate(rows):
-
-        @pl.when(lax.axis_index("col") == index)
+    col = lax.axis_index("col")
+    for index in range(2):
+
+        @pl.when(col == index)
         def _():
-            rows_ref[...] = ref[...]
+            rows_ref[...] = rows[index][...]
+
+    @pl.when(col >= 2)
+    def _():
+        rows_ref[:, :PW] = rows[2][...]
+        rows_ref[:, PW:] = rows[3][...]
 
     inv_a, across, inv_b = [ref[...] for ref in inverse]
     panel_a = dot(rows_ref[:, :PW], inv_a, 1, 1)
@@ -407,17 +413,21 @@
     *pieces, plan = local_call(pick_kernel, "pick", [(height, 2 * PW)] * 4, 1, [(4, 8)])(tile_map, front)
 
     load, lead = lax.optimization_barrier((load, lead))
-    copies = [lax.ppermute(lead, "col", [(0, to)]) for to in (1, 2, 3)]
+    near = lax.ppermute(lead, "col", [(0, 1)])
     load = local_call(partial(join_kernel, 64), "join", [(128 + BLOCK, LEAD)])(load, lax.ppermute(load, "row", every[1]))[0]
-    load, copies[0], copies[2], *pieces = lax.optimization_barrier((load, copies[0], copies[2], *pieces))
+    load, near, *pieces = lax.optimization_barrier((load, near, *pieces))
+    hold = jnp.where(lax.axis_index("col") == 1, near, lead)
+    onward = [(0, 3), (1, 2)]
+    far = [lax.ppermute(hold[:, :PW], "col", onward), hold[:, PW:]]
     load = local_call(partial(join_kernel, 128), "join", [(256 + BLOCK, LEAD)])(load, lax.ppermute(load, "row", every[2]))[0]
-    load, copies[1], *pieces = lax.optimization_barrier((load, copies[1], *pieces))
+    load, far, *pieces = lax.optimization_barrier((load, far, *pieces))
+    far[1] = lax.ppermute(far[1], "col", onward)
     gathered, block = local_call(partial(join_kernel, 256), "join", [(512, LEAD), (BLOCK, LEAD)])(
         load, lax.ppermute(load, "row", every[3])
     )
     for hop in (1, 3):
         pieces[hop] = lax.ppermute(pieces[hop], "col", ring[hop])
-    block, gathered, *pieces = lax.optimization_barrier((block, gathered, *pieces))
+    block, gathered, far, *pieces = lax.optimization_barrier((block, gathered, far, *pieces))
     other = lax.ppermute(block, "row", swap)
     late = lax.ppermute(gathered, "row", every[0])
     pieces[2] = lax.ppermute(pieces[2], "col", ring[2])
@@ -426,7 +436,7 @@
     inverse = factor(block, other)
     late, other_gathered, inverse, pieces = lax.optimization_barrier((late, other_gathered, inverse, pieces))
     other_late = lax.ppermute(late, "row", swap)
-    panel, weight = weigh([lead, *copies], inverse)
+    panel, weight = weigh([lead, near, *far], inverse)
     updated = update(plan, weight, pieces, [gathered, late, other_gathered, other_late], ancestor)
     return panel, updated
 

time: 117 us -> 111 us (0.949)
  the two profiles are of different devices: /device:TPU:1 before, /device:TPU:9 now
where the time goes in v17:
time: 111 us
  waiting for transfers between devices  38.4 us (35%)
  starting transfers between devices  35.7 us (32%)
  Pallas kernels  32.8 us (30%)
  local copies, waits for them, and re-layouts  2.72 us (2%)
    pallas_call x9, Pallas kernels, call(): pl.pallas_call(kernel, out_shape=[jax.ShapeDtypeStruct(shape, jnp.float32...  21.8 us
    ppermute x3, waiting for transfers between devices, shards(): parts[hop] = lax.ppermute(parts[hop], 'row', pairs)  10.3 us
    pallas_call x1, Pallas kernels, update(): pl.pallas_call(update_kernel, out_shape=jax.ShapeDtypeStruct(base.shape,...  8.11 us
    ppermute x1, waiting for transfers between devices, shards(): lax.ppermute(load, 'row', every[3])  8.02 us
    ppermute x1, starting transfers between devices, shards(): other = lax.ppermute(block, 'row', swap)  6.64 us
    ppermute x3, waiting for transfers between devices, shards(): parts[to] = lax.ppermute(parts[to], 'col', [(0, to)])  6.24 us
    ppermute x1, waiting for transfers between devices, shards(): lax.ppermute(load, 'row', every[2])  5.82 us
    ppermute x1, starting transfers between devices, shards(): pieces[2] = lax.ppermute(pieces[2], 'col', ring[2])  5.07 us
  transfers between devices with their start and end apart: 24, of which 9 were waited for; matrix products, arithmetic and copies ran while one was open for 0% of the time, Pallas kernels for 22%

profile of v17, /device:TPU:9, one launch (start us, length us, event | category | flops | bytes accessed | tf_op | source)
XLA Modules:
  0.0 110.8 jit_solution(1052869122295842998)
XLA Ops:
  0.6 1.1 slice.9.lead_ref.refs_0_
  1.7 0.8 collective-permute-start.3
  2.5 0.0 copy-start
  2.5 0.8 collective-permute-start.2
  3.3 0.7 collective-permute-start.1
  4.0 1.3 %collective-permute-start = (f32[136,512]{1,0:T(8,128)S(1)}, f32[136,512]{1,0:T(8,128)S(1)}, u32[]{:S(2)}, u32[]{:S(2)}) collective-permute-start(f32[136,512]{1,0:T(8,128)S(1)} %corner.1), channel_id=1, source_target_pairs={{0,1},{4,5}} | collective-permute-start | bytes 835592 | tf_op jit(solution)/shard_map/ppermute | solution.py:395
  5.3 0.0 collective-permute-done.3.mate_ref
  5.3 0.1 share.1
  5.4 1.3 %collective-permute-start.4 = (f32[2,32,512]{2,1,0:T(8,128)S(1)}, f32[2,32,512]{2,1,0:T(8,128)S(1)}, u32[]{:S(2)}, u32[]{:S(2)}) collective-permute-start(f32[2,32,512]{2,1,0:T(8,128)S(1)} %get-tuple-element.69), channel_id=1, source_target_pairs={{8,16},{12,20},{16,24},{20,28},{24,0},{28,4},{32,40},{36,44},{40,4... | collective-permute-start | bytes 393224 | tf_op jit(solution)/shard_map/ppermute | solution.py:401
  6.7 1.3 %collective-permute-start.5 = (f32[2,32,512]{2,1,0:T(8,128)S(1)}, f32[2,32,512]{2,1,0:T(8,128)S(1)}, u32[]{:S(2)}, u32[]{:S(2)}) collective-permute-start(f32[2,32,512]{2,1,0:T(8,128)S(1)} %get-tuple-element.70), channel_id=1, source_target_pairs={{8,24},{12,28},{16,0},{20,4},{24,8},{28,12},{32,48},{36,52},{40,56... | collective-permute-start | bytes 393224 | tf_op jit(solution)/shard_map/ppermute | solution.py:401
  8.0 5.6 %collective-permute-done.4.refs_1_ = f32[2,32,512]{2,1,0:T(8,128)S(1)} collective-permute-done((f32[2,32,512]{2,1,0:T(8,128)S(1)}, f32[2,32,512]{2,1,0:T(8,128)S(1)}, u32[]{:S(2)}, u32[]{:S(2)}) %collective-permute-start.4) | collective-permute-done | bytes 131104 | tf_op jit(solution)/shard_map/ppermute | solution.py:401
  13.6 1.3 %collective-permute-start.6 = (f32[2,32,512]{2,1,0:T(8,128)S(1)}, f32[2,32,512]{2,1,0:T(8,128)S(1)}, u32[]{:S(2)}, u32[]{:S(2)}) collective-permute-start(f32[2,32,512]{2,1,0:T(8,128)S(1)} %get-tuple-element.71), channel_id=1, source_target_pairs={{8,0},{12,4},{16,8},{20,12},{24,16},{28,20},{32,56},{36,60},{40,32... | collective-permute-start | bytes 393224 | tf_op jit(solution)/shard_map/ppermute | solution.py:401
  14.9 1.9 %collective-permute-done.5.refs_2_ = f32[2,32,512]{2,1,0:T(8,128)S(1)} collective-permute-done((f32[2,32,512]{2,1,0:T(8,128)S(1)}, f32[2,32,512]{2,1,0:T(8,128)S(1)}, u32[]{:S(2)}, u32[]{:S(2)}) %collective-permute-start.5) | collective-permute-done | bytes 131104 | tf_op jit(solution)/shard_map/ppermute | solution.py:401
  16.8 2.9 %collective-permute-done.6.refs_3_ = f32[2,32,512]{2,1,0:T(8,128)S(1)} collective-permute-done((f32[2,32,512]{2,1,0:T(8,128)S(1)}, f32[2,32,512]{2,1,0:T(8,128)S(1)}, u32[]{:S(2)}, u32[]{:S(2)}) %collective-permute-start.6) | collective-permute-done | bytes 131104 | tf_op jit(solution)/shard_map/ppermute | solution.py:401
  19.7 1.0 sort.1
  20.7 0.0 collective-permute-done.2
  20.7 0.0 collective-permute-done.1
  20.7 0.8 collective-permute-done
  21.5 0.1 add_add_fusion.refs_4_
  21.6 2.2 %collective-permute-start.7 = (f32[136,512]{1,0:T(8,128)S(1)}, f32[136,512]{1,0:T(8,128)S(1)}, u32[]{:S(2)}, u32[]{:S(2)}) collective-permute-start(f32[136,512]{1,0:T(8,128)S(1)} %add_add_fusion.refs_4_), channel_id=1, source_target_pairs={{0,8},{4,36},{1,9},{5,37},{2,10},{6,38},{3,11},{7,39}} | collective-permute-start | bytes 835592 | tf_op jit(solution)/shard_map/ppermute | solution.py:409
  23.8 1.3 %collective-permute-start.8 = (f32[2,32,512]{2,1,0:T(8,128)S(1)}, f32[2,32,512]{2,1,0:T(8,128)S(1)}, u32[]{:S(2)}, u32[]{:S(2)}) collective-permute-start(f32[2,32,512]{2,1,0:T(8,128)S(1)} %get-tuple-element.81), channel_id=1, source_target_pairs={{0,1},{4,5},{8,9},{12,13},{16,17},{20,21},{24,25},{28,29},{32,33},... | collective-permute-start | bytes 393224 | tf_op jit(solution)/shard_map/ppermute | solution.py:407
  25.1 0.7 collective-permute-start.9
  25.8 0.7 collective-permute-start.10
  26.5 6.2 %collective-permute-done.8.refs_1_ = f32[2,32,512]{2,1,0:T(8,128)S(1)} collective-permute-done((f32[2,32,512]{2,1,0:T(8,128)S(1)}, f32[2,32,512]{2,1,0:T(8,128)S(1)}, u32[]{:S(2)}, u32[]{:S(2)}) %collective-permute-start.8) | collective-permute-done | bytes 131104 | tf_op jit(solution)/shard_map/ppermute | solution.py:407
  32.7 0.0 collective-permute-done.9.refs_2_
  32.7 0.0 collective-permute-done.10.refs_3_
  32.7 0.0 collective-permute-done.7.refs_5_
  32.7 0.1 merge.1.own_ref
  32.8 0.1 collective-permute-start.11
  32.9 1.3 %collective-permute-start.12 = (f32[256,512]{1,0:T(8,128)S(1)}, f32[256,512]{1,0:T(8,128)S(1)}, u32[]{:S(2)}, u32[]{:S(2)}) collective-permute-start(f32[256,512]{1,0:T(8,128)S(1)} %slice.9.lead_ref.refs_0_), channel_id=1, source_target_pairs={{0,1},{4,5},{8,9},{12,13},{16,17},{20,21},{24,25},{28,29},{32,33},... | collective-permute-start | bytes 1572872 | tf_op jit(solution)/shard_map/ppermute | solution.py:416
  34.2 2.0 %pick.1 = (f32[256,512]{1,0:T(8,128)S(1)}, f32[256,512]{1,0:T(8,128)S(1)}, f32[256,512]{1,0:T(8,128)S(1)}, f32[256,512]{1,0:T(8,128)S(1)}, s32[4,8]{1,0:T(4,128)S(1)}) custom-call(s32[32]{0:T(128)S(1)} %copy-done.2, f32[256,2048]{1,0:T(8,128)S(1)} %copy-done), custom_call_target="tpu_custom_call" | custom-call | flops 1024 | bytes 1024 | tf_op jit(solution)/shard_map/pick/pallas_call | solution.py:109
  36.2 0.0 copy-start.3
  36.2 0.8 copy-done.3
  37.0 0.8 copy-done.5
  37.8 4.8 %collective-permute-done.11.got_ref = f32[264,512]{1,0:T(8,128)S(1)} collective-permute-done((f32[264,512]{1,0:T(8,128)S(1)}, f32[264,512]{1,0:T(8,128)S(1)}, u32[]{:S(2)}, u32[]{:S(2)}) %collective-permute-start.11) | collective-permute-done | bytes 540704 | tf_op jit(solution)/shard_map/ppermute | solution.py:417
  42.6 2.3 %collective-permute-done.12.refs_1_ = f32[256,512]{1,0:T(8,128)S(1)} collective-permute-done((f32[256,512]{1,0:T(8,128)S(1)}, f32[256,512]{1,0:T(8,128)S(1)}, u32[]{:S(2)}, u32[]{:S(2)}) %collective-permute-start.12) | collective-permute-done | bytes 524320 | tf_op jit(solution)/shard_map/ppermute | solution.py:416
  44.9 0.0 collective-permute-start.13
  44.9 0.1 broadcast_select_fusion
  45.0 2.5 %collective-permute-start.14 = (f32[256,256]{1,0:T(8,128)S(1)}, f32[256,256]{1,0:T(8,128)S(1)}, u32[]{:S(2)}, u32[]{:S(2)}) collective-permute-start(f32[256,256]{1,0:T(8,128)S(1)} %get-tuple-element.135), channel_id=1, source_target_pairs={{0,3},{1,2},{4,7},{5,6},{8,11},{9,10},{12,15},{13,14},{16,19},{17,... | collective-permute-start | bytes 786440 | tf_op jit(solution)/shard_map/ppermute | solution.py:421
  47.6 5.8 %collective-permute-done.13.got_ref = f32[264,512]{1,0:T(8,128)S(1)} collective-permute-done((f32[264,512]{1,0:T(8,128)S(1)}, f32[264,512]{1,0:T(8,128)S(1)}, u32[]{:S(2)}, u32[]{:S(2)}) %collective-permute-start.13) | collective-permute-done | bytes 540704 | tf_op jit(solution)/shard_map/ppermute | solution.py:422
  53.4 0.1 join.4.own_ref
  53.5 0.0 collective-permute-done.14.refs_2_
  53.5 0.1 collective-permute-start.15
  53.6 0.5 collective-permute-start.17
  54.1 1.0 collective-permute-start.18
  55.1 2.9 %collective-permute-start.16 = (f32[256,256]{1,0:T(8,128)S(1)}, f32[256,256]{1,0:T(8,128)S(1)}, u32[]{:S(2)}, u32[]{:S(2)}) collective-permute-start(f32[256,256]{1,0:T(8,128)S(1)} %get-tuple-element.106), channel_id=1, source_target_pairs={{0,3},{1,2},{4,7},{5,6},{8,11},{9,10},{12,15},{13,14},{16,19},{17,... | collective-permute-start | bytes 786440 | tf_op jit(solution)/shard_map/ppermute | solution.py:424
  58.1 8.0 %collective-permute-done.15.got_ref = f32[392,512]{1,0:T(8,128)S(1)} collective-permute-done((f32[392,512]{1,0:T(8,128)S(1)}, f32[392,512]{1,0:T(8,128)S(1)}, u32[]{:S(2)}, u32[]{:S(2)}) %collective-permute-start.15) | collective-permute-done | bytes 802848 | tf_op jit(solution)/shard_map/ppermute | solution.py:426
  66.1 0.1 join.5
  66.2 0.0 collective-permute-done.16.refs_3_
  66.2 0.0 collective-permute-done.17.refs_2_
  66.2 0.0 collective-permute-done.18.refs_4_
  66.2 6.6 %collective-permute-start.21 = (f32[136,512]{1,0:T(8,128)S(1)}, f32[136,512]{1,0:T(8,128)S(1)}, u32[]{:S(2)}, u32[]{:S(2)}) collective-permute-start(f32[136,512]{1,0:T(8,128)S(1)} %get-tuple-element.114.own_ref), channel_id=1, source_target_pairs={{0,4},{4,0},{8,12},{12,8},{16,20},{20,16},{24,28},{28,24},{32,36},... | collective-permute-start | bytes 835592 | tf_op jit(solution)/shard_map/ppermute | solution.py:431
  72.9 0.1 collective-permute-start.20
  73.0 1.6 %collective-permute-start.19 = (f32[512,512]{1,0:T(8,128)S(1)}, f32[512,512]{1,0:T(8,128)S(1)}, u32[]{:S(2)}, u32[]{:S(2)}) collective-permute-start(f32[512,512]{1,0:T(8,128)S(1)} %get-tuple-element.113.refs_5_), channel_id=1, source_target_pairs={{0,8},{4,36},{8,0},{12,44},{16,24},{20,52},{24,16},{28,60},{32,40}... | collective-permute-start | bytes 3145736 | tf_op jit(solution)/shard_map/ppermute | solution.py:432
  74.5 5.1 %collective-permute-start.22 = (f32[256,512]{1,0:T(8,128)S(1)}, f32[256,512]{1,0:T(8,128)S(1)}, u32[]{:S(2)}, u32[]{:S(2)}) collective-permute-start(f32[256,512]{1,0:T(8,128)S(1)} %get-tuple-element.120), channel_id=1, source_target_pairs={{0,2},{1,3},{2,0},{3,1},{4,6},{5,7},{6,4},{7,5},{8,10},{9,11},{10,... | collective-permute-start | bytes 1572872 | tf_op jit(solution)/shard_map/ppermute | solution.py:433
  79.6 0.0 collective-permute-done.21.other_ref
  79.6 18.4 %factor.1 = (f32[256,256]{1,0:T(8,128)S(1)}, f32[256,256]{1,0:T(8,128)S(1)}, f32[256,256]{1,0:T(8,128)S(1)}) custom-call(f32[136,512]{1,0:T(8,128)S(1)} %get-tuple-element.114.own_ref, f32[136,512]{1,0:T(8,128)S(1)} %collective-permute-done.21.other_ref), custom_call_target="tpu_custom_call" | custom-call | flops 21474836480 | bytes 1048576 | tf_op jit(solution)/shard_map/factor/pallas_call | solution.py:109
  98.0 0.0 copy-start.1
  98.1 0.0 collective-permute-done.22.refs_3_
  98.1 0.0 collective-permute-done.20.refs_7_
  98.1 0.0 collective-permute-done.19.refs_6_
  98.1 1.7 %collective-permute-start.23 = (f32[512,512]{1,0:T(8,128)S(1)}, f32[512,512]{1,0:T(8,128)S(1)}, u32[]{:S(2)}, u32[]{:S(2)}) collective-permute-start(f32[512,512]{1,0:T(8,128)S(1)} %collective-permute-done.19.refs_6_), channel_id=1, source_target_pairs={{0,4},{4,0},{8,12},{12,8},{16,20},{20,16},{24,28},{28,24},{32,36},... | collective-permute-start | bytes 3145736 | tf_op jit(solution)/shard_map/ppermute | solution.py:438
  99.8 2.9 %weigh.1 = (f32[256,512]{1,0:T(8,128)}, f32[256,512]{1,0:T(8,128)S(1)}) custom-call(f32[256,512]{1,0:T(8,128)S(1)} %slice.9.lead_ref.refs_0_, f32[256,512]{1,0:T(8,128)S(1)} %collective-permute-done.12.refs_1_, f32[256,256]{1,0:T(8,128)S(1)} %collective-permute-done.14.refs_2_, f32[256,256]{1,0:T(8,128)S(1)} %collective-permute-done.16.refs_3_, ...), custom_call_target="tpu_custom_call" | custom-call | flops 1024 | bytes 1024 | tf_op jit(solution)/shard_map/weigh/pallas_call | solution.py:307
  102.7 8.1 %update.1 = f32[256,2048]{1,0:T(8,128)} custom-call(s32[4,8]{1,0:T(4,128)S(1)} %get-tuple-element.126.plan, f32[256,512]{1,0:T(8,128)S(1)} %get-tuple-element.127.refs_0_, f32[256,512]{1,0:T(8,128)S(1)} %get-tuple-element.128.refs_1_, f32[256,512]{1,0:T(8,128)S(1)} %collective-permute-done.17.refs_2_, f32[256,512]{1,0:T(8,128)S(1)} %collective-permute-done.22.refs_3_, ...), custom_call_target="tpu_custom_call" | custom-call | tf_op jit(solution)/shard_map/update/pallas_call | solution.py:356
  (13 shorter events, 0.1 us)
Async XLA Ops:
  0.6 19.0 %copy-start.2 = (s32[32]{0:T(128)S(1)}, s32[32]{0:T(128)}, u32[]{:S(2)}) copy-start(s32[32]{0:T(128)} %map_ref.3) | copy-start | bytes 388
  1.7 3.6 %collective-permute-start.3 = (f32[256,512]{1,0:T(8,128)S(1)}, f32[256,512]{1,0:T(8,128)S(1)}, u32[]{:S(2)}, u32[]{:S(2)}) collective-permute-start(f32[256,512]{1,0:T(8,128)S(1)} %slice.9.lead_ref.refs_0_), channel_id=1, source_target_pairs={{0,4},{4,0},{8,12},{12,8},{16,20},{20,16},{24,28},{28,24},{32,36},... | collective-permute-start | bytes 1572872 | tf_op jit(solution)/shard_map/ppermute | solution.py:397
  2.5 31.7 %copy-start = (f32[256,2048]{1,0:T(8,128)S(1)}, f32[256,2048]{1,0:T(8,128)}, u32[]{:S(2)}) copy-start(f32[256,2048]{1,0:T(8,128)} %front_ref.1) | copy-start | bytes 6291460
  2.5 18.2 %collective-permute-start.2 = (f32[136,512]{1,0:T(8,128)S(1)}, f32[136,512]{1,0:T(8,128)S(1)}, u32[]{:S(2)}, u32[]{:S(2)}) collective-permute-start(f32[136,512]{1,0:T(8,128)S(1)} %corner.1), channel_id=1, source_target_pairs={{0,3},{4,7}} | collective-permute-start | bytes 835592 | tf_op jit(solution)/shard_map/ppermute | solution.py:395
  3.3 17.4 %collective-permute-start.1 = (f32[136,512]{1,0:T(8,128)S(1)}, f32[136,512]{1,0:T(8,128)S(1)}, u32[]{:S(2)}, u32[]{:S(2)}) collective-permute-start(f32[136,512]{1,0:T(8,128)S(1)} %corner.1), channel_id=1, source_target_pairs={{0,2},{4,6}} | collective-permute-start | bytes 835592 | tf_op jit(solution)/shard_map/ppermute | solution.py:395
  4.0 17.5 %collective-permute-start = (f32[136,512]{1,0:T(8,128)S(1)}, f32[136,512]{1,0:T(8,128)S(1)}, u32[]{:S(2)}, u32[]{:S(2)}) collective-permute-start(f32[136,512]{1,0:T(8,128)S(1)} %corner.1), channel_id=1, source_target_pairs={{0,1},{4,5}} | collective-permute-start | bytes 835592 | tf_op jit(solution)/shard_map/ppermute | solution.py:395
  5.4 8.2 %collective-permute-start.4 = (f32[2,32,512]{2,1,0:T(8,128)S(1)}, f32[2,32,512]{2,1,0:T(8,128)S(1)}, u32[]{:S(2)}, u32[]{:S(2)}) collective-permute-start(f32[2,32,512]{2,1,0:T(8,128)S(1)} %get-tuple-element.69), channel_id=1, source_target_pairs={{8,16},{12,20},{16,24},{20,28},{24,0},{28,4},{32,40},{36,44},{40,4... | collective-permute-start | bytes 393224 | tf_op jit(solution)/shard_map/ppermute | solution.py:401
  6.7 10.1 %collective-permute-start.5 = (f32[2,32,512]{2,1,0:T(8,128)S(1)}, f32[2,32,512]{2,1,0:T(8,128)S(1)}, u32[]{:S(2)}, u32[]{:S(2)}) collective-permute-start(f32[2,32,512]{2,1,0:T(8,128)S(1)} %get-tuple-element.70), channel_id=1, source_target_pairs={{8,24},{12,28},{16,0},{20,4},{24,8},{28,12},{32,48},{36,52},{40,56... | collective-permute-start | bytes 393224 | tf_op jit(solution)/shard_map/ppermute | solution.py:401
  13.6 6.0 %collective-permute-start.6 = (f32[2,32,512]{2,1,0:T(8,128)S(1)}, f32[2,32,512]{2,1,0:T(8,128)S(1)}, u32[]{:S(2)}, u32[]{:S(2)}) collective-permute-start(f32[2,32,512]{2,1,0:T(8,128)S(1)} %get-tuple-element.71), channel_id=1, source_target_pairs={{8,0},{12,4},{16,8},{20,12},{24,16},{28,20},{32,56},{36,60},{40,32... | collective-permute-start | bytes 393224 | tf_op jit(solution)/shard_map/ppermute | solution.py:401
  21.6 11.1 %collective-permute-start.7 = (f32[136,512]{1,0:T(8,128)S(1)}, f32[136,512]{1,0:T(8,128)S(1)}, u32[]{:S(2)}, u32[]{:S(2)}) collective-permute-start(f32[136,512]{1,0:T(8,128)S(1)} %add_add_fusion.refs_4_), channel_id=1, source_target_pairs={{0,8},{4,36},{1,9},{5,37},{2,10},{6,38},{3,11},{7,39}} | collective-permute-start | bytes 835592 | tf_op jit(solution)/shard_map/ppermute | solution.py:409
  23.8 8.9 %collective-permute-start.8 = (f32[2,32,512]{2,1,0:T(8,128)S(1)}, f32[2,32,512]{2,1,0:T(8,128)S(1)}, u32[]{:S(2)}, u32[]{:S(2)}) collective-permute-start(f32[2,32,512]{2,1,0:T(8,128)S(1)} %get-tuple-element.81), channel_id=1, source_target_pairs={{0,1},{4,5},{8,9},{12,13},{16,17},{20,21},{24,25},{28,29},{32,33},... | collective-permute-start | bytes 393224 | tf_op jit(solution)/shard_map/ppermute | solution.py:407
  25.1 7.6 %collective-permute-start.9 = (f32[2,32,512]{2,1,0:T(8,128)S(1)}, f32[2,32,512]{2,1,0:T(8,128)S(1)}, u32[]{:S(2)}, u32[]{:S(2)}) collective-permute-start(f32[2,32,512]{2,1,0:T(8,128)S(1)} %get-tuple-element.82), channel_id=1, source_target_pairs={{0,2},{4,6},{8,10},{12,14},{16,18},{20,22},{24,26},{28,30},{32,34}... | collective-permute-start | bytes 393224 | tf_op jit(solution)/shard_map/ppermute | solution.py:407
  25.8 6.9 %collective-permute-start.10 = (f32[2,32,512]{2,1,0:T(8,128)S(1)}, f32[2,32,512]{2,1,0:T(8,128)S(1)}, u32[]{:S(2)}, u32[]{:S(2)}) collective-permute-start(f32[2,32,512]{2,1,0:T(8,128)S(1)} %get-tuple-element.83), channel_id=1, source_target_pairs={{0,3},{4,7},{8,11},{12,15},{16,19},{20,23},{24,27},{28,31},{32,35}... | collective-permute-start | bytes 393224 | tf_op jit(solution)/shard_map/ppermute | solution.py:407
  32.8 9.8 %collective-permute-start.11 = (f32[264,512]{1,0:T(8,128)S(1)}, f32[264,512]{1,0:T(8,128)S(1)}, u32[]{:S(2)}, u32[]{:S(2)}) collective-permute-start(f32[264,512]{1,0:T(8,128)S(1)} %merge.1.own_ref), channel_id=1, source_target_pairs={{0,24},{4,100},{8,16},{12,108},{16,8},{20,116},{24,0},{28,124},{32... | collective-permute-start | bytes 1622024 | tf_op jit(solution)/shard_map/ppermute | solution.py:417
  32.9 12.0 %collective-permute-start.12 = (f32[256,512]{1,0:T(8,128)S(1)}, f32[256,512]{1,0:T(8,128)S(1)}, u32[]{:S(2)}, u32[]{:S(2)}) collective-permute-start(f32[256,512]{1,0:T(8,128)S(1)} %slice.9.lead_ref.refs_0_), channel_id=1, source_target_pairs={{0,1},{4,5},{8,9},{12,13},{16,17},{20,21},{24,25},{28,29},{32,33},... | collective-permute-start | bytes 1572872 | tf_op jit(solution)/shard_map/ppermute | solution.py:416
  36.2 0.8 copy-start.3
  37.0 0.8 copy-start.5
  44.9 8.7 %copy-start.6 = (f32[256,512]{1,0:T(8,128)S(1)}, f32[256,512]{1,0:T(8,128)}, u32[]{:S(2)}) copy-start(f32[256,512]{1,0:T(8,128)} %copy-done.5) | copy-start | bytes 1572868
  44.9 9.2 %copy-start.4 = (f32[256,512]{1,0:T(8,128)S(1)}, f32[256,512]{1,0:T(8,128)}, u32[]{:S(2)}) copy-start(f32[256,512]{1,0:T(8,128)} %copy-done.3) | copy-start | bytes 1572868
  44.9 8.5 %collective-permute-start.13 = (f32[264,512]{1,0:T(8,128)S(1)}, f32[264,512]{1,0:T(8,128)S(1)}, u32[]{:S(2)}, u32[]{:S(2)}) collective-permute-start(f32[264,512]{1,0:T(8,128)S(1)} %join.3.own_ref), channel_id=1, source_target_pairs={{0,32},{4,12},{8,40},{12,4},{16,48},{20,28},{24,56},{28,20},{32,0}... | collective-permute-start | bytes 1622024 | tf_op jit(solution)/shard_map/ppermute | solution.py:422
  45.0 8.4 %collective-permute-start.14 = (f32[256,256]{1,0:T(8,128)S(1)}, f32[256,256]{1,0:T(8,128)S(1)}, u32[]{:S(2)}, u32[]{:S(2)}) collective-permute-start(f32[256,256]{1,0:T(8,128)S(1)} %get-tuple-element.135), channel_id=1, source_target_pairs={{0,3},{1,2},{4,7},{5,6},{8,11},{9,10},{12,15},{13,14},{16,19},{17,... | collective-permute-start | bytes 786440 | tf_op jit(solution)/shard_map/ppermute | solution.py:421
  53.5 12.6 %collective-permute-start.15 = (f32[392,512]{1,0:T(8,128)S(1)}, f32[392,512]{1,0:T(8,128)S(1)}, u32[]{:S(2)}, u32[]{:S(2)}) collective-permute-start(f32[392,512]{1,0:T(8,128)S(1)} %join.4.own_ref), channel_id=1, source_target_pairs={{0,96},{4,28},{8,104},{12,20},{16,112},{20,12},{24,120},{28,4},{32... | collective-permute-start | bytes 2408456 | tf_op jit(solution)/shard_map/ppermute | solution.py:426
  53.6 12.6 %collective-permute-start.17 = (f32[256,512]{1,0:T(8,128)S(1)}, f32[256,512]{1,0:T(8,128)S(1)}, u32[]{:S(2)}, u32[]{:S(2)}) collective-permute-start(f32[256,512]{1,0:T(8,128)S(1)} %copy-done.6), channel_id=1, source_target_pairs={{0,1},{1,2},{2,3},{3,0},{4,5},{5,6},{6,7},{7,4},{8,9},{9,10},{10,1... | collective-permute-start | bytes 1572872 | tf_op jit(solution)/shard_map/ppermute | solution.py:429
  54.1 12.1 %collective-permute-start.18 = (f32[256,512]{1,0:T(8,128)S(1)}, f32[256,512]{1,0:T(8,128)S(1)}, u32[]{:S(2)}, u32[]{:S(2)}) collective-permute-start(f32[256,512]{1,0:T(8,128)S(1)} %copy-done.4), channel_id=1, source_target_pairs={{0,3},{1,0},{2,1},{3,2},{4,7},{5,4},{6,5},{7,6},{8,11},{9,8},{10,9... | collective-permute-start | bytes 1572872 | tf_op jit(solution)/shard_map/ppermute | solution.py:429
  55.1 11.1 %collective-permute-start.16 = (f32[256,256]{1,0:T(8,128)S(1)}, f32[256,256]{1,0:T(8,128)S(1)}, u32[]{:S(2)}, u32[]{:S(2)}) collective-permute-start(f32[256,256]{1,0:T(8,128)S(1)} %get-tuple-element.106), channel_id=1, source_target_pairs={{0,3},{1,2},{4,7},{5,6},{8,11},{9,10},{12,15},{13,14},{16,19},{17,... | collective-permute-start | bytes 786440 | tf_op jit(solution)/shard_map/ppermute | solution.py:424
  66.2 13.4 %collective-permute-start.21 = (f32[136,512]{1,0:T(8,128)S(1)}, f32[136,512]{1,0:T(8,128)S(1)}, u32[]{:S(2)}, u32[]{:S(2)}) collective-permute-start(f32[136,512]{1,0:T(8,128)S(1)} %get-tuple-element.114.own_ref), channel_id=1, source_target_pairs={{0,4},{4,0},{8,12},{12,8},{16,20},{20,16},{24,28},{28,24},{32,36},... | collective-permute-start | bytes 835592 | tf_op jit(solution)/shard_map/ppermute | solution.py:431
  72.9 25.2 %collective-permute-start.20 = (f32[512,512]{1,0:T(8,128)S(1)}, f32[512,512]{1,0:T(8,128)S(1)}, u32[]{:S(2)}, u32[]{:S(2)}) collective-permute-start(f32[512,512]{1,0:T(8,128)S(1)} %get-tuple-element.113.refs_5_), channel_id=1, source_target_pairs={{0,4},{4,0},{8,12},{12,8},{16,20},{20,16},{24,28},{28,24},{32,36},... | collective-permute-start | bytes 3145736 | tf_op jit(solution)/shard_map/ppermute | solution.py:434
  73.0 25.1 %collective-permute-start.19 = (f32[512,512]{1,0:T(8,128)S(1)}, f32[512,512]{1,0:T(8,128)S(1)}, u32[]{:S(2)}, u32[]{:S(2)}) collective-permute-start(f32[512,512]{1,0:T(8,128)S(1)} %get-tuple-element.113.refs_5_), channel_id=1, source_target_pairs={{0,8},{4,36},{8,0},{12,44},{16,24},{20,52},{24,16},{28,60},{32,40}... | collective-permute-start | bytes 3145736 | tf_op jit(solution)/shard_map/ppermute | solution.py:432
  74.5 23.5 %collective-permute-start.22 = (f32[256,512]{1,0:T(8,128)S(1)}, f32[256,512]{1,0:T(8,128)S(1)}, u32[]{:S(2)}, u32[]{:S(2)}) collective-permute-start(f32[256,512]{1,0:T(8,128)S(1)} %get-tuple-element.120), channel_id=1, source_target_pairs={{0,2},{1,3},{2,0},{3,1},{4,6},{5,7},{6,4},{7,5},{8,10},{9,11},{10,... | collective-permute-start | bytes 1572872 | tf_op jit(solution)/shard_map/ppermute | solution.py:433
  98.0 4.7 %copy-start.1 = (f32[256,2048]{1,0:T(8,128)S(1)}, f32[256,2048]{1,0:T(8,128)}, u32[]{:S(2)}) copy-start(f32[256,2048]{1,0:T(8,128)} %refs_9_.1) | copy-start | bytes 6291460
  98.1 4.6 %collective-permute-start.23 = (f32[512,512]{1,0:T(8,128)S(1)}, f32[512,512]{1,0:T(8,128)S(1)}, u32[]{:S(2)}, u32[]{:S(2)}) collective-permute-start(f32[512,512]{1,0:T(8,128)S(1)} %collective-permute-done.19.refs_6_), channel_id=1, source_target_pairs={{0,4},{4,0},{8,12},{12,8},{16,20},{20,16},{24,28},{28,24},{32,36},... | collective-permute-start | bytes 3145736 | tf_op jit(solution)/shard_map/ppermute | solution.py:438

commit v18 on v17

--- a/solution.py
+++ b/solution.py
@@ -427,7 +427,7 @@
     )
     for hop in (1, 3):
         pieces[hop] = lax.ppermute(pieces[hop], "col", ring[hop])
-    block, gathered, far, *pieces = lax.optimization_barrier((block, gathered, far, *pieces))
+    block, gathered, *pieces = lax.optimization_barrier((block, gathered, *pieces))
     other = lax.ppermute(block, "row", swap)
     late = lax.ppermute(gathered, "row", every[0])
     pieces[2] = lax.ppermute(pieces[2], "col", ring[2])

time: 111 us -> 116 us (1.045)
  the two profiles are of different devices: /device:TPU:9 before, /device:TPU:1 now
where the time goes in v18:
time: 116 us; the launch traced here: 115 us
  starting transfers between devices  41.7 us (36%)
  waiting for transfers between devices  36.9 us (32%)
  Pallas kernels  32.8 us (28%)
  local copies, waits for them, and re-layouts  2.73 us (2%)
    pallas_call x9, Pallas kernels, call(): pl.pallas_call(kernel, out_shape=[jax.ShapeDtypeStruct(shape, jnp.float32...  21.8 us
    ppermute x3, waiting for transfers between devices, shards(): parts[hop] = lax.ppermute(parts[hop], 'row', pairs)  12.5 us
    ppermute x1, waiting for transfers between devices, shards(): lax.ppermute(load, 'row', every[3])  9.27 us
    pallas_call x1, Pallas kernels, update(): pl.pallas_call(update_kernel, out_shape=jax.ShapeDtypeStruct(base.shape,...  8.11 us
    ppermute x3, starting transfers between devices, shards(): lax.ppermute(blocks[0], ('row', 'col'), [(4 * core, 4 * core + to) for co...  7.47 us
    ppermute x1, starting transfers between devices, shards(): other = lax.ppermute(block, 'row', swap)  6.63 us
    ppermute x1, waiting for transfers between devices, shards(): far[1] = lax.ppermute(far[1], 'col', onward)  5.2 us
    ppermute x1, starting transfers between devices, shards(): far = [lax.ppermute(hold[:, :PW], 'col', onward), hold[:, PW:]]  5.12 us
  transfers between devices with their start and end apart: 24, of which 8 were waited for; matrix products, arithmetic and copies ran while one was open for 0% of the time, Pallas kernels for 21%

profile of v18, /device:TPU:1, one launch (start us, length us, event | category | flops | bytes accessed | tf_op | source)
XLA Modules:
  0.0 115.3 jit_solution(7591108925254587544)
XLA Ops:
  0.6 1.1 slice.9.lead_ref.refs_0_
  1.7 1.5 %collective-permute-start.3 = (f32[256,512]{1,0:T(8,128)S(1)}, f32[256,512]{1,0:T(8,128)S(1)}, u32[]{:S(2)}, u32[]{:S(2)}) collective-permute-start(f32[256,512]{1,0:T(8,128)S(1)} %slice.9.lead_ref.refs_0_), channel_id=1, source_target_pairs={{0,4},{4,0},{8,12},{12,8},{16,20},{20,16},{24,28},{28,24},{32,36},... | collective-permute-start | bytes 1572872 | tf_op jit(solution)/shard_map/ppermute | solution.py:397
  3.3 0.0 copy-start
  3.3 4.9 %collective-permute-start.2 = (f32[136,512]{1,0:T(8,128)S(1)}, f32[136,512]{1,0:T(8,128)S(1)}, u32[]{:S(2)}, u32[]{:S(2)}) collective-permute-start(f32[136,512]{1,0:T(8,128)S(1)} %corner.1), channel_id=1, source_target_pairs={{0,3},{4,7}} | collective-permute-start | bytes 835592 | tf_op jit(solution)/shard_map/ppermute | solution.py:395
  8.2 1.3 %collective-permute-start.1 = (f32[136,512]{1,0:T(8,128)S(1)}, f32[136,512]{1,0:T(8,128)S(1)}, u32[]{:S(2)}, u32[]{:S(2)}) collective-permute-start(f32[136,512]{1,0:T(8,128)S(1)} %corner.1), channel_id=1, source_target_pairs={{0,2},{4,6}} | collective-permute-start | bytes 835592 | tf_op jit(solution)/shard_map/ppermute | solution.py:395
  9.5 1.3 %collective-permute-start = (f32[136,512]{1,0:T(8,128)S(1)}, f32[136,512]{1,0:T(8,128)S(1)}, u32[]{:S(2)}, u32[]{:S(2)}) collective-permute-start(f32[136,512]{1,0:T(8,128)S(1)} %corner.1), channel_id=1, source_target_pairs={{0,1},{4,5}} | collective-permute-start | bytes 835592 | tf_op jit(solution)/shard_map/ppermute | solution.py:395
  10.8 0.0 collective-permute-done.3.mate_ref
  10.8 0.1 share.1
  10.9 1.3 %collective-permute-start.4 = (f32[2,32,512]{2,1,0:T(8,128)S(1)}, f32[2,32,512]{2,1,0:T(8,128)S(1)}, u32[]{:S(2)}, u32[]{:S(2)}) collective-permute-start(f32[2,32,512]{2,1,0:T(8,128)S(1)} %get-tuple-element.67), channel_id=1, source_target_pairs={{8,16},{12,20},{16,24},{20,28},{24,0},{28,4},{32,40},{36,44},{40,4... | collective-permute-start | bytes 393224 | tf_op jit(solution)/shard_map/ppermute | solution.py:401
  12.2 1.3 %collective-permute-start.5 = (f32[2,32,512]{2,1,0:T(8,128)S(1)}, f32[2,32,512]{2,1,0:T(8,128)S(1)}, u32[]{:S(2)}, u32[]{:S(2)}) collective-permute-start(f32[2,32,512]{2,1,0:T(8,128)S(1)} %get-tuple-element.68), channel_id=1, source_target_pairs={{8,24},{12,28},{16,0},{20,4},{24,8},{28,12},{32,48},{36,52},{40,56... | collective-permute-start | bytes 393224 | tf_op jit(solution)/shard_map/ppermute | solution.py:401
  13.5 8.1 %collective-permute-done.4.refs_1_ = f32[2,32,512]{2,1,0:T(8,128)S(1)} collective-permute-done((f32[2,32,512]{2,1,0:T(8,128)S(1)}, f32[2,32,512]{2,1,0:T(8,128)S(1)}, u32[]{:S(2)}, u32[]{:S(2)}) %collective-permute-start.4) | collective-permute-done | bytes 131104 | tf_op jit(solution)/shard_map/ppermute | solution.py:401
  21.6 1.3 %collective-permute-start.6 = (f32[2,32,512]{2,1,0:T(8,128)S(1)}, f32[2,32,512]{2,1,0:T(8,128)S(1)}, u32[]{:S(2)}, u32[]{:S(2)}) collective-permute-start(f32[2,32,512]{2,1,0:T(8,128)S(1)} %get-tuple-element.69), channel_id=1, source_target_pairs={{8,0},{12,4},{16,8},{20,12},{24,16},{28,20},{32,56},{36,60},{40,32... | collective-permute-start | bytes 393224 | tf_op jit(solution)/shard_map/ppermute | solution.py:401
  22.9 0.0 collective-permute-done.5.refs_2_
  22.9 4.4 %collective-permute-done.6.refs_3_ = f32[2,32,512]{2,1,0:T(8,128)S(1)} collective-permute-done((f32[2,32,512]{2,1,0:T(8,128)S(1)}, f32[2,32,512]{2,1,0:T(8,128)S(1)}, u32[]{:S(2)}, u32[]{:S(2)}) %collective-permute-start.6) | collective-permute-done | bytes 131104 | tf_op jit(solution)/shard_map/ppermute | solution.py:401
  27.3 1.0 sort.1
  28.3 0.0 collective-permute-done.2
  28.3 0.0 collective-permute-done.1
  28.3 0.0 collective-permute-done
  28.3 0.1 add_add_fusion.refs_4_
  28.4 1.3 %collective-permute-start.7 = (f32[136,512]{1,0:T(8,128)S(1)}, f32[136,512]{1,0:T(8,128)S(1)}, u32[]{:S(2)}, u32[]{:S(2)}) collective-permute-start(f32[136,512]{1,0:T(8,128)S(1)} %add_add_fusion.refs_4_), channel_id=1, source_target_pairs={{0,8},{4,36},{1,9},{5,37},{2,10},{6,38},{3,11},{7,39}} | collective-permute-start | bytes 835592 | tf_op jit(solution)/shard_map/ppermute | solution.py:409
  29.7 1.3 %collective-permute-start.8 = (f32[2,32,512]{2,1,0:T(8,128)S(1)}, f32[2,32,512]{2,1,0:T(8,128)S(1)}, u32[]{:S(2)}, u32[]{:S(2)}) collective-permute-start(f32[2,32,512]{2,1,0:T(8,128)S(1)} %get-tuple-element.79), channel_id=1, source_target_pairs={{0,1},{4,5},{8,9},{12,13},{16,17},{20,21},{24,25},{28,29},{32,33},... | collective-permute-start | bytes 393224 | tf_op jit(solution)/shard_map/ppermute | solution.py:407
  31.0 1.3 %collective-permute-start.9 = (f32[2,32,512]{2,1,0:T(8,128)S(1)}, f32[2,32,512]{2,1,0:T(8,128)S(1)}, u32[]{:S(2)}, u32[]{:S(2)}) collective-permute-start(f32[2,32,512]{2,1,0:T(8,128)S(1)} %get-tuple-element.80), channel_id=1, source_target_pairs={{0,2},{4,6},{8,10},{12,14},{16,18},{20,22},{24,26},{28,30},{32,34}... | collective-permute-start | bytes 393224 | tf_op jit(solution)/shard_map/ppermute | solution.py:407
  32.3 1.3 %collective-permute-start.10 = (f32[2,32,512]{2,1,0:T(8,128)S(1)}, f32[2,32,512]{2,1,0:T(8,128)S(1)}, u32[]{:S(2)}, u32[]{:S(2)}) collective-permute-start(f32[2,32,512]{2,1,0:T(8,128)S(1)} %get-tuple-element.81), channel_id=1, source_target_pairs={{0,3},{4,7},{8,11},{12,15},{16,19},{20,23},{24,27},{28,31},{32,35}... | collective-permute-start | bytes 393224 | tf_op jit(solution)/shard_map/ppermute | solution.py:407
  33.7 0.0 collective-permute-done.8.refs_1_
  33.7 0.7 collective-permute-done.9.refs_2_
  34.3 1.2 %collective-permute-done.10.refs_3_ = f32[2,32,512]{2,1,0:T(8,128)S(1)} collective-permute-done((f32[2,32,512]{2,1,0:T(8,128)S(1)}, f32[2,32,512]{2,1,0:T(8,128)S(1)}, u32[]{:S(2)}, u32[]{:S(2)}) %collective-permute-start.10) | collective-permute-done | bytes 131104 | tf_op jit(solution)/shard_map/ppermute | solution.py:407
  35.6 0.0 collective-permute-done.7.refs_5_
  35.6 0.1 merge.1.own_ref
  35.6 0.1 collective-permute-start.11
  35.7 1.3 %collective-permute-start.12 = (f32[256,512]{1,0:T(8,128)S(1)}, f32[256,512]{1,0:T(8,128)S(1)}, u32[]{:S(2)}, u32[]{:S(2)}) collective-permute-start(f32[256,512]{1,0:T(8,128)S(1)} %slice.9.lead_ref.refs_0_), channel_id=1, source_target_pairs={{0,1},{4,5},{8,9},{12,13},{16,17},{20,21},{24,25},{28,29},{32,33},... | collective-permute-start | bytes 1572872 | tf_op jit(solution)/shard_map/ppermute | solution.py:416
  37.1 2.0 %pick.1 = (f32[256,512]{1,0:T(8,128)S(1)}, f32[256,512]{1,0:T(8,128)S(1)}, f32[256,512]{1,0:T(8,128)S(1)}, f32[256,512]{1,0:T(8,128)S(1)}, s32[4,8]{1,0:T(4,128)S(1)}) custom-call(s32[32]{0:T(128)S(1)} %copy-done.2, f32[256,2048]{1,0:T(8,128)S(1)} %copy-done), custom_call_target="tpu_custom_call" | custom-call | flops 1024 | bytes 1024 | tf_op jit(solution)/shard_map/pick/pallas_call | solution.py:109
  39.1 0.0 copy-start.3
  39.1 0.8 copy-done.3
  39.9 0.8 copy-done.5
  40.7 4.8 %collective-permute-done.11.got_ref = f32[264,512]{1,0:T(8,128)S(1)} collective-permute-done((f32[264,512]{1,0:T(8,128)S(1)}, f32[264,512]{1,0:T(8,128)S(1)}, u32[]{:S(2)}, u32[]{:S(2)}) %collective-permute-start.11) | collective-permute-done | bytes 540704 | tf_op jit(solution)/shard_map/ppermute | solution.py:417
  45.5 0.0 collective-permute-done.12.refs_1_
  45.5 0.0 copy-start.6
  45.5 0.0 copy-start.4
  45.5 0.1 collective-permute-start.13
  45.6 0.1 broadcast_select_fusion
  45.7 5.1 %collective-permute-start.14 = (f32[256,256]{1,0:T(8,128)S(1)}, f32[256,256]{1,0:T(8,128)S(1)}, u32[]{:S(2)}, u32[]{:S(2)}) collective-permute-start(f32[256,256]{1,0:T(8,128)S(1)} %get-tuple-element.131), channel_id=1, source_target_pairs={{0,3},{1,2},{4,7},{5,6},{8,11},{9,10},{12,15},{13,14},{16,19},{17,... | collective-permute-start | bytes 786440 | tf_op jit(solution)/shard_map/ppermute | solution.py:421
  50.9 3.2 %collective-permute-done.13.got_ref = f32[264,512]{1,0:T(8,128)S(1)} collective-permute-done((f32[264,512]{1,0:T(8,128)S(1)}, f32[264,512]{1,0:T(8,128)S(1)}, u32[]{:S(2)}, u32[]{:S(2)}) %collective-permute-start.13) | collective-permute-done | bytes 540704 | tf_op jit(solution)/shard_map/ppermute | solution.py:422
  54.1 0.1 join.4.own_ref
  54.2 0.0 collective-permute-done.14.refs_2_
  54.2 0.1 collective-permute-start.16
  54.3 1.5 %collective-permute-start.17 = (f32[256,512]{1,0:T(8,128)S(1)}, f32[256,512]{1,0:T(8,128)S(1)}, u32[]{:S(2)}, u32[]{:S(2)}) collective-permute-start(f32[256,512]{1,0:T(8,128)S(1)} %copy-done.6), channel_id=1, source_target_pairs={{0,1},{1,2},{2,3},{3,0},{4,5},{5,6},{6,7},{7,4},{8,9},{9,10},{10,1... | collective-permute-start | bytes 1572872 | tf_op jit(solution)/shard_map/ppermute | solution.py:429
  55.8 1.7 %collective-permute-start.18 = (f32[256,512]{1,0:T(8,128)S(1)}, f32[256,512]{1,0:T(8,128)S(1)}, u32[]{:S(2)}, u32[]{:S(2)}) collective-permute-start(f32[256,512]{1,0:T(8,128)S(1)} %copy-done.4), channel_id=1, source_target_pairs={{0,3},{1,0},{2,1},{3,2},{4,7},{5,4},{6,5},{7,6},{8,11},{9,8},{10,9... | collective-permute-start | bytes 1572872 | tf_op jit(solution)/shard_map/ppermute | solution.py:429
  57.5 9.3 %collective-permute-done.16.got_ref = f32[392,512]{1,0:T(8,128)S(1)} collective-permute-done((f32[392,512]{1,0:T(8,128)S(1)}, f32[392,512]{1,0:T(8,128)S(1)}, u32[]{:S(2)}, u32[]{:S(2)}) %collective-permute-start.16) | collective-permute-done | bytes 802848 | tf_op jit(solution)/shard_map/ppermute | solution.py:426
  66.8 0.1 join.5
  66.9 0.0 collective-permute-done.18.refs_4_
  66.9 6.6 %collective-permute-start.21 = (f32[136,512]{1,0:T(8,128)S(1)}, f32[136,512]{1,0:T(8,128)S(1)}, u32[]{:S(2)}, u32[]{:S(2)}) collective-permute-start(f32[136,512]{1,0:T(8,128)S(1)} %get-tuple-element.110.own_ref), channel_id=1, source_target_pairs={{0,4},{4,0},{8,12},{12,8},{16,20},{20,16},{24,28},{28,24},{32,36},... | collective-permute-start | bytes 835592 | tf_op jit(solution)/shard_map/ppermute | solution.py:431
  73.5 0.1 collective-permute-start.20
  73.6 1.4 %collective-permute-start.19 = (f32[512,512]{1,0:T(8,128)S(1)}, f32[512,512]{1,0:T(8,128)S(1)}, u32[]{:S(2)}, u32[]{:S(2)}) collective-permute-start(f32[512,512]{1,0:T(8,128)S(1)} %get-tuple-element.109.refs_5_), channel_id=1, source_target_pairs={{0,8},{4,36},{8,0},{12,44},{16,24},{20,52},{24,16},{28,60},{32,40}... | collective-permute-start | bytes 3145736 | tf_op jit(solution)/shard_map/ppermute | solution.py:432
  75.0 1.6 %collective-permute-start.22 = (f32[256,512]{1,0:T(8,128)S(1)}, f32[256,512]{1,0:T(8,128)S(1)}, u32[]{:S(2)}, u32[]{:S(2)}) collective-permute-start(f32[256,512]{1,0:T(8,128)S(1)} %get-tuple-element.116), channel_id=1, source_target_pairs={{0,2},{1,3},{2,0},{3,1},{4,6},{5,7},{6,4},{7,5},{8,10},{9,11},{10,... | collective-permute-start | bytes 1572872 | tf_op jit(solution)/shard_map/ppermute | solution.py:433
  76.6 0.0 collective-permute-done.21.other_ref
  76.6 18.4 %factor.1 = (f32[256,256]{1,0:T(8,128)S(1)}, f32[256,256]{1,0:T(8,128)S(1)}, f32[256,256]{1,0:T(8,128)S(1)}) custom-call(f32[136,512]{1,0:T(8,128)S(1)} %get-tuple-element.110.own_ref, f32[136,512]{1,0:T(8,128)S(1)} %collective-permute-done.21.other_ref), custom_call_target="tpu_custom_call" | custom-call | flops 21474836480 | bytes 1048576 | tf_op jit(solution)/shard_map/factor/pallas_call | solution.py:109
  95.0 0.0 copy-start.1
  95.1 0.0 collective-permute-done.22.refs_3_
  95.1 0.5 collective-permute-start.23
  95.6 3.5 %collective-permute-start.15 = (f32[256,256]{1,0:T(8,128)S(1)}, f32[256,256]{1,0:T(8,128)S(1)}, u32[]{:S(2)}, u32[]{:S(2)}) collective-permute-start(f32[256,256]{1,0:T(8,128)S(1)} %get-tuple-element.101), channel_id=1, source_target_pairs={{0,3},{1,2},{4,7},{5,6},{8,11},{9,10},{12,15},{13,14},{16,19},{17,... | collective-permute-start | bytes 786440 | tf_op jit(solution)/shard_map/ppermute | solution.py:424
  99.1 5.2 %collective-permute-done.15.refs_3_ = f32[256,256]{1,0:T(8,128)S(1)} collective-permute-done((f32[256,256]{1,0:T(8,128)S(1)}, f32[256,256]{1,0:T(8,128)S(1)}, u32[]{:S(2)}, u32[]{:S(2)}) %collective-permute-start.15) | collective-permute-done | bytes 262176 | tf_op jit(solution)/shard_map/ppermute | solution.py:424
  104.3 2.9 %weigh.1 = (f32[256,512]{1,0:T(8,128)}, f32[256,512]{1,0:T(8,128)S(1)}) custom-call(f32[256,512]{1,0:T(8,128)S(1)} %slice.9.lead_ref.refs_0_, f32[256,512]{1,0:T(8,128)S(1)} %collective-permute-done.12.refs_1_, f32[256,256]{1,0:T(8,128)S(1)} %collective-permute-done.14.refs_2_, f32[256,256]{1,0:T(8,128)S(1)} %collective-permute-done.15.refs_3_, ...), custom_call_target="tpu_custom_call" | custom-call | flops 1024 | bytes 1024 | tf_op jit(solution)/shard_map/weigh/pallas_call | solution.py:307
  107.2 0.0 collective-permute-done.23.refs_8_
  107.2 8.1 %update.1 = f32[256,2048]{1,0:T(8,128)} custom-call(s32[4,8]{1,0:T(4,128)S(1)} %get-tuple-element.122.plan, f32[256,512]{1,0:T(8,128)S(1)} %get-tuple-element.123.refs_0_, f32[256,512]{1,0:T(8,128)S(1)} %get-tuple-element.124.refs_1_, f32[256,512]{1,0:T(8,128)S(1)} %collective-permute-done.17.refs_2_, f32[256,512]{1,0:T(8,128)S(1)} %collective-permute-done.22.refs_3_, ...), custom_call_target="tpu_custom_call" | custom-call | tf_op jit(solution)/shard_map/update/pallas_call | solution.py:356
  (13 shorter events, 0.2 us)
Async XLA Ops:
  0.6 26.7 %copy-start.2 = (s32[32]{0:T(128)S(1)}, s32[32]{0:T(128)}, u32[]{:S(2)}) copy-start(s32[32]{0:T(128)} %map_ref.3) | copy-start | bytes 388
  1.7 9.1 %collective-permute-start.3 = (f32[256,512]{1,0:T(8,128)S(1)}, f32[256,512]{1,0:T(8,128)S(1)}, u32[]{:S(2)}, u32[]{:S(2)}) collective-permute-start(f32[256,512]{1,0:T(8,128)S(1)} %slice.9.lead_ref.refs_0_), channel_id=1, source_target_pairs={{0,4},{4,0},{8,12},{12,8},{16,20},{20,16},{24,28},{28,24},{32,36},... | collective-permute-start | bytes 1572872 | tf_op jit(solution)/shard_map/ppermute | solution.py:397
  3.3 33.8 %copy-start = (f32[256,2048]{1,0:T(8,128)S(1)}, f32[256,2048]{1,0:T(8,128)}, u32[]{:S(2)}) copy-start(f32[256,2048]{1,0:T(8,128)} %front_ref.1) | copy-start | bytes 6291460
  3.3 25.0 %collective-permute-start.2 = (f32[136,512]{1,0:T(8,128)S(1)}, f32[136,512]{1,0:T(8,128)S(1)}, u32[]{:S(2)}, u32[]{:S(2)}) collective-permute-start(f32[136,512]{1,0:T(8,128)S(1)} %corner.1), channel_id=1, source_target_pairs={{0,3},{4,7}} | collective-permute-start | bytes 835592 | tf_op jit(solution)/shard_map/ppermute | solution.py:395
  8.2 20.1 %collective-permute-start.1 = (f32[136,512]{1,0:T(8,128)S(1)}, f32[136,512]{1,0:T(8,128)S(1)}, u32[]{:S(2)}, u32[]{:S(2)}) collective-permute-start(f32[136,512]{1,0:T(8,128)S(1)} %corner.1), channel_id=1, source_target_pairs={{0,2},{4,6}} | collective-permute-start | bytes 835592 | tf_op jit(solution)/shard_map/ppermute | solution.py:395
  9.5 18.8 %collective-permute-start = (f32[136,512]{1,0:T(8,128)S(1)}, f32[136,512]{1,0:T(8,128)S(1)}, u32[]{:S(2)}, u32[]{:S(2)}) collective-permute-start(f32[136,512]{1,0:T(8,128)S(1)} %corner.1), channel_id=1, source_target_pairs={{0,1},{4,5}} | collective-permute-start | bytes 835592 | tf_op jit(solution)/shard_map/ppermute | solution.py:395
  10.9 10.7 %collective-permute-start.4 = (f32[2,32,512]{2,1,0:T(8,128)S(1)}, f32[2,32,512]{2,1,0:T(8,128)S(1)}, u32[]{:S(2)}, u32[]{:S(2)}) collective-permute-start(f32[2,32,512]{2,1,0:T(8,128)S(1)} %get-tuple-element.67), channel_id=1, source_target_pairs={{8,16},{12,20},{16,24},{20,28},{24,0},{28,4},{32,40},{36,44},{40,4... | collective-permute-start | bytes 393224 | tf_op jit(solution)/shard_map/ppermute | solution.py:401
  12.2 10.7 %collective-permute-start.5 = (f32[2,32,512]{2,1,0:T(8,128)S(1)}, f32[2,32,512]{2,1,0:T(8,128)S(1)}, u32[]{:S(2)}, u32[]{:S(2)}) collective-permute-start(f32[2,32,512]{2,1,0:T(8,128)S(1)} %get-tuple-element.68), channel_id=1, source_target_pairs={{8,24},{12,28},{16,0},{20,4},{24,8},{28,12},{32,48},{36,52},{40,56... | collective-permute-start | bytes 393224 | tf_op jit(solution)/shard_map/ppermute | solution.py:401
  21.6 5.7 %collective-permute-start.6 = (f32[2,32,512]{2,1,0:T(8,128)S(1)}, f32[2,32,512]{2,1,0:T(8,128)S(1)}, u32[]{:S(2)}, u32[]{:S(2)}) collective-permute-start(f32[2,32,512]{2,1,0:T(8,128)S(1)} %get-tuple-element.69), channel_id=1, source_target_pairs={{8,0},{12,4},{16,8},{20,12},{24,16},{28,20},{32,56},{36,60},{40,32... | collective-permute-start | bytes 393224 | tf_op jit(solution)/shard_map/ppermute | solution.py:401
  28.4 7.2 %collective-permute-start.7 = (f32[136,512]{1,0:T(8,128)S(1)}, f32[136,512]{1,0:T(8,128)S(1)}, u32[]{:S(2)}, u32[]{:S(2)}) collective-permute-start(f32[136,512]{1,0:T(8,128)S(1)} %add_add_fusion.refs_4_), channel_id=1, source_target_pairs={{0,8},{4,36},{1,9},{5,37},{2,10},{6,38},{3,11},{7,39}} | collective-permute-start | bytes 835592 | tf_op jit(solution)/shard_map/ppermute | solution.py:409
  29.7 3.9 %collective-permute-start.8 = (f32[2,32,512]{2,1,0:T(8,128)S(1)}, f32[2,32,512]{2,1,0:T(8,128)S(1)}, u32[]{:S(2)}, u32[]{:S(2)}) collective-permute-start(f32[2,32,512]{2,1,0:T(8,128)S(1)} %get-tuple-element.79), channel_id=1, source_target_pairs={{0,1},{4,5},{8,9},{12,13},{16,17},{20,21},{24,25},{28,29},{32,33},... | collective-permute-start | bytes 393224 | tf_op jit(solution)/shard_map/ppermute | solution.py:407
  31.0 3.3 %collective-permute-start.9 = (f32[2,32,512]{2,1,0:T(8,128)S(1)}, f32[2,32,512]{2,1,0:T(8,128)S(1)}, u32[]{:S(2)}, u32[]{:S(2)}) collective-permute-start(f32[2,32,512]{2,1,0:T(8,128)S(1)} %get-tuple-element.80), channel_id=1, source_target_pairs={{0,2},{4,6},{8,10},{12,14},{16,18},{20,22},{24,26},{28,30},{32,34}... | collective-permute-start | bytes 393224 | tf_op jit(solution)/shard_map/ppermute | solution.py:407
  32.3 3.2 %collective-permute-start.10 = (f32[2,32,512]{2,1,0:T(8,128)S(1)}, f32[2,32,512]{2,1,0:T(8,128)S(1)}, u32[]{:S(2)}, u32[]{:S(2)}) collective-permute-start(f32[2,32,512]{2,1,0:T(8,128)S(1)} %get-tuple-element.81), channel_id=1, source_target_pairs={{0,3},{4,7},{8,11},{12,15},{16,19},{20,23},{24,27},{28,31},{32,35}... | collective-permute-start | bytes 393224 | tf_op jit(solution)/shard_map/ppermute | solution.py:407
  35.6 9.8 %collective-permute-start.11 = (f32[264,512]{1,0:T(8,128)S(1)}, f32[264,512]{1,0:T(8,128)S(1)}, u32[]{:S(2)}, u32[]{:S(2)}) collective-permute-start(f32[264,512]{1,0:T(8,128)S(1)} %merge.1.own_ref), channel_id=1, source_target_pairs={{0,24},{4,100},{8,16},{12,108},{16,8},{20,116},{24,0},{28,124},{32... | collective-permute-start | bytes 1622024 | tf_op jit(solution)/shard_map/ppermute | solution.py:417
  35.7 9.8 %collective-permute-start.12 = (f32[256,512]{1,0:T(8,128)S(1)}, f32[256,512]{1,0:T(8,128)S(1)}, u32[]{:S(2)}, u32[]{:S(2)}) collective-permute-start(f32[256,512]{1,0:T(8,128)S(1)} %slice.9.lead_ref.refs_0_), channel_id=1, source_target_pairs={{0,1},{4,5},{8,9},{12,13},{16,17},{20,21},{24,25},{28,29},{32,33},... | collective-permute-start | bytes 1572872 | tf_op jit(solution)/shard_map/ppermute | solution.py:416
  39.1 0.8 copy-start.3
  39.9 0.8 copy-start.5
  45.5 8.8 %copy-start.6 = (f32[256,512]{1,0:T(8,128)S(1)}, f32[256,512]{1,0:T(8,128)}, u32[]{:S(2)}) copy-start(f32[256,512]{1,0:T(8,128)} %copy-done.5) | copy-start | bytes 1572868
  45.5 10.3 %copy-start.4 = (f32[256,512]{1,0:T(8,128)S(1)}, f32[256,512]{1,0:T(8,128)}, u32[]{:S(2)}) copy-start(f32[256,512]{1,0:T(8,128)} %copy-done.3) | copy-start | bytes 1572868
  45.5 8.6 %collective-permute-start.13 = (f32[264,512]{1,0:T(8,128)S(1)}, f32[264,512]{1,0:T(8,128)S(1)}, u32[]{:S(2)}, u32[]{:S(2)}) collective-permute-start(f32[264,512]{1,0:T(8,128)S(1)} %join.3.own_ref), channel_id=1, source_target_pairs={{0,32},{4,12},{8,40},{12,4},{16,48},{20,28},{24,56},{28,20},{32,0}... | collective-permute-start | bytes 1622024 | tf_op jit(solution)/shard_map/ppermute | solution.py:422
  45.7 8.4 %collective-permute-start.14 = (f32[256,256]{1,0:T(8,128)S(1)}, f32[256,256]{1,0:T(8,128)S(1)}, u32[]{:S(2)}, u32[]{:S(2)}) collective-permute-start(f32[256,256]{1,0:T(8,128)S(1)} %get-tuple-element.131), channel_id=1, source_target_pairs={{0,3},{1,2},{4,7},{5,6},{8,11},{9,10},{12,15},{13,14},{16,19},{17,... | collective-permute-start | bytes 786440 | tf_op jit(solution)/shard_map/ppermute | solution.py:421
  54.2 12.6 %collective-permute-start.16 = (f32[392,512]{1,0:T(8,128)S(1)}, f32[392,512]{1,0:T(8,128)S(1)}, u32[]{:S(2)}, u32[]{:S(2)}) collective-permute-start(f32[392,512]{1,0:T(8,128)S(1)} %join.4.own_ref), channel_id=1, source_target_pairs={{0,96},{4,28},{8,104},{12,20},{16,112},{20,12},{24,120},{28,4},{32... | collective-permute-start | bytes 2408456 | tf_op jit(solution)/shard_map/ppermute | solution.py:426
  54.3 12.6 %collective-permute-start.17 = (f32[256,512]{1,0:T(8,128)S(1)}, f32[256,512]{1,0:T(8,128)S(1)}, u32[]{:S(2)}, u32[]{:S(2)}) collective-permute-start(f32[256,512]{1,0:T(8,128)S(1)} %copy-done.6), channel_id=1, source_target_pairs={{0,1},{1,2},{2,3},{3,0},{4,5},{5,6},{6,7},{7,4},{8,9},{9,10},{10,1... | collective-permute-start | bytes 1572872 | tf_op jit(solution)/shard_map/ppermute | solution.py:429
  55.8 11.1 %collective-permute-start.18 = (f32[256,512]{1,0:T(8,128)S(1)}, f32[256,512]{1,0:T(8,128)S(1)}, u32[]{:S(2)}, u32[]{:S(2)}) collective-permute-start(f32[256,512]{1,0:T(8,128)S(1)} %copy-done.4), channel_id=1, source_target_pairs={{0,3},{1,0},{2,1},{3,2},{4,7},{5,4},{6,5},{7,6},{8,11},{9,8},{10,9... | collective-permute-start | bytes 1572872 | tf_op jit(solution)/shard_map/ppermute | solution.py:429
  66.9 9.7 %collective-permute-start.21 = (f32[136,512]{1,0:T(8,128)S(1)}, f32[136,512]{1,0:T(8,128)S(1)}, u32[]{:S(2)}, u32[]{:S(2)}) collective-permute-start(f32[136,512]{1,0:T(8,128)S(1)} %get-tuple-element.110.own_ref), channel_id=1, source_target_pairs={{0,4},{4,0},{8,12},{12,8},{16,20},{20,16},{24,28},{28,24},{32,36},... | collective-permute-start | bytes 835592 | tf_op jit(solution)/shard_map/ppermute | solution.py:431
  73.5 21.5 %collective-permute-start.20 = (f32[512,512]{1,0:T(8,128)S(1)}, f32[512,512]{1,0:T(8,128)S(1)}, u32[]{:S(2)}, u32[]{:S(2)}) collective-permute-start(f32[512,512]{1,0:T(8,128)S(1)} %get-tuple-element.109.refs_5_), channel_id=1, source_target_pairs={{0,4},{4,0},{8,12},{12,8},{16,20},{20,16},{24,28},{28,24},{32,36},... | collective-permute-start | bytes 3145736 | tf_op jit(solution)/shard_map/ppermute | solution.py:434
  73.6 21.5 %collective-permute-start.19 = (f32[512,512]{1,0:T(8,128)S(1)}, f32[512,512]{1,0:T(8,128)S(1)}, u32[]{:S(2)}, u32[]{:S(2)}) collective-permute-start(f32[512,512]{1,0:T(8,128)S(1)} %get-tuple-element.109.refs_5_), channel_id=1, source_target_pairs={{0,8},{4,36},{8,0},{12,44},{16,24},{20,52},{24,16},{28,60},{32,40}... | collective-permute-start | bytes 3145736 | tf_op jit(solution)/shard_map/ppermute | solution.py:432
  75.0 20.0 %collective-permute-start.22 = (f32[256,512]{1,0:T(8,128)S(1)}, f32[256,512]{1,0:T(8,128)S(1)}, u32[]{:S(2)}, u32[]{:S(2)}) collective-permute-start(f32[256,512]{1,0:T(8,128)S(1)} %get-tuple-element.116), channel_id=1, source_target_pairs={{0,2},{1,3},{2,0},{3,1},{4,6},{5,7},{6,4},{7,5},{8,10},{9,11},{10,... | collective-permute-start | bytes 1572872 | tf_op jit(solution)/shard_map/ppermute | solution.py:433
  95.0 12.2 %copy-start.1 = (f32[256,2048]{1,0:T(8,128)S(1)}, f32[256,2048]{1,0:T(8,128)}, u32[]{:S(2)}) copy-start(f32[256,2048]{1,0:T(8,128)} %refs_9_.1) | copy-start | bytes 6291460
  95.1 12.1 %collective-permute-start.23 = (f32[512,512]{1,0:T(8,128)S(1)}, f32[512,512]{1,0:T(8,128)S(1)}, u32[]{:S(2)}, u32[]{:S(2)}) collective-permute-start(f32[512,512]{1,0:T(8,128)S(1)} %collective-permute-done.19.refs_6_), channel_id=1, source_target_pairs={{0,4},{4,0},{8,12},{12,8},{16,20},{20,16},{24,28},{28,24},{32,36},... | collective-permute-start | bytes 3145736 | tf_op jit(solution)/shard_map/ppermute | solution.py:438
  95.6 8.7 %collective-permute-start.15 = (f32[256,256]{1,0:T(8,128)S(1)}, f32[256,256]{1,0:T(8,128)S(1)}, u32[]{:S(2)}, u32[]{:S(2)}) collective-permute-start(f32[256,256]{1,0:T(8,128)S(1)} %get-tuple-element.101), channel_id=1, source_target_pairs={{0,3},{1,2},{4,7},{5,6},{8,11},{9,10},{12,15},{13,14},{16,19},{17,... | collective-permute-start | bytes 786440 | tf_op jit(solution)/shard_map/ppermute | solution.py:424
